TPU v7x, 32 devices: a whole 2x2x4 slice. The times are simulated.
32 devices in a mesh: dp: 8 (over y, x, core), tensor: 4 (over z).
Axes of the slice: x: 2, y: 2, z: 4, core: 2. Of those that a mesh axis runs over, the one named last changes fastest.
Arguments:
- tokens: bfloat16 [16384, 2048], P(('dp', 'tensor')), may hold values from -6 to 6
- upstream: bfloat16 [16384, 2048], P(('dp', 'tensor')), may hold values from -8 to 8
- lengths: int32 [8, 3], P('dp'), may hold values from 1 to 1024, 1792 in all within a row
- permutation: int32 [8, 2048], P('dp'), may hold values from 0 to 2047, each once within a row
- w_query: bfloat16 [2048, 2048], P('dp', 'tensor'), may hold values from -2 to 2
- w_key: bfloat16 [2048, 2048], P('dp', 'tensor'), may hold values from -2 to 2
- w_value: bfloat16 [2048, 2048], P('dp', 'tensor'), may hold values from -0.125 to 0.125
- w_out: bfloat16 [2048, 2048], P('tensor', 'dp'), may hold values from -2 to 2
- w_gate: bfloat16 [2048, 8192], P('dp', 'tensor'), may hold values from -0.125 to 0.125
- w_up: bfloat16 [2048, 8192], P('dp', 'tensor'), may hold values from -0.125 to 0.125
- w_down: bfloat16 [8192, 2048], P('tensor', 'dp'), may hold values from -2 to 2
- q_gain: float32 [2048], replicated, may hold values from 0.25 to 1.75
- k_gain: float32 [2048], replicated, may hold values from 0.25 to 1.75
- attn_gain: float32 [2048], replicated, may hold values from 0.25 to 1.75
- ffn_gain: float32 [2048], replicated, may hold values from 0.25 to 1.75
Outputs:
- layer_out: bfloat16 [16384, 2048], P(('dp', 'tensor'))
- tokens_grad: bfloat16 [16384, 2048], P(('dp', 'tensor'))
- w_query_grad: float32 [2048, 2048], P('dp', 'tensor')
- w_key_grad: float32 [2048, 2048], P('dp', 'tensor')
- w_value_grad: float32 [2048, 2048], P('dp', 'tensor')
- w_out_grad: float32 [2048, 2048], P('tensor', 'dp')
- w_gate_grad: float32 [2048, 8192], P('dp', 'tensor')
- w_up_grad: float32 [2048, 8192], P('dp', 'tensor')
- w_down_grad: float32 [8192, 2048], P('tensor', 'dp')
- q_gain_grad: float32 [2048], replicated
- k_gain_grad: float32 [2048], replicated
- attn_gain_grad: float32 [2048], replicated
- ffn_gain_grad: float32 [2048], replicated
Inputs may be any that keep to these rules, and one draw needn't show every extreme that they name: Each group's row of lengths sums to 1792, and its longest sequence has 1024 tokens. `permutation`: each group's row holds every slot number once.
All inputs are finite; a program needn't handle non-finite values.
Results may differ from a plain program's by a relative error of at most 0.019.
The roundings to bfloat16 on the way count: a program that leaves them out, or rounds other values in their place, can miss the bound.
Values may be sent and summed in bfloat16 or wider, within the bound.
A program may use at most 320 MiB of HBM per device.

v0:
```python
import math

import jax
import jax.numpy as jnp
from jax import lax
from jax.sharding import PartitionSpec as P

D = 2048
HDIM = 128


epsilon = 1e-06
rope_base = 500000.0
masked_score = -1e30


def layout(length_row, group_rows):
    positions = jnp.arange(group_rows, dtype=jnp.int32)
    seq_ends = jnp.cumsum(length_row)
    seq_starts = seq_ends - length_row
    segment = jnp.sum((positions[:, None] >= seq_ends[None, :]).astype(jnp.int32), axis=1)
    chosen = segment[:, None] == jnp.arange(length_row.shape[0], dtype=jnp.int32)[None, :]
    offsets = jnp.sum(jnp.where(chosen, seq_starts[None, :], 0), axis=1)
    return (segment, positions - offsets)


def rotary_tables(position):
    half_dim = HDIM // 2
    exponents = jnp.arange(half_dim, dtype=jnp.float32) * (2.0 / HDIM)
    frequency = jnp.power(jnp.float32(rope_base), -exponents)
    angles = position.astype(jnp.float32)[:, None] * frequency[None, :]
    return (jnp.cos(angles), jnp.sin(angles))


def rotate(values, cosine, sine_part):
    half_dim = HDIM // 2
    first_half = values[..., :half_dim]
    second_half = values[..., half_dim:]
    cos_rows = cosine[:, None, :]
    sin_rows = sine_part[:, None, :]
    return jnp.concatenate(
        [
            first_half * cos_rows - second_half * sin_rows,
            second_half * cos_rows + first_half * sin_rows,
        ],
        axis=-1,
    )


def allowed_block(segment, first_row, block_rows, seq_count):
    query_seg = lax.dynamic_slice_in_dim(segment, first_row, block_rows)
    query_pos = first_row + jnp.arange(block_rows, dtype=jnp.int32)
    key_pos = jnp.arange(segment.shape[0], dtype=jnp.int32)
    same_seq = (
        (query_seg[:, None] == segment[None, :])
        & (query_seg[:, None] < seq_count)
        & (key_pos[None, :] <= query_pos[:, None])
    )
    return same_seq | (key_pos[None, :] == query_pos[:, None])


def contract_rows(left, right):
    return lax.dot_general(
        left, right, (((0,), (0,)), ((), ())), preferred_element_type=jnp.float32
    )


def contract_cols(left, right):
    return lax.dot_general(
        left, right, (((1,), (1,)), ((), ())), preferred_element_type=jnp.float32
    )


def rms_back(values, rstd, gain_vec, grad):
    scaled = grad * gain_vec
    row_dots = jnp.sum(values * scaled, axis=1, keepdims=True)
    return rstd * scaled - values * (rstd * rstd * rstd) * row_dots / D


def per_device(
    tokens,
    upstream,
    lengths,
    permutation,
    w_query,
    w_key,
    w_value,
    w_out,
    w_gate,
    w_up,
    w_down,
    q_gain,
    k_gain,
    attn_gain,
    ffn_gain,
):
    tensor_size = lax.axis_size("tensor")
    tensor_rank = lax.axis_index("tensor")
    own_rows = tokens.shape[0]
    group_rows = own_rows * tensor_size
    local_width = w_query.shape[1]
    local_heads = local_width // HDIM
    score_scale = 1.0 / math.sqrt(HDIM)
    block_rows = min(512, group_rows)
    block_count = group_rows // block_rows
    seq_count = lengths.shape[1]
    gathered = (
        lax.all_gather(w_query, "dp", axis=0, tiled=True),
        lax.all_gather(w_key, "dp", axis=0, tiled=True),
        lax.all_gather(w_value, "dp", axis=0, tiled=True),
        lax.all_gather(w_out, "dp", axis=1, tiled=True),
        lax.all_gather(w_gate, "dp", axis=0, tiled=True),
        lax.all_gather(w_up, "dp", axis=0, tiled=True),
        lax.all_gather(w_down, "dp", axis=1, tiled=True),
    )
    query_full, key_full, value_full, out_full, gate_full, up_full, down_full = gathered
    qkv_full = jnp.concatenate([query_full, key_full, value_full], axis=1)
    tokens_all = lax.all_gather(tokens, "tensor", axis=0, tiled=True)
    projected = jnp.dot(tokens_all, qkv_full, preferred_element_type=jnp.float32)
    q_raw = projected[:, :local_width]
    k_raw = projected[:, local_width : 2 * local_width]
    v_raw = projected[:, 2 * local_width :]
    square_q, square_k = lax.psum(
        (jnp.sum(q_raw * q_raw, axis=1), jnp.sum(k_raw * k_raw, axis=1)), "tensor"
    )
    rstd_q = lax.rsqrt(square_q / D + epsilon)[:, None]
    rstd_k = lax.rsqrt(square_k / D + epsilon)[:, None]
    gain_q = lax.dynamic_slice_in_dim(q_gain, tensor_rank * local_width, local_width)
    gain_k = lax.dynamic_slice_in_dim(k_gain, tensor_rank * local_width, local_width)
    q_norm = q_raw * rstd_q * gain_q
    k_norm = k_raw * rstd_k * gain_k
    segment, position = layout(lengths[0], group_rows)
    perm_row = permutation[0]
    inverse = (
        jnp.zeros((group_rows,), jnp.int32)
        .at[perm_row]
        .set(jnp.arange(group_rows, dtype=jnp.int32))
    )
    cosine, sine_part = rotary_tables(position)
    q_b = rotate(q_norm[perm_row].reshape(group_rows, local_heads, HDIM), cosine, sine_part).astype(
        jnp.bfloat16
    )
    k_b = rotate(k_norm[perm_row].reshape(group_rows, local_heads, HDIM), cosine, sine_part).astype(
        jnp.bfloat16
    )
    v_b = v_raw[perm_row].astype(jnp.bfloat16).reshape(group_rows, local_heads, HDIM)

    def forward_block(block_index):
        first_row = block_index * block_rows
        queries = lax.dynamic_slice_in_dim(q_b, first_row, block_rows, 0)
        scores = (
            jnp.einsum("qhd,khd->hqk", queries, k_b, preferred_element_type=jnp.float32)
            * score_scale
        )
        allowed = allowed_block(segment, first_row, block_rows, seq_count)
        masked = jnp.where(allowed[None], scores, masked_score)
        row_peak = jnp.max(masked, axis=-1, keepdims=True)
        exponent = jnp.exp(masked - row_peak)
        totals = jnp.sum(exponent, axis=-1, keepdims=True)
        probs_b = (exponent / totals).astype(jnp.bfloat16)
        attn_block = jnp.einsum("hqk,khd->qhd", probs_b, v_b, preferred_element_type=jnp.float32)
        return (attn_block.astype(jnp.bfloat16), (row_peak + jnp.log(totals))[..., 0])

    attn_blocks, log_totals = lax.map(forward_block, jnp.arange(block_count, dtype=jnp.int32))
    attn_given = attn_blocks.reshape(group_rows, local_width)[inverse]
    attn_out = lax.psum_scatter(
        jnp.dot(attn_given, out_full, preferred_element_type=jnp.float32),
        "tensor",
        scatter_dimension=0,
        tiled=True,
    )
    tokens_f = tokens.astype(jnp.float32)
    rstd_a = lax.rsqrt(jnp.mean(attn_out * attn_out, axis=1, keepdims=True) + epsilon)
    resid = tokens_f + attn_out * rstd_a * attn_gain
    resid_all = lax.all_gather(resid.astype(jnp.bfloat16), "tensor", axis=0, tiled=True)
    gate = jnp.dot(resid_all, gate_full, preferred_element_type=jnp.float32)
    up_part = jnp.dot(resid_all, up_full, preferred_element_type=jnp.float32)
    gate_sigmoid = jax.nn.sigmoid(gate)
    silu_gate = gate * gate_sigmoid
    hidden_b = (silu_gate * up_part).astype(jnp.bfloat16)
    mlp_out = lax.psum_scatter(
        jnp.dot(hidden_b, down_full, preferred_element_type=jnp.float32),
        "tensor",
        scatter_dimension=0,
        tiled=True,
    )
    rstd_m = lax.rsqrt(jnp.mean(mlp_out * mlp_out, axis=1, keepdims=True) + epsilon)
    normed_m = mlp_out * rstd_m
    layer_out = (resid + normed_m * ffn_gain).astype(jnp.bfloat16)
    back_weights = (
        lax.all_gather(w_query, "dp", axis=0, tiled=True),
        lax.all_gather(w_key, "dp", axis=0, tiled=True),
        lax.all_gather(w_value, "dp", axis=0, tiled=True),
        lax.all_gather(w_out, "dp", axis=1, tiled=True),
        lax.all_gather(w_gate, "dp", axis=0, tiled=True),
        lax.all_gather(w_up, "dp", axis=0, tiled=True),
        lax.all_gather(w_down, "dp", axis=1, tiled=True),
    )
    qkv_back = jnp.concatenate([back_weights[0], back_weights[1], back_weights[2]], axis=1)
    out_back = back_weights[3]
    gate_back = back_weights[4]
    up_back = back_weights[5]
    down_back = back_weights[6]
    grad_f = upstream.astype(jnp.float32)
    ffn_gain_part = jnp.sum(grad_f * normed_m, axis=0)
    d_mlp_b = rms_back(mlp_out, rstd_m, ffn_gain, grad_f).astype(jnp.bfloat16)
    d_mlp_all = lax.all_gather(d_mlp_b, "tensor", axis=0, tiled=True)
    d_hidden = contract_cols(d_mlp_all, down_back)
    down_grad = contract_rows(hidden_b, d_mlp_all)
    d_gate_b = (d_hidden * up_part * gate_sigmoid * (1.0 + gate * (1.0 - gate_sigmoid))).astype(
        jnp.bfloat16
    )
    d_up_b = (d_hidden * silu_gate).astype(jnp.bfloat16)
    gate_grad = contract_rows(resid_all, d_gate_b)
    up_grad = contract_rows(resid_all, d_up_b)
    d_resid = grad_f + lax.psum_scatter(
        contract_cols(d_gate_b, gate_back) + contract_cols(d_up_b, up_back),
        "tensor",
        scatter_dimension=0,
        tiled=True,
    )
    attn_gain_part = jnp.sum(d_resid * attn_out * rstd_a, axis=0)
    d_attn_b = rms_back(attn_out, rstd_a, attn_gain, d_resid).astype(jnp.bfloat16)
    d_attn_all = lax.all_gather(d_attn_b, "tensor", axis=0, tiled=True)
    out_grad = contract_rows(attn_given, d_attn_all)
    d_given_b = contract_cols(d_attn_all, out_back).astype(jnp.bfloat16)
    d_packed = d_given_b[perm_row].reshape(group_rows, local_heads, HDIM)

    def backward_block(carried, block_in):
        key_acc, value_acc = carried
        block_index, log_rows = block_in
        first_row = block_index * block_rows
        queries = lax.dynamic_slice_in_dim(q_b, first_row, block_rows, 0)
        grad_rows = lax.dynamic_slice_in_dim(d_packed, first_row, block_rows, 0)
        scores = (
            jnp.einsum("qhd,khd->hqk", queries, k_b, preferred_element_type=jnp.float32)
            * score_scale
        )
        allowed = allowed_block(segment, first_row, block_rows, seq_count)
        probs_f = jnp.where(allowed[None], jnp.exp(scores - log_rows[..., None]), 0.0)
        probs_b = probs_f.astype(jnp.bfloat16)
        d_probs = jnp.einsum("qhd,khd->hqk", grad_rows, v_b, preferred_element_type=jnp.float32)
        row_delta = jnp.sum(probs_f * d_probs, axis=-1, keepdims=True)
        d_scores_b = (probs_f * (d_probs - row_delta)).astype(jnp.bfloat16)
        d_query = (
            jnp.einsum("hqk,khd->qhd", d_scores_b, k_b, preferred_element_type=jnp.float32)
            * score_scale
        )
        key_acc = (
            key_acc
            + jnp.einsum("hqk,qhd->khd", d_scores_b, queries, preferred_element_type=jnp.float32)
            * score_scale
        )
        value_acc = value_acc + jnp.einsum(
            "hqk,qhd->khd", probs_b, grad_rows, preferred_element_type=jnp.float32
        )
        return ((key_acc, value_acc), d_query)

    zero_acc = jnp.zeros((group_rows, local_heads, HDIM), jnp.float32)
    (d_key_rot, d_value_packed), d_query_blocks = lax.scan(
        backward_block, (zero_acc, zero_acc), (jnp.arange(block_count, dtype=jnp.int32), log_totals)
    )
    d_query_rot = d_query_blocks.reshape(group_rows, local_heads, HDIM)
    d_q_norm = rotate(d_query_rot, cosine, -sine_part).reshape(group_rows, local_width)[inverse]
    d_k_norm = rotate(d_key_rot, cosine, -sine_part).reshape(group_rows, local_width)[inverse]
    d_v_given = d_value_packed.reshape(group_rows, local_width)[inverse]
    dots_q, dots_k = lax.psum(
        (jnp.sum(q_raw * gain_q * d_q_norm, axis=1), jnp.sum(k_raw * gain_k * d_k_norm, axis=1)),
        "tensor",
    )
    d_q_raw = rstd_q * gain_q * d_q_norm - q_raw * (rstd_q * rstd_q * rstd_q) * dots_q[:, None] / D
    d_k_raw = rstd_k * gain_k * d_k_norm - k_raw * (rstd_k * rstd_k * rstd_k) * dots_k[:, None] / D
    q_gain_part = jnp.sum(d_q_norm * q_raw * rstd_q, axis=0)
    k_gain_part = jnp.sum(d_k_norm * k_raw * rstd_k, axis=0)
    d_qkv_b = jnp.concatenate([d_q_raw, d_k_raw, d_v_given], axis=1).astype(jnp.bfloat16)
    qkv_grad = contract_rows(tokens_all, d_qkv_b)
    tokens_grad = (
        d_resid
        + lax.psum_scatter(
            contract_cols(d_qkv_b, qkv_back).astype(jnp.bfloat16),
            "tensor",
            scatter_dimension=0,
            tiled=True,
        ).astype(jnp.float32)
    ).astype(jnp.bfloat16)
    qkv_shard, out_shard, gate_shard, up_shard, down_shard = (
        lax.psum_scatter(
            qkv_grad.astype(jnp.bfloat16), "dp", scatter_dimension=0, tiled=True
        ).astype(jnp.float32),
        lax.psum_scatter(
            out_grad.astype(jnp.bfloat16), "dp", scatter_dimension=1, tiled=True
        ).astype(jnp.float32),
        lax.psum_scatter(
            gate_grad.astype(jnp.bfloat16), "dp", scatter_dimension=0, tiled=True
        ).astype(jnp.float32),
        lax.psum_scatter(
            up_grad.astype(jnp.bfloat16), "dp", scatter_dimension=0, tiled=True
        ).astype(jnp.float32),
        lax.psum_scatter(
            down_grad.astype(jnp.bfloat16), "dp", scatter_dimension=1, tiled=True
        ).astype(jnp.float32),
    )
    q_gain_full = lax.dynamic_update_slice_in_dim(
        jnp.zeros((D,), jnp.float32), q_gain_part, tensor_rank * local_width, 0
    )
    k_gain_full = lax.dynamic_update_slice_in_dim(
        jnp.zeros((D,), jnp.float32), k_gain_part, tensor_rank * local_width, 0
    )
    q_gain_grad, k_gain_grad, attn_gain_grad, ffn_gain_grad = lax.psum(
        (q_gain_full, k_gain_full, attn_gain_part, ffn_gain_part), ("dp", "tensor")
    )
    return (
        layer_out,
        tokens_grad,
        qkv_shard[:, :local_width],
        qkv_shard[:, local_width : 2 * local_width],
        qkv_shard[:, 2 * local_width :],
        out_shard,
        gate_shard,
        up_shard,
        down_shard,
        q_gain_grad,
        k_gain_grad,
        attn_gain_grad,
        ffn_gain_grad,
    )


def solution(mesh):
    placed = (
        P(("dp", "tensor"), None),
        P(("dp", "tensor"), None),
        P("dp", None),
        P("dp", None),
        P("dp", "tensor"),
        P("dp", "tensor"),
        P("dp", "tensor"),
        P("tensor", "dp"),
        P("dp", "tensor"),
        P("dp", "tensor"),
        P("tensor", "dp"),
        P(),
        P(),
        P(),
        P(),
    )
    return jax.shard_map(
        per_device,
        mesh=mesh,
        in_specs=placed,
        out_specs=(
            P(("dp", "tensor"), None),
            P(("dp", "tensor"), None),
            P("dp", "tensor"),
            P("dp", "tensor"),
            P("dp", "tensor"),
            P("tensor", "dp"),
            P("dp", "tensor"),
            P("dp", "tensor"),
            P("tensor", "dp"),
            P(),
            P(),
            P(),
            P(),
        ),
        check_vma=False,
    )
```

profile of v0, /device:TPU:0, one launch (start us, length us, event | category | flops | bytes accessed | tf_op | source)
XLA Modules:
  0.0 2730.9 jit_solution(9512134265611185259)
XLA Ops:
  12.9 8.0 scatter_custom_fusion
  28.8 11.8 all-gather.12.cloned.1.call-done
  43.7 26.7 all-gather.14.cloned.1.call-done
  73.5 26.7 all-gather.16.cloned.1.call-done
  103.3 148.0 %all-gather.18.cloned.1.call-done = bf16[2048,2048]{1,0:T(8,128)(2,1)} async-done(((bf16[512,2048]{1,0:T(8,128)(2,1)}), bf16[2048,2048]{1,0:T(8,128)(2,1)}) %all-gather.18.cloned.1.call-update) | async-done | bytes 8388624 | tf_op jit(solution)/shard_map/all_gather | solution.py:118
  251.3 17.5 convolution_bitcast_fusion
  274.9 16.0 all-reduce.2
  304.5 11.7 gather_fusion
  321.5 8.0 fusion.49
  334.9 11.8 gather_fusion.1
  362.6 9.2 gather_fusion.2
  385.8 79.0 %while.27 = (s32[]{:T(128)}, bf16[4,512,4,128]{3,2,1,0:T(4,128)(2,1)}, f32[4,4,512]{2,1,0:T(4,128)}, s32[4]{0:T(128)S(1)}, s32[2048]{0:T(1024)S(1)}, /*index=5*/...) while((s32[]{:T(128)}, ...), condition=%wide.region_10.11_spmd, body=%wide.region_7.10_spmd.sunk | while | flops 2204367872 | bytes 69292248 | solution.py:164
  468.9 11.1 gather_fusion.3
  480.1 12.5 fusion.51
  493.4 278.0 %reduce-scatter.10.cloned.1.call-done = f32[512,2048]{1,0:T(8,128)} async-done(((f32[2048,2048]{1,0:T(8,128)}), f32[512,2048]{1,0:T(8,128)}) %reduce-scatter.10.cloned.1.call-update) | async-done | bytes 4194320 | tf_op jit(solution)/shard_map/reduce_scatter | solution.py:166
  778.8 49.9 %all-gather.24.cloned.1.call-done = bf16[2048,2048]{1,0:T(8,128)(2,1)} async-done(((bf16[256,2048]{1,0:T(8,128)(2,1)}), bf16[2048,2048]{1,0:T(8,128)(2,1)}) %all-gather.24.cloned.1.call-update) | async-done | bytes 8388624 | tf_op jit(solution)/shard_map/all_gather | solution.py:112
  828.6 151.9 %all-gather.22.cloned.1.call-done = bf16[2048,2048]{1,0:T(8,128)(2,1)} async-done(((bf16[512,2048]{1,0:T(8,128)(2,1)}), bf16[2048,2048]{1,0:T(8,128)(2,1)}) %all-gather.22.cloned.1.call-update) | async-done | bytes 8388624 | tf_op jit(solution)/shard_map/all_gather | solution.py:175
  980.5 24.6 fusion.52
  1005.1 30.1 %all-gather.26.cloned.1.call-done = bf16[2048,2048]{1,0:T(8,128)(2,1)} async-done(((bf16[256,2048]{1,0:T(8,128)(2,1)}), bf16[2048,2048]{1,0:T(8,128)(2,1)}) %all-gather.26.cloned.1.call-update) | async-done | bytes 8388624 | tf_op jit(solution)/shard_map/all_gather | solution.py:113
  1035.2 28.0 %multiply_convert_fusion.3 = (bf16[2048,2048]{1,0:T(8,128)(2,1)}, f32[2048,2048]{1,0:T(8,128)}) fusion(f32[2048,2048]{1,0:T(8,128)} %fusion.52, bf16[2048,2048]{1,0:T(8,128)(2,1)} %all-gather.22.cloned.1.call-done, bf16[2048,2048]{1,0:T(8,128)(2,1)} %all-gather.26.cloned.1.call-done), kind=kOutput, calls=%fused_computation.61 | convolution fusion | flops 17205035008 | bytes 58720256 | tf_op jit(solution)/shard_map/dot_general | solution.py:177
  1063.2 29.8 %all-gather.28.cloned.1.call-done = bf16[2048,2048]{1,0:T(8,128)(2,1)} async-done(((bf16[2048,256]{1,0:T(8,128)(2,1)}), bf16[2048,2048]{1,0:T(8,128)(2,1)}) %all-gather.28.cloned.1.call-update) | async-done | bytes 8388624 | tf_op jit(solution)/shard_map/all_gather | solution.py:114
  1093.1 24.2 fusion.53
  1117.6 280.2 %reduce-scatter.12.cloned.1.call-done = f32[512,2048]{1,0:T(8,128)} async-done(((f32[2048,2048]{1,0:T(8,128)}), f32[512,2048]{1,0:T(8,128)}) %reduce-scatter.12.cloned.1.call-update) | async-done | bytes 4194320 | tf_op jit(solution)/shard_map/reduce_scatter | solution.py:181
  1405.6 150.5 %all-gather.30.cloned.1.call-done = bf16[2048,2048]{1,0:T(8,128)(2,1)} async-done(((bf16[512,2048]{1,0:T(8,128)(2,1)}), bf16[2048,2048]{1,0:T(8,128)(2,1)}) %all-gather.30.cloned.1.call-update) | async-done | bytes 8388624 | tf_op jit(solution)/shard_map/all_gather | solution.py:207
  1556.1 34.4 %multiply_convert_fusion.1 = (bf16[2048,2048]{1,0:T(8,128)(2,1)}, bf16[2048,2048]{1,0:T(8,128)(2,1)}) fusion(f32[2048,2048]{1,0:T(8,128)} %fusion.52, f32[2048,2048]{1,0:T(8,128)} %get-tuple-element.357, bf16[2048,2048]{1,0:T(8,128)(2,1)} %all-gather.30.cloned.1.call-done, bf16[2048,2048]{1,0:T(8,128)(2,1)} %all-gather.28.cloned.1.call-done), kind=kOutput, calls=%fused_computation.59 | convolution fusion | flops 17234395136 | bytes 67108864 | tf_op jit(solution)/shard_map/dot_general | solution.py:69
  1590.5 24.3 fusion.54
  1614.8 26.5 convolution_add_fusion
  1641.4 278.6 %reduce-scatter.14.cloned.1.call-done = f32[512,2048]{1,0:T(8,128)} async-done(((f32[2048,2048]{1,0:T(8,128)}), f32[512,2048]{1,0:T(8,128)}) %reduce-scatter.14.cloned.1.call-update) | async-done | bytes 4194320 | tf_op jit(solution)/shard_map/reduce_scatter | solution.py:216
  1932.3 24.2 convolution_convert_fusion
  1956.5 23.8 convolution_convert_fusion.2
  1980.4 24.0 convolution_convert_fusion.1
  2004.4 78.3 %all-gather.32.cloned.1.call-done = bf16[2048,2048]{1,0:T(8,128)(2,1)} async-done(((bf16[512,2048]{1,0:T(8,128)(2,1)}), bf16[2048,2048]{1,0:T(8,128)(2,1)}) %all-gather.32.cloned.1.call-update) | async-done | bytes 8388624 | tf_op jit(solution)/shard_map/all_gather | solution.py:224
  2082.7 8.5 convolution_convert_fusion.6
  2091.3 9.2 gather_fusion.4
  2104.6 267.5 %while.28 = (s32[]{:T(128)}, f32[2048,4,128]{0,2,1:T(8,128)}, f32[2048,4,128]{0,2,1:T(8,128)}, f32[4,512,4,128]{3,1,0,2:T(8,128)}, s32[4]{0:T(128)S(1)}, /*index...) while((s32[]{:T(128)}, f32[2048,4,128]{0,2,1:T(8,128)}, ...), condition=%wide.region_21.22_spmd.clone, body=%wide.region_19.21_spmd.clone.sunk | while | flops 5443419136 | bytes 203501424 | solution.py:260
  2108.5 9.4 fusion.124
  2119.9 12.7 multiply_reduce_fusion.12
  2132.6 15.3 multiply_convert_fusion.5
  2158.8 10.7 bitcast_add_fusion.5
  2173.0 9.5 fusion.124
  2184.4 12.5 multiply_reduce_fusion.12
  2197.0 15.7 multiply_convert_fusion.5
  2212.7 9.4 bitcast_add_fusion.4
  2225.4 11.8 bitcast_add_fusion.5
  2240.6 11.3 fusion.124
  2253.9 12.5 multiply_reduce_fusion.12
  2266.4 16.1 multiply_convert_fusion.5
  2282.5 8.8 bitcast_add_fusion.4
  2294.6 11.8 bitcast_add_fusion.5
  2309.8 9.3 fusion.124
  2321.1 12.5 multiply_reduce_fusion.12
  2333.6 14.8 multiply_convert_fusion.5
  2348.4 8.7 bitcast_add_fusion.4
  2360.4 11.6 bitcast_add_fusion.5
  2377.6 9.7 multiply_subtract_fusion.1
  2390.4 11.8 gather_fusion.6
  2414.1 11.7 gather_fusion.5
  2434.6 9.2 gather_fusion.7
  2455.0 9.1 convolution_convert_fusion.5
  2464.2 18.0 all-reduce.1
  2491.1 17.5 fusion.33
  2508.7 19.1 convolution_convert_fusion.4
  2537.0 39.2 %all-reduce = (f32[2048]{0:T(1024)}, f32[2048]{0:T(1024)}, f32[2048]{0:T(1024)}, f32[2048]{0:T(1024)}) all-reduce(f32[2048]{0:T(1024)S(1)} %dynamic_update_slice.18, f32[2048]{0:T(1024)S(1)} %dynamic_update_slice.19, f32[2048]{0:T(1024)S(1)} %copy-done.43, f32[2048]{0:T(1024)S(1)} %copy-done.42), channel_id=1, replica_groups=mesh['dp'=8,'tensor'=4] {'dp','tensor'}, use_global_device_ids=true, to_apply=%region_33.34 | all-reduce | flops 8192 | bytes 65536 | tf_op jit(solution)/shard_map/psum | solution.py:309
  2584.2 134.5 %reduce-scatter.16.cloned.1.call-done = bf16[512,2048]{1,0:T(8,128)(2,1)} async-done(((bf16[2048,2048]{1,0:T(8,128)(2,1)}), bf16[512,2048]{1,0:T(8,128)(2,1)}) %reduce-scatter.16.cloned.1.call-update) | async-done | bytes 2097168 | tf_op jit(solution)/shard_map/reduce_scatter | solution.py:279
  (312 shorter events, 307.4 us)
Async XLA Ops:
  7.2 33.4 %all-gather.12.cloned.1.call-start = ((), (), s32[]{:S(2)}) async-start(), calls=%async_computation.9 | async-start | bytes 2359296 | tf_op jit(solution)/shard_map/all_gather | solution.py:108
  7.9 62.5 %all-gather.14.cloned.1.call-start = ((), (), s32[]{:S(2)}) async-start(), calls=%async_computation.10 | async-start | bytes 2359296 | tf_op jit(solution)/shard_map/all_gather | solution.py:109
  8.7 91.5 %all-gather.16.cloned.1.call-start = ((), (), s32[]{:S(2)}) async-start(), calls=%async_computation.11 | async-start | bytes 2359296 | tf_op jit(solution)/shard_map/all_gather | solution.py:110
  9.4 241.9 %all-gather.18.cloned.1.call-start = ((), (), s32[]{:S(2)}) async-start(), calls=%async_computation.12 | async-start | bytes 10485760 | tf_op jit(solution)/shard_map/all_gather | solution.py:118
  10.0 470.1 %all-gather.20.cloned.1.call-start = ((), (), s32[]{:S(2)}) async-start(), calls=%async_computation.13 | async-start | bytes 2359296 | tf_op jit(solution)/shard_map/all_gather | solution.py:111
  10.6 760.9 %reduce-scatter.10.cloned.1.call-start = ((), (), s32[]{:S(2)}) async-start(), calls=%async_computation.14 | async-start | bytes 20971520 | tf_op jit(solution)/shard_map/reduce_scatter | solution.py:166
  11.4 280.1 %copy-start.46 = (f32[512]{0:T(512)}, f32[512]{0:T(512)S(1)}, u32[]{:S(2)}) copy-start(f32[512]{0:T(512)S(1)} %dynamic_slice.32) | copy-start | bytes 6148
  12.2 279.4 %copy-start.48 = (f32[512]{0:T(512)}, f32[512]{0:T(512)S(1)}, u32[]{:S(2)}) copy-start(f32[512]{0:T(512)S(1)} %dynamic_slice.33) | copy-start | bytes 6148
  21.6 341.0 %copy-start.28 = (s32[2048]{0:T(1024)}, s32[2048]{0:T(1024)S(1)}, u32[]{:S(2)}) copy-start(s32[2048]{0:T(1024)S(1)} %get-tuple-element.361) | copy-start | bytes 24580
  28.8 346.4 %copy-start.18 = (f32[2048,64]{1,0:T(8,128)}, f32[2048,64]{1,0:T(8,128)S(1)}, u32[]{:S(2)}) copy-start(f32[2048,64]{1,0:T(8,128)S(1)} %get-tuple-element.347) | copy-start | bytes 1572868
  291.5 7.6 copy-start.30
  291.5 7.6 copy-start.32
  393.9 5.0 copy-start.4
  464.9 15.2 copy-start.1
  464.9 15.2 copy-start.24
  492.6 282.7 %copy-start.15 = (bf16[512,2048]{1,0:T(8,128)(2,1)S(1)}, bf16[512,2048]{1,0:T(8,128)(2,1)}, u32[]{:S(2)}) copy-start(bf16[512,2048]{1,0:T(8,128)(2,1)} %param.19) | copy-start | bytes 6291460
  492.6 282.7 %copy-start.36 = (f32[2048]{0:T(1024)S(1)}, f32[2048]{0:T(1024)}, u32[]{:S(2)}) copy-start(f32[2048]{0:T(1024)} %param.32) | copy-start | bytes 24580
  492.6 336.0 %all-gather.24.cloned.1.call-start = ((), (), s32[]{:S(2)}) async-start(), calls=%async_computation.16 | async-start | bytes 9437184 | tf_op jit(solution)/shard_map/all_gather | solution.py:112
  493.3 487.1 %all-gather.22.cloned.1.call-start = ((), (), s32[]{:S(2)}) async-start(), calls=%async_computation.15 | async-start | bytes 10485760 | tf_op jit(solution)/shard_map/all_gather | solution.py:175
  777.4 257.8 %all-gather.26.cloned.1.call-start = ((), (), s32[]{:S(2)}) async-start(), calls=%async_computation.17 | async-start | bytes 9437184 | tf_op jit(solution)/shard_map/all_gather | solution.py:113
  778.1 315.0 %all-gather.28.cloned.1.call-start = ((), (), s32[]{:S(2)}) async-start(), calls=%async_computation.18 | async-start | bytes 9437184 | tf_op jit(solution)/shard_map/all_gather | solution.py:114
  778.7 619.1 %reduce-scatter.12.cloned.1.call-start = ((), (), s32[]{:S(2)}) async-start(), calls=%async_computation.19 | async-start | bytes 20971520 | tf_op jit(solution)/shard_map/reduce_scatter | solution.py:181
  1117.3 283.2 %copy-start.12 = (bf16[512,2048]{1,0:T(8,128)(2,1)S(1)}, bf16[512,2048]{1,0:T(8,128)(2,1)}, u32[]{:S(2)}) copy-start(bf16[512,2048]{1,0:T(8,128)(2,1)} %param.20) | copy-start | bytes 6291460
  1117.3 283.2 %copy-start.34 = (f32[2048]{0:T(1024)S(1)}, f32[2048]{0:T(1024)}, u32[]{:S(2)}) copy-start(f32[2048]{0:T(1024)} %param.33) | copy-start | bytes 24580
  1117.3 438.7 %all-gather.30.cloned.1.call-start = ((), (), s32[]{:S(2)}) async-start(), calls=%async_computation.20 | async-start | bytes 10485760 | tf_op jit(solution)/shard_map/all_gather | solution.py:207
  1405.5 514.5 %reduce-scatter.14.cloned.1.call-start = ((), (), s32[]{:S(2)}) async-start(), calls=%async_computation.21 | async-start | bytes 20971520 | tf_op jit(solution)/shard_map/reduce_scatter | solution.py:216
  1641.3 278.7 %copy-start.13 = (bf16[512,2048]{1,0:T(8,128)(2,1)S(1)}, bf16[512,2048]{1,0:T(8,128)(2,1)}, u32[]{:S(2)}) copy-start(bf16[512,2048]{1,0:T(8,128)(2,1)} %param.20) | copy-start | bytes 6291460
  1641.3 278.7 %copy-start.37 = (f32[2048]{0:T(1024)S(1)}, f32[2048]{0:T(1024)}, u32[]{:S(2)}) copy-start(f32[2048]{0:T(1024)} %param.32) | copy-start | bytes 24580
  1641.3 278.7 %copy-start.45 = (f32[512]{0:T(512)S(1)}, f32[512]{0:T(512)}, u32[]{:S(2)}) copy-start(f32[512]{0:T(512)} %copy-done.44) | copy-start | bytes 6148
  1641.3 284.3 %copy-start.35 = (f32[2048]{0:T(1024)S(1)}, f32[2048]{0:T(1024)}, u32[]{:S(2)}) copy-start(f32[2048]{0:T(1024)} %param.33) | copy-start | bytes 24580
  1641.3 284.3 %copy-start.41 = (f32[512]{0:T(512)S(1)}, f32[512]{0:T(512)}, u32[]{:S(2)}) copy-start(f32[512]{0:T(512)} %copy-done.40) | copy-start | bytes 6148
  1641.4 284.3 %copy-start.50 = (f32[512]{0:T(512)S(1)}, f32[512]{0:T(512)}, u32[]{:S(2)}) copy-start(f32[512]{0:T(512)} %get-tuple-element.352) | copy-start | bytes 6148
  1641.4 441.4 %all-gather.32.cloned.1.call-start = ((), (), s32[]{:S(2)}) async-start(), calls=%async_computation.22 | async-start | bytes 10485760 | tf_op jit(solution)/shard_map/all_gather | solution.py:224
  1920.0 5.6 copy-start.7
  1920.0 5.9 copy-start.9
  1920.1 6.5 copy-start.16
  1932.2 595.7 %reduce-scatter.26.cloned.1.call-start = ((), (), s32[]{:S(2)}) async-start(), calls=%async_computation.28 | async-start | bytes 9437184 | tf_op jit(solution)/shard_map/reduce_scatter | solution.py:299
  1956.5 574.2 %reduce-scatter.22.cloned.1.call-start = ((), (), s32[]{:S(2)}) async-start(), calls=%async_computation.26 | async-start | bytes 9437184 | tf_op jit(solution)/shard_map/reduce_scatter | solution.py:293
  1980.3 553.1 %reduce-scatter.24.cloned.1.call-start = ((), (), s32[]{:S(2)}) async-start(), calls=%async_computation.27 | async-start | bytes 9437184 | tf_op jit(solution)/shard_map/reduce_scatter | solution.py:296
  2004.4 86.9 %copy-start.29 = (s32[2048]{0:T(1024)S(1)}, s32[2048]{0:T(1024)}, u32[]{:S(2)}) copy-start(s32[2048]{0:T(1024)} %copy-done.28) | copy-start | bytes 24580
  2004.4 571.8 %reduce-scatter.20.cloned.1.call-start = ((), (), s32[]{:S(2)}) async-start(), calls=%async_computation.25 | async-start | bytes 2359296 | tf_op jit(solution)/shard_map/reduce_scatter | solution.py:290
  2108.5 11.4 copy-start.5
  2119.1 13.5 copy-start.10
  2147.9 7.6 copy-start
  2172.9 11.5 copy-start.5
  2183.7 13.3 copy-start.10
  2212.7 9.4 copy-start
  2240.6 13.3 copy-start.5
  2253.2 13.2 copy-start.10
  2282.5 8.8 copy-start
  2309.8 11.3 copy-start.5
  2320.4 13.2 copy-start.10
  2348.4 8.7 copy-start
  2372.1 5.5 copy-start.19
  2372.1 5.5 copy-start.20
  2447.8 7.1 copy-start.21
  2455.0 27.2 copy-start.38
  2455.0 27.2 copy-start.39
  2464.1 113.9 %reduce-scatter.18.cloned.1.call-start = ((), (), s32[]{:S(2)}) async-start(), calls=%async_computation.24 | async-start | bytes 7077888 | tf_op jit(solution)/shard_map/reduce_scatter | solution.py:287
  2482.2 9.0 copy-start.23
  2508.7 210.0 %reduce-scatter.16.cloned.1.call-start = ((), (), s32[]{:S(2)}) async-start(), calls=%async_computation.23 | async-start | bytes 10485760 | tf_op jit(solution)/shard_map/reduce_scatter | solution.py:279
  2527.9 9.1 copy-start.42
  2527.9 9.1 copy-start.43
  2536.5 182.1 %copy-start.14 = (bf16[512,2048]{1,0:T(8,128)(2,1)S(1)}, bf16[512,2048]{1,0:T(8,128)(2,1)}, u32[]{:S(2)}) copy-start(bf16[512,2048]{1,0:T(8,128)(2,1)} %param.20) | copy-start | bytes 6291460
  (22 other events, 79.4 us)
Sparse Core Ops, SparseCore 0:
  9.9 30.6 all-gather.11
  42.4 27.8 all-gather.13
  72.3 27.8 all-gather.15
  101.6 149.6 all-gather.17
  253.0 26.4 all-gather.19
  492.7 278.6 reduce-scatter.9
  773.5 55.1 all-gather.23
  830.8 149.6 all-gather.21
  982.5 52.6 all-gather.25
  1037.1 55.9 all-gather.27
  1117.5 280.2 reduce-scatter.11
  1405.7 150.3 all-gather.29
  1641.5 278.5 reduce-scatter.13
  1932.3 150.3 all-gather.31
  2086.4 69.5 reduce-scatter.25
  2159.3 71.2 reduce-scatter.21
  2234.3 71.2 reduce-scatter.23
  2464.2 41.3 reduce-scatter.19
  2509.4 62.6 reduce-scatter.17
  2574.3 144.3 reduce-scatter.15
where the time goes:
time: 2740 us; the launch traced here: 2730 us
  waiting for transfers between devices  1680 us (61%)
  matrix products  542 us (20%)
  local copies, waits for them, and re-layouts  213 us (8%)
  other arithmetic  201 us (7%)
  blocking collectives  73.2 us (3%)
    reduce_scatter x1, waiting for transfers between devices, per_device(): lax.psum_scatter(jnp.dot(hidden_b, down_full, preferred_element_type=jnp....  280 us
    reduce_scatter x1, waiting for transfers between devices, per_device(): lax.psum_scatter(contract_cols(d_gate_b, gate_back) + contract_cols(d_up_...  279 us
    reduce_scatter x1, waiting for transfers between devices, per_device(): lax.psum_scatter(jnp.dot(attn_given, out_full, preferred_element_type=jnp...  278 us
    all_gather x1, waiting for transfers between devices, per_device(): lax.all_gather(resid.astype(jnp.bfloat16), 'tensor', axis=0, tiled=True)  152 us
    all_gather x1, waiting for transfers between devices, per_device(): d_mlp_all = lax.all_gather(d_mlp_b, 'tensor', axis=0, tiled=True)  150 us
    all_gather x1, waiting for transfers between devices, per_device(): tokens_all = lax.all_gather(tokens, 'tensor', axis=0, tiled=True)  148 us
    reduce_scatter x1, waiting for transfers between devices, per_device(): lax.psum_scatter(contract_cols(d_qkv_b, qkv_back).astype(jnp.bfloat16), '...  134 us
    dot_general x5, matrix products, contract_cols(): lax.dot_general(left, right, (((1,), (1,)), ((), ())), preferred_element_...  113 us
  transfers between devices with their start and end apart: 20, of which 14 were waited for; matrix products, arithmetic and copies ran while one was open for 29% of the time, Pallas kernels for 0%

commit v1 on v0

v1 whole, which is shorter than its diff:
```python
import math

import jax
import jax.numpy as jnp
from jax import lax
from jax.sharding import Mesh, PartitionSpec as P

D = 2048
HDIM = 128

epsilon = 1e-06
rope_base = 500000.0
masked_score = -1e30

SWAP = [(0, 1), (1, 0)]
TURN = [(0, 0), (1, 2), (2, 1), (3, 3)]
CYCLE = [(0, 1), (1, 3), (3, 2), (2, 0)]
CYCLE_BACK = [(d, s) for s, d in CYCLE]
DP = ("a", "b", "core")
TENSOR = ("th", "tl")
RANK = ("core", "tl")


def swap(value, axis):
    return lax.ppermute(value, axis, SWAP)


def turn(value):
    return lax.ppermute(value, ("core", "th"), TURN)


def small_grid():
    return lax.axis_size("a") == 2 and lax.axis_size("tl") == 2


def part(value, dim, index, count):
    size = value.shape[dim] // count
    return lax.slice_in_dim(value, index * size, (index + 1) * size, axis=dim)


def gather_weight(shard, dim):
    first = turn(shard)
    second = lax.ppermute(shard, ("core", "th"), CYCLE)
    if not small_grid():
        upper = lax.axis_index("th") == 0
        pair = jnp.concatenate(
            [jnp.where(upper, first, second), jnp.where(upper, second, first)], axis=dim
        )
        return lax.all_gather(pair, ("a", "b"), axis=dim, tiled=True)
    first_b, first_a = swap(first, "b"), swap(first, "a")
    second_b, second_a = swap(second, "b"), swap(second, "a")
    first_d, second_d = swap(first_b, "a"), swap(second_a, "b")
    return jnp.concatenate(
        [first, second, first_b, second_b, first_a, second_a, first_d, second_d], axis=dim
    )


def scatter_weight(total, dim):
    total = total.astype(jnp.bfloat16)

    def add(left, right):
        return (left.astype(jnp.float32) + right.astype(jnp.float32)).astype(jnp.bfloat16)

    if not small_grid():
        pair = lax.psum_scatter(total, ("a", "b"), scatter_dimension=dim, tiled=True)
        upper = lax.axis_index("th") == 0
        low_part, high_part = part(pair, dim, 0, 2), part(pair, dim, 1, 2)
        first = jnp.where(upper, low_part, high_part)
        second = jnp.where(upper, high_part, low_part)
    else:
        blocks = [part(total, dim, index, 8) for index in range(8)]
        first, second, first_b, second_b, first_a, second_a, first_d, second_d = blocks
        first_b = add(first_b, swap(first_d, "a"))
        second_a = add(second_a, swap(second_d, "b"))
        first = (
            first.astype(jnp.float32)
            + swap(first_b, "b").astype(jnp.float32)
            + swap(first_a, "a").astype(jnp.float32)
        ).astype(jnp.bfloat16)
        second = (
            second.astype(jnp.float32)
            + swap(second_b, "b").astype(jnp.float32)
            + swap(second_a, "a").astype(jnp.float32)
        ).astype(jnp.bfloat16)
    return turn(first).astype(jnp.float32) + lax.ppermute(
        second, ("core", "th"), CYCLE_BACK
    ).astype(jnp.float32)


def swap_features(value):
    if not small_grid():
        return value
    size = value.shape[-1] // 8
    mask = 4 * lax.axis_index("a") + 2 * lax.axis_index("b") + lax.axis_index("th")
    return jnp.concatenate(
        [
            lax.dynamic_slice_in_dim(value, (index ^ mask) * size, size, axis=value.ndim - 1)
            for index in range(8)
        ],
        axis=value.ndim - 1,
    )


def row_place(row, own_rows):
    if not small_grid():
        return row
    mask = 2 * lax.axis_index("core") + lax.axis_index("tl")
    block = (row // own_rows) ^ mask
    block = (block // 2) + 2 * (block % 2)
    return block * own_rows + row % own_rows


def gather_rows(value):
    if not small_grid():
        return [lax.all_gather(value, RANK, axis=0, tiled=True)]
    far = swap(value, "tl")
    near_peer = swap(value, "core")
    far_peer = swap(far, "core")
    return [
        jnp.concatenate([value, near_peer], axis=0),
        jnp.concatenate([far, far_peer], axis=0),
    ]


def scatter_rows(pieces):
    if not small_grid():
        return lax.psum_scatter(
            pieces[0].astype(jnp.bfloat16), RANK, scatter_dimension=0, tiled=True
        ).astype(jnp.float32)
    near, far = pieces
    rows = near.shape[0] // 2
    far_peer = swap(far[rows:].astype(jnp.bfloat16), "core")
    far_sum = (far[:rows] + far_peer.astype(jnp.float32)).astype(jnp.bfloat16)
    from_far = swap(far_sum, "tl")
    near_peer = swap(near[rows:].astype(jnp.bfloat16), "core")
    return near[:rows] + near_peer.astype(jnp.float32) + from_far.astype(jnp.float32)


def sum_over(value, axes):
    for axis in axes:
        if lax.axis_size(axis) == 2:
            value = value + swap(value, axis)
        else:
            value = lax.psum(value, axis)
    return value


def layout(length_row, group_rows):
    count = length_row.shape[0]
    positions = jnp.arange(group_rows, dtype=jnp.int32)
    start = jnp.int32(0)
    segment = jnp.zeros((group_rows,), jnp.int32)
    offset = jnp.zeros((group_rows,), jnp.int32)
    for index in range(count):
        end = start + length_row[index]
        inside = (positions >= start) & (positions < end)
        offset = jnp.where(inside, start, offset)
        segment = segment + (positions >= end).astype(jnp.int32)
        start = end
    return (segment, positions - offset)


def rotary_tables(position):
    half_dim = HDIM // 2
    exponents = jnp.arange(half_dim, dtype=jnp.float32) * (2.0 / HDIM)
    frequency = jnp.power(jnp.float32(rope_base), -exponents)
    angles = position.astype(jnp.float32)[:, None] * frequency[None, :]
    return (jnp.cos(angles), jnp.sin(angles))


def rotate(values, cosine, sine_part):
    half_dim = HDIM // 2
    first_half = values[..., :half_dim]
    second_half = values[..., half_dim:]
    cos_rows = cosine[:, None, :]
    sin_rows = sine_part[:, None, :]
    return jnp.concatenate(
        [
            first_half * cos_rows - second_half * sin_rows,
            second_half * cos_rows + first_half * sin_rows,
        ],
        axis=-1,
    )


def allowed_block(segment, first_row, block_rows, seq_count):
    query_seg = lax.dynamic_slice_in_dim(segment, first_row, block_rows)
    query_pos = first_row + jnp.arange(block_rows, dtype=jnp.int32)
    key_pos = jnp.arange(segment.shape[0], dtype=jnp.int32)
    same_seq = (
        (query_seg[:, None] == segment[None, :])
        & (query_seg[:, None] < seq_count)
        & (key_pos[None, :] <= query_pos[:, None])
    )
    return same_seq | (key_pos[None, :] == query_pos[:, None])


def dot(left, right):
    return jnp.dot(left, right, preferred_element_type=jnp.float32)


def contract_rows(left, right):
    return lax.dot_general(
        left, right, (((0,), (0,)), ((), ())), preferred_element_type=jnp.float32
    )


def contract_cols(left, right):
    return lax.dot_general(
        left, right, (((1,), (1,)), ((), ())), preferred_element_type=jnp.float32
    )


def rms_back(values, rstd, gain_vec, grad):
    scaled = grad * gain_vec
    row_dots = jnp.sum(values * scaled, axis=1, keepdims=True)
    return rstd * scaled - values * (rstd * rstd * rstd) * row_dots / D


def per_device(
    tokens,
    upstream,
    lengths,
    permutation,
    w_query,
    w_key,
    w_value,
    w_out,
    w_gate,
    w_up,
    w_down,
    q_gain,
    k_gain,
    attn_gain,
    ffn_gain,
):
    rank = lax.axis_index("core") * lax.axis_size("tl") + lax.axis_index("tl")
    own_rows = tokens.shape[0]
    group_rows = own_rows * 2 * lax.axis_size("tl")
    local_width = w_query.shape[1]
    local_heads = local_width // HDIM
    score_scale = 1.0 / math.sqrt(HDIM)
    block_rows = min(512, group_rows)
    block_count = group_rows // block_rows
    seq_count = lengths.shape[1]

    own_group = lax.axis_index("core") == lax.axis_index("th")
    length_row = jnp.where(own_group, lengths, swap(lengths, "core"))[0]
    perm_row = jnp.where(own_group, permutation, swap(permutation, "core"))[0]

    tokens = swap_features(turn(tokens))
    qkv_full = gather_weight(jnp.concatenate([w_query, w_key, w_value], axis=1), 0)
    tokens_all = jnp.concatenate(gather_rows(tokens), axis=0)
    out_full = gather_weight(w_out, 1)
    gate_full = gather_weight(w_gate, 0)
    up_full = gather_weight(w_up, 0)
    down_full = gather_weight(w_down, 1)
    upstream = swap_features(turn(upstream))
    attn_gain = swap_features(attn_gain)
    ffn_gain = swap_features(ffn_gain)

    perm_row = row_place(perm_row, own_rows)
    slots = jnp.arange(group_rows, dtype=jnp.int32)
    inverse = jnp.zeros((group_rows,), jnp.int32).at[perm_row].set(slots)
    segment, position = layout(length_row, group_rows)
    cosine, sine_part = rotary_tables(position)

    packed = tokens_all[perm_row]
    projected = dot(packed, qkv_full)
    q_raw = projected[:, :local_width]
    k_raw = projected[:, local_width : 2 * local_width]
    v_raw = projected[:, 2 * local_width :]
    squares = sum_over(
        jnp.stack([jnp.sum(q_raw * q_raw, axis=1), jnp.sum(k_raw * k_raw, axis=1)]), RANK
    )
    rstd_q = lax.rsqrt(squares[0] / D + epsilon)[:, None]
    rstd_k = lax.rsqrt(squares[1] / D + epsilon)[:, None]
    gain_q = lax.dynamic_slice_in_dim(q_gain, rank * local_width, local_width)
    gain_k = lax.dynamic_slice_in_dim(k_gain, rank * local_width, local_width)
    q_norm = q_raw * rstd_q * gain_q
    k_norm = k_raw * rstd_k * gain_k
    q_b = rotate(q_norm.reshape(group_rows, local_heads, HDIM), cosine, sine_part).astype(
        jnp.bfloat16
    )
    k_b = rotate(k_norm.reshape(group_rows, local_heads, HDIM), cosine, sine_part).astype(
        jnp.bfloat16
    )
    v_b = v_raw.astype(jnp.bfloat16).reshape(group_rows, local_heads, HDIM)

    def forward_block(block_index):
        first_row = block_index * block_rows
        queries = lax.dynamic_slice_in_dim(q_b, first_row, block_rows, 0)
        scores = (
            jnp.einsum("qhd,khd->hqk", queries, k_b, preferred_element_type=jnp.float32)
            * score_scale
        )
        allowed = allowed_block(segment, first_row, block_rows, seq_count)
        masked = jnp.where(allowed[None], scores, masked_score)
        row_peak = jnp.max(masked, axis=-1, keepdims=True)
        exponent = jnp.exp(masked - row_peak)
        totals = jnp.sum(exponent, axis=-1, keepdims=True)
        probs_b = (exponent / totals).astype(jnp.bfloat16)
        attn_block = jnp.einsum("hqk,khd->qhd", probs_b, v_b, preferred_element_type=jnp.float32)
        return (attn_block.astype(jnp.bfloat16), (row_peak + jnp.log(totals))[..., 0])

    attn_blocks, log_totals = lax.map(forward_block, jnp.arange(block_count, dtype=jnp.int32))
    attn_given = attn_blocks.reshape(group_rows, local_width)[inverse]

    def pieces_of(value):
        if not small_grid():
            return [value]
        return [part(value, 0, 0, 2), part(value, 0, 1, 2)]

    attn_out = scatter_rows([dot(piece, out_full) for piece in pieces_of(attn_given)])
    rstd_a = lax.rsqrt(jnp.mean(attn_out * attn_out, axis=1, keepdims=True) + epsilon)
    resid = tokens.astype(jnp.float32) + attn_out * rstd_a * attn_gain
    resid_pieces = gather_rows(resid.astype(jnp.bfloat16))
    gates, ups, hiddens, sums = [], [], [], []
    for piece in resid_pieces:
        gate = dot(piece, gate_full)
        up_part = dot(piece, up_full)
        hidden_b = (gate * jax.nn.sigmoid(gate) * up_part).astype(jnp.bfloat16)
        gates.append(gate)
        ups.append(up_part)
        hiddens.append(hidden_b)
        sums.append(dot(hidden_b, down_full))
    mlp_out = scatter_rows(sums)
    rstd_m = lax.rsqrt(jnp.mean(mlp_out * mlp_out, axis=1, keepdims=True) + epsilon)
    normed_m = mlp_out * rstd_m
    layer_out = turn(swap_features((resid + normed_m * ffn_gain).astype(jnp.bfloat16)))

    grad_f = upstream.astype(jnp.float32)
    ffn_gain_part = jnp.sum(grad_f * normed_m, axis=0)
    d_mlp_b = rms_back(mlp_out, rstd_m, ffn_gain, grad_f).astype(jnp.bfloat16)
    d_mlp_pieces = gather_rows(d_mlp_b)
    d_gates, d_ups, sums = [], [], []
    for gate, up_part, d_mlp in zip(gates, ups, d_mlp_pieces):
        gate_sigmoid = jax.nn.sigmoid(gate)
        d_hidden = contract_cols(d_mlp, down_full)
        d_gate_b = (
            d_hidden * up_part * gate_sigmoid * (1.0 + gate * (1.0 - gate_sigmoid))
        ).astype(jnp.bfloat16)
        d_up_b = (d_hidden * gate * gate_sigmoid).astype(jnp.bfloat16)
        d_gates.append(d_gate_b)
        d_ups.append(d_up_b)
        sums.append(contract_cols(d_gate_b, gate_full) + contract_cols(d_up_b, up_full))
    d_resid = grad_f + scatter_rows(sums)

    def rows(pieces):
        return jnp.concatenate(pieces, axis=0)

    down_shard = scatter_weight(contract_rows(rows(hiddens), rows(d_mlp_pieces)), 1)
    gate_shard = scatter_weight(contract_rows(rows(resid_pieces), rows(d_gates)), 0)
    up_shard = scatter_weight(contract_rows(rows(resid_pieces), rows(d_ups)), 0)

    attn_gain_part = jnp.sum(d_resid * attn_out * rstd_a, axis=0)
    d_attn_b = rms_back(attn_out, rstd_a, attn_gain, d_resid).astype(jnp.bfloat16)
    d_attn_pieces = gather_rows(d_attn_b)
    d_attn_all = rows(d_attn_pieces)
    out_shard = scatter_weight(contract_rows(attn_given, d_attn_all), 1)
    d_given_b = rows([contract_cols(piece, out_full).astype(jnp.bfloat16) for piece in d_attn_pieces])
    d_packed = d_given_b[perm_row].reshape(group_rows, local_heads, HDIM)

    def backward_block(carried, block_in):
        key_acc, value_acc = carried
        block_index, log_rows = block_in
        first_row = block_index * block_rows
        queries = lax.dynamic_slice_in_dim(q_b, first_row, block_rows, 0)
        grad_rows = lax.dynamic_slice_in_dim(d_packed, first_row, block_rows, 0)
        scores = (
            jnp.einsum("qhd,khd->hqk", queries, k_b, preferred_element_type=jnp.float32)
            * score_scale
        )
        allowed = allowed_block(segment, first_row, block_rows, seq_count)
        probs_f = jnp.where(allowed[None], jnp.exp(scores - log_rows[..., None]), 0.0)
        probs_b = probs_f.astype(jnp.bfloat16)
        d_probs = jnp.einsum("qhd,khd->hqk", grad_rows, v_b, preferred_element_type=jnp.float32)
        row_delta = jnp.sum(probs_f * d_probs, axis=-1, keepdims=True)
        d_scores_b = (probs_f * (d_probs - row_delta)).astype(jnp.bfloat16)
        d_query = (
            jnp.einsum("hqk,khd->qhd", d_scores_b, k_b, preferred_element_type=jnp.float32)
            * score_scale
        )
        key_acc = (
            key_acc
            + jnp.einsum("hqk,qhd->khd", d_scores_b, queries, preferred_element_type=jnp.float32)
            * score_scale
        )
        value_acc = value_acc + jnp.einsum(
            "hqk,qhd->khd", probs_b, grad_rows, preferred_element_type=jnp.float32
        )
        return ((key_acc, value_acc), d_query)

    zero_acc = jnp.zeros((group_rows, local_heads, HDIM), jnp.float32)
    (d_key_rot, d_value), d_query_blocks = lax.scan(
        backward_block, (zero_acc, zero_acc), (jnp.arange(block_count, dtype=jnp.int32), log_totals)
    )
    d_query_rot = d_query_blocks.reshape(group_rows, local_heads, HDIM)
    d_q_norm = rotate(d_query_rot, cosine, -sine_part).reshape(group_rows, local_width)
    d_k_norm = rotate(d_key_rot, cosine, -sine_part).reshape(group_rows, local_width)
    d_v = d_value.reshape(group_rows, local_width)
    dots = sum_over(
        jnp.stack(
            [
                jnp.sum(q_raw * gain_q * d_q_norm, axis=1),
                jnp.sum(k_raw * gain_k * d_k_norm, axis=1),
            ]
        ),
        RANK,
    )
    d_q_raw = rstd_q * gain_q * d_q_norm - q_raw * (rstd_q * rstd_q * rstd_q) * dots[0][:, None] / D
    d_k_raw = rstd_k * gain_k * d_k_norm - k_raw * (rstd_k * rstd_k * rstd_k) * dots[1][:, None] / D
    q_gain_part = jnp.sum(d_q_norm * q_raw * rstd_q, axis=0)
    k_gain_part = jnp.sum(d_k_norm * k_raw * rstd_k, axis=0)
    d_qkv_b = jnp.concatenate([d_q_raw, d_k_raw, d_v], axis=1).astype(jnp.bfloat16)
    d_qkv_given = d_qkv_b[inverse]
    input_grad = scatter_rows(
        [contract_cols(piece, qkv_full) for piece in pieces_of(d_qkv_given)]
    )
    qkv_shard = scatter_weight(contract_rows(packed, d_qkv_b), 0)
    tokens_grad = turn(swap_features((d_resid + input_grad).astype(jnp.bfloat16)))

    def placed(part_sum):
        return lax.dynamic_update_slice_in_dim(
            jnp.zeros((D,), jnp.float32), part_sum, rank * local_width, 0
        )

    gain_grads = sum_over(
        jnp.stack(
            [
                placed(q_gain_part),
                placed(k_gain_part),
                swap_features(attn_gain_part),
                swap_features(ffn_gain_part),
            ]
        ),
        DP + TENSOR,
    )
    return (
        layer_out,
        tokens_grad,
        qkv_shard[:, :local_width],
        qkv_shard[:, local_width : 2 * local_width],
        qkv_shard[:, 2 * local_width :],
        out_shard,
        gate_shard,
        up_shard,
        down_shard,
        gain_grads[0],
        gain_grads[1],
        gain_grads[2],
        gain_grads[3],
    )


def solution(mesh):
    dp, tensor = mesh.shape["dp"], mesh.shape["tensor"]
    fine = Mesh(mesh.devices.reshape(dp // 4, 2, 2, 2, tensor // 2), DP + TENSOR)
    rows, weight, weight_out = P(DP + TENSOR, None), P(DP, TENSOR), P(TENSOR, DP)
    return jax.shard_map(
        per_device,
        mesh=fine,
        in_specs=(rows, rows, P(DP, None), P(DP, None))
        + (weight,) * 3
        + (weight_out, weight, weight, weight_out)
        + (P(),) * 4,
        out_specs=(rows, rows)
        + (weight,) * 3
        + (weight_out, weight, weight, weight_out)
        + (P(),) * 4,
        check_vma=False,
    )
```

time: 2740 us -> 1950 us (0.71)
  waiting for transfers between devices: 1680 us -> 582 us
  starting transfers between devices: 0.97 us -> 283 us
  blocking collectives: 73.2 us -> 0 us
  local copies, waits for them, and re-layouts: 213 us -> 266 us
  other arithmetic: 201 us -> 250 us
    reduce_scatter x9 -> x0, waiting for transfers between devices: 971 us -> none  [the longest x1 280 us: per_device(): lax.psum_scatter(jnp.dot(hidden_b, down_full, preferred_element_type=jnp....]
    all_gather x11 -> x0, waiting for transfers between devices: 704 us -> none  [the longest x1 152 us: per_device(): lax.all_gather(resid.astype(jnp.bfloat16), 'tensor', axis=0, tiled=True)]
    ppermute x0 -> x119, waiting for transfers between devices: none -> 582 us  [the longest x95 506 us: swap(): return lax.ppermute(value, axis, SWAP)]
    ppermute x0 -> x119, starting transfers between devices: none -> 283 us  [the longest x14 101 us: turn(): return lax.ppermute(value, ('core', 'th'), TURN)]
    unnamed x98 -> x327, local copies, waits for them, and re-layouts: 21.8 us -> 109 us
    psum x3 -> x0, blocking collectives: 73.2 us -> none  [the longest x1 39.2 us: per_device(): lax.psum((q_gain_full, k_gain_full, attn_gain_part, ffn_gain_part), ('dp'...]
    gather x9 -> x2, local copies, waits for them, and re-layouts: 80.1 us -> 37.9 us  [the longest x1 20.8 us: per_device(): packed = tokens_all[perm_row]]
    concatenate x0 -> x3, other arithmetic: none -> 28.3 us  [the longest x1 16.9 us: per_device(): tokens_all = jnp.concatenate(gather_rows(tokens), axis=0)]
  transfers between devices with their start and end apart: 20 -> 119, of which waited for: 14 -> 45; matrix products, arithmetic and copies ran while one was open for 29% -> 49% of each run, Pallas kernels for 0% -> 0%
where the time goes in v1:
time: 1950 us; the launch traced here: 1930 us
  waiting for transfers between devices  582 us (30%)
  matrix products  542 us (28%)
  starting transfers between devices  283 us (15%)
  local copies, waits for them, and re-layouts  266 us (14%)
  other arithmetic  250 us (13%)
    ppermute x95, waiting for transfers between devices, swap(): return lax.ppermute(value, axis, SWAP)  506 us
    dot_general x10, matrix products, contract_cols(): lax.dot_general(left, right, (((1,), (1,)), ((), ())), preferred_element_...  118 us
    unnamed x327, local copies, waits for them, and re-layouts  109 us
    dot_general x9, matrix products, dot(): return jnp.dot(left, right, preferred_element_type=jnp.float32)  107 us
    ppermute x14, starting transfers between devices, turn(): return lax.ppermute(value, ('core', 'th'), TURN)  101 us
    dot_general x5, matrix products, contract_rows(): lax.dot_general(left, right, (((0,), (0,)), ((), ())), preferred_element_...  98 us
    ppermute x95, starting transfers between devices, swap(): return lax.ppermute(value, axis, SWAP)  94.8 us
    ppermute x5, starting transfers between devices, gather_weight(): second = lax.ppermute(shard, ('core', 'th'), CYCLE)  84.6 us
  transfers between devices with their start and end apart: 119, of which 45 were waited for; matrix products, arithmetic and copies ran while one was open for 49% of the time, Pallas kernels for 0%

profile of v1, /device:TPU:0, one launch (start us, length us, event | category | flops | bytes accessed | tf_op | source)
XLA Modules:
  0.0 1934.1 jit_solution(13248110608505479088)
XLA Ops:
  2.9 17.2 collective-permute-start.58
  65.6 79.8 %collective-permute-start.17 = (bf16[512,256]{1,0:T(8,128)(2,1)}, bf16[512,256]{1,0:T(8,128)(2,1)}, u32[]{:S(2)}, u32[]{:S(2)}) collective-permute-start(bf16[512,256]{1,0:T(8,128)(2,1)} %param.26), channel_id=1, source_target_pairs={{0,2},{2,6},{6,4},{4,0},{1,3},{3,7},{7,5},{5,1},{8,10},{10,14},{14... | collective-permute-start | bytes 786440 | tf_op jit(solution)/shard_map/ppermute | solution.py:43
  239.8 16.9 pad_maximum_fusion
  256.7 20.8 %gather_fusion = bf16[2048,2048]{1,0:T(8,128)(2,1)} fusion(bf16[2048,2048]{1,0:T(8,128)(2,1)} %pad_maximum_fusion, s32[2048]{0:T(1024)S(1)} %broadcast_clamp_fusion), kind=kCustom, calls=%fused_computation | custom fusion | bytes 16785408 | tf_op jit(solution)/shard_map/gather | solution.py:268
  277.5 17.7 fusion.172
  357.1 78.8 %while.27 = (s32[]{:T(128)}, bf16[4,512,4,128]{3,2,1,0:T(4,128)(2,1)}, f32[4,4,512]{2,1,0:T(4,128)}, s32[4]{0:T(128)S(1)}, s32[2048]{0:T(1024)S(1)}, /*index=5*/...) while((s32[]{:T(128)}, ...), condition=%wide.region_5.6_spmd, body=%wide.region_2.5_spmd.sunk | while | flops 2204367872 | bytes 69292248 | solution.py:306
  440.0 11.3 gather_fusion.1
  476.9 11.1 collective-permute-done.30
  490.8 19.6 %collective-permute-done.31 = bf16[256,2048]{1,0:T(8,128)(2,1)S(1)} collective-permute-done((bf16[256,2048]{1,0:T(8,128)(2,1)}, bf16[256,2048]{1,0:T(8,128)(2,1)S(1)}, u32[]{:S(2)}, u32[]{:S(2)}) %collective-permute-start.31) | collective-permute-done | bytes 1048608 | tf_op jit(solution)/shard_map/ppermute | solution.py:25
  517.9 15.0 collective-permute-done.38
  534.6 20.4 %collective-permute-done.39 = bf16[256,2048]{1,0:T(8,128)(2,1)S(1)} collective-permute-done((bf16[256,2048]{1,0:T(8,128)(2,1)}, bf16[256,2048]{1,0:T(8,128)(2,1)S(1)}, u32[]{:S(2)}, u32[]{:S(2)}) %collective-permute-start.39) | collective-permute-done | bytes 1048608 | tf_op jit(solution)/shard_map/ppermute | solution.py:25
  564.6 16.7 collective-permute-done.46
  587.8 15.9 collective-permute-done.47
  613.4 20.9 %collective-permute-done.34 = bf16[256,2048]{1,0:T(8,128)(2,1)S(1)} collective-permute-done((bf16[256,2048]{1,0:T(8,128)(2,1)S(1)}, bf16[256,2048]{1,0:T(8,128)(2,1)S(1)}, u32[]{:S(2)}, u32[]{:S(2)}) %collective-permute-start.34) | collective-permute-done | bytes 1048608 | tf_op jit(solution)/shard_map/ppermute | solution.py:25
  639.5 17.2 collective-permute-done.42
  662.6 13.6 collective-permute-done.50
  678.7 12.5 fusion.120
  692.8 13.4 fusion.174
  706.2 13.8 multiply_convert_fusion.5
  720.0 12.9 fusion.175
  733.7 17.0 multiply_convert_fusion.6
  750.8 12.6 fusion.173
  773.4 39.3 %collective-permute-done.56 = bf16[512,2048]{1,0:T(8,128)(2,1)S(1)} collective-permute-done((bf16[512,2048]{1,0:T(8,128)(2,1)S(1)}, bf16[512,2048]{1,0:T(8,128)(2,1)S(1)}, u32[]{:S(2)}, u32[]{:S(2)}) %collective-permute-start.56) | collective-permute-done | bytes 2097184 | tf_op jit(solution)/shard_map/ppermute | solution.py:25
  820.8 19.6 %multiply_convert_fusion.4 = (bf16[1024,2048]{1,0:T(8,128)(2,1)}, bf16[1024,2048]{1,0:T(8,128)(2,1)}) fusion(f32[1024,2048]{1,0:T(8,128)} %fusion.120, f32[1024,2048]{1,0:T(8,128)} %get-tuple-element.337, bf16[2048,2048]{1,0:T(8,128)(2,1)} %constant_dynamic-update-slice_fusion.36, bf16[512,2048]{1,0:T(8,128)(2,1)} %collective-permute-done.59, ...), kind=kOutput, calls=%fused_computation.87 | convolution fusion | flops 8625586176 | bytes 37748736 | tf_op jit(solution)/shard_map/dot_general | solution.py:209
  840.4 14.9 fusion.176
  855.3 10.6 collective-permute-done.61
  865.9 12.8 convolution_add_fusion.1
  883.6 19.6 %multiply_convert_fusion.2 = (bf16[1024,2048]{1,0:T(8,128)(2,1)}, bf16[1024,2048]{1,0:T(8,128)(2,1)}) fusion(f32[1024,2048]{1,0:T(8,128)} %fusion.174, f32[1024,2048]{1,0:T(8,128)} %get-tuple-element.335, bf16[2048,2048]{1,0:T(8,128)(2,1)} %constant_dynamic-update-slice_fusion.36, bf16[512,2048]{1,0:T(8,128)(2,1)} %collective-permute-done.62, ...), kind=kOutput, calls=%fused_computation.85 | convolution fusion | flops 8625586176 | bytes 37748736 | tf_op jit(solution)/shard_map/dot_general | solution.py:209
  903.2 14.7 fusion.177
  917.9 13.0 convolution_add_fusion
  936.3 24.4 %fusion.65 = bf16[2048,2048]{1,0:T(8,128)(2,1)} fusion(bf16[512,2048]{1,0:T(8,128)(2,1)} %collective-permute-done.62, bf16[512,2048]{1,0:T(8,128)(2,1)} %collective-permute-done.61, bf16[512,2048]{1,0:T(8,128)(2,1)} %collective-permute-done.59, bf16[512,2048]{1,0:T(8,128)(2,1)S(1)} %fusion.73, bf16[1024,2048]{1,0:T(8,128)(2,1)} %get-tuple-element.334, ...), kind=kOutput, calls=%fused_computation.94 | convolution fusion | flops 17234395136 | bytes 25165824 | tf_op jit(solution)/shard_map/dot_general | solution.py:203
  968.9 24.5 %fusion.59 = bf16[2048,2048]{1,0:T(8,128)(2,1)} fusion(bf16[1024,2048]{1,0:T(8,128)(2,1)} %get-tuple-element.260, bf16[1024,2048]{1,0:T(8,128)(2,1)} %get-tuple-element.258, bf16[512,2048]{1,0:T(8,128)(2,1)} %copy-done.44, bf16[512,2048]{1,0:T(8,128)(2,1)S(1)} %copy-done.42, bf16[512,2048]{1,0:T(8,128)(2,1)} %copy-done.104, bf16[512,2048]{1,0:T(8,128)(2,1)} %copy-done.45), kind=kOutput, calls=%fused_computation.92 | convolution fusion | flops 17234395136 | bytes 25165824 | tf_op jit(solution)/shard_map/dot_general | solution.py:203
  998.2 24.9 %fusion.62 = bf16[2048,2048]{1,0:T(8,128)(2,1)} fusion(bf16[1024,2048]{1,0:T(8,128)(2,1)} %get-tuple-element.259, bf16[1024,2048]{1,0:T(8,128)(2,1)} %get-tuple-element.257, bf16[512,2048]{1,0:T(8,128)(2,1)} %copy-done.44, bf16[512,2048]{1,0:T(8,128)(2,1)S(1)} %copy-done.42, bf16[512,2048]{1,0:T(8,128)(2,1)} %copy-done.104, bf16[512,2048]{1,0:T(8,128)(2,1)} %copy-done.45), kind=kOutput, calls=%fused_computation.93 | convolution fusion | flops 17234395136 | bytes 25165824 | tf_op jit(solution)/shard_map/dot_general | solution.py:203
  1042.2 16.6 collective-permute-done.90
  1060.9 20.4 %collective-permute-done.100 = bf16[256,2048]{1,0:T(8,128)(2,1)S(1)} collective-permute-done((bf16[256,2048]{1,0:T(8,128)(2,1)S(1)}, bf16[256,2048]{1,0:T(8,128)(2,1)S(1)}, u32[]{:S(2)}, u32[]{:S(2)}) %collective-permute-start.100) | collective-permute-done | bytes 1048608 | tf_op jit(solution)/shard_map/ppermute | solution.py:25
  1086.9 15.8 collective-permute-done.92
  1110.8 20.8 %collective-permute-done.99 = bf16[256,2048]{1,0:T(8,128)(2,1)S(1)} collective-permute-done((bf16[256,2048]{1,0:T(8,128)(2,1)S(1)}, bf16[256,2048]{1,0:T(8,128)(2,1)S(1)}, u32[]{:S(2)}, u32[]{:S(2)}) %collective-permute-start.99) | collective-permute-done | bytes 1048608 | tf_op jit(solution)/shard_map/ppermute | solution.py:25
  1137.5 16.7 collective-permute-done.91
  1158.2 18.4 collective-permute-done.110
  1203.8 13.3 collective-permute-done.104
  1220.8 11.6 collective-permute-done.96
  1240.2 45.0 %collective-permute-done.66 = bf16[512,2048]{1,0:T(8,128)(2,1)S(1)} collective-permute-done((bf16[512,2048]{1,0:T(8,128)(2,1)S(1)}, bf16[512,2048]{1,0:T(8,128)(2,1)S(1)}, u32[]{:S(2)}, u32[]{:S(2)}) %collective-permute-start.66) | collective-permute-done | bytes 2097184 | tf_op jit(solution)/shard_map/ppermute | solution.py:25
  1300.0 17.2 collective-permute-start.57
  1337.8 261.1 %while.28 = (s32[]{:T(128)}, f32[2048,4,128]{0,2,1:T(8,128)}, f32[2048,4,128]{0,2,1:T(8,128)}, f32[4,512,4,128]{3,1,0,2:T(8,128)}, s32[4]{0:T(128)S(1)}, /*index...) while((s32[]{:T(128)}, f32[2048,4,128]{0,2,1:T(8,128)}, ...), condition=%wide.region_13.14_spmd.clone, body=%wide.region_11.13_spmd.clone.sunk | while | flops 5443419136 | bytes 203501424 | solution.py:395
  1352.9 12.5 multiply_reduce_fusion.8
  1365.4 14.8 multiply_convert_fusion.8
  1391.2 10.4 bitcast_add_fusion.5
  1416.2 12.5 multiply_reduce_fusion.8
  1428.8 14.8 multiply_convert_fusion.8
  1455.7 11.6 bitcast_add_fusion.5
  1482.0 12.5 multiply_reduce_fusion.8
  1494.5 14.8 multiply_convert_fusion.8
  1521.4 11.6 bitcast_add_fusion.5
  1547.7 12.5 multiply_reduce_fusion.8
  1560.2 14.8 multiply_convert_fusion.8
  1587.1 11.6 bitcast_add_fusion.5
  1660.2 17.8 convolution_convert_fusion
  1677.9 11.3 pad_maximum_fusion.2
  1697.9 17.1 gather_fusion.3
  1717.2 9.9 fusion.112
  1759.8 13.2 collective-permute-done.74
  1786.3 10.4 collective-permute-done.76
  1798.7 16.7 collective-permute-done.75
  1849.5 76.5 %collective-permute-done.89 = bf16[512,256]{1,0:T(8,128)(2,1)S(1)} collective-permute-done((bf16[512,256]{1,0:T(8,128)(2,1)S(1)}, bf16[512,256]{1,0:T(8,128)(2,1)S(1)}, u32[]{:S(2)}, u32[]{:S(2)}) %collective-permute-start.89) | collective-permute-done | bytes 262176 | tf_op jit(solution)/shard_map/ppermute | solution.py:85
  (789 shorter events, 785.2 us)
Async XLA Ops:
  0.6 43.2 %collective-permute-start = (bf16[512,2048]{1,0:T(8,128)(2,1)}, bf16[512,2048]{1,0:T(8,128)(2,1)S(1)}, u32[]{:S(2)}, u32[]{:S(2)}) collective-permute-start(bf16[512,2048]{1,0:T(8,128)(2,1)} %param.19), channel_id=1, source_target_pairs={{0,0},{2,4},{4,2},{6,6},{1,1},{3,5},{5,3},{7,7},{8,8},{10,12},{12,... | collective-permute-start | bytes 6291464 | tf_op jit(solution)/shard_map/ppermute | solution.py:29
  2.9 44.6 %collective-permute-start.58 = (bf16[512,2048]{1,0:T(8,128)(2,1)}, bf16[512,2048]{1,0:T(8,128)(2,1)}, u32[]{:S(2)}, u32[]{:S(2)}) collective-permute-start(bf16[512,2048]{1,0:T(8,128)(2,1)} %param.20), channel_id=1, source_target_pairs={{0,0},{2,4},{4,2},{6,6},{1,1},{3,5},{5,3},{7,7},{8,8},{10,12},{12,... | collective-permute-start | bytes 6291464 | tf_op jit(solution)/shard_map/ppermute | solution.py:29
  25.1 130.7 %collective-permute-start.6 = (bf16[256,1536]{1,0:T(8,128)(2,1)}, bf16[256,1536]{1,0:T(8,128)(2,1)}, u32[]{:S(2)}, u32[]{:S(2)}) collective-permute-start(bf16[256,1536]{1,0:T(8,128)(2,1)} %constant_dynamic-update-slice_fusion), channel_id=1, source_target_pairs={{0,0},{2,4},{4,2},{6,6},{1,1},{3,5},{5,3},{7,7},{8,8},{10,12},{12,... | collective-permute-start | bytes 2359304 | tf_op jit(solution)/shard_map/ppermute | solution.py:29
  32.5 137.8 %collective-permute-start.7 = (bf16[256,1536]{1,0:T(8,128)(2,1)}, bf16[256,1536]{1,0:T(8,128)(2,1)}, u32[]{:S(2)}, u32[]{:S(2)}) collective-permute-start(bf16[256,1536]{1,0:T(8,128)(2,1)} %constant_dynamic-update-slice_fusion), channel_id=1, source_target_pairs={{0,2},{2,6},{6,4},{4,0},{1,3},{3,7},{7,5},{5,1},{8,10},{10,14},{14... | collective-permute-start | bytes 2359304 | tf_op jit(solution)/shard_map/ppermute | solution.py:43
  43.9 109.8 %collective-permute-start.16 = (bf16[512,256]{1,0:T(8,128)(2,1)}, bf16[512,256]{1,0:T(8,128)(2,1)}, u32[]{:S(2)}, u32[]{:S(2)}) collective-permute-start(bf16[512,256]{1,0:T(8,128)(2,1)} %param.26), channel_id=1, source_target_pairs={{0,0},{2,4},{4,2},{6,6},{1,1},{3,5},{5,3},{7,7},{8,8},{10,12},{12,... | collective-permute-start | bytes 786440 | tf_op jit(solution)/shard_map/ppermute | solution.py:29
  56.2 122.1 %collective-permute-start.3 = (bf16[512,2048]{1,0:T(8,128)(2,1)S(1)}, bf16[512,2048]{1,0:T(8,128)(2,1)}, u32[]{:S(2)}, u32[]{:S(2)}) collective-permute-start(bf16[512,2048]{1,0:T(8,128)(2,1)S(1)} %dynamic-slice_dynamic-update-slice_fusion.24), channel_id=1, source_target_pairs={{0,1},{1,0},{2,3},{3,2},{4,5},{5,4},{6,7},{7,6},{8,9},{9,8},{10,11... | collective-permute-start | bytes 6291464 | tf_op jit(solution)/shard_map/ppermute | solution.py:25
  65.6 89.6 %collective-permute-start.17 = (bf16[512,256]{1,0:T(8,128)(2,1)}, bf16[512,256]{1,0:T(8,128)(2,1)}, u32[]{:S(2)}, u32[]{:S(2)}) collective-permute-start(bf16[512,256]{1,0:T(8,128)(2,1)} %param.26), channel_id=1, source_target_pairs={{0,2},{2,6},{6,4},{4,0},{1,3},{3,7},{7,5},{5,1},{8,10},{10,14},{14... | collective-permute-start | bytes 786440 | tf_op jit(solution)/shard_map/ppermute | solution.py:43
  178.3 57.4 %collective-permute-start.2 = (bf16[512,2048]{1,0:T(8,128)(2,1)S(1)}, bf16[512,2048]{1,0:T(8,128)(2,1)S(1)}, u32[]{:S(2)}, u32[]{:S(2)}) collective-permute-start(bf16[512,2048]{1,0:T(8,128)(2,1)S(1)} %dynamic-slice_dynamic-update-slice_fusion.24), channel_id=1, source_target_pairs={{0,4},{4,0},{1,5},{5,1},{2,6},{6,2},{3,7},{7,3},{8,12},{12,8},{9,1... | collective-permute-start | bytes 6291464 | tf_op jit(solution)/shard_map/ppermute | solution.py:25
  178.3 57.7 %collective-permute-start.4 = (bf16[512,2048]{1,0:T(8,128)(2,1)}, bf16[512,2048]{1,0:T(8,128)(2,1)S(1)}, u32[]{:S(2)}, u32[]{:S(2)}) collective-permute-start(bf16[512,2048]{1,0:T(8,128)(2,1)} %collective-permute-done.3), channel_id=1, source_target_pairs={{0,4},{4,0},{1,5},{5,1},{2,6},{6,2},{3,7},{7,3},{8,12},{12,8},{9,1... | collective-permute-start | bytes 6291464 | tf_op jit(solution)/shard_map/ppermute | solution.py:25
  209.5 246.4 %collective-permute-start.28 = (bf16[256,2048]{1,0:T(8,128)(2,1)}, bf16[256,2048]{1,0:T(8,128)(2,1)}, u32[]{:S(2)}, u32[]{:S(2)}) collective-permute-start(bf16[256,2048]{1,0:T(8,128)(2,1)} %param.27), channel_id=1, source_target_pairs={{0,0},{2,4},{4,2},{6,6},{1,1},{3,5},{5,3},{7,7},{8,8},{10,12},{12,... | collective-permute-start | bytes 3145736 | tf_op jit(solution)/shard_map/ppermute | solution.py:29
  221.6 240.2 %collective-permute-start.29 = (bf16[256,2048]{1,0:T(8,128)(2,1)}, bf16[256,2048]{1,0:T(8,128)(2,1)}, u32[]{:S(2)}, u32[]{:S(2)}) collective-permute-start(bf16[256,2048]{1,0:T(8,128)(2,1)} %param.27), channel_id=1, source_target_pairs={{0,2},{2,6},{6,4},{4,0},{1,3},{3,7},{7,5},{5,1},{8,10},{10,14},{14... | collective-permute-start | bytes 3145736 | tf_op jit(solution)/shard_map/ppermute | solution.py:43
  226.1 230.9 %collective-permute-start.36 = (bf16[256,2048]{1,0:T(8,128)(2,1)}, bf16[256,2048]{1,0:T(8,128)(2,1)}, u32[]{:S(2)}, u32[]{:S(2)}) collective-permute-start(bf16[256,2048]{1,0:T(8,128)(2,1)} %param.28), channel_id=1, source_target_pairs={{0,0},{2,4},{4,2},{6,6},{1,1},{3,5},{5,3},{7,7},{8,8},{10,12},{12,... | collective-permute-start | bytes 3145736 | tf_op jit(solution)/shard_map/ppermute | solution.py:29
  235.6 233.1 %collective-permute-start.37 = (bf16[256,2048]{1,0:T(8,128)(2,1)}, bf16[256,2048]{1,0:T(8,128)(2,1)}, u32[]{:S(2)}, u32[]{:S(2)}) collective-permute-start(bf16[256,2048]{1,0:T(8,128)(2,1)} %param.28), channel_id=1, source_target_pairs={{0,2},{2,6},{6,4},{4,0},{1,3},{3,7},{7,5},{5,1},{8,10},{10,14},{14... | collective-permute-start | bytes 3145736 | tf_op jit(solution)/shard_map/ppermute | solution.py:43
  238.3 57.9 %collective-permute-start.22 = (bf16[512,256]{1,0:T(8,128)(2,1)S(1)}, bf16[512,256]{1,0:T(8,128)(2,1)}, u32[]{:S(2)}, u32[]{:S(2)}) collective-permute-start(bf16[512,256]{1,0:T(8,128)(2,1)S(1)} %collective-permute-done.18), channel_id=1, source_target_pairs={{0,16},{16,0},{1,17},{17,1},{2,18},{18,2},{3,19},{19,3},{4,20},{20... | collective-permute-start | bytes 786440 | tf_op jit(solution)/shard_map/ppermute | solution.py:25
  311.4 154.3 %collective-permute-start.44 = (bf16[2048,256]{1,0:T(8,128)(2,1)}, bf16[2048,256]{1,0:T(8,128)(2,1)}, u32[]{:S(2)}, u32[]{:S(2)}) collective-permute-start(bf16[2048,256]{1,0:T(8,128)(2,1)} %param.29), channel_id=1, source_target_pairs={{0,0},{2,4},{4,2},{6,6},{1,1},{3,5},{5,3},{7,7},{8,8},{10,12},{12,... | collective-permute-start | bytes 3145736 | tf_op jit(solution)/shard_map/ppermute | solution.py:29
  465.6 44.8 %collective-permute-start.31 = (bf16[256,2048]{1,0:T(8,128)(2,1)}, bf16[256,2048]{1,0:T(8,128)(2,1)S(1)}, u32[]{:S(2)}, u32[]{:S(2)}) collective-permute-start(bf16[256,2048]{1,0:T(8,128)(2,1)} %collective-permute-done.29), channel_id=1, source_target_pairs={{0,8},{8,0},{1,9},{9,1},{2,10},{10,2},{3,11},{11,3},{4,12},{12,4},... | collective-permute-start | bytes 3145736 | tf_op jit(solution)/shard_map/ppermute | solution.py:25
  471.6 44.7 %collective-permute-start.33 = (bf16[256,2048]{1,0:T(8,128)(2,1)}, bf16[256,2048]{1,0:T(8,128)(2,1)S(1)}, u32[]{:S(2)}, u32[]{:S(2)}) collective-permute-start(bf16[256,2048]{1,0:T(8,128)(2,1)} %collective-permute-done.29), channel_id=1, source_target_pairs={{0,16},{16,0},{1,17},{17,1},{2,18},{18,2},{3,19},{19,3},{4,20},{20... | collective-permute-start | bytes 3145736 | tf_op jit(solution)/shard_map/ppermute | solution.py:25
  488.0 44.9 %collective-permute-start.38 = (bf16[256,2048]{1,0:T(8,128)(2,1)}, bf16[256,2048]{1,0:T(8,128)(2,1)S(1)}, u32[]{:S(2)}, u32[]{:S(2)}) collective-permute-start(bf16[256,2048]{1,0:T(8,128)(2,1)} %collective-permute-done.36), channel_id=1, source_target_pairs={{0,8},{8,0},{1,9},{9,1},{2,10},{10,2},{3,11},{11,3},{4,12},{12,4},... | collective-permute-start | bytes 3145736 | tf_op jit(solution)/shard_map/ppermute | solution.py:25
  489.5 65.5 %collective-permute-start.39 = (bf16[256,2048]{1,0:T(8,128)(2,1)}, bf16[256,2048]{1,0:T(8,128)(2,1)S(1)}, u32[]{:S(2)}, u32[]{:S(2)}) collective-permute-start(bf16[256,2048]{1,0:T(8,128)(2,1)} %collective-permute-done.37), channel_id=1, source_target_pairs={{0,8},{8,0},{1,9},{9,1},{2,10},{10,2},{3,11},{11,3},{4,12},{12,4},... | collective-permute-start | bytes 3145736 | tf_op jit(solution)/shard_map/ppermute | solution.py:25
  510.5 72.5 %collective-permute-start.24 = (bf16[512,2048]{1,0:T(8,128)(2,1)S(1)}, bf16[512,2048]{1,0:T(8,128)(2,1)S(1)}, u32[]{:S(2)}, u32[]{:S(2)}) collective-permute-start(bf16[512,2048]{1,0:T(8,128)(2,1)S(1)} %slice.544), channel_id=1, source_target_pairs={{0,4},{4,0},{1,5},{5,1},{2,6},{6,2},{3,7},{7,3},{8,12},{12,8},{9,1... | collective-permute-start | bytes 6291464 | tf_op jit(solution)/shard_map/ppermute | solution.py:25
  510.5 74.0 %collective-permute-start.26 = (bf16[512,2048]{1,0:T(8,128)(2,1)S(1)}, bf16[512,2048]{1,0:T(8,128)(2,1)S(1)}, u32[]{:S(2)}, u32[]{:S(2)}) collective-permute-start(bf16[512,2048]{1,0:T(8,128)(2,1)S(1)} %fusion.84), channel_id=1, source_target_pairs={{0,1},{1,0},{2,3},{3,2},{4,5},{5,4},{6,7},{7,6},{8,9},{9,8},{10,11... | collective-permute-start | bytes 6291464 | tf_op jit(solution)/shard_map/ppermute | solution.py:25
  516.3 43.5 %collective-permute-start.40 = (bf16[256,2048]{1,0:T(8,128)(2,1)}, bf16[256,2048]{1,0:T(8,128)(2,1)S(1)}, u32[]{:S(2)}, u32[]{:S(2)}) collective-permute-start(bf16[256,2048]{1,0:T(8,128)(2,1)} %collective-permute-done.36), channel_id=1, source_target_pairs={{0,16},{16,0},{1,17},{17,1},{2,18},{18,2},{3,19},{19,3},{4,20},{20... | collective-permute-start | bytes 3145736 | tf_op jit(solution)/shard_map/ppermute | solution.py:25
  559.8 44.0 %collective-permute-start.47 = (bf16[2048,256]{1,0:T(8,128)(2,1)S(1)}, bf16[2048,256]{1,0:T(8,128)(2,1)S(1)}, u32[]{:S(2)}, u32[]{:S(2)}) collective-permute-start(bf16[2048,256]{1,0:T(8,128)(2,1)S(1)} %collective-permute-done.45), channel_id=1, source_target_pairs={{0,8},{8,0},{1,9},{9,1},{2,10},{10,2},{3,11},{11,3},{4,12},{12,4},... | collective-permute-start | bytes 3145736 | tf_op jit(solution)/shard_map/ppermute | solution.py:25
  582.9 51.3 %collective-permute-start.34 = (bf16[256,2048]{1,0:T(8,128)(2,1)S(1)}, bf16[256,2048]{1,0:T(8,128)(2,1)S(1)}, u32[]{:S(2)}, u32[]{:S(2)}) collective-permute-start(bf16[256,2048]{1,0:T(8,128)(2,1)S(1)} %collective-permute-done.30), channel_id=1, source_target_pairs={{0,16},{16,0},{1,17},{17,1},{2,18},{18,2},{3,19},{19,3},{4,20},{20... | collective-permute-start | bytes 3145736 | tf_op jit(solution)/shard_map/ppermute | solution.py:25
  584.4 52.2 %collective-permute-start.35 = (bf16[256,2048]{1,0:T(8,128)(2,1)S(1)}, bf16[256,2048]{1,0:T(8,128)(2,1)S(1)}, u32[]{:S(2)}, u32[]{:S(2)}) collective-permute-start(bf16[256,2048]{1,0:T(8,128)(2,1)S(1)} %collective-permute-done.33), channel_id=1, source_target_pairs={{0,8},{8,0},{1,9},{9,1},{2,10},{10,2},{3,11},{11,3},{4,12},{12,4},... | collective-permute-start | bytes 3145736 | tf_op jit(solution)/shard_map/ppermute | solution.py:25
  603.7 52.9 %collective-permute-start.42 = (bf16[256,2048]{1,0:T(8,128)(2,1)S(1)}, bf16[256,2048]{1,0:T(8,128)(2,1)S(1)}, u32[]{:S(2)}, u32[]{:S(2)}) collective-permute-start(bf16[256,2048]{1,0:T(8,128)(2,1)S(1)} %collective-permute-done.38), channel_id=1, source_target_pairs={{0,16},{16,0},{1,17},{17,1},{2,18},{18,2},{3,19},{19,3},{4,20},{20... | collective-permute-start | bytes 3145736 | tf_op jit(solution)/shard_map/ppermute | solution.py:25
  605.5 72.9 %collective-permute-start.53 = (bf16[512,2048]{1,0:T(8,128)(2,1)S(1)}, bf16[512,2048]{1,0:T(8,128)(2,1)S(1)}, u32[]{:S(2)}, u32[]{:S(2)}) collective-permute-start(bf16[512,2048]{1,0:T(8,128)(2,1)S(1)} %fusion.121), channel_id=1, source_target_pairs={{0,1},{1,0},{2,3},{3,2},{4,5},{5,4},{6,7},{7,6},{8,9},{9,8},{10,11... | collective-permute-start | bytes 6291464 | tf_op jit(solution)/shard_map/ppermute | solution.py:25
  611.9 49.6 %collective-permute-start.43 = (bf16[256,2048]{1,0:T(8,128)(2,1)S(1)}, bf16[256,2048]{1,0:T(8,128)(2,1)S(1)}, u32[]{:S(2)}, u32[]{:S(2)}) collective-permute-start(bf16[256,2048]{1,0:T(8,128)(2,1)S(1)} %collective-permute-done.41), channel_id=1, source_target_pairs={{0,8},{8,0},{1,9},{9,1},{2,10},{10,2},{3,11},{11,3},{4,12},{12,4},... | collective-permute-start | bytes 3145736 | tf_op jit(solution)/shard_map/ppermute | solution.py:25
  634.2 44.4 %collective-permute-start.27 = (bf16[512,2048]{1,0:T(8,128)(2,1)S(1)}, bf16[512,2048]{1,0:T(8,128)(2,1)S(1)}, u32[]{:S(2)}, u32[]{:S(2)}) collective-permute-start(bf16[512,2048]{1,0:T(8,128)(2,1)S(1)} %fusion.121), channel_id=1, source_target_pairs={{0,4},{4,0},{1,5},{5,1},{2,6},{6,2},{3,7},{7,3},{8,12},{12,8},{9,1... | collective-permute-start | bytes 6291464 | tf_op jit(solution)/shard_map/ppermute | solution.py:25
  764.6 48.1 %collective-permute-start.56 = (bf16[512,2048]{1,0:T(8,128)(2,1)S(1)}, bf16[512,2048]{1,0:T(8,128)(2,1)S(1)}, u32[]{:S(2)}, u32[]{:S(2)}) collective-permute-start(bf16[512,2048]{1,0:T(8,128)(2,1)S(1)} %fusion.82), channel_id=1, source_target_pairs={{0,1},{1,0},{2,3},{3,2},{4,5},{5,4},{6,7},{7,6},{8,9},{9,8},{10,11... | collective-permute-start | bytes 6291464 | tf_op jit(solution)/shard_map/ppermute | solution.py:25
  817.8 48.1 %collective-permute-start.61 = (bf16[512,2048]{1,0:T(8,128)(2,1)S(1)}, bf16[512,2048]{1,0:T(8,128)(2,1)}, u32[]{:S(2)}, u32[]{:S(2)}) collective-permute-start(bf16[512,2048]{1,0:T(8,128)(2,1)S(1)} %fusion.73), channel_id=1, source_target_pairs={{0,1},{1,0},{2,3},{3,2},{4,5},{5,4},{6,7},{7,6},{8,9},{9,8},{10,11... | collective-permute-start | bytes 6291464 | tf_op jit(solution)/shard_map/ppermute | solution.py:25
  935.8 147.1 %collective-permute-start.63 = (bf16[512,2048]{1,0:T(8,128)(2,1)}, bf16[512,2048]{1,0:T(8,128)(2,1)}, u32[]{:S(2)}, u32[]{:S(2)}) collective-permute-start(bf16[512,2048]{1,0:T(8,128)(2,1)} %slice.539), channel_id=1, source_target_pairs={{0,4},{4,0},{1,5},{5,1},{2,6},{6,2},{3,7},{7,3},{8,12},{12,8},{9,1... | collective-permute-start | bytes 6291464 | tf_op jit(solution)/shard_map/ppermute | solution.py:25
  965.1 61.8 %collective-permute-start.106 = (bf16[2048,256]{1,0:T(8,128)(2,1)}, bf16[2048,256]{1,0:T(8,128)(2,1)}, u32[]{:S(2)}, u32[]{:S(2)}) collective-permute-start(bf16[2048,256]{1,0:T(8,128)(2,1)} %get-tuple-element.271), channel_id=1, source_target_pairs={{0,16},{16,0},{1,17},{17,1},{2,18},{18,2},{3,19},{19,3},{4,20},{20... | collective-permute-start | bytes 3145736 | tf_op jit(solution)/shard_map/ppermute | solution.py:25
  965.7 73.2 %collective-permute-start.108 = (bf16[2048,256]{1,0:T(8,128)(2,1)}, bf16[2048,256]{1,0:T(8,128)(2,1)S(1)}, u32[]{:S(2)}, u32[]{:S(2)}) collective-permute-start(bf16[2048,256]{1,0:T(8,128)(2,1)} %get-tuple-element.274), channel_id=1, source_target_pairs={{0,16},{16,0},{1,17},{17,1},{2,18},{18,2},{3,19},{19,3},{4,20},{20... | collective-permute-start | bytes 3145736 | tf_op jit(solution)/shard_map/ppermute | solution.py:25
  967.2 73.4 %collective-permute-start.111 = (bf16[2048,256]{1,0:T(8,128)(2,1)}, bf16[2048,256]{1,0:T(8,128)(2,1)}, u32[]{:S(2)}, u32[]{:S(2)}) collective-permute-start(bf16[2048,256]{1,0:T(8,128)(2,1)} %get-tuple-element.272), channel_id=1, source_target_pairs={{0,8},{8,0},{1,9},{9,1},{2,10},{10,2},{3,11},{11,3},{4,12},{12,4},... | collective-permute-start | bytes 3145736 | tf_op jit(solution)/shard_map/ppermute | solution.py:25
  1036.4 44.8 %collective-permute-start.100 = (bf16[256,2048]{1,0:T(8,128)(2,1)S(1)}, bf16[256,2048]{1,0:T(8,128)(2,1)S(1)}, u32[]{:S(2)}, u32[]{:S(2)}) collective-permute-start(bf16[256,2048]{1,0:T(8,128)(2,1)S(1)} %copy-done.54), channel_id=1, source_target_pairs={{0,16},{16,0},{1,17},{17,1},{2,18},{18,2},{3,19},{19,3},{4,20},{20... | collective-permute-start | bytes 3145736 | tf_op jit(solution)/shard_map/ppermute | solution.py:25
  1038.9 47.9 %collective-permute-start.103 = (bf16[256,2048]{1,0:T(8,128)(2,1)S(1)}, bf16[256,2048]{1,0:T(8,128)(2,1)S(1)}, u32[]{:S(2)}, u32[]{:S(2)}) collective-permute-start(bf16[256,2048]{1,0:T(8,128)(2,1)S(1)} %copy-done.53), channel_id=1, source_target_pairs={{0,8},{8,0},{1,9},{9,1},{2,10},{10,2},{3,11},{11,3},{4,12},{12,4},... | collective-permute-start | bytes 3145736 | tf_op jit(solution)/shard_map/ppermute | solution.py:25
  1040.6 62.2 %collective-permute-start.92 = (bf16[256,2048]{1,0:T(8,128)(2,1)S(1)}, bf16[256,2048]{1,0:T(8,128)(2,1)S(1)}, u32[]{:S(2)}, u32[]{:S(2)}) collective-permute-start(bf16[256,2048]{1,0:T(8,128)(2,1)S(1)} %get-tuple-element.286), channel_id=1, source_target_pairs={{0,16},{16,0},{1,17},{17,1},{2,18},{18,2},{3,19},{19,3},{4,20},{20... | collective-permute-start | bytes 3145736 | tf_op jit(solution)/shard_map/ppermute | solution.py:25
  1058.8 45.7 %collective-permute-start.107 = (bf16[2048,256]{1,0:T(8,128)(2,1)S(1)}, bf16[2048,256]{1,0:T(8,128)(2,1)S(1)}, u32[]{:S(2)}, u32[]{:S(2)}) collective-permute-start(bf16[2048,256]{1,0:T(8,128)(2,1)S(1)} %add_convert_fusion.6), channel_id=1, source_target_pairs={{0,8},{8,0},{1,9},{9,1},{2,10},{10,2},{3,11},{11,3},{4,12},{12,4},... | collective-permute-start | bytes 3145736 | tf_op jit(solution)/shard_map/ppermute | solution.py:25
  1082.9 48.7 %collective-permute-start.99 = (bf16[256,2048]{1,0:T(8,128)(2,1)S(1)}, bf16[256,2048]{1,0:T(8,128)(2,1)S(1)}, u32[]{:S(2)}, u32[]{:S(2)}) collective-permute-start(bf16[256,2048]{1,0:T(8,128)(2,1)S(1)} %add_convert_fusion.10), channel_id=1, source_target_pairs={{0,8},{8,0},{1,9},{9,1},{2,10},{10,2},{3,11},{11,3},{4,12},{12,4},... | collective-permute-start | bytes 3145736 | tf_op jit(solution)/shard_map/ppermute | solution.py:25
  1086.9 103.5 %collective-permute-start.60 = (bf16[512,2048]{1,0:T(8,128)(2,1)S(1)}, bf16[512,2048]{1,0:T(8,128)(2,1)S(1)}, u32[]{:S(2)}, u32[]{:S(2)}) collective-permute-start(bf16[512,2048]{1,0:T(8,128)(2,1)S(1)} %copy-done.43), channel_id=1, source_target_pairs={{0,4},{4,0},{1,5},{5,1},{2,6},{6,2},{3,7},{7,3},{8,12},{12,8},{9,1... | collective-permute-start | bytes 6291464 | tf_op jit(solution)/shard_map/ppermute | solution.py:25
  1102.8 51.4 %collective-permute-start.91 = (bf16[256,2048]{1,0:T(8,128)(2,1)S(1)}, bf16[256,2048]{1,0:T(8,128)(2,1)S(1)}, u32[]{:S(2)}, u32[]{:S(2)}) collective-permute-start(bf16[256,2048]{1,0:T(8,128)(2,1)S(1)} %add_convert_fusion.14), channel_id=1, source_target_pairs={{0,8},{8,0},{1,9},{9,1},{2,10},{10,2},{3,11},{11,3},{4,12},{12,4},... | collective-permute-start | bytes 3145736 | tf_op jit(solution)/shard_map/ppermute | solution.py:25
  1104.5 88.2 %collective-permute-start.64 = (bf16[512,2048]{1,0:T(8,128)(2,1)S(1)}, bf16[512,2048]{1,0:T(8,128)(2,1)S(1)}, u32[]{:S(2)}, u32[]{:S(2)}) collective-permute-start(bf16[512,2048]{1,0:T(8,128)(2,1)S(1)} %fusion.80), channel_id=1, source_target_pairs={{0,1},{1,0},{2,3},{3,2},{4,5},{5,4},{6,7},{7,6},{8,9},{9,8},{10,11... | collective-permute-start | bytes 6291464 | tf_op jit(solution)/shard_map/ppermute | solution.py:25
  1109.3 67.3 %collective-permute-start.110 = (bf16[2048,256]{1,0:T(8,128)(2,1)}, bf16[2048,256]{1,0:T(8,128)(2,1)S(1)}, u32[]{:S(2)}, u32[]{:S(2)}) collective-permute-start(bf16[2048,256]{1,0:T(8,128)(2,1)} %get-tuple-element.273), channel_id=1, source_target_pairs={{0,8},{8,0},{1,9},{9,1},{2,10},{10,2},{3,11},{11,3},{4,12},{12,4},... | collective-permute-start | bytes 3145736 | tf_op jit(solution)/shard_map/ppermute | solution.py:25
  1131.7 46.6 %collective-permute-start.112 = (bf16[2048,256]{1,0:T(8,128)(2,1)S(1)}, bf16[2048,256]{1,0:T(8,128)(2,1)S(1)}, u32[]{:S(2)}, u32[]{:S(2)}) collective-permute-start(bf16[2048,256]{1,0:T(8,128)(2,1)S(1)} %get-tuple-element.270), channel_id=1, source_target_pairs={{0,16},{16,0},{1,17},{17,1},{2,18},{18,2},{3,19},{19,3},{4,20},{20... | collective-permute-start | bytes 3145736 | tf_op jit(solution)/shard_map/ppermute | solution.py:25
  1154.2 48.8 %collective-permute-start.102 = (bf16[256,2048]{1,0:T(8,128)(2,1)}, bf16[256,2048]{1,0:T(8,128)(2,1)}, u32[]{:S(2)}, u32[]{:S(2)}) collective-permute-start(bf16[256,2048]{1,0:T(8,128)(2,1)} %get-tuple-element.279), channel_id=1, source_target_pairs={{0,8},{8,0},{1,9},{9,1},{2,10},{10,2},{3,11},{11,3},{4,12},{12,4},... | collective-permute-start | bytes 3145736 | tf_op jit(solution)/shard_map/ppermute | solution.py:25
  1176.6 44.1 %collective-permute-start.94 = (bf16[256,2048]{1,0:T(8,128)(2,1)}, bf16[256,2048]{1,0:T(8,128)(2,1)}, u32[]{:S(2)}, u32[]{:S(2)}) collective-permute-start(bf16[256,2048]{1,0:T(8,128)(2,1)} %get-tuple-element.285), channel_id=1, source_target_pairs={{0,8},{8,0},{1,9},{9,1},{2,10},{10,2},{3,11},{11,3},{4,12},{12,4},... | collective-permute-start | bytes 3145736 | tf_op jit(solution)/shard_map/ppermute | solution.py:25
  1178.3 61.3 %collective-permute-start.109 = (bf16[2048,256]{1,0:T(8,128)(2,1)}, bf16[2048,256]{1,0:T(8,128)(2,1)}, u32[]{:S(2)}, u32[]{:S(2)}) collective-permute-start(bf16[2048,256]{1,0:T(8,128)(2,1)} %get-tuple-element.269), channel_id=1, source_target_pairs={{0,0},{2,4},{4,2},{6,6},{1,1},{3,5},{5,3},{7,7},{8,8},{10,12},{12,... | collective-permute-start | bytes 3145736 | tf_op jit(solution)/shard_map/ppermute | solution.py:29
  1202.9 97.1 %collective-permute-start.101 = (bf16[256,2048]{1,0:T(8,128)(2,1)S(1)}, bf16[256,2048]{1,0:T(8,128)(2,1)S(1)}, u32[]{:S(2)}, u32[]{:S(2)}) collective-permute-start(bf16[256,2048]{1,0:T(8,128)(2,1)S(1)} %get-tuple-element.275), channel_id=1, source_target_pairs={{0,0},{2,4},{4,2},{6,6},{1,1},{3,5},{5,3},{7,7},{8,8},{10,12},{12,... | collective-permute-start | bytes 3145736 | tf_op jit(solution)/shard_map/ppermute | solution.py:29
  1217.1 68.1 %collective-permute-start.66 = (bf16[512,2048]{1,0:T(8,128)(2,1)S(1)}, bf16[512,2048]{1,0:T(8,128)(2,1)S(1)}, u32[]{:S(2)}, u32[]{:S(2)}) collective-permute-start(bf16[512,2048]{1,0:T(8,128)(2,1)S(1)} %get-tuple-element.297), channel_id=1, source_target_pairs={{0,1},{1,0},{2,3},{3,2},{4,5},{5,4},{6,7},{7,6},{8,9},{9,8},{10,11... | collective-permute-start | bytes 6291464 | tf_op jit(solution)/shard_map/ppermute | solution.py:25
  1220.7 66.9 %collective-permute-start.113 = (bf16[2048,256]{1,0:T(8,128)(2,1)S(1)}, bf16[2048,256]{1,0:T(8,128)(2,1)S(1)}, u32[]{:S(2)}, u32[]{:S(2)}) collective-permute-start(bf16[2048,256]{1,0:T(8,128)(2,1)S(1)} %copy-done.52), channel_id=1, source_target_pairs={{2,0},{6,2},{4,6},{0,4},{3,1},{7,3},{5,7},{1,5},{10,8},{14,10},{12... | collective-permute-start | bytes 3145736 | tf_op jit(solution)/shard_map/ppermute | solution.py:85
  1235.4 83.5 %collective-permute-start.65 = (bf16[512,2048]{1,0:T(8,128)(2,1)S(1)}, bf16[512,2048]{1,0:T(8,128)(2,1)S(1)}, u32[]{:S(2)}, u32[]{:S(2)}) collective-permute-start(bf16[512,2048]{1,0:T(8,128)(2,1)S(1)} %get-tuple-element.297), channel_id=1, source_target_pairs={{0,4},{4,0},{1,5},{5,1},{2,6},{6,2},{3,7},{7,3},{8,12},{12,8},{9,1... | collective-permute-start | bytes 6291464 | tf_op jit(solution)/shard_map/ppermute | solution.py:25
  1239.6 60.4 %collective-permute-start.105 = (bf16[256,2048]{1,0:T(8,128)(2,1)S(1)}, bf16[256,2048]{1,0:T(8,128)(2,1)S(1)}, u32[]{:S(2)}, u32[]{:S(2)}) collective-permute-start(bf16[256,2048]{1,0:T(8,128)(2,1)S(1)} %add_convert_fusion.7), channel_id=1, source_target_pairs={{2,0},{6,2},{4,6},{0,4},{3,1},{7,3},{5,7},{1,5},{10,8},{14,10},{12... | collective-permute-start | bytes 3145736 | tf_op jit(solution)/shard_map/ppermute | solution.py:85
  1287.6 463.9 %collective-permute-start.93 = (bf16[256,2048]{1,0:T(8,128)(2,1)}, bf16[256,2048]{1,0:T(8,128)(2,1)}, u32[]{:S(2)}, u32[]{:S(2)}) collective-permute-start(bf16[256,2048]{1,0:T(8,128)(2,1)} %get-tuple-element.281), channel_id=1, source_target_pairs={{0,0},{2,4},{4,2},{6,6},{1,1},{3,5},{5,3},{7,7},{8,8},{10,12},{12,... | collective-permute-start | bytes 3145736 | tf_op jit(solution)/shard_map/ppermute | solution.py:29
  1300.0 451.6 %collective-permute-start.97 = (bf16[256,2048]{1,0:T(8,128)(2,1)}, bf16[256,2048]{1,0:T(8,128)(2,1)}, u32[]{:S(2)}, u32[]{:S(2)}) collective-permute-start(bf16[256,2048]{1,0:T(8,128)(2,1)} %add_convert_fusion.11), channel_id=1, source_target_pairs={{2,0},{6,2},{4,6},{0,4},{3,1},{7,3},{5,7},{1,5},{10,8},{14,10},{12... | collective-permute-start | bytes 3145736 | tf_op jit(solution)/shard_map/ppermute | solution.py:85
  1300.0 459.2 %collective-permute-start.57 = (bf16[512,2048]{1,0:T(8,128)(2,1)}, bf16[512,2048]{1,0:T(8,128)(2,1)}, u32[]{:S(2)}, u32[]{:S(2)}) collective-permute-start(bf16[512,2048]{1,0:T(8,128)(2,1)} %dynamic-slice_dynamic-update-slice_fusion.16), channel_id=1, source_target_pairs={{0,0},{2,4},{4,2},{6,6},{1,1},{3,5},{5,3},{7,7},{8,8},{10,12},{12,... | collective-permute-start | bytes 6291464 | tf_op jit(solution)/shard_map/ppermute | solution.py:29
  1641.8 73.2 %collective-permute-start.114 = (f32[4,2048]{1,0:T(4,128)S(1)}, f32[4,2048]{1,0:T(4,128)S(1)}, u32[]{:S(2)}, u32[]{:S(2)}) collective-permute-start(f32[4,2048]{1,0:T(4,128)S(1)} %pad_maximum_fusion.13), channel_id=1, source_target_pairs={{0,16},{16,0},{1,17},{17,1},{2,18},{18,2},{3,19},{19,3},{4,20},{20... | collective-permute-start | bytes 98312 | tf_op jit(solution)/shard_map/ppermute | solution.py:25
  1751.5 67.3 %collective-permute-start.70 = (bf16[512,2048]{1,0:T(8,128)(2,1)S(1)}, bf16[512,2048]{1,0:T(8,128)(2,1)S(1)}, u32[]{:S(2)}, u32[]{:S(2)}) collective-permute-start(bf16[512,2048]{1,0:T(8,128)(2,1)S(1)} %slice.538), channel_id=1, source_target_pairs={{0,4},{4,0},{1,5},{5,1},{2,6},{6,2},{3,7},{7,3},{8,12},{12,8},{9,1... | collective-permute-start | bytes 6291464 | tf_op jit(solution)/shard_map/ppermute | solution.py:25
  1756.1 66.3 %collective-permute-start.72 = (bf16[512,2048]{1,0:T(8,128)(2,1)S(1)}, bf16[512,2048]{1,0:T(8,128)(2,1)S(1)}, u32[]{:S(2)}, u32[]{:S(2)}) collective-permute-start(bf16[512,2048]{1,0:T(8,128)(2,1)S(1)} %fusion.76), channel_id=1, source_target_pairs={{0,1},{1,0},{2,3},{3,2},{4,5},{5,4},{6,7},{7,6},{8,9},{9,8},{10,11... | collective-permute-start | bytes 6291464 | tf_op jit(solution)/shard_map/ppermute | solution.py:25
  1796.7 49.8 %collective-permute-start.86 = (bf16[512,256]{1,0:T(8,128)(2,1)}, bf16[512,256]{1,0:T(8,128)(2,1)}, u32[]{:S(2)}, u32[]{:S(2)}) collective-permute-start(bf16[512,256]{1,0:T(8,128)(2,1)} %get-tuple-element.307), channel_id=1, source_target_pairs={{0,8},{8,0},{1,9},{9,1},{2,10},{10,2},{3,11},{11,3},{4,12},{12,4},... | collective-permute-start | bytes 786440 | tf_op jit(solution)/shard_map/ppermute | solution.py:25
  1835.8 91.9 %collective-permute-start.77 = (bf16[256,1536]{1,0:T(8,128)(2,1)S(1)}, bf16[256,1536]{1,0:T(8,128)(2,1)S(1)}, u32[]{:S(2)}, u32[]{:S(2)}) collective-permute-start(bf16[256,1536]{1,0:T(8,128)(2,1)S(1)} %copy-done.55), channel_id=1, source_target_pairs={{0,0},{2,4},{4,2},{6,6},{1,1},{3,5},{5,3},{7,7},{8,8},{10,12},{12,... | collective-permute-start | bytes 2359304 | tf_op jit(solution)/shard_map/ppermute | solution.py:29
  1844.2 84.9 %collective-permute-start.73 = (bf16[512,2048]{1,0:T(8,128)(2,1)S(1)}, bf16[512,2048]{1,0:T(8,128)(2,1)S(1)}, u32[]{:S(2)}, u32[]{:S(2)}) collective-permute-start(bf16[512,2048]{1,0:T(8,128)(2,1)S(1)} %dynamic-slice_dynamic-update-slice_fusion), channel_id=1, source_target_pairs={{0,0},{2,4},{4,2},{6,6},{1,1},{3,5},{5,3},{7,7},{8,8},{10,12},{12,... | collective-permute-start | bytes 6291464 | tf_op jit(solution)/shard_map/ppermute | solution.py:29
  1846.5 81.3 %collective-permute-start.81 = (bf16[256,1536]{1,0:T(8,128)(2,1)S(1)}, bf16[256,1536]{1,0:T(8,128)(2,1)S(1)}, u32[]{:S(2)}, u32[]{:S(2)}) collective-permute-start(bf16[256,1536]{1,0:T(8,128)(2,1)S(1)} %add_convert_fusion.15), channel_id=1, source_target_pairs={{2,0},{6,2},{4,6},{0,4},{3,1},{7,3},{5,7},{1,5},{10,8},{14,10},{12... | collective-permute-start | bytes 2359304 | tf_op jit(solution)/shard_map/ppermute | solution.py:85
  1848.8 77.2 %collective-permute-start.89 = (bf16[512,256]{1,0:T(8,128)(2,1)S(1)}, bf16[512,256]{1,0:T(8,128)(2,1)S(1)}, u32[]{:S(2)}, u32[]{:S(2)}) collective-permute-start(bf16[512,256]{1,0:T(8,128)(2,1)S(1)} %add_convert_fusion.19), channel_id=1, source_target_pairs={{2,0},{6,2},{4,6},{0,4},{3,1},{7,3},{5,7},{1,5},{10,8},{14,10},{12... | collective-permute-start | bytes 786440 | tf_op jit(solution)/shard_map/ppermute | solution.py:85
  (189 other events, 4358.5 us)

commit v2 on v1

v2 whole, which is shorter than its diff:
```python
import functools
import math

import jax
import jax.numpy as jnp
from jax import lax
from jax.experimental import pallas as pl
from jax.experimental.pallas import tpu as pltpu
from jax.sharding import Mesh, PartitionSpec as P

D = 2048
HDIM = 128

epsilon = 1e-06
rope_base = 500000.0
masked_score = -1e30
BLOCK = 256
VMEM_BYTES = 48 * 1024 * 1024
MESH = pl.DeviceIdType.MESH

SWAP = [(0, 1), (1, 0)]
TURN = [(1, 2), (2, 1)]
CYCLE = [(0, 1), (1, 3), (3, 2), (2, 0)]
CYCLE_BACK = [(d, s) for s, d in CYCLE]
DP = ("a", "b", "core")
TENSOR = ("th", "tl")
RANK = ("core", "tl")


def swap(value, axis):
    return lax.ppermute(value, axis, SWAP)


def turn(value):
    stays = lax.axis_index("core") == lax.axis_index("th")
    return jnp.where(stays, value, lax.ppermute(value, ("core", "th"), TURN))


def small_grid():
    return lax.axis_size("a") == 2 and lax.axis_size("tl") == 2


def part(value, dim, index, count):
    size = value.shape[dim] // count
    return lax.slice_in_dim(value, index * size, (index + 1) * size, axis=dim)


def pieces_of_weight(shard):
    return turn(shard), lax.ppermute(shard, ("core", "th"), CYCLE)


def gather_weight(pieces):
    first, second = pieces
    upper = lax.axis_index("th") == 0
    pair = jnp.concatenate(
        [jnp.where(upper, first, second), jnp.where(upper, second, first)], axis=0
    )
    return lax.all_gather(pair, ("a", "b"), axis=0, tiled=True)


def finish_scatter(first, second):
    return turn(first).astype(jnp.float32) + lax.ppermute(
        second, ("core", "th"), CYCLE_BACK
    ).astype(jnp.float32)


def in_turn(low_part, high_part):
    upper = lax.axis_index("th") == 0
    return jnp.where(upper, low_part, high_part), jnp.where(upper, high_part, low_part)


def scatter_weight(total):
    pair = lax.psum_scatter(
        total.astype(jnp.bfloat16), ("a", "b"), scatter_dimension=0, tiled=True
    )
    return finish_scatter(*in_turn(part(pair, 0, 0, 2), part(pair, 0, 1, 2)))


def greet():
    a, b, core = lax.axis_index("a"), lax.axis_index("b"), lax.axis_index("core")
    th, tl = lax.axis_index("th"), lax.axis_index("tl")
    barrier = pltpu.get_barrier_semaphore()
    others = (
        {"a": 1 - a},
        {"b": 1 - b},
        {"core": 1 - core},
        {"tl": 1 - tl},
        {"th": 1 - th},
        {"core": 1 - core, "th": 1 - th},
    )
    for other in others:
        pl.semaphore_signal(barrier, inc=1, device_id=other, device_id_type=MESH)
    pl.semaphore_wait(barrier, len(others))


CHUNKS = 4


def entry_slots(plan):
    return 4 * CHUNKS + sum(3 * len(units) + 6 for units in plan)


def entry_kernel(plan, *refs):
    shard_count = sum(len(units) for units in plan)
    tokens, shards = refs[0], refs[1 : 1 + shard_count]
    tokens_all, fulls = refs[1 + shard_count], refs[2 + shard_count : -3]
    send, recv, local = refs[-3:]
    a, b, core = lax.axis_index("a"), lax.axis_index("b"), lax.axis_index("core")
    th, tl = lax.axis_index("th"), lax.axis_index("tl")
    stays = core == th
    greet()
    used = [0]

    def slots(count):
        used[0] += count
        return used[0] - count

    def remote(source, target, slot, to):
        return pltpu.make_async_remote_copy(
            src_ref=source,
            dst_ref=target,
            send_sem=send.at[slot],
            recv_sem=recv.at[slot],
            device_id=to,
            device_id_type=MESH,
        )

    def arrived(target, slot):
        remote(target, target, slot, {"core": 1 - core}).wait_recv()

    stages, taken = [], 0
    for full, units in zip(fulls, plan):
        stage = []
        for column in units:
            shard = shards[taken]
            base = slots(3)
            height, width = shard.shape

            def place(sub, full=full, column=column, height=height, width=width):
                row = pl.multiple_of((4 * a + 2 * b + sub) * height, height)
                return full.at[pl.ds(row, height), pl.ds(column, width)]

            stage.append((shard, place, base, taken))
            taken += 1
        stages.append(stage)

    def near_copy(shard, place, base):
        return remote(shard, place(core), base + 2, {"core": 1 - core})

    def far_copy(shard, place, base):
        return remote(shard, place(core), base + core, {"core": th, "th": 1 - th})

    def start_stage(stage):
        for shard, place, base, index in stage:
            far_copy(shard, place, base).start()

            @pl.when(stays)
            def _():
                pltpu.make_async_copy(shard, place(core), local.at[index]).start()

            @pl.when(jnp.logical_not(stays))
            def _():
                near_copy(shard, place, base).start()

    def finish_stage(stage):
        for shard, place, base, index in stage:

            @pl.when(stays)
            def _():
                pltpu.make_async_copy(shard, place(core), local.at[index]).wait()
                arrived(place(1 - core), base + 2)

            @pl.when(jnp.logical_not(stays))
            def _():
                arrived(place(0), base)
                arrived(place(1), base + 1)

    def piece(full, block_a, block_b, sub):
        height = full.shape[0] // 8
        row = pl.multiple_of((4 * block_a + 2 * block_b + sub) * height, height)
        return full.at[pl.ds(row, height), :]

    def ring(full, base):
        to_a, to_b = {"a": 1 - a}, {"b": 1 - b}
        return (
            [remote(piece(full, a, b, sub), piece(full, a, b, sub), base + sub, to_b) for sub in (0, 1)],
            [remote(piece(full, a, b, sub), piece(full, a, b, sub), base + 2 + sub, to_a) for sub in (0, 1)],
            remote(piece(full, a, 1 - b, 0), piece(full, a, 1 - b, 0), base + 4, to_a),
            remote(piece(full, 1 - a, b, 1), piece(full, 1 - a, b, 1), base + 5, to_b),
        )

    ring_base = [slots(6) for _ in fulls]

    def start_ring(index):
        over_b, over_a, _, _ = ring(fulls[index], ring_base[index])
        for copy in (over_b[0], over_a[1], over_b[1], over_a[0]):
            copy.start()

    def forward_ring(index):
        full, base = fulls[index], ring_base[index]
        arrived(piece(full, a, 1 - b, 0), base)
        ring(full, base)[2].start()
        arrived(piece(full, 1 - a, b, 1), base + 3)
        ring(full, base)[3].start()

    def finish_ring(index):
        full, base = fulls[index], ring_base[index]
        arrived(piece(full, a, 1 - b, 1), base + 1)
        arrived(piece(full, 1 - a, b, 0), base + 2)
        arrived(piece(full, 1 - a, 1 - b, 0), base + 4)
        arrived(piece(full, 1 - a, 1 - b, 1), base + 5)
        over_b, over_a, first, second = ring(full, base)
        for copy in (*over_b, *over_a, first, second):
            copy.wait_send()

    rows = tokens.shape[0]
    step = rows // CHUNKS
    row_base = slots(4 * CHUNKS)

    def rows_of(block_core, block_tl, chunk):
        row = pl.multiple_of((2 * block_core + block_tl) * rows + chunk * step, step)
        return tokens_all.at[pl.ds(row, step), :]

    def row_copies(chunk):
        slot = row_base + 4 * chunk
        own, other = rows_of(core, tl, chunk), rows_of(core, 1 - tl, chunk)
        return (
            remote(
                tokens.at[pl.ds(chunk * step, step), :],
                rows_of(th, tl, chunk),
                slot,
                {"core": th, "th": core},
            ),
            remote(own, own, slot + 1, {"tl": 1 - tl}),
            remote(own, own, slot + 2, {"core": 1 - core}),
            remote(other, other, slot + 3, {"core": 1 - core}),
        )

    def own_rows(chunk):
        return pltpu.make_async_copy(
            tokens.at[pl.ds(chunk * step, step), :],
            rows_of(core, tl, chunk),
            local.at[shard_count + chunk],
        )

    for chunk in range(CHUNKS):

        @pl.when(stays)
        def _():
            own_rows(chunk).start()

    start_stage(stages[0])
    start_stage(stages[1])
    finish_stage(stages[0])
    start_ring(0)
    for stage in stages[2:]:
        start_stage(stage)
    finish_stage(stages[1])
    start_ring(1)
    for chunk in range(CHUNKS):

        @pl.when(jnp.logical_not(stays))
        def _():
            row_copies(chunk)[0].start()

        @pl.when(stays)
        def _():
            own_rows(chunk).wait()
            row_copies(chunk)[1].start()
            row_copies(chunk)[2].start()

    forward_ring(0)
    forward_ring(1)
    for index in range(2, len(fulls)):
        finish_stage(stages[index])
        start_ring(index)
    for chunk in range(CHUNKS):

        @pl.when(jnp.logical_not(stays))
        def _():
            arrived(rows_of(core, tl, chunk), row_base + 4 * chunk)
            row_copies(chunk)[1].start()
            row_copies(chunk)[2].start()

        arrived(rows_of(core, 1 - tl, chunk), row_base + 4 * chunk + 1)
        row_copies(chunk)[3].start()
    for index in range(2, len(fulls)):
        forward_ring(index)
    for index in range(len(fulls)):
        finish_ring(index)
    for chunk in range(CHUNKS):
        arrived(rows_of(1 - core, tl, chunk), row_base + 4 * chunk + 2)
        arrived(rows_of(1 - core, 1 - tl, chunk), row_base + 4 * chunk + 3)

        @pl.when(jnp.logical_not(stays))
        def _():
            row_copies(chunk)[0].wait_send()

        for copy in row_copies(chunk)[1:]:
            copy.wait_send()
    for stage in stages:
        for shard, place, base, _ in stage:
            far_copy(shard, place, base).wait_send()

            @pl.when(jnp.logical_not(stays))
            def _():
                near_copy(shard, place, base).wait_send()


def leave_kernel(cuts, *refs):
    count = len(cuts)
    partial, resid, totals = refs[0], refs[1], refs[2 : 2 + count]
    outs = refs[2 + count : 2 + count + 1 + sum(len(cut) for cut in cuts)]
    rows_out, shard_outs = outs[0], outs[1:]
    scratch = refs[2 + count + len(outs) :]
    peer_far, peer_near, far_sum, from_far, done_rows = scratch[:5]
    boxes = [scratch[5 + 7 * index : 12 + 7 * index] for index in range(count)]
    send, recv, local = scratch[-3:]
    a, b, core = lax.axis_index("a"), lax.axis_index("b"), lax.axis_index("core")
    th, tl = lax.axis_index("th"), lax.axis_index("tl")
    stays = core == th
    to_a, to_b, to_core, to_tl = {"a": 1 - a}, {"b": 1 - b}, {"core": 1 - core}, {"tl": 1 - tl}
    greet()

    def remote(source, target, slot, to, send_slot=None):
        return pltpu.make_async_remote_copy(
            src_ref=source,
            dst_ref=target,
            send_sem=send.at[slot if send_slot is None else send_slot],
            recv_sem=recv.at[slot],
            device_id=to,
            device_id_type=MESH,
        )

    def arrived(target, slot):
        remote(target, target, slot, to_core).wait_recv()

    def add(target, target_row, height, *sources):
        step = 16

        def one(index, unused):
            value = None
            for source, first in sources:
                here = pl.ds(pl.multiple_of(first + index * step, step), step)
                term = source[here, :].astype(jnp.float32)
                value = term if value is None else value + term
            there = pl.ds(pl.multiple_of(target_row + index * step, step), step)
            target[there, :] = value.astype(target.dtype)
            return unused

        lax.fori_loop(0, height // step, one, 0)

    rows = resid.shape[0]
    step = rows // CHUNKS

    own, peer, far, peer_of_far = range(4)

    def row_of(block, chunk):
        return block * rows + chunk * step

    def at(ref, row):
        return ref.at[pl.ds(row, step), :]

    def row_copies(chunk):
        here = chunk * step
        return (
            remote(at(partial, row_of(peer_of_far, chunk)), at(peer_far, here), 4 * chunk, to_core),
            remote(at(partial, row_of(peer, chunk)), at(peer_near, here), 4 * chunk + 1, to_core),
            remote(at(far_sum, here), at(from_far, here), 4 * chunk + 2, to_tl),
            remote(at(done_rows, here), at(rows_out, here), 4 * chunk + 3, {"core": th, "th": core}),
        )

    def kept_rows(chunk):
        here = chunk * step
        return pltpu.make_async_copy(at(done_rows, here), at(rows_out, here), local.at[chunk])

    base = 4 * CHUNKS

    def piece(ref, block_a, block_b, sub):
        height = ref.shape[0] // 8
        return pl.multiple_of((4 * block_a + 2 * block_b + sub) * height, height), height

    def slice_of(ref, block_a, block_b, sub):
        row, height = piece(ref, block_a, block_b, sub)
        return ref.at[pl.ds(row, height), :]

    def copies(index):
        total = totals[index]
        over_a, over_b, send_b, send_a, from_b, from_a, _ = boxes[index]
        slot = base + 10 * index
        height = total.shape[0] // 8

        def half(ref, sub):
            return ref.at[pl.ds(sub * height, height), :]

        return (
            remote(slice_of(total, 1 - a, 1 - b, 0), over_a, slot, to_a),
            remote(slice_of(total, 1 - a, 1 - b, 1), over_b, slot + 1, to_b),
            remote(slice_of(total, a, 1 - b, 1), half(from_b, 1), slot + 2, to_b),
            remote(slice_of(total, 1 - a, b, 0), half(from_a, 0), slot + 3, to_a),
            remote(send_b, half(from_b, 0), slot + 4, to_b),
            remote(send_a, half(from_a, 1), slot + 5, to_a),
        )

    def last_copies(index):
        sums = boxes[index][6]
        slot = base + 10 * index + 6
        return (
            remote(sums.at[1 - core], sums.at[2], slot, to_core),
            remote(sums.at[0], sums.at[3], slot + 1, {"core": 0, "th": core}),
            remote(sums.at[1], sums.at[3], slot + 1, {"core": 1, "th": core}, slot + 2),
        )

    for index in range(count):
        for copy in copies(index)[:2]:
            copy.start()
    for chunk in range(CHUNKS):
        row_copies(chunk)[0].start()
    for index in range(count):
        for copy in copies(index)[2:4]:
            copy.start()
    for chunk in range(CHUNKS):
        row_copies(chunk)[1].start()
    for chunk in range(CHUNKS):
        arrived(at(peer_far, chunk * step), 4 * chunk)
        add(
            far_sum,
            chunk * step,
            step,
            (partial, row_of(far, chunk)),
            (peer_far, chunk * step),
        )
        row_copies(chunk)[2].start()
    for index in range(count):
        total = totals[index]
        over_a, over_b, send_b, send_a, _, _, _ = boxes[index]
        height = total.shape[0] // 8
        arrived(over_a, base + 10 * index)
        add(send_b, 0, height, (total, piece(total, a, 1 - b, 0)[0]), (over_a, 0))
        copies(index)[4].start()
        arrived(over_b, base + 10 * index + 1)
        add(send_a, 0, height, (total, piece(total, 1 - a, b, 1)[0]), (over_b, 0))
        copies(index)[5].start()
    for chunk in range(CHUNKS):
        here = chunk * step
        arrived(at(peer_near, here), 4 * chunk + 1)
        arrived(at(from_far, here), 4 * chunk + 2)
        add(
            done_rows,
            here,
            step,
            (partial, row_of(own, chunk)),
            (peer_near, here),
            (from_far, here),
            (resid, here),
        )

        @pl.when(stays)
        def _():
            kept_rows(chunk).start()

        @pl.when(jnp.logical_not(stays))
        def _():
            row_copies(chunk)[3].start()

    for index in range(count):
        total = totals[index]
        _, _, _, _, from_b, from_a, sums = boxes[index]
        height = total.shape[0] // 8
        slot = base + 10 * index
        for sub in (0, 1):
            arrived(from_b.at[pl.ds(sub * height, height), :], slot + (4 if sub == 0 else 2))
            arrived(from_a.at[pl.ds(sub * height, height), :], slot + (3 if sub == 0 else 5))
            add(
                sums.at[sub],
                0,
                height,
                (total, piece(total, a, b, sub)[0]),
                (from_b, sub * height),
                (from_a, sub * height),
            )
        near, zero, one = last_copies(index)

        @pl.when(stays)
        def _():
            near.start()

        @pl.when(jnp.logical_not(stays))
        def _():
            zero.start()
            one.start()

    taken = 0
    for index, cut in enumerate(cuts):
        total = totals[index]
        sums = boxes[index][6]
        slot = base + 10 * index + 6
        arrived(sums.at[3], slot + 1)

        @pl.when(jnp.logical_not(stays))
        def _():
            arrived(sums.at[2], slot)

        first = 0
        for end in cut:
            out = shard_outs[taken]
            taken += 1

            def one(step_index, unused, out=out, first=first, end=end, sums=sums):
                here = pl.ds(pl.multiple_of(step_index * 16, 16), 16)

                @pl.when(stays)
                def _():
                    out[here, :] = sums[core, here, first:end].astype(jnp.float32) + sums[
                        3, here, first:end
                    ].astype(jnp.float32)

                @pl.when(jnp.logical_not(stays))
                def _():
                    out[here, :] = sums[2, here, first:end].astype(jnp.float32) + sums[
                        3, here, first:end
                    ].astype(jnp.float32)

                return unused

            lax.fori_loop(0, out.shape[0] // 16, one, 0)
            first = end
    for chunk in range(CHUNKS):
        for copy in row_copies(chunk)[:3]:
            copy.wait_send()

        @pl.when(stays)
        def _():
            kept_rows(chunk).wait()

        @pl.when(jnp.logical_not(stays))
        def _():
            row_copies(chunk)[3].wait_send()
            arrived(at(rows_out, chunk * step), 4 * chunk + 3)

    for index in range(count):
        for copy in copies(index):
            copy.wait_send()
        near, zero, one = last_copies(index)

        @pl.when(stays)
        def _():
            near.wait_send()

        @pl.when(jnp.logical_not(stays))
        def _():
            zero.wait_send()
            one.wait_send()


def leave(partial, resid, totals):
    if not small_grid():
        summed, _ = scatter_rows([partial])
        shards = []
        for total, parts in totals:
            shard, first = scatter_weight(total), 0
            for width in parts:
                shards.append(shard[:, first : first + width])
                first += width
        return [turn((resid + summed).astype(jnp.bfloat16))] + shards
    rows, columns = resid.shape
    cuts, scratch, outs = [], [], [jax.ShapeDtypeStruct((rows, columns), jnp.bfloat16)]
    for total, parts in totals:
        height, width = total.shape[0] // 8, total.shape[1]
        cuts.append(tuple(sum(parts[: index + 1]) for index in range(len(parts))))
        outs += [jax.ShapeDtypeStruct((height, part_width), jnp.float32) for part_width in parts]
        for shape in [(height, width)] * 4 + [(2 * height, width)] * 2 + [(4, height, width)]:
            scratch.append(pltpu.VMEM(shape, jnp.bfloat16))
    slots = 4 * CHUNKS + 10 * len(totals)
    vmem = pl.BlockSpec(memory_space=pltpu.VMEM)
    return pl.pallas_call(
        functools.partial(leave_kernel, tuple(cuts)),
        in_specs=[vmem] * (2 + len(totals)),
        out_specs=[pl.BlockSpec(memory_space=pl.ANY)] + [vmem] * (len(outs) - 1),
        out_shape=outs,
        scratch_shapes=[pltpu.VMEM((rows, columns), jnp.bfloat16)] * 5
        + scratch
        + [
            pltpu.SemaphoreType.DMA((slots,)),
            pltpu.SemaphoreType.DMA((slots,)),
            pltpu.SemaphoreType.DMA((CHUNKS,)),
        ],
        compiler_params=pltpu.CompilerParams(
            collective_id=1, has_side_effects=True, vmem_limit_bytes=60 * 1024 * 1024
        ),
        cost_estimate=pl.CostEstimate(flops=0, bytes_accessed=1 << 27, transcendentals=0),
        name="leave",
    )(partial.astype(jnp.bfloat16), resid, *[total.astype(jnp.bfloat16) for total, _ in totals])


def enter(tokens, matrices):
    if not small_grid():
        own = turn(tokens)
        return [lax.all_gather(own, RANK, axis=0, tiled=True)] + [
            gather_weight(pieces_of_weight(jnp.concatenate(shards, axis=1))) for shards in matrices
        ]
    plan, outs = [], [jax.ShapeDtypeStruct((4 * tokens.shape[0], tokens.shape[1]), tokens.dtype)]
    for shards in matrices:
        columns = [0]
        for shard in shards:
            columns.append(columns[-1] + shard.shape[1])
        plan.append(tuple(columns[:-1]))
        outs.append(jax.ShapeDtypeStruct((8 * shards[0].shape[0], columns[-1]), tokens.dtype))
    flat = [shard for shards in matrices for shard in shards]
    slots = entry_slots(plan)
    anywhere = pl.BlockSpec(memory_space=pl.ANY)
    return pl.pallas_call(
        functools.partial(entry_kernel, tuple(plan)),
        in_specs=[anywhere] * (1 + len(flat)),
        out_specs=[anywhere] * len(outs),
        out_shape=outs,
        scratch_shapes=[
            pltpu.SemaphoreType.DMA((slots,)),
            pltpu.SemaphoreType.DMA((slots,)),
            pltpu.SemaphoreType.DMA((len(flat) + CHUNKS,)),
        ],
        compiler_params=pltpu.CompilerParams(collective_id=0, has_side_effects=True),
        cost_estimate=pl.CostEstimate(flops=0, bytes_accessed=1 << 27, transcendentals=0),
        name="enter",
    )(tokens, *flat)


def row_place(row, own_rows):
    if not small_grid():
        return row
    mask = 2 * lax.axis_index("core") + lax.axis_index("tl")
    block = (row // own_rows) ^ mask
    block = (block // 2) + 2 * (block % 2)
    return block * own_rows + row % own_rows


def gather_rows(value):
    if not small_grid():
        return [lax.all_gather(value, RANK, axis=0, tiled=True)]
    far = swap(value, "tl")
    near_peer = swap(value, "core")
    far_peer = swap(far, "core")
    return [
        jnp.concatenate([value, near_peer], axis=0),
        jnp.concatenate([far, far_peer], axis=0),
    ]


def scatter_rows(pieces, beside=()):
    if not small_grid():
        total = lax.psum_scatter(
            pieces[0].astype(jnp.bfloat16), RANK, scatter_dimension=0, tiled=True
        ).astype(jnp.float32)
        return total, beside
    near, far = pieces
    rows = near.shape[0] // 2
    far_peer = swap(far[rows:].astype(jnp.bfloat16), "core")
    far_sum = (far[:rows].astype(jnp.float32) + far_peer.astype(jnp.float32)).astype(jnp.bfloat16)
    from_far = swap(far_sum, "tl")
    near_peer = swap(near[rows:].astype(jnp.bfloat16), "core")
    from_far, beside = lax.optimization_barrier((from_far, beside))
    total = (
        near[:rows].astype(jnp.float32)
        + near_peer.astype(jnp.float32)
        + from_far.astype(jnp.float32)
    )
    return total, beside


def sum_over(value, axes):
    for axis in axes:
        if lax.axis_size(axis) == 2:
            value = value + swap(value, axis)
        else:
            value = lax.psum(value, axis)
    return value


def layout(length_row, group_rows):
    positions = jnp.arange(group_rows, dtype=jnp.int32)
    start = jnp.int32(0)
    offset = jnp.zeros((group_rows,), jnp.int32)
    starts = positions
    for index in range(length_row.shape[0]):
        end = start + length_row[index]
        inside = (positions >= start) & (positions < end)
        offset = jnp.where(inside, start, offset)
        starts = jnp.where(inside, start, starts)
        start = end
    return (positions - offset, starts)


def rotary_tables(position):
    half_dim = HDIM // 2
    exponents = jnp.arange(half_dim, dtype=jnp.float32) * (2.0 / HDIM)
    frequency = jnp.power(jnp.float32(rope_base), -exponents)
    angles = position.astype(jnp.float32)[:, None] * frequency[None, :]
    cosine, sine = jnp.cos(angles), jnp.sin(angles)
    return (
        jnp.concatenate([cosine, cosine], axis=1),
        jnp.concatenate([-sine, sine], axis=1),
    )


def columns_of(rows, index):
    chosen = (lax.broadcasted_iota(jnp.int32, (rows.shape[0], HDIM), 0) == index).astype(
        jnp.float32
    )
    return lax.dot_general(
        rows,
        chosen,
        (((0,), (0,)), ((), ())),
        precision=lax.Precision.HIGHEST,
        preferred_element_type=jnp.float32,
    )


def row_sums(values):
    ones = jnp.ones((8, values.shape[1]), jnp.float32)
    return lax.dot_general(
        ones,
        values,
        (((1,), (1,)), ((), ())),
        precision=lax.Precision.HIGHEST,
        preferred_element_type=jnp.float32,
    )[:1]


def rstd_of(squares, index):
    return lax.rsqrt(columns_of(squares, index) * (1.0 / D) + epsilon)


def prepare_kernel(raw, squares, gain_q, gain_k, cosine, sine, q_out, k_out, v_out):
    width = q_out.shape[1]
    table_c, table_s = cosine[...], sine[...]
    both = squares[...]
    for index, (gain, out) in enumerate(((gain_q, q_out), (gain_k, k_out))):
        rstd = rstd_of(both, index)
        for head in range(width // HDIM):
            cols = slice(head * HDIM, (head + 1) * HDIM)
            base = index * width + head * HDIM
            norm = raw[:, base : base + HDIM] * rstd * gain[:, cols]
            turned = norm * table_c + pltpu.roll(norm, HDIM // 2, 1) * table_s
            out[:, cols] = turned.astype(jnp.bfloat16)
    v_out[...] = raw[:, 2 * width :].astype(jnp.bfloat16)


def prepare(raw, squares, gain_q, gain_k, cosine, sine):
    rows, width = raw.shape[0], raw.shape[1] // 3
    whole = pl.BlockSpec((1, width), lambda i: (0, 0))
    table = pl.BlockSpec((BLOCK, HDIM), lambda i: (i, 0))
    out = pl.BlockSpec((BLOCK, width), lambda i: (i, 0))
    return pl.pallas_call(
        prepare_kernel,
        grid=(rows // BLOCK,),
        in_specs=[
            pl.BlockSpec((BLOCK, 3 * width), lambda i: (i, 0)),
            pl.BlockSpec((2, BLOCK), lambda i: (0, i)),
            whole,
            whole,
            table,
            table,
        ],
        out_specs=[out] * 3,
        out_shape=[jax.ShapeDtypeStruct((rows, width), jnp.bfloat16)] * 3,
        cost_estimate=pl.CostEstimate(
            flops=rows * width * 20, bytes_accessed=rows * width * 20, transcendentals=0
        ),
        name="prepare",
    )(raw, squares, gain_q[None], gain_k[None], cosine, sine)


def allowed_keys(starts, first_key, first_query):
    shape = (BLOCK, BLOCK)
    keys = first_key + lax.broadcasted_iota(jnp.int32, shape, 0)
    queries = first_query + lax.broadcasted_iota(jnp.int32, shape, 1)
    return (keys >= starts) & (keys <= queries)


def forward_kernel(low_ref, q_ref, k_ref, v_ref, start_ref, attn_ref, full_ref, log_ref):
    block = pl.program_id(1)
    queries = q_ref[...]
    starts = start_ref[...]
    scale = 1.0 / math.sqrt(HDIM)

    def step(index, carried):
        peak, total, acc = carried
        rows = pl.ds(pl.multiple_of(index * BLOCK, BLOCK), BLOCK)
        scores = contract_cols(k_ref[rows, :], queries) * scale
        scores = jnp.where(
            allowed_keys(starts, index * BLOCK, block * BLOCK), scores, masked_score
        )
        new_peak = jnp.maximum(peak, jnp.max(scores, axis=0, keepdims=True))
        fade = jnp.exp(peak - new_peak)
        weights = jnp.exp(scores - new_peak)
        total = total * fade + jnp.sum(weights, axis=0, keepdims=True)
        acc = acc * fade + contract_rows(v_ref[rows, :], weights.astype(jnp.bfloat16))
        return (new_peak, total, acc)

    start = (
        jnp.full((1, BLOCK), masked_score, jnp.float32),
        jnp.zeros((1, BLOCK), jnp.float32),
        jnp.zeros((HDIM, BLOCK), jnp.float32),
    )
    carried = step(block, start)
    peak, total, acc = lax.fori_loop(low_ref[block], block, step, carried)
    out = jnp.transpose(acc / total)
    full_ref[...] = out
    attn_ref[...] = out.astype(jnp.bfloat16)
    log_ref[...] = peak + jnp.log(total)


def attention_forward(q_b, k_b, v_b, starts, low_block):
    rows, width = q_b.shape
    heads = width // HDIM
    own = pl.BlockSpec((BLOCK, HDIM), lambda h, i, low: (i, h))
    whole = pl.BlockSpec((rows, HDIM), lambda h, i, low: (0, h))
    return pl.pallas_call(
        forward_kernel,
        grid_spec=pltpu.PrefetchScalarGridSpec(
            num_scalar_prefetch=1,
            grid=(heads, rows // BLOCK),
            in_specs=[own, whole, whole, pl.BlockSpec((1, BLOCK), lambda h, i, low: (0, i))],
            out_specs=[own, own, pl.BlockSpec((None, 1, BLOCK), lambda h, i, low: (h, 0, i))],
        ),
        out_shape=[
            jax.ShapeDtypeStruct((rows, width), jnp.bfloat16),
            jax.ShapeDtypeStruct((rows, width), jnp.float32),
            jax.ShapeDtypeStruct((heads, 1, rows), jnp.float32),
        ],
        compiler_params=pltpu.CompilerParams(vmem_limit_bytes=VMEM_BYTES),
        cost_estimate=pl.CostEstimate(
            flops=heads * rows * rows * HDIM, bytes_accessed=rows * width * 12, transcendentals=heads * rows * rows // 4
        ),
        name="attention_forward",
    )(low_block, q_b, k_b, v_b, starts)


def backward_kernel(
    high_ref, q_ref, k_ref, v_ref, grad_ref, full_ref, log_ref, start_ref, dq_ref, dk_ref, dv_ref, delta
):
    block = pl.program_id(1)
    blocks = pl.num_programs(1)
    scale = 1.0 / math.sqrt(HDIM)

    @pl.when(block == 0)
    def _():
        dq_ref[...] = jnp.zeros_like(dq_ref)

        def one(index, unused):
            rows = pl.ds(pl.multiple_of(index * BLOCK, BLOCK), BLOCK)
            delta[:, rows] = row_sums(grad_ref[rows, :].astype(jnp.float32) * full_ref[rows, :])
            return unused

        lax.fori_loop(0, blocks, one, 0)

    here = pl.ds(pl.multiple_of(block * BLOCK, BLOCK), BLOCK)
    keys, values = k_ref[here, :], v_ref[here, :]

    def step(index, carried):
        dk, dv = carried
        rows = pl.ds(pl.multiple_of(index * BLOCK, BLOCK), BLOCK)
        queries, grads = q_ref[rows, :], grad_ref[rows, :]
        scores = contract_cols(keys, queries) * scale
        allowed = allowed_keys(start_ref[:, rows], block * BLOCK, index * BLOCK)
        probs = jnp.where(allowed, jnp.exp(scores - log_ref[:, rows]), 0.0)
        dv = dv + dot(probs.astype(jnp.bfloat16), grads)
        d_probs = contract_cols(values, grads)
        d_scores = (probs * (d_probs - delta[:, rows])).astype(jnp.bfloat16)
        dk = dk + dot(d_scores, queries)
        dq_ref[rows, :] += contract_rows(d_scores, keys)
        return (dk, dv)

    zero = jnp.zeros((BLOCK, HDIM), jnp.float32)
    dk, dv = lax.fori_loop(block, high_ref[block] + 1, step, (zero, zero))
    dk_ref[...] = dk * scale
    dv_ref[...] = dv

    @pl.when(block == blocks - 1)
    def _():
        dq_ref[...] = dq_ref[...] * scale


def attention_backward(q_b, k_b, v_b, grads, full, logs, starts, high_block):
    rows, width = q_b.shape
    heads = width // HDIM
    own = pl.BlockSpec((BLOCK, HDIM), lambda h, i, high: (i, h))
    whole = pl.BlockSpec((rows, HDIM), lambda h, i, high: (0, h))
    out = jax.ShapeDtypeStruct((rows, width), jnp.float32)
    return pl.pallas_call(
        backward_kernel,
        grid_spec=pltpu.PrefetchScalarGridSpec(
            num_scalar_prefetch=1,
            grid=(heads, rows // BLOCK),
            in_specs=[whole] * 5
            + [
                pl.BlockSpec((None, 1, rows), lambda h, i, high: (h, 0, 0)),
                pl.BlockSpec((1, rows), lambda h, i, high: (0, 0)),
            ],
            out_specs=[whole, own, own],
            scratch_shapes=[pltpu.VMEM((1, rows), jnp.float32)],
        ),
        out_shape=[out] * 3,
        compiler_params=pltpu.CompilerParams(vmem_limit_bytes=VMEM_BYTES),
        cost_estimate=pl.CostEstimate(
            flops=heads * rows * rows * HDIM * 3, bytes_accessed=rows * width * 24, transcendentals=heads * rows * rows // 4
        ),
        name="attention_backward",
    )(high_block, q_b, k_b, v_b, grads, full, logs, starts)


def norm_grads_kernel(
    dq_ref, dk_ref, raw, squares, gain_q, gain_k, cosine, sine, dq_out, dk_out, dots, q_part, k_part
):
    width = dq_ref.shape[1]
    table_c, table_s = cosine[...], sine[...]
    both = squares[...]

    @pl.when(pl.program_id(0) == 0)
    def _():
        q_part[...] = jnp.zeros_like(q_part)
        k_part[...] = jnp.zeros_like(k_part)

    for index, (grad, gain, out, gain_part) in enumerate(
        ((dq_ref, gain_q, dq_out, q_part), (dk_ref, gain_k, dk_out, k_part))
    ):
        rstd = rstd_of(both, index)
        products = jnp.zeros((BLOCK, HDIM), jnp.float32)
        for head in range(width // HDIM):
            cols = slice(head * HDIM, (head + 1) * HDIM)
            base = index * width + head * HDIM
            turned = grad[:, cols]
            norm = turned * table_c - pltpu.roll(turned, HDIM // 2, 1) * table_s
            out[:, cols] = norm
            product = raw[:, base : base + HDIM] * norm
            gain_part[:, cols] += jnp.sum((product * rstd).reshape(BLOCK // 8, 8, HDIM), axis=0)
            products = products + product * gain[:, cols]
        dots[index : index + 1, :] = row_sums(products)


def norm_grads(d_q_rot, d_k_rot, raw, squares, gain_q, gain_k, cosine, sine):
    rows, width = d_q_rot.shape
    whole = pl.BlockSpec((1, width), lambda i: (0, 0))
    table = pl.BlockSpec((BLOCK, HDIM), lambda i: (i, 0))
    own = pl.BlockSpec((BLOCK, width), lambda i: (i, 0))
    pair = pl.BlockSpec((2, BLOCK), lambda i: (0, i))
    total = pl.BlockSpec((8, width), lambda i: (0, 0))
    grad = jax.ShapeDtypeStruct((rows, width), jnp.float32)
    return pl.pallas_call(
        norm_grads_kernel,
        grid=(rows // BLOCK,),
        in_specs=[
            own,
            own,
            pl.BlockSpec((BLOCK, 3 * width), lambda i: (i, 0)),
            pair,
            whole,
            whole,
            table,
            table,
        ],
        out_specs=[own, own, pair, total, total],
        out_shape=[
            grad,
            grad,
            jax.ShapeDtypeStruct((2, rows), jnp.float32),
            jax.ShapeDtypeStruct((8, width), jnp.float32),
            jax.ShapeDtypeStruct((8, width), jnp.float32),
        ],
        cost_estimate=pl.CostEstimate(
            flops=rows * width * 30, bytes_accessed=rows * width * 32, transcendentals=0
        ),
        name="norm_grads",
    )(d_q_rot, d_k_rot, raw, squares, gain_q[None], gain_k[None], cosine, sine)


def raw_grads_kernel(dq_ref, dk_ref, dv_ref, raw, squares, dots, gain_q, gain_k, out):
    width = dq_ref.shape[1]
    both, sums = squares[...], dots[...]
    for index, (grad, gain) in enumerate(((dq_ref, gain_q), (dk_ref, gain_k))):
        rstd = rstd_of(both, index)
        share = rstd * rstd * rstd * columns_of(sums, index) * (1.0 / D)
        for head in range(width // HDIM):
            cols = slice(head * HDIM, (head + 1) * HDIM)
            base = index * width + head * HDIM
            value = rstd * gain[:, cols] * grad[:, cols] - raw[:, base : base + HDIM] * share
            out[:, base : base + HDIM] = value.astype(jnp.bfloat16)
    out[:, 2 * width :] = dv_ref[...].astype(jnp.bfloat16)


def raw_grads(d_q_norm, d_k_norm, d_v, raw, squares, dots, gain_q, gain_k):
    rows, width = d_q_norm.shape
    whole = pl.BlockSpec((1, width), lambda i: (0, 0))
    own = pl.BlockSpec((BLOCK, width), lambda i: (i, 0))
    wide = pl.BlockSpec((BLOCK, 3 * width), lambda i: (i, 0))
    pair = pl.BlockSpec((2, BLOCK), lambda i: (0, i))
    return pl.pallas_call(
        raw_grads_kernel,
        grid=(rows // BLOCK,),
        in_specs=[own, own, own, wide, pair, pair, whole, whole],
        out_specs=wide,
        out_shape=jax.ShapeDtypeStruct((rows, 3 * width), jnp.bfloat16),
        cost_estimate=pl.CostEstimate(
            flops=rows * width * 20, bytes_accessed=rows * width * 30, transcendentals=0
        ),
        name="raw_grads",
    )(d_q_norm, d_k_norm, d_v, raw, squares, dots, gain_q[None], gain_k[None])


def dot(left, right):
    return jnp.dot(left, right, preferred_element_type=jnp.float32)


def contract_rows(left, right):
    return lax.dot_general(
        left, right, (((0,), (0,)), ((), ())), preferred_element_type=jnp.float32
    )


def contract_cols(left, right):
    return lax.dot_general(
        left, right, (((1,), (1,)), ((), ())), preferred_element_type=jnp.float32
    )


def rms_back(values, rstd, gain_vec, grad):
    scaled = grad * gain_vec
    row_dots = jnp.sum(values * scaled, axis=1, keepdims=True)
    return rstd * scaled - values * (rstd * rstd * rstd) * row_dots / D


def per_device(
    tokens,
    upstream,
    lengths,
    permutation,
    w_query,
    w_key,
    w_value,
    w_out,
    w_gate,
    w_up,
    w_down,
    q_gain,
    k_gain,
    attn_gain,
    ffn_gain,
):
    rank = lax.axis_index("core") * lax.axis_size("tl") + lax.axis_index("tl")
    own_rows = tokens.shape[0]
    group_rows = own_rows * 2 * lax.axis_size("tl")
    local_width = w_query.shape[1]

    own_group = lax.axis_index("core") == lax.axis_index("th")
    length_row = jnp.where(own_group, lengths, swap(lengths, "core"))[0]
    perm_row = jnp.where(own_group, permutation, swap(permutation, "core"))[0]

    tokens_all, qkv_full, out_full, gate_full = enter(
        tokens, [(w_query, w_key, w_value), (w_out.T,), (w_gate,)]
    )
    (up_shard, down_shard), tokens_all = lax.optimization_barrier(((w_up, w_down.T), tokens_all))
    up_pieces, down_pieces = pieces_of_weight(up_shard), pieces_of_weight(down_shard)
    tokens = lax.dynamic_slice_in_dim(tokens_all, rank * own_rows, own_rows)
    upstream = turn(upstream)

    perm_place = row_place(perm_row, own_rows)
    slots = jnp.arange(group_rows, dtype=jnp.int32)
    inverse = jnp.zeros((group_rows,), jnp.int32).at[perm_place].set(slots)
    position, starts = layout(length_row, group_rows)
    cosine, sine = rotary_tables(position)
    blocks = group_rows // BLOCK
    low_block = starts[::BLOCK] // BLOCK
    last_keys = (jnp.arange(blocks, dtype=jnp.int32) + 1) * BLOCK - 1
    reached = jnp.sum((starts[None, :] <= last_keys[:, None]).astype(jnp.int32), axis=1)
    high_block = (reached - 1) // BLOCK

    packed = tokens_all[perm_row]
    raw = dot(packed, qkv_full)
    up_pieces, raw = lax.optimization_barrier((up_pieces, raw))
    up_full = gather_weight(up_pieces)
    q_raw = raw[:, :local_width]
    k_raw = raw[:, local_width : 2 * local_width]
    squares = sum_over(
        jnp.stack([jnp.sum(q_raw * q_raw, axis=1), jnp.sum(k_raw * k_raw, axis=1)]), RANK
    )
    gain_q = lax.dynamic_slice_in_dim(q_gain, rank * local_width, local_width)
    gain_k = lax.dynamic_slice_in_dim(k_gain, rank * local_width, local_width)
    q_b, k_b, v_b = prepare(raw, squares, gain_q, gain_k, cosine, sine)
    attn_b, attn_f, logs = attention_forward(q_b, k_b, v_b, starts[None], low_block)
    down_pieces, attn_b = lax.optimization_barrier((down_pieces, attn_b))
    down_full = gather_weight(down_pieces)
    attn_given = attn_b[inverse]

    def pieces_of(value):
        if not small_grid():
            return [value]
        return [part(value, 0, 0, 2), part(value, 0, 1, 2)]

    attn_out, _ = scatter_rows(
        [contract_cols(piece, out_full) for piece in pieces_of(attn_given)]
    )
    rstd_a = lax.rsqrt(jnp.mean(attn_out * attn_out, axis=1, keepdims=True) + epsilon)
    resid = tokens.astype(jnp.float32) + attn_out * rstd_a * attn_gain
    resid_pieces = gather_rows(resid.astype(jnp.bfloat16))
    gates, ups, hiddens, sums = [], [], [], []
    for index in range(len(resid_pieces)):
        piece = resid_pieces[index]
        gate = dot(piece, gate_full)
        up_part = dot(piece, up_full)
        hidden_b = (gate * jax.nn.sigmoid(gate) * up_part).astype(jnp.bfloat16)
        gates.append(gate)
        ups.append(up_part)
        hiddens.append(hidden_b)
        sums.append(contract_cols(hidden_b, down_full).astype(jnp.bfloat16))
        if index + 1 < len(resid_pieces):
            resid_pieces[index + 1], gates[-1], ups[-1], hiddens[-1] = lax.optimization_barrier(
                (resid_pieces[index + 1], gates[-1], ups[-1], hiddens[-1])
            )
    mlp_out, _ = scatter_rows(sums)
    rstd_m = lax.rsqrt(jnp.mean(mlp_out * mlp_out, axis=1, keepdims=True) + epsilon)
    normed_m = mlp_out * rstd_m
    layer_out = turn((resid + normed_m * ffn_gain).astype(jnp.bfloat16))

    grad_f = upstream.astype(jnp.float32)
    ffn_gain_part = jnp.sum(grad_f * normed_m, axis=0)
    d_mlp_b = rms_back(mlp_out, rstd_m, ffn_gain, grad_f).astype(jnp.bfloat16)
    d_mlp_pieces = gather_rows(d_mlp_b)
    d_gates, d_ups, sums = [], [], []
    for index in range(len(d_mlp_pieces)):
        gate, up_part, d_mlp = gates[index], ups[index], d_mlp_pieces[index]
        gate_sigmoid = jax.nn.sigmoid(gate)
        d_hidden = dot(d_mlp, down_full)
        d_gate_b = (
            d_hidden * up_part * gate_sigmoid * (1.0 + gate * (1.0 - gate_sigmoid))
        ).astype(jnp.bfloat16)
        d_up_b = (d_hidden * gate * gate_sigmoid).astype(jnp.bfloat16)
        d_gates.append(d_gate_b)
        d_ups.append(d_up_b)
        sums.append(
            (contract_cols(d_gate_b, gate_full) + contract_cols(d_up_b, up_full)).astype(
                jnp.bfloat16
            )
        )
        if index + 1 < len(d_mlp_pieces):
            d_mlp_pieces[index + 1], d_gates[-1], d_ups[-1], sums[-1] = lax.optimization_barrier(
                (d_mlp_pieces[index + 1], d_gates[-1], d_ups[-1], sums[-1])
            )

    def rows(pieces):
        return jnp.concatenate(pieces, axis=0)

    down_grad = contract_rows(rows(d_mlp_pieces), rows(hiddens)).astype(jnp.bfloat16)
    gate_grad = contract_rows(rows(resid_pieces), rows(d_gates)).astype(jnp.bfloat16)
    d_sums, (down_grad, gate_grad) = scatter_rows(sums, (down_grad, gate_grad))
    d_resid = grad_f + d_sums
    up_grad = contract_rows(rows(resid_pieces), rows(d_ups)).astype(jnp.bfloat16)

    attn_gain_part = jnp.sum(d_resid * attn_out * rstd_a, axis=0)
    d_attn_b = rms_back(attn_out, rstd_a, attn_gain, d_resid).astype(jnp.bfloat16)
    d_attn_pieces = gather_rows(d_attn_b)
    d_attn_pieces[-1], up_grad = lax.optimization_barrier((d_attn_pieces[-1], up_grad))
    down_shard = scatter_weight(down_grad).T
    gate_shard = scatter_weight(gate_grad)
    up_shard = scatter_weight(up_grad)
    d_attn_all = rows(d_attn_pieces)
    d_given_b = rows([dot(piece, out_full).astype(jnp.bfloat16) for piece in d_attn_pieces])
    d_packed = d_given_b[perm_place]
    d_q_rot, d_k_rot, d_v = attention_backward(
        q_b, k_b, v_b, d_packed, attn_f, logs, starts[None], high_block
    )
    d_q_norm, d_k_norm, dots, q_parts, k_parts = norm_grads(
        d_q_rot, d_k_rot, raw, squares, gain_q, gain_k, cosine, sine
    )
    q_gain_part, k_gain_part = jnp.sum(q_parts, axis=0), jnp.sum(k_parts, axis=0)
    dots = sum_over(dots, RANK)
    d_qkv_b = raw_grads(d_q_norm, d_k_norm, d_v, raw, squares, dots, gain_q, gain_k)
    d_qkv_given = d_qkv_b[inverse]
    tokens_grad, query_shard, key_shard, value_shard, out_shard = leave(
        contract_cols(d_qkv_given, qkv_full),
        d_resid,
        [
            (contract_rows(packed, d_qkv_b), [local_width] * 3),
            (contract_rows(d_attn_all, attn_given), [local_width]),
        ],
    )

    def placed(part_sum):
        return lax.dynamic_update_slice_in_dim(
            jnp.zeros((D,), jnp.float32), part_sum, rank * local_width, 0
        )

    gain_grads = sum_over(
        jnp.stack(
            [
                placed(q_gain_part),
                placed(k_gain_part),
                attn_gain_part,
                ffn_gain_part,
            ]
        ),
        DP + TENSOR,
    )
    return (
        layer_out,
        tokens_grad,
        query_shard,
        key_shard,
        value_shard,
        out_shard.T,
        gate_shard,
        up_shard,
        down_shard,
        gain_grads[0],
        gain_grads[1],
        gain_grads[2],
        gain_grads[3],
    )


def solution(mesh):
    dp, tensor = mesh.shape["dp"], mesh.shape["tensor"]
    fine = Mesh(mesh.devices.reshape(dp // 4, 2, 2, 2, tensor // 2), DP + TENSOR)
    rows, weight, weight_out = P(DP + TENSOR, None), P(DP, TENSOR), P(TENSOR, DP)
    return jax.shard_map(
        per_device,
        mesh=fine,
        in_specs=(rows, rows, P(DP, None), P(DP, None))
        + (weight,) * 3
        + (weight_out, weight, weight, weight_out)
        + (P(),) * 4,
        out_specs=(rows, rows)
        + (weight,) * 3
        + (weight_out, weight, weight, weight_out)
        + (P(),) * 4,
        check_vma=False,
    )
```

time: 1950 us -> 1450 us (0.74)
  Pallas kernels: 0 us -> 471 us
  waiting for transfers between devices: 582 us -> 321 us
  matrix products: 542 us -> 323 us
  local copies, waits for them, and re-layouts: 266 us -> 102 us
  starting transfers between devices: 283 us -> 121 us
  other arithmetic: 250 us -> 92.3 us
    pallas_call x0 -> x7, Pallas kernels: none -> 471 us  [the longest x1 202 us: enter(): pl.pallas_call(functools.partial(entry_kernel, tuple(plan)), in_specs=[an...]
    ppermute x95 -> x29, waiting for transfers between devices: 506 us -> 259 us  [swap(): return lax.ppermute(value, axis, SWAP)]
    dot_general x28 -> x0, matrix products: 220 us -> none  [the longest x4 50.1 us: backward_block(): jnp.einsum('qhd,khd->hqk', grad_rows, v_b, preferred_element_type=jnp.flo...]
    ppermute x24 -> x12, starting transfers between devices: 188 us -> 86.9 us  [the longest x3 64.1 us: finish_scatter(): lax.ppermute(second, ('core', 'th'), CYCLE_BACK).astype(jnp.float32)]
    unnamed x327 -> x116, local copies, waits for them, and re-layouts: 109 us -> 25.6 us
    convert_element_type x24 -> x4, other arithmetic: 100 us -> 17.5 us  [the longest x1 9.71 us: per_device(): d_up_b = (d_hidden * gate * gate_sigmoid).astype(jnp.bfloat16)]
    ppermute x95 -> x29, starting transfers between devices: 94.8 us -> 34 us  [swap(): return lax.ppermute(value, axis, SWAP)]
    concatenate x18 -> x0, local copies, waits for them, and re-layouts: 29.2 us -> none  [the longest x2 10.8 us: rotate(): jnp.concatenate([first_half * cos_rows - second_half * sin_rows, second_h...]
  transfers between devices with their start and end apart: 119 -> 46, of which waited for: 45 -> 15; matrix products, arithmetic and copies ran while one was open for 49% -> 29% of each run, Pallas kernels for 0% -> 33%
where the time goes in v2:
time: 1450 us
  Pallas kernels  471 us (32%)
  matrix products  323 us (22%)
  waiting for transfers between devices  321 us (22%)
  starting transfers between devices  121 us (8%)
  local copies, waits for them, and re-layouts  102 us (7%)
  other arithmetic  92.3 us (6%)
  between operations  16.8 us (1%)
    ppermute x29, waiting for transfers between devices, swap(): return lax.ppermute(value, axis, SWAP)  259 us
    pallas_call x1, Pallas kernels, enter(): pl.pallas_call(functools.partial(entry_kernel, tuple(plan)), in_specs=[an...  202 us
    pallas_call x1, Pallas kernels, leave(): pl.pallas_call(functools.partial(leave_kernel, tuple(cuts)), in_specs=[vm...  131 us
    dot_general x9, matrix products, dot(): return jnp.dot(left, right, preferred_element_type=jnp.float32)  117 us
    dot_general x9, matrix products, contract_cols(): lax.dot_general(left, right, (((1,), (1,)), ((), ())), preferred_element_...  106 us
    dot_general x5, matrix products, contract_rows(): lax.dot_general(left, right, (((0,), (0,)), ((), ())), preferred_element_...  100 us
    ppermute x3, starting transfers between devices, finish_scatter(): lax.ppermute(second, ('core', 'th'), CYCLE_BACK).astype(jnp.float32)  64.1 us
    ppermute x3, waiting for transfers between devices, finish_scatter(): lax.ppermute(second, ('core', 'th'), CYCLE_BACK).astype(jnp.float32)  60.7 us
  transfers between devices with their start and end apart: 46, of which 15 were waited for; matrix products, arithmetic and copies ran while one was open for 29% of the time, Pallas kernels for 33%

profile of v2, /device:TPU:0, one launch (start us, length us, event | category | flops | bytes accessed | tf_op | source)
XLA Modules:
  0.0 1447.1 jit_solution(6328686656011043596)
XLA Ops:
  11.8 202.2 %enter.1 = (bf16[2048,2048]{1,0:T(8,128)(2,1)}, bf16[2048,1536]{1,0:T(8,128)(2,1)}, bf16[2048,512]{1,0:T(8,128)(2,1)}, bf16[2048,2048]{1,0:T(8,128)(2,1)}) custom-call(bf16[512,2048]{1,0:T(8,128)(2,1)} %refs_0_.1, bf16[256,512]{1,0:T(8,128)(2,1)} %refs_1_.1, bf16[256,512]{1,0:T(8,128)(2,1)} %refs_2_.1, bf16[256,512]{1,0:T(8,128)(2,1)} %refs_3_.1, ...), custom_call_target="tpu_custom_call" | custom-call | bytes 134217728 | tf_op jit(solution)/shard_map/enter/pallas_call | solution.py:612
  214.8 7.0 collective-permute-start.4
  222.0 20.8 %gather_fusion = bf16[2048,2048]{1,0:T(8,128)(2,1)} fusion(bf16[2048,2048]{1,0:T(8,128)(2,1)} %get-tuple-element.59, s32[2048]{0:T(1024)S(1)} %broadcast_clamp_fusion.1), kind=kCustom, calls=%fused_computation | custom fusion | bytes 16785408 | tf_op jit(solution)/shard_map/gather | solution.py:1077
  242.7 19.3 %fusion.86.raw = f32[2048,1536]{1,0:T(8,128)} fusion(bf16[2048,2048]{1,0:T(8,128)(2,1)} %gather_fusion, bf16[2048,1536]{1,0:T(8,128)(2,1)} %get-tuple-element.62), kind=kOutput, calls=%fused_computation.187 | convolution fusion | flops 12884901888 | bytes 27262976 | tf_op jit(solution)/shard_map/dot_general | solution.py:1011
  264.7 7.0 collective-permute-start.1
  279.0 3.7 fusion.63
  285.3 8.6 scatter_custom_fusion
  293.9 4.1 multiply_reduce_fusion.5
  301.3 16.9 %collective-permute-done.7 = f32[2,2048]{1,0:T(2,128)S(1)} collective-permute-done((f32[2,2048]{1,0:T(2,128)S(1)}, f32[2,2048]{1,0:T(2,128)S(1)}, u32[]{:S(2)}, u32[]{:S(2)}) %collective-permute-start.7) | collective-permute-done | bytes 16416 | tf_op jit(solution)/shard_map/ppermute | solution.py:31
  318.8 11.9 prepare.1
  332.3 37.8 %attention_forward.1 = (bf16[2048,512]{1,0:T(8,128)(2,1)S(1)}, f32[2048,512]{1,0:T(8,128)}, f32[4,1,2048]{2,1,0:T(1,128)S(1)}) custom-call(s32[8]{0:T(128)S(1)} %and_select_fusion.7.low_ref, bf16[2048,512]{1,0:T(8,128)(2,1)S(1)} %copy-done, bf16[2048,512]{1,0:T(8,128)(2,1)} %get-tuple-element.65.k_ref, bf16[2048,512]{1,0:T(8,128)(2,1)} %get-tuple-element.66.v_ref, ...), custom_call_target="tpu_custom_call" | custom-call | flops 2147483648 | bytes 12582912 | tf_op jit(solution)/shard_map/attention_forward/pallas_call | solution.py:818
  370.1 9.2 gather_fusion.1
  379.3 4.3 fusion.59
  397.0 41.8 %collective-permute-done.10 = bf16[512,2048]{1,0:T(8,128)(2,1)} collective-permute-done((bf16[512,2048]{1,0:T(8,128)(2,1)}, bf16[512,2048]{1,0:T(8,128)(2,1)}, u32[]{:S(2)}, u32[]{:S(2)}) %collective-permute-start.10) | collective-permute-done | bytes 2097184 | tf_op jit(solution)/shard_map/ppermute | solution.py:31
  438.8 4.3 multiply_reduce_fusion.3
  443.8 3.6 fusion.55
  447.6 46.6 %collective-permute-done.13 = bf16[512,2048]{1,0:T(8,128)(2,1)S(1)} collective-permute-done((bf16[512,2048]{1,0:T(8,128)(2,1)S(1)}, bf16[512,2048]{1,0:T(8,128)(2,1)S(1)}, u32[]{:S(2)}, u32[]{:S(2)}) %collective-permute-start.13) | collective-permute-done | bytes 2097184 | tf_op jit(solution)/shard_map/ppermute | solution.py:31
  494.3 14.0 fusion.54
  510.7 17.2 %multiply_convert_fusion.5 = (bf16[1024,2048]{1,0:T(8,128)(2,1)}, f32[1024,2048]{1,0:T(8,128)}) fusion(f32[1024,2048]{1,0:T(8,128)} %fusion.54, bf16[2048,2048]{1,0:T(8,128)(2,1)} %all-gather.3.cloned.1.call-done, bf16[512,2048]{1,0:T(8,128)(2,1)} %copy-done.49, bf16[512,2048]{1,0:T(8,128)(2,1)S(1)} %fusion.55), kind=kOutput, calls=%fused_computation.38 | convolution fusion | flops 8610906112 | bytes 33554432 | tf_op jit(solution)/shard_map/dot_general | solution.py:1011
  527.9 13.4 fusion.87
  541.3 13.9 multiply_convert_fusion.4
  555.2 12.7 convolution_convert_fusion.2
  568.7 10.9 convolution_convert_fusion.3
  582.2 68.5 %collective-permute-done.16 = bf16[512,2048]{1,0:T(8,128)(2,1)S(1)} collective-permute-done((bf16[512,2048]{1,0:T(8,128)(2,1)S(1)}, bf16[512,2048]{1,0:T(8,128)(2,1)S(1)}, u32[]{:S(2)}, u32[]{:S(2)}) %collective-permute-start.16) | collective-permute-done | bytes 2097184 | tf_op jit(solution)/shard_map/ppermute | solution.py:31
  651.7 3.6 fusion.39
  655.4 6.1 fusion.37
  661.5 4.1 collective-permute-done.21
  667.0 13.2 fusion.42
  680.2 9.7 multiply_convert_fusion.2
  689.9 16.0 %fusion.88 = f32[1024,2048]{1,0:T(8,128)} fusion(bf16[1024,2048]{1,0:T(8,128)(2,1)} %get-tuple-element.81, bf16[2048,2048]{1,0:T(8,128)(2,1)} %get-tuple-element.70), kind=kOutput, calls=%fused_computation.189 | convolution fusion | flops 8589934592 | bytes 20971520 | tf_op jit(solution)/shard_map/dot_general | solution.py:1021
  705.9 3.6 collective-permute-done.19
  709.5 14.6 %add_convert_fusion.1 = bf16[1024,2048]{1,0:T(8,128)(2,1)} fusion(f32[1024,2048]{1,0:T(8,128)} %fusion.88, bf16[1024,2048]{1,0:T(8,128)(2,1)S(1)} %get-tuple-element.83, bf16[2048,2048]{1,0:T(8,128)(2,1)} %all-gather.3.cloned.1.call-done), kind=kOutput, calls=%fused_computation.32 | convolution fusion | flops 8594128896 | bytes 25165824 | tf_op jit(solution)/shard_map/dot_general | solution.py:1021
  724.4 19.2 %multiply_convert_fusion = (bf16[1024,2048]{1,0:T(8,128)(2,1)}, bf16[1024,2048]{1,0:T(8,128)(2,1)}) fusion(f32[1024,2048]{1,0:T(8,128)} %fusion.87, f32[1024,2048]{1,0:T(8,128)} %get-tuple-element.187, bf16[1024,2048]{1,0:T(8,128)(2,1)S(1)} %pad_maximum_fusion.3, bf16[2048,2048]{1,0:T(8,128)(2,1)} %all-gather.5.cloned.1.call-done), kind=kOutput, calls=%fused_computation.30 | convolution fusion | flops 8617197568 | bytes 37748736 | tf_op jit(solution)/shard_map/dot_general | solution.py:1011
  743.6 12.8 fusion.89
  756.4 12.6 add_convert_fusion
  772.9 25.0 %fusion.26 = bf16[2048,2048]{1,0:T(8,128)(2,1)} fusion(bf16[1024,2048]{1,0:T(8,128)(2,1)} %get-tuple-element.153, bf16[1024,2048]{1,0:T(8,128)(2,1)} %get-tuple-element.81, bf16[1024,2048]{1,0:T(8,128)(2,1)} %pad_maximum_fusion.2, bf16[512,2048]{1,0:T(8,128)(2,1)} %copy-done.49, bf16[512,2048]{1,0:T(8,128)(2,1)} %copy-done.20), kind=kOutput, calls=%fused_computation.40 | convolution fusion | flops 17226006528 | bytes 25165824 | tf_op jit(solution)/shard_map/dot_general | solution.py:1015
  797.9 4.4 add_convert_fusion.2
  802.6 24.6 %fusion.29 = bf16[2048,2048]{1,0:T(8,128)(2,1)} fusion(bf16[1024,2048]{1,0:T(8,128)(2,1)} %get-tuple-element.186, bf16[1024,2048]{1,0:T(8,128)(2,1)} %get-tuple-element.80, bf16[1024,2048]{1,0:T(8,128)(2,1)} %copy-done.14, bf16[512,2048]{1,0:T(8,128)(2,1)} %copy-done.51, bf16[512,2048]{1,0:T(8,128)(2,1)S(1)} %get-tuple-element.156), kind=kOutput, calls=%fused_computation.41 | convolution fusion | flops 17226006528 | bytes 25165824 | tf_op jit(solution)/shard_map/dot_general | solution.py:1015
  827.2 23.0 %collective-permute-done.24 = bf16[512,2048]{1,0:T(8,128)(2,1)} collective-permute-done((bf16[512,2048]{1,0:T(8,128)(2,1)}, bf16[512,2048]{1,0:T(8,128)(2,1)}, u32[]{:S(2)}, u32[]{:S(2)}) %collective-permute-start.24) | collective-permute-done | bytes 2097184 | tf_op jit(solution)/shard_map/ppermute | solution.py:31
  852.8 4.1 collective-permute-done.22
  857.0 4.7 multiply_reduce_fusion
  865.2 46.5 %collective-permute-done.26 = bf16[512,2048]{1,0:T(8,128)(2,1)} collective-permute-done((bf16[512,2048]{1,0:T(8,128)(2,1)S(1)}, bf16[512,2048]{1,0:T(8,128)(2,1)}, u32[]{:S(2)}, u32[]{:S(2)}) %collective-permute-start.26) | collective-permute-done | bytes 2097184 | tf_op jit(solution)/shard_map/ppermute | solution.py:31
  911.7 24.2 %fusion.23 = bf16[2048,2048]{1,0:T(8,128)(2,1)} fusion(bf16[1024,2048]{1,0:T(8,128)(2,1)} %get-tuple-element.152, bf16[1024,2048]{1,0:T(8,128)(2,1)} %copy-done.15, bf16[1024,2048]{1,0:T(8,128)(2,1)} %pad_maximum_fusion.2, bf16[512,2048]{1,0:T(8,128)(2,1)} %copy-done.49, bf16[512,2048]{1,0:T(8,128)(2,1)S(1)} %copy-done.21), kind=kOutput, calls=%fused_computation.39 | convolution fusion | flops 17226006528 | bytes 25165824 | tf_op jit(solution)/shard_map/dot_general | solution.py:1015
  935.9 4.7 pad_maximum_fusion.4
  946.5 4.7 fusion.56
  955.0 11.2 gather_fusion.2
  967.9 59.5 %attention_backward.1 = (f32[2048,512]{1,0:T(8,128)}, f32[2048,512]{1,0:T(8,128)}, f32[2048,512]{1,0:T(8,128)}) custom-call(s32[8]{0:T(128)S(1)} %and_select_fusion.6.high_ref, bf16[2048,512]{1,0:T(8,128)(2,1)S(1)} %copy-done.1, bf16[2048,512]{1,0:T(8,128)(2,1)S(1)} %copy-done.2, bf16[2048,512]{1,0:T(8,128)(2,1)} %get-tuple-element.66.v_ref, ...), custom_call_target="tpu_custom_call" | custom-call | flops 6442450944 | bytes 25165824 | tf_op jit(solution)/shard_map/attention_backward/pallas_call | solution.py:890
  1027.4 13.4 norm_grads.1
  1042.6 23.7 %collective-permute-start.36 = (f32[4,2048]{1,0:T(4,128)S(1)}, f32[4,2048]{1,0:T(4,128)S(1)}, u32[]{:S(2)}, u32[]{:S(2)}) collective-permute-start(f32[4,2048]{1,0:T(4,128)S(1)} %pad_maximum_fusion.14), channel_id=1, source_target_pairs={{0,16},{16,0},{1,17},{17,1},{2,18},{18,2},{3,19},{19,3},{4,20},{20... | collective-permute-start | bytes 98312 | tf_op jit(solution)/shard_map/ppermute | solution.py:31
  1069.9 3.1 broadcast_select_fusion.1
  1074.3 7.3 fusion.50.refs_3_
  1082.2 14.8 %raw_grads.1 = bf16[2048,1536]{1,0:T(8,128)(2,1)} custom-call(f32[2048,512]{1,0:T(8,128)} %get-tuple-element.89.dq_ref, f32[2048,512]{1,0:T(8,128)} %get-tuple-element.90.dk_ref, f32[2048,512]{1,0:T(8,128)} %get-tuple-element.91.dv_ref, f32[2048,1536]{1,0:T(8,128)} %fusion.86.raw, f32[2,2048]{1,0:T(2,128)} %fusion.124.squares, f32[2,2048]{1,0:T(2,128)} %add.275.dots, ...), custom_call_target="tpu_custom_call" | custom-call | flops 20971520 | bytes 31457280 | tf_op jit(solution)/shard_map/raw_grads/pallas_call | solution.py:997
  1099.4 19.1 %convolution_convert_fusion.1.refs_2_ = bf16[2048,1536]{1,0:T(8,128)(2,1)} fusion(bf16[2048,2048]{1,0:T(8,128)(2,1)} %gather_fusion, bf16[2048,1536]{1,0:T(8,128)(2,1)} %raw_grads.1), kind=kOutput, calls=%fused_computation.43 | convolution fusion | flops 12888047616 | bytes 20971520 | tf_op jit(solution)/shard_map/dot_general | solution.py:1015
  1118.6 16.9 %gather_fusion.3 = bf16[2048,1536]{1,0:T(8,128)(2,1)} fusion(bf16[2048,1536]{1,0:T(8,128)(2,1)} %raw_grads.1, s32[2048]{0:T(1024)S(1)} %copy-done.33), kind=kCustom, calls=%fused_computation.3 | custom fusion | bytes 12591104 | tf_op jit(solution)/shard_map/gather | solution.py:1177
  1136.0 19.5 %convolution_convert_fusion.refs_0_ = bf16[2048,2048]{1,0:T(8,128)(2,1)} fusion(bf16[2048,1536]{1,0:T(8,128)(2,1)} %gather_fusion.3, bf16[2048,1536]{1,0:T(8,128)(2,1)} %get-tuple-element.62), kind=kOutput, calls=%fused_computation.42 | convolution fusion | flops 12889096192 | bytes 20971520 | tf_op jit(solution)/shard_map/dot_general | solution.py:1021
  1155.6 131.5 %leave.1 = (bf16[512,2048]{1,0:T(8,128)(2,1)}, f32[256,512]{1,0:T(8,128)}, f32[256,512]{1,0:T(8,128)}, f32[256,512]{1,0:T(8,128)}, f32[256,512]{1,0:T(8,128)}) custom-call(bf16[2048,2048]{1,0:T(8,128)(2,1)} %convolution_convert_fusion.refs_0_, f32[512,2048]{1,0:T(8,128)} %copy-done.6, bf16[2048,1536]{1,0:T(8,128)(2,1)} %convolution_convert_fusion.1.refs_2_, ...), custom_call_target="tpu_custom_call" | custom-call | bytes 134217728 | tf_op jit(solution)/shard_map/leave/pallas_call | solution.py:576
  1292.1 3.8 collective-permute-start.35
  1303.6 3.0 broadcast_select_fusion.5
  1308.3 57.3 %collective-permute-start.33 = (bf16[256,2048]{1,0:T(8,128)(2,1)}, bf16[256,2048]{1,0:T(8,128)(2,1)}, u32[]{:S(2)}, u32[]{:S(2)}) collective-permute-start(bf16[256,2048]{1,0:T(8,128)(2,1)} %get-tuple-element.161), channel_id=1, source_target_pairs={{2,0},{6,2},{4,6},{0,4},{3,1},{7,3},{5,7},{1,5},{10,8},{14,10},{12... | collective-permute-start | bytes 3145736 | tf_op jit(solution)/shard_map/ppermute | solution.py:62
  1365.6 22.7 %collective-permute-done.35 = bf16[256,2048]{1,0:T(8,128)(2,1)} collective-permute-done((bf16[256,2048]{1,0:T(8,128)(2,1)S(1)}, bf16[256,2048]{1,0:T(8,128)(2,1)}, u32[]{:S(2)}, u32[]{:S(2)}) %collective-permute-start.35) | collective-permute-done | bytes 1048608 | tf_op jit(solution)/shard_map/ppermute | solution.py:62
  1391.9 18.9 %collective-permute-done.31 = bf16[256,2048]{1,0:T(8,128)(2,1)} collective-permute-done((bf16[256,2048]{1,0:T(8,128)(2,1)}, bf16[256,2048]{1,0:T(8,128)(2,1)}, u32[]{:S(2)}, u32[]{:S(2)}) %collective-permute-start.31) | collective-permute-done | bytes 1048608 | tf_op jit(solution)/shard_map/ppermute | solution.py:62
  1410.8 3.4 convert_add_fusion.3
  1414.2 19.1 %collective-permute-done.33 = bf16[256,2048]{1,0:T(8,128)(2,1)} collective-permute-done((bf16[256,2048]{1,0:T(8,128)(2,1)}, bf16[256,2048]{1,0:T(8,128)(2,1)}, u32[]{:S(2)}, u32[]{:S(2)}) %collective-permute-start.33) | collective-permute-done | bytes 1048608 | tf_op jit(solution)/shard_map/ppermute | solution.py:62
  1433.2 3.4 convert_add_fusion.2
  (260 shorter events, 97.4 us)
Async XLA Ops:
  7.2 214.6 %copy-start.43 = (s32[1,2048]{1,0:T(1,128)S(1)}, s32[1,2048]{1,0:T(1,128)}, u32[]{:S(2)}) copy-start(s32[1,2048]{1,0:T(1,128)} %param.18) | copy-start | bytes 24580
  7.2 206.9 %copy-start.24 = (bf16[256,2048]{1,0:T(8,128)(2,1)S(1)}, bf16[256,2048]{1,0:T(8,128)(2,1)}, u32[]{:S(2)}) copy-start(bf16[256,2048]{1,0:T(8,128)(2,1)} %param.24) | copy-start | bytes 3145732
  7.2 503.5 %all-gather.3.cloned.1.call-start = ((), (), s32[]{:S(2)}) async-start(), calls=%async_computation.3 | async-start | bytes 10485760 | tf_op jit(solution)/shard_map/all_gather | solution.py:58
  7.2 214.5 %collective-permute-start.5 = (s32[1,2048]{1,0:T(1,128)}, s32[1,2048]{1,0:T(1,128)S(1)}, u32[]{:S(2)}, u32[]{:S(2)}) collective-permute-start(s32[1,2048]{1,0:T(1,128)} %param.18), channel_id=1, source_target_pairs={{0,4},{4,0},{1,5},{5,1},{2,6},{6,2},{3,7},{7,3},{8,12},{12,8},{9,1... | collective-permute-start | bytes 24584 | tf_op jit(solution)/shard_map/ppermute | solution.py:31
  214.1 48.0 %collective-permute-start.3 = (bf16[256,2048]{1,0:T(8,128)(2,1)S(1)}, bf16[256,2048]{1,0:T(8,128)(2,1)S(1)}, u32[]{:S(2)}, u32[]{:S(2)}) collective-permute-start(bf16[256,2048]{1,0:T(8,128)(2,1)S(1)} %copy-done.24), channel_id=1, source_target_pairs={{2,4},{4,2},{3,5},{5,3},{10,12},{12,10},{11,13},{13,11},{18,20},{2... | collective-permute-start | bytes 3145736 | tf_op jit(solution)/shard_map/ppermute | solution.py:36
  214.8 47.4 %collective-permute-start.4 = (bf16[256,2048]{1,0:T(8,128)(2,1)S(1)}, bf16[256,2048]{1,0:T(8,128)(2,1)S(1)}, u32[]{:S(2)}, u32[]{:S(2)}) collective-permute-start(bf16[256,2048]{1,0:T(8,128)(2,1)S(1)} %copy-done.24), channel_id=1, source_target_pairs={{0,2},{2,6},{6,4},{4,0},{1,3},{3,7},{7,5},{5,1},{8,10},{10,14},{14... | collective-permute-start | bytes 3145736 | tf_op jit(solution)/shard_map/ppermute | solution.py:49
  221.9 63.4 %copy-start.39 = (s32[2048,1]{0,1:T(1,128)}, s32[2048,1]{0,1:T(1,128)S(1)}, u32[]{:S(2)}) copy-start(s32[2048,1]{0,1:T(1,128)S(1)} %get-tuple-element.172) | copy-start | bytes 24580
  263.9 291.3 %all-gather.5.cloned.1.call-start = ((), (), s32[]{:S(2)}) async-start(), calls=%async_computation.4 | async-start | bytes 10485760 | tf_op jit(solution)/shard_map/all_gather | solution.py:58
  263.9 36.0 %collective-permute-start = (bf16[256,2048]{1,0:T(8,128)(2,1)}, bf16[256,2048]{1,0:T(8,128)(2,1)S(1)}, u32[]{:S(2)}, u32[]{:S(2)}) collective-permute-start(bf16[256,2048]{1,0:T(8,128)(2,1)} %bitcast), channel_id=1, source_target_pairs={{2,4},{4,2},{3,5},{5,3},{10,12},{12,10},{11,13},{13,11},{18,20},{2... | collective-permute-start | bytes 3145736 | tf_op jit(solution)/shard_map/ppermute | solution.py:36
  264.7 105.5 %collective-permute-start.1 = (bf16[256,2048]{1,0:T(8,128)(2,1)}, bf16[256,2048]{1,0:T(8,128)(2,1)}, u32[]{:S(2)}, u32[]{:S(2)}) collective-permute-start(bf16[256,2048]{1,0:T(8,128)(2,1)} %bitcast), channel_id=1, source_target_pairs={{0,2},{2,6},{6,4},{4,0},{1,3},{3,7},{7,5},{5,1},{8,10},{10,14},{14... | collective-permute-start | bytes 3145736 | tf_op jit(solution)/shard_map/ppermute | solution.py:49
  271.7 2.7 collective-permute-start.2
  298.0 1.4 collective-permute-start.6
  298.6 71.6 %copy-start.32 = (s32[2048]{0:T(1024)}, s32[2048]{0:T(1024)S(1)}, u32[]{:S(2)}) copy-start(s32[2048]{0:T(1024)S(1)} %fusion.66) | copy-start | bytes 24580
  299.4 18.8 %collective-permute-start.7 = (f32[2,2048]{1,0:T(2,128)S(1)}, f32[2,2048]{1,0:T(2,128)S(1)}, u32[]{:S(2)}, u32[]{:S(2)}) collective-permute-start(f32[2,2048]{1,0:T(2,128)S(1)} %fusion.81), channel_id=1, source_target_pairs={{0,1},{1,0},{2,3},{3,2},{4,5},{5,4},{6,7},{7,6},{8,9},{9,8},{10,11... | collective-permute-start | bytes 49160 | tf_op jit(solution)/shard_map/ppermute | solution.py:31
  384.0 4.3 collective-permute-start.9
  390.8 48.0 %collective-permute-start.10 = (bf16[512,2048]{1,0:T(8,128)(2,1)}, bf16[512,2048]{1,0:T(8,128)(2,1)}, u32[]{:S(2)}, u32[]{:S(2)}) collective-permute-start(bf16[512,2048]{1,0:T(8,128)(2,1)} %fusion.40), channel_id=1, source_target_pairs={{0,1},{1,0},{2,3},{3,2},{4,5},{5,4},{6,7},{7,6},{8,9},{9,8},{10,11... | collective-permute-start | bytes 6291464 | tf_op jit(solution)/shard_map/ppermute | solution.py:31
  393.8 45.0 %collective-permute-start.8 = (bf16[512,2048]{1,0:T(8,128)(2,1)}, bf16[512,2048]{1,0:T(8,128)(2,1)}, u32[]{:S(2)}, u32[]{:S(2)}) collective-permute-start(bf16[512,2048]{1,0:T(8,128)(2,1)} %slice.196), channel_id=1, source_target_pairs={{0,4},{4,0},{1,5},{5,1},{2,6},{6,2},{3,7},{7,3},{8,12},{12,8},{9,1... | collective-permute-start | bytes 6291464 | tf_op jit(solution)/shard_map/ppermute | solution.py:31
  396.9 46.9 %copy-start.30 = (f32[2048]{0:T(1024)S(1)}, f32[2048]{0:T(1024)}, u32[]{:S(2)}) copy-start(f32[2048]{0:T(1024)} %param.28) | copy-start | bytes 24580
  396.9 892.8 %reduce-scatter.8.cloned.1.call-start = ((), (), s32[]{:S(2)}) async-start(), calls=%async_computation.7 | async-start | bytes 10485760 | tf_op jit(solution)/shard_map/reduce_scatter | solution.py:73
  443.7 211.6 %copy-start.34 = (f32[512]{0:T(512)}, f32[512]{0:T(512)S(1)}, u32[]{:S(2)}) copy-start(f32[512]{0:T(512)S(1)} %get-tuple-element.178) | copy-start | bytes 6148
  447.4 63.3 %copy-start.20 = (bf16[512,2048]{1,0:T(8,128)(2,1)}, bf16[512,2048]{1,0:T(8,128)(2,1)S(1)}, u32[]{:S(2)}) copy-start(bf16[512,2048]{1,0:T(8,128)(2,1)S(1)} %fusion.55) | copy-start | bytes 6291460
  447.4 46.9 %collective-permute-start.13 = (bf16[512,2048]{1,0:T(8,128)(2,1)S(1)}, bf16[512,2048]{1,0:T(8,128)(2,1)S(1)}, u32[]{:S(2)}, u32[]{:S(2)}) collective-permute-start(bf16[512,2048]{1,0:T(8,128)(2,1)S(1)} %fusion.55), channel_id=1, source_target_pairs={{0,1},{1,0},{2,3},{3,2},{4,5},{5,4},{6,7},{7,6},{8,9},{9,8},{10,11... | collective-permute-start | bytes 6291464 | tf_op jit(solution)/shard_map/ppermute | solution.py:31
  447.6 46.6 %collective-permute-start.11 = (bf16[512,2048]{1,0:T(8,128)(2,1)S(1)}, bf16[512,2048]{1,0:T(8,128)(2,1)S(1)}, u32[]{:S(2)}, u32[]{:S(2)}) collective-permute-start(bf16[512,2048]{1,0:T(8,128)(2,1)S(1)} %fusion.55), channel_id=1, source_target_pairs={{0,4},{4,0},{1,5},{5,1},{2,6},{6,2},{3,7},{7,3},{8,12},{12,8},{9,1... | collective-permute-start | bytes 6291464 | tf_op jit(solution)/shard_map/ppermute | solution.py:31
  494.3 14.0 collective-permute-start.14
  568.2 11.5 collective-permute-start.15
  580.6 70.1 %collective-permute-start.16 = (bf16[512,2048]{1,0:T(8,128)(2,1)S(1)}, bf16[512,2048]{1,0:T(8,128)(2,1)S(1)}, u32[]{:S(2)}, u32[]{:S(2)}) collective-permute-start(bf16[512,2048]{1,0:T(8,128)(2,1)S(1)} %add_convert_fusion.4), channel_id=1, source_target_pairs={{0,1},{1,0},{2,3},{3,2},{4,5},{5,4},{6,7},{7,6},{8,9},{9,8},{10,11... | collective-permute-start | bytes 6291464 | tf_op jit(solution)/shard_map/ppermute | solution.py:31
  581.3 70.4 %copy-start.36 = (f32[2048]{0:T(1024)S(1)}, f32[2048]{0:T(1024)}, u32[]{:S(2)}) copy-start(f32[2048]{0:T(1024)} %param.29) | copy-start | bytes 24580
  581.3 69.4 %collective-permute-start.12 = (bf16[512,2048]{1,0:T(8,128)(2,1)S(1)}, bf16[512,2048]{1,0:T(8,128)(2,1)S(1)}, u32[]{:S(2)}, u32[]{:S(2)}) collective-permute-start(bf16[512,2048]{1,0:T(8,128)(2,1)S(1)} %slice.140), channel_id=1, source_target_pairs={{0,4},{4,0},{1,5},{5,1},{2,6},{6,2},{3,7},{7,3},{8,12},{12,8},{9,1... | collective-permute-start | bytes 6291464 | tf_op jit(solution)/shard_map/ppermute | solution.py:31
  581.4 70.3 %collective-permute-start.18 = (bf16[512,2048]{1,0:T(8,128)(2,1)S(1)}, bf16[512,2048]{1,0:T(8,128)(2,1)S(1)}, u32[]{:S(2)}, u32[]{:S(2)}) collective-permute-start(bf16[512,2048]{1,0:T(8,128)(2,1)S(1)} %copy-done.19), channel_id=1, source_target_pairs={{2,4},{4,2},{3,5},{5,3},{10,12},{12,10},{11,13},{13,11},{18,20},{2... | collective-permute-start | bytes 6291464 | tf_op jit(solution)/shard_map/ppermute | solution.py:36
  655.3 24.8 %slice-start = ((s8[8388608]{0:T(1024)(128)(4,1)}), s8[4194304]{0:T(1024)(128)(4,1)S(1)}, s32[]{:S(2)}) async-start(s8[8388608]{0:T(1024)(128)(4,1)} %bitcast.61), calls=%async_computation.8 | async-start | bytes 8388608
  661.5 4.2 collective-permute-start.21
  661.5 48.0 %collective-permute-start.19 = (bf16[512,2048]{1,0:T(8,128)(2,1)S(1)}, bf16[512,2048]{1,0:T(8,128)(2,1)S(1)}, u32[]{:S(2)}, u32[]{:S(2)}) collective-permute-start(bf16[512,2048]{1,0:T(8,128)(2,1)S(1)} %get-tuple-element.156), channel_id=1, source_target_pairs={{0,1},{1,0},{2,3},{3,2},{4,5},{5,4},{6,7},{7,6},{8,9},{9,8},{10,11... | collective-permute-start | bytes 6291464 | tf_op jit(solution)/shard_map/ppermute | solution.py:31
  709.5 14.6 %collective-permute-start.20 = (bf16[512,2048]{1,0:T(8,128)(2,1)S(1)}, bf16[512,2048]{1,0:T(8,128)(2,1)S(1)}, u32[]{:S(2)}, u32[]{:S(2)}) collective-permute-start(bf16[512,2048]{1,0:T(8,128)(2,1)S(1)} %collective-permute-done.19), channel_id=1, source_target_pairs={{0,4},{4,0},{1,5},{5,1},{2,6},{6,2},{3,7},{7,3},{8,12},{12,8},{9,1... | collective-permute-start | bytes 6291464 | tf_op jit(solution)/shard_map/ppermute | solution.py:31
  772.4 25.5 %collective-permute-start.23 = (bf16[512,2048]{1,0:T(8,128)(2,1)}, bf16[512,2048]{1,0:T(8,128)(2,1)}, u32[]{:S(2)}, u32[]{:S(2)}) collective-permute-start(bf16[512,2048]{1,0:T(8,128)(2,1)} %slice.144), channel_id=1, source_target_pairs={{0,4},{4,0},{1,5},{5,1},{2,6},{6,2},{3,7},{7,3},{8,12},{12,8},{9,1... | collective-permute-start | bytes 6291464 | tf_op jit(solution)/shard_map/ppermute | solution.py:31
  802.3 47.9 %collective-permute-start.24 = (bf16[512,2048]{1,0:T(8,128)(2,1)}, bf16[512,2048]{1,0:T(8,128)(2,1)}, u32[]{:S(2)}, u32[]{:S(2)}) collective-permute-start(bf16[512,2048]{1,0:T(8,128)(2,1)} %add_convert_fusion.2), channel_id=1, source_target_pairs={{0,1},{1,0},{2,3},{3,2},{4,5},{5,4},{6,7},{7,6},{8,9},{9,8},{10,11... | collective-permute-start | bytes 6291464 | tf_op jit(solution)/shard_map/ppermute | solution.py:31
  850.2 445.8 %reduce-scatter.4.cloned.1.call-start = ((), (), s32[]{:S(2)}) async-start(), calls=%async_computation.5 | async-start | bytes 10485760 | tf_op jit(solution)/shard_map/reduce_scatter | solution.py:73
  850.8 452.8 %reduce-scatter.6.cloned.1.call-start = ((), (), s32[]{:S(2)}) async-start(), calls=%async_computation.6 | async-start | bytes 10485760 | tf_op jit(solution)/shard_map/reduce_scatter | solution.py:73
  852.7 4.2 collective-permute-start.22
  861.7 49.9 %copy-start.21 = (bf16[512,2048]{1,0:T(8,128)(2,1)S(1)}, bf16[512,2048]{1,0:T(8,128)(2,1)}, u32[]{:S(2)}) copy-start(bf16[512,2048]{1,0:T(8,128)(2,1)} %copy-done.20) | copy-start | bytes 6291460
  863.9 47.8 %collective-permute-start.26 = (bf16[512,2048]{1,0:T(8,128)(2,1)S(1)}, bf16[512,2048]{1,0:T(8,128)(2,1)}, u32[]{:S(2)}, u32[]{:S(2)}) collective-permute-start(bf16[512,2048]{1,0:T(8,128)(2,1)S(1)} %subtract_convert_fusion), channel_id=1, source_target_pairs={{0,1},{1,0},{2,3},{3,2},{4,5},{5,4},{6,7},{7,6},{8,9},{9,8},{10,11... | collective-permute-start | bytes 6291464 | tf_op jit(solution)/shard_map/ppermute | solution.py:31
  911.7 24.3 %collective-permute-start.27 = (bf16[512,2048]{1,0:T(8,128)(2,1)}, bf16[512,2048]{1,0:T(8,128)(2,1)}, u32[]{:S(2)}, u32[]{:S(2)}) collective-permute-start(bf16[512,2048]{1,0:T(8,128)(2,1)} %collective-permute-done.26), channel_id=1, source_target_pairs={{0,4},{4,0},{1,5},{5,1},{2,6},{6,2},{3,7},{7,3},{8,12},{12,8},{9,1... | collective-permute-start | bytes 6291464 | tf_op jit(solution)/shard_map/ppermute | solution.py:31
  942.3 4.2 collective-permute-start.25
  943.0 126.9 %collective-permute-start.17 = (bf16[512,2048]{1,0:T(8,128)(2,1)}, bf16[512,2048]{1,0:T(8,128)(2,1)}, u32[]{:S(2)}, u32[]{:S(2)}) collective-permute-start(bf16[512,2048]{1,0:T(8,128)(2,1)} %get-tuple-element.157), channel_id=1, source_target_pairs={{2,4},{4,2},{3,5},{5,3},{10,12},{12,10},{11,13},{13,11},{18,20},{2... | collective-permute-start | bytes 6291464 | tf_op jit(solution)/shard_map/ppermute | solution.py:36
  1040.8 32.2 %copy-start.41 = (f32[2,2048]{1,0:T(2,128)S(1)}, f32[2,2048]{1,0:T(2,128)}, u32[]{:S(2)}) copy-start(f32[2,2048]{1,0:T(2,128)} %get-tuple-element.92) | copy-start | bytes 49156
  1040.8 33.4 %copy-start.17 = (bf16[2048,512]{1,0:T(8,128)(2,1)S(1)}, bf16[2048,512]{1,0:T(8,128)(2,1)}, u32[]{:S(2)}) copy-start(bf16[2048,512]{1,0:T(8,128)(2,1)} %gather_fusion.1) | copy-start | bytes 6291460
  1042.5 31.8 %copy-start.13 = (bf16[1024,2048]{1,0:T(8,128)(2,1)S(1)}, bf16[1024,2048]{1,0:T(8,128)(2,1)}, u32[]{:S(2)}) copy-start(bf16[1024,2048]{1,0:T(8,128)(2,1)} %pad_maximum_fusion.4) | copy-start | bytes 12582916
  1042.6 26.5 %collective-permute-start.36 = (f32[4,2048]{1,0:T(4,128)S(1)}, f32[4,2048]{1,0:T(4,128)S(1)}, u32[]{:S(2)}, u32[]{:S(2)}) collective-permute-start(f32[4,2048]{1,0:T(4,128)S(1)} %pad_maximum_fusion.14), channel_id=1, source_target_pairs={{0,16},{16,0},{1,17},{17,1},{2,18},{18,2},{3,19},{19,3},{4,20},{20... | collective-permute-start | bytes 98312 | tf_op jit(solution)/shard_map/ppermute | solution.py:31
  1066.2 6.8 collective-permute-start.28
  1069.2 5.0 collective-permute-start.37
  1073.1 8.5 collective-permute-start.29
  1074.2 22.8 %collective-permute-start.38 = (f32[4,2048]{1,0:T(4,128)S(1)}, f32[4,2048]{1,0:T(4,128)S(1)}, u32[]{:S(2)}, u32[]{:S(2)}) collective-permute-start(f32[4,2048]{1,0:T(4,128)S(1)} %fusion.123), channel_id=1, source_target_pairs={{0,4},{4,0},{1,5},{5,1},{2,6},{6,2},{3,7},{7,3},{8,12},{12,8},{9,1... | collective-permute-start | bytes 98312 | tf_op jit(solution)/shard_map/ppermute | solution.py:31
  1097.0 21.5 %copy-start.33 = (s32[2048]{0:T(1024)S(1)}, s32[2048]{0:T(1024)}, u32[]{:S(2)}) copy-start(s32[2048]{0:T(1024)} %copy-done.32) | copy-start | bytes 24580
  1097.0 38.4 %collective-permute-start.39 = (f32[4,2048]{1,0:T(4,128)S(1)}, f32[4,2048]{1,0:T(4,128)S(1)}, u32[]{:S(2)}, u32[]{:S(2)}) collective-permute-start(f32[4,2048]{1,0:T(4,128)S(1)} %add.281), channel_id=1, source_target_pairs={{0,2},{2,0},{1,3},{3,1},{4,6},{6,4},{5,7},{7,5},{8,10},{10,8},{9,1... | collective-permute-start | bytes 98312 | tf_op jit(solution)/shard_map/ppermute | solution.py:31
  1135.5 153.6 %collective-permute-start.40 = (f32[4,2048]{1,0:T(4,128)S(1)}, f32[4,2048]{1,0:T(4,128)S(1)}, u32[]{:S(2)}, u32[]{:S(2)}) collective-permute-start(f32[4,2048]{1,0:T(4,128)S(1)} %add.282), channel_id=1, source_target_pairs={{0,1},{1,0},{2,3},{3,2},{4,5},{5,4},{6,7},{7,6},{8,9},{9,8},{10,11... | collective-permute-start | bytes 98312 | tf_op jit(solution)/shard_map/ppermute | solution.py:31
  1291.4 16.9 %collective-permute-start.34 = (bf16[256,2048]{1,0:T(8,128)(2,1)S(1)}, bf16[256,2048]{1,0:T(8,128)(2,1)S(1)}, u32[]{:S(2)}, u32[]{:S(2)}) collective-permute-start(bf16[256,2048]{1,0:T(8,128)(2,1)S(1)} %get-tuple-element.158), channel_id=1, source_target_pairs={{2,4},{4,2},{3,5},{5,3},{10,12},{12,10},{11,13},{13,11},{18,20},{2... | collective-permute-start | bytes 3145736 | tf_op jit(solution)/shard_map/ppermute | solution.py:36
  1292.1 96.2 %collective-permute-start.35 = (bf16[256,2048]{1,0:T(8,128)(2,1)S(1)}, bf16[256,2048]{1,0:T(8,128)(2,1)}, u32[]{:S(2)}, u32[]{:S(2)}) collective-permute-start(bf16[256,2048]{1,0:T(8,128)(2,1)S(1)} %get-tuple-element.159), channel_id=1, source_target_pairs={{2,0},{6,2},{4,6},{0,4},{3,1},{7,3},{5,7},{1,5},{10,8},{14,10},{12... | collective-permute-start | bytes 3145736 | tf_op jit(solution)/shard_map/ppermute | solution.py:62
  1299.0 92.9 %collective-permute-start.30 = (bf16[256,2048]{1,0:T(8,128)(2,1)}, bf16[256,2048]{1,0:T(8,128)(2,1)}, u32[]{:S(2)}, u32[]{:S(2)}) collective-permute-start(bf16[256,2048]{1,0:T(8,128)(2,1)} %get-tuple-element.162), channel_id=1, source_target_pairs={{2,4},{4,2},{3,5},{5,3},{10,12},{12,10},{11,13},{13,11},{18,20},{2... | collective-permute-start | bytes 3145736 | tf_op jit(solution)/shard_map/ppermute | solution.py:36
  1300.6 110.1 %collective-permute-start.31 = (bf16[256,2048]{1,0:T(8,128)(2,1)}, bf16[256,2048]{1,0:T(8,128)(2,1)}, u32[]{:S(2)}, u32[]{:S(2)}) collective-permute-start(bf16[256,2048]{1,0:T(8,128)(2,1)} %get-tuple-element.163), channel_id=1, source_target_pairs={{2,0},{6,2},{4,6},{0,4},{3,1},{7,3},{5,7},{1,5},{10,8},{14,10},{12... | collective-permute-start | bytes 3145736 | tf_op jit(solution)/shard_map/ppermute | solution.py:62
  1306.6 107.5 %collective-permute-start.32 = (bf16[256,2048]{1,0:T(8,128)(2,1)}, bf16[256,2048]{1,0:T(8,128)(2,1)}, u32[]{:S(2)}, u32[]{:S(2)}) collective-permute-start(bf16[256,2048]{1,0:T(8,128)(2,1)} %get-tuple-element.160), channel_id=1, source_target_pairs={{2,4},{4,2},{3,5},{5,3},{10,12},{12,10},{11,13},{13,11},{18,20},{2... | collective-permute-start | bytes 3145736 | tf_op jit(solution)/shard_map/ppermute | solution.py:36
  1308.3 57.3 %copy-start.25 = (bf16[256,2048]{1,0:T(8,128)(2,1)}, bf16[256,2048]{1,0:T(8,128)(2,1)S(1)}, u32[]{:S(2)}) copy-start(bf16[256,2048]{1,0:T(8,128)(2,1)S(1)} %collective-permute-done.34) | copy-start | bytes 3145732
  1308.3 125.0 %collective-permute-start.33 = (bf16[256,2048]{1,0:T(8,128)(2,1)}, bf16[256,2048]{1,0:T(8,128)(2,1)}, u32[]{:S(2)}, u32[]{:S(2)}) collective-permute-start(bf16[256,2048]{1,0:T(8,128)(2,1)} %get-tuple-element.161), channel_id=1, source_target_pairs={{2,0},{6,2},{4,6},{0,4},{3,1},{7,3},{5,7},{1,5},{10,8},{14,10},{12... | collective-permute-start | bytes 3145736 | tf_op jit(solution)/shard_map/ppermute | solution.py:62
  1391.9 44.8 %copy-start.18 = (bf16[512,2048]{1,0:T(8,128)(2,1)S(1)}, bf16[512,2048]{1,0:T(8,128)(2,1)}, u32[]{:S(2)}) copy-start(bf16[512,2048]{1,0:T(8,128)(2,1)} %get-tuple-element.204) | copy-start | bytes 6291460
  1414.2 23.8 %copy-start.28 = (f32[256,512]{1,0:T(8,128)S(1)}, f32[256,512]{1,0:T(8,128)}, u32[]{:S(2)}) copy-start(f32[256,512]{1,0:T(8,128)} %get-tuple-element.205) | copy-start | bytes 1572868
  1414.2 24.6 %copy-start.27 = (f32[256,512]{1,0:T(8,128)S(1)}, f32[256,512]{1,0:T(8,128)}, u32[]{:S(2)}) copy-start(f32[256,512]{1,0:T(8,128)} %get-tuple-element.206) | copy-start | bytes 1572868
  (36 other events, 250.9 us)
Sparse Core Ops, SparseCore 0:
  264.0 89.6 all-gather.2
  397.0 93.7 all-gather.4
  850.3 93.4 reduce-scatter.7
  947.1 86.4 reduce-scatter.3
  1036.5 87.2 reduce-scatter.5

commit v3 on v2

--- a/solution.py
+++ b/solution.py
@@ -17,6 +17,8 @@
 BLOCK = 256
 VMEM_BYTES = 48 * 1024 * 1024
 MESH = pl.DeviceIdType.MESH
+BESIDE = pl.CostEstimate(flops=1, bytes_accessed=1, transcendentals=0)
+PARTS = 2
 
 SWAP = [(0, 1), (1, 0)]
 TURN = [(1, 2), (2, 1)]
@@ -31,9 +33,17 @@
     return lax.ppermute(value, axis, SWAP)
 
 
+def start_turn(value):
+    return value, lax.ppermute(value, ("core", "th"), TURN)
+
+
+def finish_turn(kept, arrived):
+    stays = lax.axis_index("core") == lax.axis_index("th")
+    return jnp.where(stays, kept, arrived)
+
+
 def turn(value):
-    stays = lax.axis_index("core") == lax.axis_index("th")
-    return jnp.where(stays, value, lax.ppermute(value, ("core", "th"), TURN))
+    return finish_turn(*start_turn(value))
 
 
 def small_grid():
@@ -45,35 +55,33 @@
     return lax.slice_in_dim(value, index * size, (index + 1) * size, axis=dim)
 
 
-def pieces_of_weight(shard):
-    return turn(shard), lax.ppermute(shard, ("core", "th"), CYCLE)
-
-
-def gather_weight(pieces):
-    first, second = pieces
+def in_turn(left, right):
     upper = lax.axis_index("th") == 0
-    pair = jnp.concatenate(
-        [jnp.where(upper, first, second), jnp.where(upper, second, first)], axis=0
-    )
+    return jnp.where(upper, left, right), jnp.where(upper, right, left)
+
+
+def pair_of_weight(shard):
+    second = lax.ppermute(shard, ("core", "th"), CYCLE)
+    return jnp.concatenate(in_turn(turn(shard), second), axis=0)
+
+
+def gather_weight(pair):
     return lax.all_gather(pair, ("a", "b"), axis=0, tiled=True)
 
 
-def finish_scatter(first, second):
-    return turn(first).astype(jnp.float32) + lax.ppermute(
-        second, ("core", "th"), CYCLE_BACK
-    ).astype(jnp.float32)
-
-
-def in_turn(low_part, high_part):
-    upper = lax.axis_index("th") == 0
-    return jnp.where(upper, low_part, high_part), jnp.where(upper, high_part, low_part)
-
-
-def scatter_weight(total):
-    pair = lax.psum_scatter(
+def scatter_pair(total):
+    return lax.psum_scatter(
         total.astype(jnp.bfloat16), ("a", "b"), scatter_dimension=0, tiled=True
     )
-    return finish_scatter(*in_turn(part(pair, 0, 0, 2), part(pair, 0, 1, 2)))
+
+
+def start_split(pair):
+    first, second = in_turn(part(pair, 0, 0, 2), part(pair, 0, 1, 2))
+    return first, start_turn(first)[1], lax.ppermute(second, ("core", "th"), CYCLE_BACK)
+
+
+def finish_split(first, arrived, other):
+    return finish_turn(first, arrived).astype(jnp.float32) + other.astype(jnp.float32)
 
 
 def greet():
@@ -97,11 +105,11 @@
 
 
 def entry_slots(plan):
-    return 4 * CHUNKS + sum(3 * len(units) + 6 for units in plan)
+    return 4 * CHUNKS + sum(3 * len(units) + 6 for units, _ in plan)
 
 
 def entry_kernel(plan, *refs):
-    shard_count = sum(len(units) for units in plan)
+    shard_count = sum(len(units) for units, _ in plan)
     tokens, shards = refs[0], refs[1 : 1 + shard_count]
     tokens_all, fulls = refs[1 + shard_count], refs[2 + shard_count : -3]
     send, recv, local = refs[-3:]
@@ -129,15 +137,16 @@
         remote(target, target, slot, {"core": 1 - core}).wait_recv()
 
     stages, taken = [], 0
-    for full, units in zip(fulls, plan):
+    for full, (units, rings) in zip(fulls, plan):
         stage = []
         for column in units:
             shard = shards[taken]
             base = slots(3)
             height, width = shard.shape
 
-            def place(sub, full=full, column=column, height=height, width=width):
-                row = pl.multiple_of((4 * a + 2 * b + sub) * height, height)
+            def place(sub, full=full, column=column, height=height, width=width, rings=rings):
+                block = 4 * a + 2 * b if rings else 0
+                row = pl.multiple_of((block + sub) * height, height)
                 return full.at[pl.ds(row, height), pl.ds(column, width)]
 
             stage.append((shard, place, base, taken))
@@ -249,14 +258,9 @@
         def _():
             own_rows(chunk).start()
 
-    start_stage(stages[0])
-    start_stage(stages[1])
-    finish_stage(stages[0])
-    start_ring(0)
-    for stage in stages[2:]:
-        start_stage(stage)
-    finish_stage(stages[1])
-    start_ring(1)
+    ringed = [index for index, (_, rings) in enumerate(plan) if rings]
+    for index in ringed:
+        start_stage(stages[index])
     for chunk in range(CHUNKS):
 
         @pl.when(jnp.logical_not(stays))
@@ -269,11 +273,12 @@
             row_copies(chunk)[1].start()
             row_copies(chunk)[2].start()
 
-    forward_ring(0)
-    forward_ring(1)
-    for index in range(2, len(fulls)):
+    for index in ringed:
         finish_stage(stages[index])
         start_ring(index)
+    for index in range(len(plan)):
+        if index not in ringed:
+            start_stage(stages[index])
     for chunk in range(CHUNKS):
 
         @pl.when(jnp.logical_not(stays))
@@ -282,12 +287,16 @@
             row_copies(chunk)[1].start()
             row_copies(chunk)[2].start()
 
+    for index in ringed:
+        forward_ring(index)
+    for chunk in range(CHUNKS):
         arrived(rows_of(core, 1 - tl, chunk), row_base + 4 * chunk + 1)
         row_copies(chunk)[3].start()
-    for index in range(2, len(fulls)):
-        forward_ring(index)
-    for index in range(len(fulls)):
+    for index in ringed:
         finish_ring(index)
+    for index in range(len(plan)):
+        if index not in ringed:
+            finish_stage(stages[index])
     for chunk in range(CHUNKS):
         arrived(rows_of(1 - core, tl, chunk), row_base + 4 * chunk + 2)
         arrived(rows_of(1 - core, 1 - tl, chunk), row_base + 4 * chunk + 3)
@@ -307,15 +316,19 @@
                 near_copy(shard, place, base).wait_send()
 
 
-def leave_kernel(cuts, *refs):
+def leave_kernel(cuts, paired, *refs):
     count = len(cuts)
-    partial, resid, totals = refs[0], refs[1], refs[2 : 2 + count]
-    outs = refs[2 + count : 2 + count + 1 + sum(len(cut) for cut in cuts)]
-    rows_out, shard_outs = outs[0], outs[1:]
-    scratch = refs[2 + count + len(outs) :]
+    ringed = [index for index in range(count) if not paired[index]]
+    partial, resid, gains, totals = refs[0], refs[1], refs[2], refs[3 : 3 + count]
+    outs = refs[3 + count : 3 + count + 2 + sum(len(cut) for cut in cuts)]
+    rows_out, gains_out, shard_outs = outs[0], outs[1], outs[2:]
+    scratch = refs[3 + count + len(outs) :]
     peer_far, peer_near, far_sum, from_far, done_rows = scratch[:5]
-    boxes = [scratch[5 + 7 * index : 12 + 7 * index] for index in range(count)]
-    send, recv, local = scratch[-3:]
+    boxes, taken = [], 5
+    for alone in paired:
+        boxes.append(scratch[taken : taken + (1 if alone else 8)])
+        taken += 1 if alone else 8
+    gain_box, send, recv, local = scratch[-4:]
     a, b, core = lax.axis_index("a"), lax.axis_index("b"), lax.axis_index("core")
     th, tl = lax.axis_index("th"), lax.axis_index("tl")
     stays = core == th
@@ -355,8 +368,11 @@
 
     own, peer, far, peer_of_far = range(4)
 
+    size = rows // PARTS
+
     def row_of(block, chunk):
-        return block * rows + chunk * step
+        place = chunk * step
+        return (place // size) * 4 * size + block * size + place % size
 
     def at(ref, row):
         return ref.at[pl.ds(row, step), :]
@@ -386,7 +402,7 @@
 
     def copies(index):
         total = totals[index]
-        over_a, over_b, send_b, send_a, from_b, from_a, _ = boxes[index]
+        _, over_a, over_b, send_b, send_a, from_b, from_a, _ = boxes[index]
         slot = base + 10 * index
         height = total.shape[0] // 8
 
@@ -402,38 +418,58 @@
             remote(send_a, half(from_a, 1), slot + 5, to_a),
         )
 
+    def own_sum(index, sub):
+        sums = totals[index] if paired[index] else boxes[index][7]
+        height = sums.shape[0] // 2
+        return sums.at[pl.ds(pl.multiple_of(sub * height, height), height), :]
+
     def last_copies(index):
-        sums = boxes[index][6]
+        inbox = boxes[index][0]
         slot = base + 10 * index + 6
         return (
-            remote(sums.at[1 - core], sums.at[2], slot, to_core),
-            remote(sums.at[0], sums.at[3], slot + 1, {"core": 0, "th": core}),
-            remote(sums.at[1], sums.at[3], slot + 1, {"core": 1, "th": core}, slot + 2),
+            remote(own_sum(index, 1 - core), inbox.at[0], slot, to_core),
+            remote(own_sum(index, 0), inbox.at[1], slot + 1, {"core": 0, "th": core}),
+            remote(own_sum(index, 1), inbox.at[1], slot + 1, {"core": 1, "th": core}, slot + 2),
         )
 
-    for index in range(count):
-        for copy in copies(index)[:2]:
+    def start_last(index):
+        @pl.when(stays)
+        def _():
+            last_copies(index)[0].start()
+
+        @pl.when(jnp.logical_not(stays))
+        def _():
+            last_copies(index)[1].start()
+            last_copies(index)[2].start()
+
+    gain_axes = ({"core": 1 - core}, {"tl": 1 - tl}, {"b": 1 - b}, {"a": 1 - a}, {"th": 1 - th})
+
+    def gain_copy(turn_index):
+        source = gains if turn_index == 0 else gain_box.at[4 + turn_index]
+        return remote(
+            source,
+            gain_box.at[turn_index],
+            base + 10 * count + turn_index,
+            gain_axes[turn_index],
+        )
+
+    def gain_step(turn_index):
+        arrived(gain_box.at[turn_index], base + 10 * count + turn_index)
+        mine = gains[...] if turn_index == 0 else gain_box[4 + turn_index]
+        total = mine + gain_box[turn_index]
+        if turn_index == 4:
+            gains_out[...] = total
+        else:
+            gain_box[5 + turn_index] = total
+            gain_copy(turn_index + 1).start()
+
+    def start_ring(index):
+        for copy in copies(index)[:4]:
             copy.start()
-    for chunk in range(CHUNKS):
-        row_copies(chunk)[0].start()
-    for index in range(count):
-        for copy in copies(index)[2:4]:
-            copy.start()
-    for chunk in range(CHUNKS):
-        row_copies(chunk)[1].start()
-    for chunk in range(CHUNKS):
-        arrived(at(peer_far, chunk * step), 4 * chunk)
-        add(
-            far_sum,
-            chunk * step,
-            step,
-            (partial, row_of(far, chunk)),
-            (peer_far, chunk * step),
-        )
-        row_copies(chunk)[2].start()
-    for index in range(count):
+
+    def turn_ring(index):
         total = totals[index]
-        over_a, over_b, send_b, send_a, _, _, _ = boxes[index]
+        _, over_a, over_b, send_b, send_a, _, _, _ = boxes[index]
         height = total.shape[0] // 8
         arrived(over_a, base + 10 * index)
         add(send_b, 0, height, (total, piece(total, a, 1 - b, 0)[0]), (over_a, 0))
@@ -441,7 +477,26 @@
         arrived(over_b, base + 10 * index + 1)
         add(send_a, 0, height, (total, piece(total, 1 - a, b, 1)[0]), (over_b, 0))
         copies(index)[5].start()
-    for chunk in range(CHUNKS):
+
+    def finish_ring(index):
+        total = totals[index]
+        _, _, _, _, _, from_b, from_a, sums = boxes[index]
+        height = total.shape[0] // 8
+        slot = base + 10 * index
+        for sub in (0, 1):
+            arrived(from_b.at[pl.ds(sub * height, height), :], slot + (4 if sub == 0 else 2))
+            arrived(from_a.at[pl.ds(sub * height, height), :], slot + (3 if sub == 0 else 5))
+            add(
+                sums,
+                sub * height,
+                height,
+                (total, piece(total, a, b, sub)[0]),
+                (from_b, sub * height),
+                (from_a, sub * height),
+            )
+        start_last(index)
+
+    def finish_chunk(chunk):
         here = chunk * step
         arrived(at(peer_near, here), 4 * chunk + 1)
         arrived(at(from_far, here), 4 * chunk + 2)
@@ -463,68 +518,72 @@
         def _():
             row_copies(chunk)[3].start()
 
+    for chunk in range(CHUNKS):
+        row_copies(chunk)[0].start()
+    for chunk in range(CHUNKS):
+        row_copies(chunk)[1].start()
     for index in range(count):
-        total = totals[index]
-        _, _, _, _, from_b, from_a, sums = boxes[index]
-        height = total.shape[0] // 8
-        slot = base + 10 * index
-        for sub in (0, 1):
-            arrived(from_b.at[pl.ds(sub * height, height), :], slot + (4 if sub == 0 else 2))
-            arrived(from_a.at[pl.ds(sub * height, height), :], slot + (3 if sub == 0 else 5))
-            add(
-                sums.at[sub],
-                0,
-                height,
-                (total, piece(total, a, b, sub)[0]),
-                (from_b, sub * height),
-                (from_a, sub * height),
-            )
-        near, zero, one = last_copies(index)
-
-        @pl.when(stays)
-        def _():
-            near.start()
+        if paired[index]:
+            start_last(index)
+    for chunk in range(CHUNKS):
+        arrived(at(peer_far, chunk * step), 4 * chunk)
+        add(
+            far_sum,
+            chunk * step,
+            step,
+            (partial, row_of(far, chunk)),
+            (peer_far, chunk * step),
+        )
+        row_copies(chunk)[2].start()
+    for index in ringed:
+        start_ring(index)
+    gain_copy(0).start()
+    gain_step(0)
+    for place in range(max(len(ringed), CHUNKS)):
+        if place < len(ringed):
+            turn_ring(ringed[place])
+        if place < CHUNKS:
+            finish_chunk(place)
+    for step_index in (1, 2, 3):
+        gain_step(step_index)
+    for index in ringed:
+        finish_ring(index)
+    gain_step(4)
+    for index, cut in sorted(enumerate(cuts), key=lambda pair: not paired[pair[0]]):
+        inbox = boxes[index][0]
+        sums = totals[index] if paired[index] else boxes[index][-1]
+        height = inbox.shape[1]
+        slot = base + 10 * index + 6
+        taken = sum(len(other) for other in cuts[:index])
+        arrived(inbox.at[1], slot + 1)
 
         @pl.when(jnp.logical_not(stays))
         def _():
-            zero.start()
-            one.start()
-
-    taken = 0
-    for index, cut in enumerate(cuts):
-        total = totals[index]
-        sums = boxes[index][6]
-        slot = base + 10 * index + 6
-        arrived(sums.at[3], slot + 1)
-
-        @pl.when(jnp.logical_not(stays))
-        def _():
-            arrived(sums.at[2], slot)
-
-        first = 0
-        for end in cut:
-            out = shard_outs[taken]
-            taken += 1
-
-            def one(step_index, unused, out=out, first=first, end=end, sums=sums):
-                here = pl.ds(pl.multiple_of(step_index * 16, 16), 16)
-
-                @pl.when(stays)
-                def _():
-                    out[here, :] = sums[core, here, first:end].astype(jnp.float32) + sums[
-                        3, here, first:end
-                    ].astype(jnp.float32)
-
-                @pl.when(jnp.logical_not(stays))
-                def _():
-                    out[here, :] = sums[2, here, first:end].astype(jnp.float32) + sums[
-                        3, here, first:end
-                    ].astype(jnp.float32)
-
-                return unused
-
-            lax.fori_loop(0, out.shape[0] // 16, one, 0)
-            first = end
+            arrived(inbox.at[0], slot)
+
+        def one(step_index, unused, cut=cut, taken=taken, sums=sums, inbox=inbox, height=height):
+            row = pl.multiple_of(step_index * 16, 16)
+            here = pl.ds(row, 16)
+            other = inbox[1, here, :].astype(jnp.float32)
+
+            def store(value):
+                first = 0
+                for offset, end in enumerate(cut):
+                    shard_outs[taken + offset][here, :] = (value + other)[:, first:end]
+                    first = end
+
+            @pl.when(stays)
+            def _():
+                own_row = pl.multiple_of(core * height + row, 16)
+                store(sums[pl.ds(own_row, 16), :].astype(jnp.float32))
+
+            @pl.when(jnp.logical_not(stays))
+            def _():
+                store(inbox[0, here, :].astype(jnp.float32))
+
+            return unused
+
+        lax.fori_loop(0, height // 16, one, 0)
     for chunk in range(CHUNKS):
         for copy in row_copies(chunk)[:3]:
             copy.wait_send()
@@ -538,49 +597,60 @@
             row_copies(chunk)[3].wait_send()
             arrived(at(rows_out, chunk * step), 4 * chunk + 3)
 
-    for index in range(count):
+    for turn_index in range(5):
+        gain_copy(turn_index).wait_send()
+    for index in ringed:
         for copy in copies(index):
             copy.wait_send()
-        near, zero, one = last_copies(index)
+    for index in range(count):
 
         @pl.when(stays)
         def _():
-            near.wait_send()
+            last_copies(index)[0].wait_send()
 
         @pl.when(jnp.logical_not(stays))
         def _():
-            zero.wait_send()
-            one.wait_send()
-
-
-def leave(partial, resid, totals):
+            last_copies(index)[1].wait_send()
+            last_copies(index)[2].wait_send()
+
+
+def leave(partial, resid, gains, totals):
     if not small_grid():
-        summed, _ = scatter_rows([partial])
+        summed = finish_scatter_rows(start_scatter([partial.astype(jnp.bfloat16)]), None)
         shards = []
-        for total, parts in totals:
-            shard, first = scatter_weight(total), 0
+        for total, parts, alone in totals:
+            shard, first = finish_split(*start_split(total if alone else scatter_pair(total))), 0
             for width in parts:
                 shards.append(shard[:, first : first + width])
                 first += width
-        return [turn((resid + summed).astype(jnp.bfloat16))] + shards
+        total_gains = sum_over(gains, DP + TENSOR)
+        return [turn((resid + summed).astype(jnp.bfloat16)), total_gains] + shards
     rows, columns = resid.shape
-    cuts, scratch, outs = [], [], [jax.ShapeDtypeStruct((rows, columns), jnp.bfloat16)]
-    for total, parts in totals:
-        height, width = total.shape[0] // 8, total.shape[1]
+    cuts, scratch = [], []
+    outs = [
+        jax.ShapeDtypeStruct((rows, columns), jnp.bfloat16),
+        jax.ShapeDtypeStruct(gains.shape, jnp.float32),
+    ]
+    for total, parts, alone in totals:
+        height, width = total.shape[0] // (2 if alone else 8), total.shape[1]
         cuts.append(tuple(sum(parts[: index + 1]) for index in range(len(parts))))
         outs += [jax.ShapeDtypeStruct((height, part_width), jnp.float32) for part_width in parts]
-        for shape in [(height, width)] * 4 + [(2 * height, width)] * 2 + [(4, height, width)]:
-            scratch.append(pltpu.VMEM(shape, jnp.bfloat16))
-    slots = 4 * CHUNKS + 10 * len(totals)
+        shapes = [(2, height, width)]
+        if not alone:
+            shapes += [(height, width)] * 4 + [(2 * height, width)] * 3
+        scratch += [pltpu.VMEM(shape, jnp.bfloat16) for shape in shapes]
+    paired = tuple(alone for _, _, alone in totals)
+    slots = 4 * CHUNKS + 10 * len(totals) + 5
     vmem = pl.BlockSpec(memory_space=pltpu.VMEM)
     return pl.pallas_call(
-        functools.partial(leave_kernel, tuple(cuts)),
-        in_specs=[vmem] * (2 + len(totals)),
+        functools.partial(leave_kernel, tuple(cuts), paired),
+        in_specs=[vmem] * (3 + len(totals)),
         out_specs=[pl.BlockSpec(memory_space=pl.ANY)] + [vmem] * (len(outs) - 1),
         out_shape=outs,
         scratch_shapes=[pltpu.VMEM((rows, columns), jnp.bfloat16)] * 5
         + scratch
         + [
+            pltpu.VMEM((9, *gains.shape), jnp.float32),
             pltpu.SemaphoreType.DMA((slots,)),
             pltpu.SemaphoreType.DMA((slots,)),
             pltpu.SemaphoreType.DMA((CHUNKS,)),
@@ -588,25 +658,29 @@
         compiler_params=pltpu.CompilerParams(
             collective_id=1, has_side_effects=True, vmem_limit_bytes=60 * 1024 * 1024
         ),
-        cost_estimate=pl.CostEstimate(flops=0, bytes_accessed=1 << 27, transcendentals=0),
+        cost_estimate=BESIDE,
         name="leave",
-    )(partial.astype(jnp.bfloat16), resid, *[total.astype(jnp.bfloat16) for total, _ in totals])
+    )(partial.astype(jnp.bfloat16), resid, gains, *[total.astype(jnp.bfloat16) for total, _, _ in totals])
 
 
 def enter(tokens, matrices):
     if not small_grid():
         own = turn(tokens)
+        pairs = [
+            (pair_of_weight(jnp.concatenate(shards, axis=1)), whole) for shards, whole in matrices
+        ]
         return [lax.all_gather(own, RANK, axis=0, tiled=True)] + [
-            gather_weight(pieces_of_weight(jnp.concatenate(shards, axis=1))) for shards in matrices
+            gather_weight(pair) if whole else pair for pair, whole in pairs
         ]
     plan, outs = [], [jax.ShapeDtypeStruct((4 * tokens.shape[0], tokens.shape[1]), tokens.dtype)]
-    for shards in matrices:
+    for shards, whole in matrices:
         columns = [0]
         for shard in shards:
             columns.append(columns[-1] + shard.shape[1])
-        plan.append(tuple(columns[:-1]))
-        outs.append(jax.ShapeDtypeStruct((8 * shards[0].shape[0], columns[-1]), tokens.dtype))
-    flat = [shard for shards in matrices for shard in shards]
+        plan.append((tuple(columns[:-1]), whole))
+        height = (8 if whole else 2) * shards[0].shape[0]
+        outs.append(jax.ShapeDtypeStruct((height, columns[-1]), tokens.dtype))
+    flat = [shard for shards, _ in matrices for shard in shards]
     slots = entry_slots(plan)
     anywhere = pl.BlockSpec(memory_space=pl.ANY)
     return pl.pallas_call(
@@ -620,7 +694,7 @@
             pltpu.SemaphoreType.DMA((len(flat) + CHUNKS,)),
         ],
         compiler_params=pltpu.CompilerParams(collective_id=0, has_side_effects=True),
-        cost_estimate=pl.CostEstimate(flops=0, bytes_accessed=1 << 27, transcendentals=0),
+        cost_estimate=BESIDE,
         name="enter",
     )(tokens, *flat)
 
@@ -631,40 +705,39 @@
     mask = 2 * lax.axis_index("core") + lax.axis_index("tl")
     block = (row // own_rows) ^ mask
     block = (block // 2) + 2 * (block % 2)
-    return block * own_rows + row % own_rows
-
-
-def gather_rows(value):
+    size = own_rows // PARTS
+    place = row % own_rows
+    return (place // size) * 4 * size + block * size + place % size
+
+
+def after(token, value):
+    return value if token is None else lax.optimization_barrier((value, token))[0]
+
+
+def start_gather(value):
     if not small_grid():
-        return [lax.all_gather(value, RANK, axis=0, tiled=True)]
-    far = swap(value, "tl")
-    near_peer = swap(value, "core")
-    far_peer = swap(far, "core")
-    return [
-        jnp.concatenate([value, near_peer], axis=0),
-        jnp.concatenate([far, far_peer], axis=0),
-    ]
-
-
-def scatter_rows(pieces, beside=()):
+        return lax.all_gather(value, RANK, axis=0, tiled=True), None
+    return jnp.concatenate([value, swap(value, "core")], axis=0), swap(value, "tl")
+
+
+def forward_rows(rows, token):
+    far = after(token, rows[1])
+    return jnp.concatenate([far, swap(far, "core")], axis=0)
+
+
+def start_scatter(pieces):
     if not small_grid():
-        total = lax.psum_scatter(
-            pieces[0].astype(jnp.bfloat16), RANK, scatter_dimension=0, tiled=True
-        ).astype(jnp.float32)
-        return total, beside
+        return (lax.psum_scatter(pieces[0], RANK, scatter_dimension=0, tiled=True),)
     near, far = pieces
     rows = near.shape[0] // 2
-    far_peer = swap(far[rows:].astype(jnp.bfloat16), "core")
+    far_peer = swap(far[rows:], "core")
     far_sum = (far[:rows].astype(jnp.float32) + far_peer.astype(jnp.float32)).astype(jnp.bfloat16)
-    from_far = swap(far_sum, "tl")
-    near_peer = swap(near[rows:].astype(jnp.bfloat16), "core")
-    from_far, beside = lax.optimization_barrier((from_far, beside))
-    total = (
-        near[:rows].astype(jnp.float32)
-        + near_peer.astype(jnp.float32)
-        + from_far.astype(jnp.float32)
-    )
-    return total, beside
+    return near[:rows], swap(near[rows:], "core"), swap(far_sum, "tl")
+
+
+def finish_scatter_rows(terms, token):
+    terms = [*terms[:-1], after(token, terms[-1])]
+    return sum(term.astype(jnp.float32) for term in terms)
 
 
 def sum_over(value, axes):
@@ -763,9 +836,7 @@
         ],
         out_specs=[out] * 3,
         out_shape=[jax.ShapeDtypeStruct((rows, width), jnp.bfloat16)] * 3,
-        cost_estimate=pl.CostEstimate(
-            flops=rows * width * 20, bytes_accessed=rows * width * 20, transcendentals=0
-        ),
+        cost_estimate=BESIDE,
         name="prepare",
     )(raw, squares, gain_q[None], gain_k[None], cosine, sine)
 
@@ -829,9 +900,7 @@
             jax.ShapeDtypeStruct((heads, 1, rows), jnp.float32),
         ],
         compiler_params=pltpu.CompilerParams(vmem_limit_bytes=VMEM_BYTES),
-        cost_estimate=pl.CostEstimate(
-            flops=heads * rows * rows * HDIM, bytes_accessed=rows * width * 12, transcendentals=heads * rows * rows // 4
-        ),
+        cost_estimate=BESIDE,
         name="attention_forward",
     )(low_block, q_b, k_b, v_b, starts)
 
@@ -902,9 +971,7 @@
         ),
         out_shape=[out] * 3,
         compiler_params=pltpu.CompilerParams(vmem_limit_bytes=VMEM_BYTES),
-        cost_estimate=pl.CostEstimate(
-            flops=heads * rows * rows * HDIM * 3, bytes_accessed=rows * width * 24, transcendentals=heads * rows * rows // 4
-        ),
+        cost_estimate=BESIDE,
         name="attention_backward",
     )(high_block, q_b, k_b, v_b, grads, full, logs, starts)
 
@@ -967,9 +1034,7 @@
             jax.ShapeDtypeStruct((8, width), jnp.float32),
             jax.ShapeDtypeStruct((8, width), jnp.float32),
         ],
-        cost_estimate=pl.CostEstimate(
-            flops=rows * width * 30, bytes_accessed=rows * width * 32, transcendentals=0
-        ),
+        cost_estimate=BESIDE,
         name="norm_grads",
     )(d_q_rot, d_k_rot, raw, squares, gain_q[None], gain_k[None], cosine, sine)
 
@@ -1000,9 +1065,7 @@
         in_specs=[own, own, own, wide, pair, pair, whole, whole],
         out_specs=wide,
         out_shape=jax.ShapeDtypeStruct((rows, 3 * width), jnp.bfloat16),
-        cost_estimate=pl.CostEstimate(
-            flops=rows * width * 20, bytes_accessed=rows * width * 30, transcendentals=0
-        ),
+        cost_estimate=BESIDE,
         name="raw_grads",
     )(d_q_norm, d_k_norm, d_v, raw, squares, dots, gain_q[None], gain_k[None])
 
@@ -1021,6 +1084,232 @@
     return lax.dot_general(
         left, right, (((1,), (1,)), ((), ())), preferred_element_type=jnp.float32
     )
+
+
+def column_block(rows, width):
+    return min(width, 512 if rows <= 1024 else 256)
+
+
+def matmul_params():
+    return pltpu.CompilerParams(vmem_limit_bytes=56 * 1024 * 1024)
+
+
+def hidden_kernel(x_ref, gate_w, up_w, gate_out, up_out, hidden_out):
+    gate = dot(x_ref[...], gate_w[...])
+    up_part = dot(x_ref[...], up_w[...])
+    gate_out[...] = gate
+    up_out[...] = up_part
+    hidden_out[...] = (gate * jax.nn.sigmoid(gate) * up_part).astype(jnp.bfloat16)
+
+
+def hidden_units(x, gate_full, up_full):
+    rows, depth = x.shape
+    width = gate_full.shape[1]
+    block = column_block(rows, width)
+    weight = pl.BlockSpec((depth, block), lambda j: (0, j))
+    out = pl.BlockSpec((rows, block), lambda j: (0, j))
+    return pl.pallas_call(
+        hidden_kernel,
+        grid=(width // block,),
+        in_specs=[pl.BlockSpec((rows, depth), lambda j: (0, 0)), weight, weight],
+        out_specs=[out] * 3,
+        out_shape=[
+            jax.ShapeDtypeStruct((rows, width), jnp.float32),
+            jax.ShapeDtypeStruct((rows, width), jnp.float32),
+            jax.ShapeDtypeStruct((rows, width), jnp.bfloat16),
+        ],
+        compiler_params=matmul_params(),
+        cost_estimate=BESIDE,
+        name="hidden_units",
+    )(x, gate_full, up_full)
+
+
+def hidden_grads_kernel(grad_ref, weight, gate_ref, up_ref, gate_out, up_out):
+    d_hidden = dot(grad_ref[...], weight[...])
+    gate = gate_ref[...]
+    gate_sigmoid = jax.nn.sigmoid(gate)
+    silu = gate * gate_sigmoid
+    gate_out[...] = (
+        d_hidden * up_ref[...] * (gate_sigmoid * (1.0 + gate * (1.0 - gate_sigmoid)))
+    ).astype(jnp.bfloat16)
+    up_out[...] = (d_hidden * silu).astype(jnp.bfloat16)
+
+
+def hidden_grads(grad, down_full, gate, up_part):
+    rows, depth = grad.shape
+    width = down_full.shape[1]
+    block = column_block(rows, width)
+    part_spec = pl.BlockSpec((rows, block), lambda j: (0, j))
+    out = jax.ShapeDtypeStruct((rows, width), jnp.bfloat16)
+    return pl.pallas_call(
+        hidden_grads_kernel,
+        grid=(width // block,),
+        in_specs=[
+            pl.BlockSpec((rows, depth), lambda j: (0, 0)),
+            pl.BlockSpec((depth, block), lambda j: (0, j)),
+            part_spec,
+            part_spec,
+        ],
+        out_specs=[part_spec] * 2,
+        out_shape=[out] * 2,
+        compiler_params=matmul_params(),
+        cost_estimate=BESIDE,
+        name="hidden_grads",
+    )(grad, down_full, gate, up_part)
+
+
+def products_kernel(count, *refs):
+    total = None
+    for left, right in zip(refs[:count], refs[count : 2 * count]):
+        term = contract_cols(left[...], right[...])
+        total = term if total is None else total + term
+    refs[-1][...] = total.astype(jnp.bfloat16)
+
+
+def sum_products(lefts, rights):
+    rows, depth = lefts[0].shape
+    width = rights[0].shape[0]
+    block = column_block(rows, width)
+    return pl.pallas_call(
+        functools.partial(products_kernel, len(lefts)),
+        grid=(width // block,),
+        in_specs=[pl.BlockSpec((rows, depth), lambda j: (0, 0)) for _ in lefts]
+        + [pl.BlockSpec((block, depth), lambda j: (j, 0)) for _ in rights],
+        out_specs=pl.BlockSpec((rows, block), lambda j: (0, j)),
+        out_shape=jax.ShapeDtypeStruct((rows, width), jnp.bfloat16),
+        compiler_params=matmul_params(),
+        cost_estimate=BESIDE,
+        name="sum_products",
+    )(*lefts, *rights)
+
+
+def weight_grad_kernel(count, *refs):
+    total = None
+    for left, right in zip(refs[:count], refs[count : 2 * count]):
+        term = contract_rows(left[...], right[...])
+        total = term if total is None else total + term
+    refs[-1][...] = total.astype(jnp.bfloat16)
+
+
+def weight_grad(lefts, rights, first=0, width=None):
+    height, width = lefts[0].shape[1], rights[0].shape[1] if width is None else width
+    tall, wide = min(height, 512), min(width, 1024)
+    blocks = width // wide
+    return pl.pallas_call(
+        functools.partial(weight_grad_kernel, len(lefts)),
+        grid=(width // wide, height // tall),
+        in_specs=[pl.BlockSpec((left.shape[0], tall), lambda j, i: (0, i)) for left in lefts]
+        + [pl.BlockSpec((right.shape[0], wide), lambda j, i: (0, first * blocks + j)) for right in rights],
+        out_specs=pl.BlockSpec((tall, wide), lambda j, i: (i, j)),
+        out_shape=jax.ShapeDtypeStruct((height, width), jnp.bfloat16),
+        compiler_params=matmul_params(),
+        cost_estimate=BESIDE,
+        name="weight_grad",
+    )(*lefts, *rights)
+
+
+def move_rows(places, wanted_first, count, rows_ref):
+    wanted = wanted_first + lax.broadcasted_iota(jnp.int32, (count, places.shape[1]), 0)
+    chosen = jnp.where(places == wanted, 1.0, 0.0).astype(jnp.bfloat16)
+    return dot(chosen, rows_ref[...]).astype(jnp.bfloat16)
+
+
+def pick_rows(places, rows_ref):
+    columns = lax.broadcasted_iota(jnp.int32, (places.shape[0], rows_ref.shape[0]), 1)
+    chosen = jnp.where(places == columns, 1.0, 0.0).astype(jnp.bfloat16)
+    return dot(chosen, rows_ref[...]).astype(jnp.bfloat16)
+
+
+def pack_kernel(places, tokens_ref, weight, packed_out, raw_out, squares_out):
+    packed = pick_rows(places[...], tokens_ref)
+    packed_out[...] = packed
+    raw = dot(packed, weight[...])
+    raw_out[...] = raw
+    width = raw.shape[1] // 3
+    for index in range(2):
+        cols = raw[:, index * width : (index + 1) * width]
+        squares_out[index : index + 1, :] = row_sums(cols * cols)
+
+
+def pack(perm_row, tokens_all, qkv_full):
+    rows, depth = tokens_all.shape
+    width = qkv_full.shape[1]
+    return pl.pallas_call(
+        pack_kernel,
+        grid=(rows // BLOCK,),
+        in_specs=[
+            pl.BlockSpec((BLOCK, 1), lambda i: (i, 0)),
+            pl.BlockSpec((rows, depth), lambda i: (0, 0)),
+            pl.BlockSpec((depth, width), lambda i: (0, 0)),
+        ],
+        out_specs=[
+            pl.BlockSpec((BLOCK, depth), lambda i: (i, 0)),
+            pl.BlockSpec((BLOCK, width), lambda i: (i, 0)),
+            pl.BlockSpec((2, BLOCK), lambda i: (0, i)),
+        ],
+        out_shape=[
+            jax.ShapeDtypeStruct((rows, depth), jnp.bfloat16),
+            jax.ShapeDtypeStruct((rows, width), jnp.float32),
+            jax.ShapeDtypeStruct((2, rows), jnp.float32),
+        ],
+        compiler_params=matmul_params(),
+        cost_estimate=BESIDE,
+        name="pack",
+    )(perm_row[:, None], tokens_all, qkv_full)
+
+
+def given_kernel(count, places, rows_ref, weight, moved_out, product_out):
+    moved = move_rows(places[...], pl.program_id(0) * count, count, rows_ref)
+    moved_out[...] = moved
+    product_out[...] = contract_cols(moved, weight[...]).astype(jnp.bfloat16)
+
+
+def give_back(place_row, value, weight):
+    rows, depth = value.shape
+    width = weight.shape[0]
+    count = 512
+    return pl.pallas_call(
+        functools.partial(given_kernel, count),
+        grid=(rows // count,),
+        in_specs=[
+            pl.BlockSpec((1, rows), lambda i: (0, 0)),
+            pl.BlockSpec((rows, depth), lambda i: (0, 0)),
+            pl.BlockSpec((width, depth), lambda i: (0, 0)),
+        ],
+        out_specs=[
+            pl.BlockSpec((count, depth), lambda i: (i, 0)),
+            pl.BlockSpec((count, width), lambda i: (i, 0)),
+        ],
+        out_shape=[
+            jax.ShapeDtypeStruct((rows, depth), jnp.bfloat16),
+            jax.ShapeDtypeStruct((rows, width), jnp.bfloat16),
+        ],
+        compiler_params=matmul_params(),
+        cost_estimate=BESIDE,
+        name="give_back",
+    )(place_row[None], value, weight)
+
+
+def pick_kernel(places, rows_ref, out):
+    out[...] = pick_rows(places[...], rows_ref)
+
+
+def pick(place_row, value):
+    rows, depth = value.shape
+    count = 512
+    return pl.pallas_call(
+        pick_kernel,
+        grid=(rows // count,),
+        in_specs=[
+            pl.BlockSpec((count, 1), lambda i: (i, 0)),
+            pl.BlockSpec((rows, depth), lambda i: (0, 0)),
+        ],
+        out_specs=pl.BlockSpec((count, depth), lambda i: (i, 0)),
+        out_shape=jax.ShapeDtypeStruct((rows, depth), jnp.bfloat16),
+        compiler_params=matmul_params(),
+        cost_estimate=BESIDE,
+        name="pick",
+    )(place_row[:, None], value)
 
 
 def rms_back(values, rstd, gain_vec, grad):
@@ -1052,20 +1341,20 @@
     local_width = w_query.shape[1]
 
     own_group = lax.axis_index("core") == lax.axis_index("th")
-    length_row = jnp.where(own_group, lengths, swap(lengths, "core"))[0]
-    perm_row = jnp.where(own_group, permutation, swap(permutation, "core"))[0]
-
-    tokens_all, qkv_full, out_full, gate_full = enter(
-        tokens, [(w_query, w_key, w_value), (w_out.T,), (w_gate,)]
+    layout_row = jnp.concatenate([permutation, lengths], axis=1)
+    layout_row = jnp.where(own_group, layout_row, swap(layout_row, "core"))[0]
+    perm_row, length_row = layout_row[:group_rows], layout_row[group_rows:]
+
+    tokens_all, qkv_full, out_full, gate_pair = enter(
+        tokens,
+        [((w_query, w_key, w_value), True), ((w_out.T,), True), ((w_gate,), False)],
     )
-    (up_shard, down_shard), tokens_all = lax.optimization_barrier(((w_up, w_down.T), tokens_all))
-    up_pieces, down_pieces = pieces_of_weight(up_shard), pieces_of_weight(down_shard)
+    gate_full = gather_weight(gate_pair)
+    up_shard, tokens_all = lax.optimization_barrier((w_up, tokens_all))
+    up_pair = pair_of_weight(up_shard)
     tokens = lax.dynamic_slice_in_dim(tokens_all, rank * own_rows, own_rows)
-    upstream = turn(upstream)
 
     perm_place = row_place(perm_row, own_rows)
-    slots = jnp.arange(group_rows, dtype=jnp.int32)
-    inverse = jnp.zeros((group_rows,), jnp.int32).at[perm_place].set(slots)
     position, starts = layout(length_row, group_rows)
     cosine, sine = rotary_tables(position)
     blocks = group_rows // BLOCK
@@ -1074,132 +1363,219 @@
     reached = jnp.sum((starts[None, :] <= last_keys[:, None]).astype(jnp.int32), axis=1)
     high_block = (reached - 1) // BLOCK
 
-    packed = tokens_all[perm_row]
-    raw = dot(packed, qkv_full)
-    up_pieces, raw = lax.optimization_barrier((up_pieces, raw))
-    up_full = gather_weight(up_pieces)
-    q_raw = raw[:, :local_width]
-    k_raw = raw[:, local_width : 2 * local_width]
-    squares = sum_over(
-        jnp.stack([jnp.sum(q_raw * q_raw, axis=1), jnp.sum(k_raw * k_raw, axis=1)]), RANK
-    )
+    packed, raw, squares = pack(perm_row, tokens_all, qkv_full)
+    up_pair, raw = lax.optimization_barrier((up_pair, raw))
+    up_full = gather_weight(up_pair)
+    squares = sum_over(squares, RANK)
+    down_shard, squares = lax.optimization_barrier((w_down.T, squares))
+    down_pair = pair_of_weight(down_shard)
     gain_q = lax.dynamic_slice_in_dim(q_gain, rank * local_width, local_width)
     gain_k = lax.dynamic_slice_in_dim(k_gain, rank * local_width, local_width)
     q_b, k_b, v_b = prepare(raw, squares, gain_q, gain_k, cosine, sine)
     attn_b, attn_f, logs = attention_forward(q_b, k_b, v_b, starts[None], low_block)
-    down_pieces, attn_b = lax.optimization_barrier((down_pieces, attn_b))
-    down_full = gather_weight(down_pieces)
-    attn_given = attn_b[inverse]
-
-    def pieces_of(value):
-        if not small_grid():
-            return [value]
-        return [part(value, 0, 0, 2), part(value, 0, 1, 2)]
-
-    attn_out, _ = scatter_rows(
-        [contract_cols(piece, out_full) for piece in pieces_of(attn_given)]
+
+    parts = PARTS if small_grid() else 1
+    part_rows = own_rows // parts
+
+    def part_of(value, index):
+        return part(value, 0, index, parts)
+
+    def pieces_of(value, index):
+        whole = part_of(value, index)
+        return [part(whole, 0, 0, 2), part(whole, 0, 1, 2)] if small_grid() else [whole]
+
+    sides = 2 if small_grid() else 1
+    attn_given, attn_parts = give_back(perm_place, attn_b, out_full)
+    down_pair, attn_parts = lax.optimization_barrier((down_pair, attn_parts))
+    down_full = gather_weight(down_pair)
+    order = [(side, index) for side in range(sides) for index in range(parts)]
+    token = None
+
+    def pass_through(make_rows, begin, finish, late, between=None):
+        nonlocal token
+        gathered, far_pieces, begun, sums, scattered = {}, {}, {}, {}, []
+
+        def complete(side, index):
+            nonlocal token
+            sums[side, index] = finish(*begun[side, index], token)
+            token = sums[side, index]
+
+        def scatter(index):
+            scattered.append(start_scatter([sums[side, index] for side in range(sides)]))
+
+        for side, index in order:
+            if side == 0:
+                gathered[index] = start_gather(make_rows(index, token))
+                if sides == 2 and index > 0:
+                    far_pieces[index - 1] = forward_rows(gathered[index - 1], token)
+                piece = gathered[index][0]
+            else:
+                if index == 0:
+                    far_pieces[parts - 1] = forward_rows(gathered[parts - 1], token)
+                    if between is not None:
+                        near = [gathered[each][0] for each in range(parts)]
+                        token = between(near, [far_pieces[each] for each in range(parts)], token)
+                piece = far_pieces[index]
+            begun[side, index] = begin((index, side), piece, token)
+            token = begun[side, index][0]
+            if not late:
+                complete(side, index)
+                if side == sides - 1:
+                    scatter(index)
+        if late:
+            for index in range(parts):
+                for side in reversed(range(sides)):
+                    complete(side, index)
+                scatter(index)
+        return scattered
+
+    attn_sums = [start_scatter(pieces_of(attn_parts, index)) for index in range(parts)]
+    attn_outs, resids, saved = [], [], {}
+
+    def resid_rows(index, token):
+        attn_out = finish_scatter_rows(attn_sums[index], token)
+        rstd_a = lax.rsqrt(jnp.mean(attn_out * attn_out, axis=1, keepdims=True) + epsilon)
+        attn_outs.append((attn_out, rstd_a))
+        resids.append(part_of(tokens, index).astype(jnp.float32) + attn_out * rstd_a * attn_gain)
+        return resids[-1].astype(jnp.bfloat16)
+
+    def feed_forward(key, piece, token):
+        gate, up_part, hidden_b = hidden_units(after(token, piece), gate_full, up_full)
+        saved[key] = (piece, gate, up_part, hidden_b)
+        return (hidden_b,)
+
+    def feed_down(hidden_b, token):
+        return sum_products([after(token, hidden_b)], [down_full])
+
+    upstream_turn = start_turn(after(attn_parts, upstream))
+    mlp_sums = pass_through(resid_rows, feed_forward, feed_down, True)
+    token, upstream_turn = lax.optimization_barrier((token, upstream_turn))
+    upstream = finish_turn(*upstream_turn)
+    layer_outs, gain_parts, grads_f, back = [], [], [], {}
+
+    def d_mlp_rows(index, token):
+        mlp_out = finish_scatter_rows(mlp_sums[index], token)
+        rstd_m = lax.rsqrt(jnp.mean(mlp_out * mlp_out, axis=1, keepdims=True) + epsilon)
+        normed_m = mlp_out * rstd_m
+        layer_outs.append((resids[index] + normed_m * ffn_gain).astype(jnp.bfloat16))
+        grads_f.append(part_of(upstream, index).astype(jnp.float32))
+        gain_parts.append(jnp.sum(grads_f[index] * normed_m, axis=0))
+        return rms_back(mlp_out, rstd_m, ffn_gain, grads_f[index]).astype(jnp.bfloat16)
+
+    def feed_back(key, piece, token):
+        _, gate, up_part, _ = saved[key]
+        d_gate_b, d_up_b = hidden_grads(after(token, piece), down_full, gate, up_part)
+        back[key] = (piece, d_gate_b, d_up_b)
+        return d_gate_b, d_up_b
+
+    def feed_up(d_gate_b, d_up_b, token):
+        return sum_products([after(token, d_gate_b), d_up_b], [gate_full, up_full])
+
+    weight_grads = []
+
+    def first_weight_grad(near, far, token):
+        grads = [piece for index in range(parts) for piece in (near[index], far[index])]
+        weight_grads.append(weight_grad(after(token, grads), [saved[key][3] for key in sorted(saved)]))
+        return weight_grads[0]
+
+    resid_sums = pass_through(d_mlp_rows, feed_back, feed_up, False, first_weight_grad)
+    layer_out = jnp.concatenate(layer_outs, axis=0)
+    keys = sorted(saved)
+    ffn_gain_part = sum(gain_parts)
+    attn_gain_part = 0.0
+    d_resids, gathered = [], []
+    operands = [
+        ([back[key][0] for key in keys], [saved[key][3] for key in keys]),
+        ([saved[key][0] for key in keys], [back[key][1] for key in keys]),
+        ([saved[key][0] for key in keys], [back[key][2] for key in keys]),
+    ]
+
+    def next_weight_grad(token):
+        left, right = operands[len(weight_grads)]
+        left, right = after(token, (left, right))
+        weight_grads.append(weight_grad(left, right))
+        return weight_grads[-1]
+
+    for index in range(parts):
+        terms = resid_sums[index]
+        if index == 0:
+            d_sums = finish_scatter_rows(terms, token)
+        else:
+            last, weight_grads[-1] = lax.optimization_barrier((terms[-1], weight_grads[-1]))
+            d_sums = finish_scatter_rows([*terms[:-1], last], None)
+        attn_out, rstd_a = attn_outs[index]
+        d_resid = grads_f[index] + d_sums
+        d_resids.append(d_resid)
+        attn_gain_part = attn_gain_part + jnp.sum(d_resid * attn_out * rstd_a, axis=0)
+        d_attn_b = rms_back(attn_out, rstd_a, attn_gain, d_resid).astype(jnp.bfloat16)
+        gathered.append(start_gather(d_attn_b))
+        token = next_weight_grad((d_attn_b, token))
+    far_pieces = []
+    for index in range(parts):
+        if sides == 2:
+            far, weight_grads[-1] = lax.optimization_barrier((gathered[index][1], weight_grads[-1]))
+            far_pieces.append(jnp.concatenate([far, swap(far, "core")], axis=0))
+            token = far
+        if len(weight_grads) < 3:
+            token = next_weight_grad(token)
+    while len(weight_grads) < 3:
+        token = next_weight_grad(token)
+    down_grad, gate_grad, up_grad = weight_grads
+    d_attn_pieces = []
+    for index in range(parts):
+        d_attn_pieces.append(gathered[index][0])
+        if sides == 2:
+            d_attn_pieces.append(far_pieces[index])
+    d_givens = [dot(piece, out_full).astype(jnp.bfloat16) for piece in d_attn_pieces]
+    d_resid = jnp.concatenate(d_resids, axis=0)
+    d_given_b = jnp.concatenate(d_givens, axis=0)
+    out_total = weight_grad(
+        d_attn_pieces,
+        [piece for index in range(parts) for piece in pieces_of(attn_given, index)],
     )
-    rstd_a = lax.rsqrt(jnp.mean(attn_out * attn_out, axis=1, keepdims=True) + epsilon)
-    resid = tokens.astype(jnp.float32) + attn_out * rstd_a * attn_gain
-    resid_pieces = gather_rows(resid.astype(jnp.bfloat16))
-    gates, ups, hiddens, sums = [], [], [], []
-    for index in range(len(resid_pieces)):
-        piece = resid_pieces[index]
-        gate = dot(piece, gate_full)
-        up_part = dot(piece, up_full)
-        hidden_b = (gate * jax.nn.sigmoid(gate) * up_part).astype(jnp.bfloat16)
-        gates.append(gate)
-        ups.append(up_part)
-        hiddens.append(hidden_b)
-        sums.append(contract_cols(hidden_b, down_full).astype(jnp.bfloat16))
-        if index + 1 < len(resid_pieces):
-            resid_pieces[index + 1], gates[-1], ups[-1], hiddens[-1] = lax.optimization_barrier(
-                (resid_pieces[index + 1], gates[-1], ups[-1], hiddens[-1])
-            )
-    mlp_out, _ = scatter_rows(sums)
-    rstd_m = lax.rsqrt(jnp.mean(mlp_out * mlp_out, axis=1, keepdims=True) + epsilon)
-    normed_m = mlp_out * rstd_m
-    layer_out = turn((resid + normed_m * ffn_gain).astype(jnp.bfloat16))
-
-    grad_f = upstream.astype(jnp.float32)
-    ffn_gain_part = jnp.sum(grad_f * normed_m, axis=0)
-    d_mlp_b = rms_back(mlp_out, rstd_m, ffn_gain, grad_f).astype(jnp.bfloat16)
-    d_mlp_pieces = gather_rows(d_mlp_b)
-    d_gates, d_ups, sums = [], [], []
-    for index in range(len(d_mlp_pieces)):
-        gate, up_part, d_mlp = gates[index], ups[index], d_mlp_pieces[index]
-        gate_sigmoid = jax.nn.sigmoid(gate)
-        d_hidden = dot(d_mlp, down_full)
-        d_gate_b = (
-            d_hidden * up_part * gate_sigmoid * (1.0 + gate * (1.0 - gate_sigmoid))
-        ).astype(jnp.bfloat16)
-        d_up_b = (d_hidden * gate * gate_sigmoid).astype(jnp.bfloat16)
-        d_gates.append(d_gate_b)
-        d_ups.append(d_up_b)
-        sums.append(
-            (contract_cols(d_gate_b, gate_full) + contract_cols(d_up_b, up_full)).astype(
-                jnp.bfloat16
-            )
-        )
-        if index + 1 < len(d_mlp_pieces):
-            d_mlp_pieces[index + 1], d_gates[-1], d_ups[-1], sums[-1] = lax.optimization_barrier(
-                (d_mlp_pieces[index + 1], d_gates[-1], d_ups[-1], sums[-1])
-            )
-
-    def rows(pieces):
-        return jnp.concatenate(pieces, axis=0)
-
-    down_grad = contract_rows(rows(d_mlp_pieces), rows(hiddens)).astype(jnp.bfloat16)
-    gate_grad = contract_rows(rows(resid_pieces), rows(d_gates)).astype(jnp.bfloat16)
-    d_sums, (down_grad, gate_grad) = scatter_rows(sums, (down_grad, gate_grad))
-    d_resid = grad_f + d_sums
-    up_grad = contract_rows(rows(resid_pieces), rows(d_ups)).astype(jnp.bfloat16)
-
-    attn_gain_part = jnp.sum(d_resid * attn_out * rstd_a, axis=0)
-    d_attn_b = rms_back(attn_out, rstd_a, attn_gain, d_resid).astype(jnp.bfloat16)
-    d_attn_pieces = gather_rows(d_attn_b)
-    d_attn_pieces[-1], up_grad = lax.optimization_barrier((d_attn_pieces[-1], up_grad))
-    down_shard = scatter_weight(down_grad).T
-    gate_shard = scatter_weight(gate_grad)
-    up_shard = scatter_weight(up_grad)
-    d_attn_all = rows(d_attn_pieces)
-    d_given_b = rows([dot(piece, out_full).astype(jnp.bfloat16) for piece in d_attn_pieces])
-    d_packed = d_given_b[perm_place]
+    d_given_b, out_total = lax.optimization_barrier((d_given_b, out_total))
+    down_split, gate_split = start_split(scatter_pair(down_grad)), start_split(scatter_pair(gate_grad))
+    up_sum = scatter_pair(up_grad)
+    d_packed = pick(perm_place, d_given_b)
     d_q_rot, d_k_rot, d_v = attention_backward(
         q_b, k_b, v_b, d_packed, attn_f, logs, starts[None], high_block
     )
+    d_q_rot, down_split, gate_split = lax.optimization_barrier((d_q_rot, down_split, gate_split))
     d_q_norm, d_k_norm, dots, q_parts, k_parts = norm_grads(
         d_q_rot, d_k_rot, raw, squares, gain_q, gain_k, cosine, sine
     )
+    up_split = start_split(after(d_q_norm, up_sum))
+    layer_turn = start_turn(after(d_q_norm, layer_out))
     q_gain_part, k_gain_part = jnp.sum(q_parts, axis=0), jnp.sum(k_parts, axis=0)
     dots = sum_over(dots, RANK)
     d_qkv_b = raw_grads(d_q_norm, d_k_norm, d_v, raw, squares, dots, gain_q, gain_k)
-    d_qkv_given = d_qkv_b[inverse]
-    tokens_grad, query_shard, key_shard, value_shard, out_shard = leave(
-        contract_cols(d_qkv_given, qkv_full),
-        d_resid,
-        [
-            (contract_rows(packed, d_qkv_b), [local_width] * 3),
-            (contract_rows(d_attn_all, attn_given), [local_width]),
-        ],
-    )
+    qkv_totals = [weight_grad([packed], [d_qkv_b], index, local_width) for index in range(3)]
+    last_total, d_qkv_b = lax.optimization_barrier((qkv_totals[-1], d_qkv_b))
+    _, input_parts = give_back(perm_place, d_qkv_b, qkv_full)
+    input_parts, up_split, layer_turn = lax.optimization_barrier((input_parts, up_split, layer_turn))
+    layer_out = finish_turn(*layer_turn)
+    down_shard = finish_split(*down_split).T
+    gate_shard, up_shard = finish_split(*gate_split), finish_split(*up_split)
 
     def placed(part_sum):
         return lax.dynamic_update_slice_in_dim(
             jnp.zeros((D,), jnp.float32), part_sum, rank * local_width, 0
         )
 
-    gain_grads = sum_over(
-        jnp.stack(
-            [
-                placed(q_gain_part),
-                placed(k_gain_part),
-                attn_gain_part,
-                ffn_gain_part,
-            ]
-        ),
-        DP + TENSOR,
+    gains = jnp.stack(
+        [placed(q_gain_part), placed(k_gain_part), attn_gain_part, ffn_gain_part]
+        + [jnp.zeros((D,), jnp.float32)] * 4
     )
+    tokens_grad, gain_grads, out_shard, query_shard, key_shard, value_shard = leave(
+        input_parts,
+        d_resid,
+        gains,
+        [
+            (out_total, [local_width], False),
+            *[(total, [local_width], False) for total in qkv_totals],
+        ],
+    )
+
     return (
         layer_out,
         tokens_grad,

time: 1450 us -> 1210 us (0.83)
  Pallas kernels: 471 us -> 853 us
  matrix products: 323 us -> 7.86 us
  waiting for transfers between devices: 321 us -> 113 us
  starting transfers between devices: 121 us -> 52.5 us
  local copies, waits for them, and re-layouts: 102 us -> 54.6 us
    pallas_call x1 -> x28, Pallas kernels: 131 us -> 575 us  [the longest x1 171 us: leave(): pl.pallas_call(functools.partial(leave_kernel, tuple(cuts), paired), in_s...]
    dot_general x14 -> x0, matrix products: 206 us -> none  [the longest x9 106 us: contract_cols(): lax.dot_general(left, right, (((1,), (1,)), ((), ())), preferred_element_...]
    ppermute x29 -> x41, waiting for transfers between devices: 259 us -> 101 us  [swap(): return lax.ppermute(value, axis, SWAP)]
    dot_general x9 -> x4, matrix products: 117 us -> 7.86 us  [dot(): return jnp.dot(left, right, preferred_element_type=jnp.float32)]
    ppermute x12, starting transfers between devices: 86.9 us -> 16.5 us  [the longest x7 10.9 us: start_turn(): return (value, lax.ppermute(value, ('core', 'th'), TURN))]
    pallas_call x1, Pallas kernels: 202 us -> 137 us  [enter(): pl.pallas_call(functools.partial(entry_kernel, tuple(plan)), in_specs=[an...]
    gather x4 -> x0, local copies, waits for them, and re-layouts: 58.1 us -> none  [the longest x1 20.8 us: per_device(): packed = tokens_all[perm_row]]
    ppermute x12, waiting for transfers between devices: 60.7 us -> 9.41 us  [the longest x3 9.39 us: start_split(): lax.ppermute(second, ('core', 'th'), CYCLE_BACK)]
  transfers between devices with their start and end apart: 46 -> 59, of which waited for: 15 -> 16; matrix products, arithmetic and copies ran while one was open for 29% -> 11% of each run, Pallas kernels for 33% -> 43%
where the time goes in v3:
time: 1210 us; the launch traced here: 1200 us
  Pallas kernels  853 us (70%)
  waiting for transfers between devices  113 us (9%)
  other arithmetic  101 us (8%)
  local copies, waits for them, and re-layouts  54.6 us (5%)
  starting transfers between devices  52.5 us (4%)
  between operations  17.2 us (1%)
    pallas_call x1, Pallas kernels, leave(): pl.pallas_call(functools.partial(leave_kernel, tuple(cuts), paired), in_s...  171 us
    pallas_call x1, Pallas kernels, enter(): pl.pallas_call(functools.partial(entry_kernel, tuple(plan)), in_specs=[an...  137 us
    pallas_call x7, Pallas kernels, weight_grad(): pl.pallas_call(functools.partial(weight_grad_kernel, len(lefts)), grid=(w...  108 us
    ppermute x41, waiting for transfers between devices, swap(): return lax.ppermute(value, axis, SWAP)  101 us
    pallas_call x8, Pallas kernels, sum_products(): pl.pallas_call(functools.partial(products_kernel, len(lefts)), grid=(widt...  91.3 us
    pallas_call x1, Pallas kernels, attention_backward(): pl.pallas_call(backward_kernel, grid_spec=pltpu.PrefetchScalarGridSpec(nu...  62.3 us
    pallas_call x4, Pallas kernels, hidden_units(): pl.pallas_call(hidden_kernel, grid=(width // block,), in_specs=[pl.BlockS...  57.4 us
    pallas_call x4, Pallas kernels, hidden_grads(): pl.pallas_call(hidden_grads_kernel, grid=(width // block,), in_specs=[pl....  47.5 us
  transfers between devices with their start and end apart: 59, of which 16 were waited for; matrix products, arithmetic and copies ran while one was open for 11% of the time, Pallas kernels for 43%

profile of v3, /device:TPU:0, one launch (start us, length us, event | category | flops | bytes accessed | tf_op | source)
XLA Modules:
  0.0 1198.2 jit_solution(3608792594427734827)
XLA Ops:
  9.0 136.7 %enter.1 = (bf16[2048,2048]{1,0:T(8,128)(2,1)}, bf16[2048,1536]{1,0:T(8,128)(2,1)}, bf16[2048,512]{1,0:T(8,128)(2,1)}, bf16[512,2048]{1,0:T(8,128)(2,1)}) custom-call(bf16[512,2048]{1,0:T(8,128)(2,1)} %refs_0_.1, bf16[256,512]{1,0:T(8,128)(2,1)} %refs_1_.1, bf16[256,512]{1,0:T(8,128)(2,1)} %refs_2_.1, bf16[256,512]{1,0:T(8,128)(2,1)} %refs_3_.1, ...), custom_call_target="tpu_custom_call" | custom-call | flops 1 | bytes 1 | tf_op jit(solution)/shard_map/enter/pallas_call | solution.py:686
  146.5 5.4 collective-permute-start
  154.9 44.9 %pack.1 = (bf16[2048,2048]{1,0:T(8,128)(2,1)}, f32[2048,1536]{1,0:T(8,128)}, f32[2,2048]{1,0:T(2,128)}) custom-call(s32[2048,1]{1,0:T(8,128)} %copy.51.places, bf16[2048,2048]{1,0:T(8,128)(2,1)} %get-tuple-element.143.tokens_ref, bf16[2048,1536]{1,0:T(8,128)(2,1)} %get-tuple-element.144.weight), custom_call_target="tpu_custom_call" | custom-call | flops 1 | bytes 1 | tf_op jit(solution)/shard_map/pack/pallas_call | solution.py:1237
  212.7 4.1 collective-permute-start.4
  221.2 3.7 fusion.31
  227.6 11.8 prepare.1
  241.0 39.7 %attention_forward.1 = (bf16[2048,512]{1,0:T(8,128)(2,1)S(1)}, f32[2048,512]{1,0:T(8,128)}, f32[4,1,2048]{2,1,0:T(1,128)S(1)}) custom-call(s32[8]{0:T(128)S(1)} %and_select_fusion.8.low_ref, bf16[2048,512]{1,0:T(8,128)(2,1)S(1)} %copy-done, bf16[2048,512]{1,0:T(8,128)(2,1)} %get-tuple-element.152.k_ref, bf16[2048,512]{1,0:T(8,128)(2,1)} %get-tuple-element.153.v_ref, ...), custom_call_target="tpu_custom_call" | custom-call | flops 1 | bytes 1 | tf_op jit(solution)/shard_map/attention_forward/pallas_call | solution.py:889
  282.0 13.9 %give_back.2 = (bf16[2048,512]{1,0:T(8,128)(2,1)}, bf16[2048,2048]{1,0:T(8,128)(2,1)}) custom-call(s32[1,2048]{1,0:T(1,128)} %get-tuple-element.371.places, bf16[2048,512]{1,0:T(8,128)(2,1)} %copy-done.3, bf16[2048,512]{1,0:T(8,128)(2,1)} %get-tuple-element.156.weight), custom_call_target="tpu_custom_call" | custom-call | flops 1 | bytes 1 | tf_op jit(solution)/shard_map/give_back/pallas_call | solution.py:1271
  297.9 3.6 fusion.37
  308.3 23.7 %collective-permute-done.9 = bf16[256,2048]{1,0:T(8,128)(2,1)S(1)} collective-permute-done((bf16[256,2048]{1,0:T(8,128)(2,1)S(1)}, bf16[256,2048]{1,0:T(8,128)(2,1)S(1)}, u32[]{:S(2)}, u32[]{:S(2)}) %collective-permute-start.9) | collective-permute-done | bytes 1048608 | tf_op jit(solution)/shard_map/ppermute | solution.py:33
  332.0 3.3 multiply_reduce_fusion.7
  339.7 2.9 pad_maximum_fusion.3.x_ref.refs_0_
  342.6 14.3 %hidden_units.4 = (f32[512,2048]{1,0:T(8,128)}, f32[512,2048]{1,0:T(8,128)}, bf16[512,2048]{1,0:T(8,128)(2,1)}) custom-call(bf16[512,2048]{1,0:T(8,128)(2,1)} %pad_maximum_fusion.3.x_ref.refs_0_, bf16[2048,2048]{1,0:T(8,128)(2,1)} %all-gather.4.cloned.1.call-done.gate_w.refs_2_, bf16[2048,2048]{1,0:T(8,128)(2,1)} %all-gather.6.cloned.1.call-done.up_w.refs_3_), custom_call_target="tpu_custom_call" | custom-call | flops 1 | bytes 1 | tf_op jit(solution)/shard_map/hidden_units/pallas_call | solution.py:1111
  356.9 6.3 collective-permute-done.12
  370.0 15.8 %collective-permute-done.17 = bf16[256,2048]{1,0:T(8,128)(2,1)} collective-permute-done((bf16[256,2048]{1,0:T(8,128)(2,1)S(1)}, bf16[256,2048]{1,0:T(8,128)(2,1)}, u32[]{:S(2)}, u32[]{:S(2)}) %collective-permute-start.17) | collective-permute-done | bytes 1048608 | tf_op jit(solution)/shard_map/ppermute | solution.py:33
  387.3 14.4 %hidden_units.5 = (f32[512,2048]{1,0:T(8,128)}, f32[512,2048]{1,0:T(8,128)}, bf16[512,2048]{1,0:T(8,128)(2,1)}) custom-call(bf16[512,2048]{1,0:T(8,128)(2,1)} %pad_maximum_fusion.4.x_ref.refs_2_, bf16[2048,2048]{1,0:T(8,128)(2,1)} %all-gather.4.cloned.1.call-done.gate_w.refs_2_, bf16[2048,2048]{1,0:T(8,128)(2,1)} %all-gather.6.cloned.1.call-done.up_w.refs_3_), custom_call_target="tpu_custom_call" | custom-call | flops 1 | bytes 1 | tf_op jit(solution)/shard_map/hidden_units/pallas_call | solution.py:1111
  401.7 6.0 collective-permute-done.15
  412.8 14.3 %hidden_units.6 = (f32[512,2048]{1,0:T(8,128)}, f32[512,2048]{1,0:T(8,128)}, bf16[512,2048]{1,0:T(8,128)(2,1)}) custom-call(bf16[512,2048]{1,0:T(8,128)(2,1)} %copy-done.9, bf16[2048,2048]{1,0:T(8,128)(2,1)} %all-gather.4.cloned.1.call-done.gate_w.refs_2_, bf16[2048,2048]{1,0:T(8,128)(2,1)} %all-gather.6.cloned.1.call-done.up_w.refs_3_), custom_call_target="tpu_custom_call" | custom-call | flops 1 | bytes 1 | tf_op jit(solution)/shard_map/hidden_units/pallas_call | solution.py:1111
  428.7 14.3 %hidden_units.7 = (f32[512,2048]{1,0:T(8,128)}, f32[512,2048]{1,0:T(8,128)}, bf16[512,2048]{1,0:T(8,128)(2,1)}) custom-call(bf16[512,2048]{1,0:T(8,128)(2,1)} %copy-done.10, bf16[2048,2048]{1,0:T(8,128)(2,1)} %all-gather.4.cloned.1.call-done.gate_w.refs_2_, bf16[2048,2048]{1,0:T(8,128)(2,1)} %all-gather.6.cloned.1.call-done.up_w.refs_3_), custom_call_target="tpu_custom_call" | custom-call | flops 1 | bytes 1 | tf_op jit(solution)/shard_map/hidden_units/pallas_call | solution.py:1111
  443.1 8.8 sum_products.8
  453.3 2.6 collective-permute-start.21
  461.3 8.8 sum_products.9
  472.6 8.9 sum_products.10
  481.4 9.0 sum_products.11
  497.8 3.3 fusion.8
  505.9 2.8 pad_maximum_fusion.5.grad_ref.refs_0_
  508.7 11.8 hidden_grads.4
  520.5 13.9 %sum_products.12 = bf16[512,2048]{1,0:T(8,128)(2,1)} custom-call(bf16[512,2048]{1,0:T(8,128)(2,1)} %get-tuple-element.217.refs_0_.refs_4_, bf16[512,2048]{1,0:T(8,128)(2,1)} %get-tuple-element.226.refs_1_.refs_4_, bf16[2048,2048]{1,0:T(8,128)(2,1)} %all-gather.4.cloned.1.call-done.gate_w.refs_2_, bf16[2048,2048]{1,0:T(8,128)(2,1)} %all-gather.6.cloned.1.call-done.up_w.refs_3_), custom_call_target="tpu_custom_call" | custom-call | flops 1 | bytes 1 | tf_op jit(solution)/shard_map/sum_products/pallas_call | solution.py:1173
  534.3 2.6 multiply_reduce_fusion.4
  536.9 7.0 add_convert_fusion.1
  546.8 4.5 collective-permute-done.25
  552.9 11.6 hidden_grads.5
  564.5 13.9 %sum_products.13 = bf16[512,2048]{1,0:T(8,128)(2,1)} custom-call(bf16[512,2048]{1,0:T(8,128)(2,1)} %get-tuple-element.219.refs_0_.refs_6_, bf16[512,2048]{1,0:T(8,128)(2,1)} %get-tuple-element.228.refs_1_.refs_6_, bf16[2048,2048]{1,0:T(8,128)(2,1)} %all-gather.4.cloned.1.call-done.gate_w.refs_2_, bf16[2048,2048]{1,0:T(8,128)(2,1)} %all-gather.6.cloned.1.call-done.up_w.refs_3_), custom_call_target="tpu_custom_call" | custom-call | flops 1 | bytes 1 | tf_op jit(solution)/shard_map/sum_products/pallas_call | solution.py:1173
  584.3 23.8 %weight_grad.7 = bf16[2048,2048]{1,0:T(8,128)(2,1)} custom-call(bf16[512,2048]{1,0:T(8,128)(2,1)} %pad_maximum_fusion.5.grad_ref.refs_0_, bf16[512,2048]{1,0:T(8,128)(2,1)} %copy-done.19, bf16[512,2048]{1,0:T(8,128)(2,1)} %pad_maximum_fusion.6.grad_ref.refs_2_, bf16[512,2048]{1,0:T(8,128)(2,1)} %copy-done.18, ...), custom_call_target="tpu_custom_call" | custom-call | flops 1 | bytes 1 | tf_op jit(solution)/shard_map/weight_grad/pallas_call | solution.py:1198
  608.2 12.1 %hidden_grads.6 = (bf16[512,2048]{1,0:T(8,128)(2,1)}, bf16[512,2048]{1,0:T(8,128)(2,1)}) custom-call(bf16[512,2048]{1,0:T(8,128)(2,1)} %copy-done.19, bf16[2048,2048]{1,0:T(8,128)(2,1)} %all-gather.8.cloned.1.call-done.refs_1_.weight, f32[512,2048]{1,0:T(8,128)} %get-tuple-element.201.gate_ref, f32[512,2048]{1,0:T(8,128)} %get-tuple-element.202.up_ref), custom_call_target="tpu_custom_call" | custom-call | flops 1 | bytes 1 | tf_op jit(solution)/shard_map/hidden_grads/pallas_call | solution.py:1144
  620.3 13.9 %sum_products.14 = bf16[512,2048]{1,0:T(8,128)(2,1)} custom-call(bf16[512,2048]{1,0:T(8,128)(2,1)} %get-tuple-element.218.refs_0_.refs_5_, bf16[512,2048]{1,0:T(8,128)(2,1)} %get-tuple-element.227.refs_1_.refs_5_, bf16[2048,2048]{1,0:T(8,128)(2,1)} %all-gather.4.cloned.1.call-done.gate_w.refs_2_, bf16[2048,2048]{1,0:T(8,128)(2,1)} %all-gather.6.cloned.1.call-done.up_w.refs_3_), custom_call_target="tpu_custom_call" | custom-call | flops 1 | bytes 1 | tf_op jit(solution)/shard_map/sum_products/pallas_call | solution.py:1173
  635.6 12.1 %hidden_grads.7 = (bf16[512,2048]{1,0:T(8,128)(2,1)}, bf16[512,2048]{1,0:T(8,128)(2,1)}) custom-call(bf16[512,2048]{1,0:T(8,128)(2,1)} %copy-done.18, bf16[2048,2048]{1,0:T(8,128)(2,1)} %all-gather.8.cloned.1.call-done.refs_1_.weight, f32[512,2048]{1,0:T(8,128)} %get-tuple-element.207.gate_ref, f32[512,2048]{1,0:T(8,128)} %get-tuple-element.208.up_ref), custom_call_target="tpu_custom_call" | custom-call | flops 1 | bytes 1 | tf_op jit(solution)/shard_map/hidden_grads/pallas_call | solution.py:1144
  647.7 14.2 %sum_products.15 = bf16[512,2048]{1,0:T(8,128)(2,1)} custom-call(bf16[512,2048]{1,0:T(8,128)(2,1)} %get-tuple-element.220.refs_0_.refs_7_, bf16[512,2048]{1,0:T(8,128)(2,1)} %get-tuple-element.229.refs_1_.refs_7_, bf16[2048,2048]{1,0:T(8,128)(2,1)} %all-gather.4.cloned.1.call-done.gate_w.refs_2_, bf16[2048,2048]{1,0:T(8,128)(2,1)} %all-gather.6.cloned.1.call-done.up_w.refs_3_), custom_call_target="tpu_custom_call" | custom-call | flops 1 | bytes 1 | tf_op jit(solution)/shard_map/sum_products/pallas_call | solution.py:1173
  668.8 21.6 %collective-permute-done.34 = bf16[256,2048]{1,0:T(8,128)(2,1)S(1)} collective-permute-done((bf16[256,2048]{1,0:T(8,128)(2,1)S(1)}, bf16[256,2048]{1,0:T(8,128)(2,1)S(1)}, u32[]{:S(2)}, u32[]{:S(2)}) %collective-permute-start.34) | collective-permute-done | bytes 1048608 | tf_op jit(solution)/shard_map/ppermute | solution.py:33
  693.7 23.9 %weight_grad.8 = bf16[2048,2048]{1,0:T(8,128)(2,1)} custom-call(bf16[512,2048]{1,0:T(8,128)(2,1)} %pad_maximum_fusion.3.x_ref.refs_0_, bf16[512,2048]{1,0:T(8,128)(2,1)} %copy-done.9, bf16[512,2048]{1,0:T(8,128)(2,1)} %pad_maximum_fusion.4.x_ref.refs_2_, bf16[512,2048]{1,0:T(8,128)(2,1)} %copy-done.10, bf16[512,2048]{1,0:T(8,128)(2,1)} %get-tuple-element.217.refs_0_.refs_4_, ...), custom_call_target="tpu_custom_call" | custom-call | flops 1 | bytes 1 | tf_op jit(solution)/shard_map/weight_grad/pallas_call | solution.py:1198
  722.0 3.1 multiply_reduce_fusion
  727.9 24.5 %weight_grad.9 = bf16[2048,2048]{1,0:T(8,128)(2,1)} custom-call(bf16[512,2048]{1,0:T(8,128)(2,1)} %pad_maximum_fusion.3.x_ref.refs_0_, bf16[512,2048]{1,0:T(8,128)(2,1)} %copy-done.9, bf16[512,2048]{1,0:T(8,128)(2,1)} %pad_maximum_fusion.4.x_ref.refs_2_, bf16[512,2048]{1,0:T(8,128)(2,1)} %copy-done.10, bf16[512,2048]{1,0:T(8,128)(2,1)} %get-tuple-element.226.refs_1_.refs_4_, ...), custom_call_target="tpu_custom_call" | custom-call | flops 1 | bytes 1 | tf_op jit(solution)/shard_map/weight_grad/pallas_call | solution.py:1198
  752.4 15.1 %collective-permute-done.42 = bf16[256,2048]{1,0:T(8,128)(2,1)} collective-permute-done((bf16[256,2048]{1,0:T(8,128)(2,1)}, bf16[256,2048]{1,0:T(8,128)(2,1)}, u32[]{:S(2)}, u32[]{:S(2)}) %collective-permute-start.42) | collective-permute-done | bytes 1048608 | tf_op jit(solution)/shard_map/ppermute | solution.py:33
  767.6 3.8 fusion.16.places
  779.5 2.8 pad_maximum_fusion.8.refs_2_
  784.9 3.3 convolution_convert_fusion.1
  792.3 9.3 weight_grad.10.refs_3_
  801.5 2.7 broadcast_select_fusion.8
  809.5 3.1 broadcast_select_fusion.6
  814.3 2.8 collective-permute-start.47
  821.3 7.9 pick.1.grad_ref
  829.2 62.3 %attention_backward.1 = (f32[2048,512]{1,0:T(8,128)}, f32[2048,512]{1,0:T(8,128)}, f32[2048,512]{1,0:T(8,128)}) custom-call(s32[8]{0:T(128)S(1)} %and_select_fusion.9.high_ref, bf16[2048,512]{1,0:T(8,128)(2,1)S(1)} %copy-done.1, bf16[2048,512]{1,0:T(8,128)(2,1)S(1)} %copy-done.2, bf16[2048,512]{1,0:T(8,128)(2,1)} %get-tuple-element.153.v_ref, ...), custom_call_target="tpu_custom_call" | custom-call | flops 1 | bytes 1 | tf_op jit(solution)/shard_map/attention_backward/pallas_call | solution.py:959
  891.5 8.3 collective-permute-done.47
  899.9 13.1 %norm_grads.1 = (f32[2048,512]{1,0:T(8,128)}, f32[2048,512]{1,0:T(8,128)}, f32[2,2048]{1,0:T(2,128)}, f32[8,512]{1,0:T(8,128)}, f32[8,512]{1,0:T(8,128)}) custom-call(f32[2048,512]{1,0:T(8,128)} %get-tuple-element.239.dq_ref, f32[2048,512]{1,0:T(8,128)} %get-tuple-element.240.dk_ref, f32[2048,1536]{1,0:T(8,128)} %get-tuple-element.148.raw, ...), custom_call_target="tpu_custom_call" | custom-call | flops 1 | bytes 1 | tf_op jit(solution)/shard_map/norm_grads/pallas_call | solution.py:1016
  915.0 2.8 broadcast_select_fusion.4
  922.1 4.7 add_bitcast_fusion
  931.6 14.5 %raw_grads.1.refs_1_.rows_ref = bf16[2048,1536]{1,0:T(8,128)(2,1)} custom-call(f32[2048,512]{1,0:T(8,128)} %get-tuple-element.241.dq_ref, f32[2048,512]{1,0:T(8,128)} %get-tuple-element.242.dk_ref, f32[2048,512]{1,0:T(8,128)} %get-tuple-element.243.dv_ref, f32[2048,1536]{1,0:T(8,128)} %get-tuple-element.148.raw, f32[2,2048]{1,0:T(2,128)} %add.322.squares, ...), custom_call_target="tpu_custom_call" | custom-call | flops 1 | bytes 1 | tf_op jit(solution)/shard_map/raw_grads/pallas_call | solution.py:1062
  946.1 8.8 weight_grad.11.refs_6_
  954.9 8.8 weight_grad.12.refs_4_
  963.7 8.8 weight_grad.13.refs_5_
  972.5 32.7 %give_back.3 = (bf16[2048,1536]{1,0:T(8,128)(2,1)}, bf16[2048,2048]{1,0:T(8,128)(2,1)}) custom-call(s32[1,2048]{1,0:T(1,128)} %get-tuple-element.371.places, bf16[2048,1536]{1,0:T(8,128)(2,1)} %raw_grads.1.refs_1_.rows_ref, bf16[2048,1536]{1,0:T(8,128)(2,1)} %get-tuple-element.144.weight), custom_call_target="tpu_custom_call" | custom-call | flops 1 | bytes 1 | tf_op jit(solution)/shard_map/give_back/pallas_call | solution.py:1271
  1006.2 171.1 %leave.1 = (bf16[512,2048]{1,0:T(8,128)(2,1)}, f32[8,2048]{1,0:T(8,128)}, f32[256,512]{1,0:T(8,128)}, f32[256,512]{1,0:T(8,128)}, f32[256,512]{1,0:T(8,128)}, /*index=5*/f32[256,512]{1,0:T(8,128)}) custom-call(bf16[2048,2048]{1,0:T(8,128)(2,1)} %get-tuple-element.252.refs_0_, f32[512,2048]{1,0:T(8,128)} %pad_maximum_fusion.refs_1_, ...), custom_call_target="tpu_custom_call" | custom-call | flops 1 | bytes 1 | tf_op jit(solution)/shard_map/leave/pallas_call | solution.py:645
  1181.0 3.1 broadcast_select_fusion
  1184.1 3.2 convert_add_fusion.2
  (317 shorter events, 150.4 us)
Async XLA Ops:
  7.2 335.4 %all-gather.4.cloned.1.call-start = ((), (), s32[]{:S(2)}) async-start(), calls=%async_computation.3 | async-start | bytes 10485760 | tf_op jit(solution)/shard_map/all_gather | solution.py:69
  145.8 196.8 %all-gather.6.cloned.1.call-start = ((), (), s32[]{:S(2)}) async-start(), calls=%async_computation.4 | async-start | bytes 10485760 | tf_op jit(solution)/shard_map/all_gather | solution.py:69
  146.5 6.3 collective-permute-start
  151.9 47.9 %collective-permute-start.2 = (bf16[256,2048]{1,0:T(8,128)(2,1)S(1)}, bf16[256,2048]{1,0:T(8,128)(2,1)S(1)}, u32[]{:S(2)}, u32[]{:S(2)}) collective-permute-start(bf16[256,2048]{1,0:T(8,128)(2,1)S(1)} %copy-done.39), channel_id=1, source_target_pairs={{0,2},{2,6},{6,4},{4,0},{1,3},{3,7},{7,5},{5,1},{8,10},{10,14},{14... | collective-permute-start | bytes 3145736 | tf_op jit(solution)/shard_map/ppermute | solution.py:64
  152.0 47.8 %collective-permute-start.1 = (bf16[256,2048]{1,0:T(8,128)(2,1)S(1)}, bf16[256,2048]{1,0:T(8,128)(2,1)S(1)}, u32[]{:S(2)}, u32[]{:S(2)}) collective-permute-start(bf16[256,2048]{1,0:T(8,128)(2,1)S(1)} %copy-done.39), channel_id=1, source_target_pairs={{2,4},{4,2},{3,5},{5,3},{10,12},{12,10},{11,13},{13,11},{18,20},{2... | collective-permute-start | bytes 3145736 | tf_op jit(solution)/shard_map/ppermute | solution.py:37
  201.6 241.4 %all-gather.8.cloned.1.call-start = ((), (), s32[]{:S(2)}) async-start(), calls=%async_computation.5 | async-start | bytes 10485760 | tf_op jit(solution)/shard_map/all_gather | solution.py:69
  206.2 6.5 collective-permute-start.3
  212.7 5.8 collective-permute-start.4
  219.2 76.7 %collective-permute-start.6 = (bf16[256,2048]{1,0:T(8,128)(2,1)S(1)}, bf16[256,2048]{1,0:T(8,128)(2,1)S(1)}, u32[]{:S(2)}, u32[]{:S(2)}) collective-permute-start(bf16[256,2048]{1,0:T(8,128)(2,1)S(1)} %bitcast.26), channel_id=1, source_target_pairs={{0,2},{2,6},{6,4},{4,0},{1,3},{3,7},{7,5},{5,1},{8,10},{10,14},{14... | collective-permute-start | bytes 3145736 | tf_op jit(solution)/shard_map/ppermute | solution.py:64
  219.7 76.2 %collective-permute-start.5 = (bf16[256,2048]{1,0:T(8,128)(2,1)S(1)}, bf16[256,2048]{1,0:T(8,128)(2,1)S(1)}, u32[]{:S(2)}, u32[]{:S(2)}) collective-permute-start(bf16[256,2048]{1,0:T(8,128)(2,1)S(1)} %bitcast.27), channel_id=1, source_target_pairs={{2,4},{4,2},{3,5},{5,3},{10,12},{12,10},{11,13},{13,11},{18,20},{2... | collective-permute-start | bytes 3145736 | tf_op jit(solution)/shard_map/ppermute | solution.py:37
  297.7 503.9 %reduce-scatter.4.cloned.1.call-start = ((), (), s32[]{:S(2)}) async-start(), calls=%async_computation.6 | async-start | bytes 10485760 | tf_op jit(solution)/shard_map/reduce_scatter | solution.py:73
  301.5 3.3 collective-permute-start.8
  302.5 5.8 collective-permute-start.7
  302.5 5.8 collective-permute-start.11
  306.4 28.8 %copy-start.45 = (f32[2048]{0:T(1024)S(1)}, f32[2048]{0:T(1024)}, u32[]{:S(2)}) copy-start(f32[2048]{0:T(1024)} %param.28) | copy-start | bytes 24580
  306.4 25.5 %collective-permute-start.9 = (bf16[256,2048]{1,0:T(8,128)(2,1)S(1)}, bf16[256,2048]{1,0:T(8,128)(2,1)S(1)}, u32[]{:S(2)}, u32[]{:S(2)}) collective-permute-start(bf16[256,2048]{1,0:T(8,128)(2,1)S(1)} %add_convert_fusion.7), channel_id=1, source_target_pairs={{0,1},{1,0},{2,3},{3,2},{4,5},{5,4},{6,7},{7,6},{8,9},{9,8},{10,11... | collective-permute-start | bytes 3145736 | tf_op jit(solution)/shard_map/ppermute | solution.py:33
  336.9 2.9 collective-permute-start.13
  336.9 26.3 %collective-permute-start.12 = (bf16[256,2048]{1,0:T(8,128)(2,1)}, bf16[256,2048]{1,0:T(8,128)(2,1)}, u32[]{:S(2)}, u32[]{:S(2)}) collective-permute-start(bf16[256,2048]{1,0:T(8,128)(2,1)} %get-tuple-element.343), channel_id=1, source_target_pairs={{0,1},{1,0},{2,3},{3,2},{4,5},{5,4},{6,7},{7,6},{8,9},{9,8},{10,11... | collective-permute-start | bytes 3145736 | tf_op jit(solution)/shard_map/ppermute | solution.py:33
  338.8 24.5 %collective-permute-start.10 = (bf16[256,2048]{1,0:T(8,128)(2,1)}, bf16[256,2048]{1,0:T(8,128)(2,1)}, u32[]{:S(2)}, u32[]{:S(2)}) collective-permute-start(bf16[256,2048]{1,0:T(8,128)(2,1)} %get-tuple-element.339), channel_id=1, source_target_pairs={{0,4},{4,0},{1,5},{5,1},{2,6},{6,2},{3,7},{7,3},{8,12},{12,8},{9,1... | collective-permute-start | bytes 3145736 | tf_op jit(solution)/shard_map/ppermute | solution.py:33
  338.9 46.8 %collective-permute-start.17 = (bf16[256,2048]{1,0:T(8,128)(2,1)S(1)}, bf16[256,2048]{1,0:T(8,128)(2,1)}, u32[]{:S(2)}, u32[]{:S(2)}) collective-permute-start(bf16[256,2048]{1,0:T(8,128)(2,1)S(1)} %fusion.12), channel_id=1, source_target_pairs={{0,1},{1,0},{2,3},{3,2},{4,5},{5,4},{6,7},{7,6},{8,9},{9,8},{10,11... | collective-permute-start | bytes 3145736 | tf_op jit(solution)/shard_map/ppermute | solution.py:33
  368.1 17.6 %collective-permute-start.14 = (bf16[256,2048]{1,0:T(8,128)(2,1)S(1)}, bf16[256,2048]{1,0:T(8,128)(2,1)S(1)}, u32[]{:S(2)}, u32[]{:S(2)}) collective-permute-start(bf16[256,2048]{1,0:T(8,128)(2,1)S(1)} %fusion.13), channel_id=1, source_target_pairs={{0,4},{4,0},{1,5},{5,1},{2,6},{6,2},{3,7},{7,3},{8,12},{12,8},{9,1... | collective-permute-start | bytes 3145736 | tf_op jit(solution)/shard_map/ppermute | solution.py:33
  368.2 39.5 %collective-permute-start.15 = (bf16[256,2048]{1,0:T(8,128)(2,1)S(1)}, bf16[256,2048]{1,0:T(8,128)(2,1)S(1)}, u32[]{:S(2)}, u32[]{:S(2)}) collective-permute-start(bf16[256,2048]{1,0:T(8,128)(2,1)S(1)} %fusion.13), channel_id=1, source_target_pairs={{0,1},{1,0},{2,3},{3,2},{4,5},{5,4},{6,7},{7,6},{8,9},{9,8},{10,11... | collective-permute-start | bytes 3145736 | tf_op jit(solution)/shard_map/ppermute | solution.py:33
  385.8 25.6 %collective-permute-start.18 = (bf16[256,2048]{1,0:T(8,128)(2,1)}, bf16[256,2048]{1,0:T(8,128)(2,1)S(1)}, u32[]{:S(2)}, u32[]{:S(2)}) collective-permute-start(bf16[256,2048]{1,0:T(8,128)(2,1)} %collective-permute-done.17), channel_id=1, source_target_pairs={{0,4},{4,0},{1,5},{5,1},{2,6},{6,2},{3,7},{7,3},{8,12},{12,8},{9,1... | collective-permute-start | bytes 3145736 | tf_op jit(solution)/shard_map/ppermute | solution.py:33
  407.7 19.6 %collective-permute-start.16 = (bf16[256,2048]{1,0:T(8,128)(2,1)S(1)}, bf16[256,2048]{1,0:T(8,128)(2,1)S(1)}, u32[]{:S(2)}, u32[]{:S(2)}) collective-permute-start(bf16[256,2048]{1,0:T(8,128)(2,1)S(1)} %collective-permute-done.15), channel_id=1, source_target_pairs={{0,4},{4,0},{1,5},{5,1},{2,6},{6,2},{3,7},{7,3},{8,12},{12,8},{9,1... | collective-permute-start | bytes 3145736 | tf_op jit(solution)/shard_map/ppermute | solution.py:33
  407.7 82.8 %collective-permute-start.19 = (bf16[512,2048]{1,0:T(8,128)(2,1)}, bf16[512,2048]{1,0:T(8,128)(2,1)}, u32[]{:S(2)}, u32[]{:S(2)}) collective-permute-start(bf16[512,2048]{1,0:T(8,128)(2,1)} %param.16), channel_id=1, source_target_pairs={{2,4},{4,2},{3,5},{5,3},{10,12},{12,10},{11,13},{13,11},{18,20},{2... | collective-permute-start | bytes 6291464 | tf_op jit(solution)/shard_map/ppermute | solution.py:37
  453.3 4.9 collective-permute-start.21
  459.6 33.4 %collective-permute-start.22 = (bf16[256,2048]{1,0:T(8,128)(2,1)}, bf16[256,2048]{1,0:T(8,128)(2,1)S(1)}, u32[]{:S(2)}, u32[]{:S(2)}) collective-permute-start(bf16[256,2048]{1,0:T(8,128)(2,1)} %add_convert_fusion.5), channel_id=1, source_target_pairs={{0,1},{1,0},{2,3},{3,2},{4,5},{5,4},{6,7},{7,6},{8,9},{9,8},{10,11... | collective-permute-start | bytes 3145736 | tf_op jit(solution)/shard_map/ppermute | solution.py:33
  472.5 20.5 %collective-permute-start.20 = (bf16[256,2048]{1,0:T(8,128)(2,1)}, bf16[256,2048]{1,0:T(8,128)(2,1)}, u32[]{:S(2)}, u32[]{:S(2)}) collective-permute-start(bf16[256,2048]{1,0:T(8,128)(2,1)} %slice.227), channel_id=1, source_target_pairs={{0,4},{4,0},{1,5},{5,1},{2,6},{6,2},{3,7},{7,3},{8,12},{12,8},{9,1... | collective-permute-start | bytes 3145736 | tf_op jit(solution)/shard_map/ppermute | solution.py:33
  490.5 10.7 collective-permute-start.28
  492.9 51.0 %copy-start.7 = (bf16[512,2048]{1,0:T(8,128)(2,1)}, bf16[512,2048]{1,0:T(8,128)(2,1)S(1)}, u32[]{:S(2)}) copy-start(bf16[512,2048]{1,0:T(8,128)(2,1)S(1)} %broadcast_select_fusion.1) | copy-start | bytes 6291460
  501.1 4.8 collective-permute-start.23
  502.6 31.8 %collective-permute-start.29 = (bf16[256,2048]{1,0:T(8,128)(2,1)}, bf16[256,2048]{1,0:T(8,128)(2,1)}, u32[]{:S(2)}, u32[]{:S(2)}) collective-permute-start(bf16[256,2048]{1,0:T(8,128)(2,1)} %add_convert_fusion.4), channel_id=1, source_target_pairs={{0,1},{1,0},{2,3},{3,2},{4,5},{5,4},{6,7},{7,6},{8,9},{9,8},{10,11... | collective-permute-start | bytes 3145736 | tf_op jit(solution)/shard_map/ppermute | solution.py:33
  504.1 30.2 %collective-permute-start.27 = (bf16[256,2048]{1,0:T(8,128)(2,1)}, bf16[256,2048]{1,0:T(8,128)(2,1)}, u32[]{:S(2)}, u32[]{:S(2)}) collective-permute-start(bf16[256,2048]{1,0:T(8,128)(2,1)} %slice.233), channel_id=1, source_target_pairs={{0,4},{4,0},{1,5},{5,1},{2,6},{6,2},{3,7},{7,3},{8,12},{12,8},{9,1... | collective-permute-start | bytes 3145736 | tf_op jit(solution)/shard_map/ppermute | solution.py:33
  504.2 47.2 %collective-permute-start.25 = (bf16[256,2048]{1,0:T(8,128)(2,1)}, bf16[256,2048]{1,0:T(8,128)(2,1)}, u32[]{:S(2)}, u32[]{:S(2)}) collective-permute-start(bf16[256,2048]{1,0:T(8,128)(2,1)} %fusion.8), channel_id=1, source_target_pairs={{0,1},{1,0},{2,3},{3,2},{4,5},{5,4},{6,7},{7,6},{8,9},{9,8},{10,11... | collective-permute-start | bytes 3145736 | tf_op jit(solution)/shard_map/ppermute | solution.py:33
  546.3 5.0 collective-permute-start.30
  546.4 31.9 %collective-permute-start.31 = (bf16[256,2048]{1,0:T(8,128)(2,1)S(1)}, bf16[256,2048]{1,0:T(8,128)(2,1)S(1)}, u32[]{:S(2)}, u32[]{:S(2)}) collective-permute-start(bf16[256,2048]{1,0:T(8,128)(2,1)S(1)} %fusion.5), channel_id=1, source_target_pairs={{0,1},{1,0},{2,3},{3,2},{4,5},{5,4},{6,7},{7,6},{8,9},{9,8},{10,11... | collective-permute-start | bytes 3145736 | tf_op jit(solution)/shard_map/ppermute | solution.py:33
  551.3 29.0 %collective-permute-start.26 = (bf16[256,2048]{1,0:T(8,128)(2,1)}, bf16[256,2048]{1,0:T(8,128)(2,1)}, u32[]{:S(2)}, u32[]{:S(2)}) collective-permute-start(bf16[256,2048]{1,0:T(8,128)(2,1)} %collective-permute-done.25), channel_id=1, source_target_pairs={{0,4},{4,0},{1,5},{5,1},{2,6},{6,2},{3,7},{7,3},{8,12},{12,8},{9,1... | collective-permute-start | bytes 3145736 | tf_op jit(solution)/shard_map/ppermute | solution.py:33
  578.4 3.3 collective-permute-start.32
  608.2 201.3 %reduce-scatter.6.cloned.1.call-start = ((), (), s32[]{:S(2)}) async-start(), calls=%async_computation.7 | async-start | bytes 10485760 | tf_op jit(solution)/shard_map/reduce_scatter | solution.py:73
  635.5 28.4 %collective-permute-start.33 = (bf16[256,2048]{1,0:T(8,128)(2,1)S(1)}, bf16[256,2048]{1,0:T(8,128)(2,1)S(1)}, u32[]{:S(2)}, u32[]{:S(2)}) collective-permute-start(bf16[256,2048]{1,0:T(8,128)(2,1)S(1)} %slice.238), channel_id=1, source_target_pairs={{0,4},{4,0},{1,5},{5,1},{2,6},{6,2},{3,7},{7,3},{8,12},{12,8},{9,1... | collective-permute-start | bytes 3145736 | tf_op jit(solution)/shard_map/ppermute | solution.py:33
  663.4 2.8 collective-permute-start.38
  664.3 26.0 %collective-permute-start.34 = (bf16[256,2048]{1,0:T(8,128)(2,1)S(1)}, bf16[256,2048]{1,0:T(8,128)(2,1)S(1)}, u32[]{:S(2)}, u32[]{:S(2)}) collective-permute-start(bf16[256,2048]{1,0:T(8,128)(2,1)S(1)} %add_convert_fusion.3), channel_id=1, source_target_pairs={{0,1},{1,0},{2,3},{3,2},{4,5},{5,4},{6,7},{7,6},{8,9},{9,8},{10,11... | collective-permute-start | bytes 3145736 | tf_op jit(solution)/shard_map/ppermute | solution.py:33
  665.6 24.7 %copy-start.8 = (bf16[512,2048]{1,0:T(8,128)(2,1)S(1)}, bf16[512,2048]{1,0:T(8,128)(2,1)}, u32[]{:S(2)}) copy-start(bf16[512,2048]{1,0:T(8,128)(2,1)} %copy-done.7) | copy-start | bytes 6291460
  665.6 24.7 %collective-permute-start.24 = (bf16[256,2048]{1,0:T(8,128)(2,1)S(1)}, bf16[256,2048]{1,0:T(8,128)(2,1)S(1)}, u32[]{:S(2)}, u32[]{:S(2)}) collective-permute-start(bf16[256,2048]{1,0:T(8,128)(2,1)S(1)} %slice.231), channel_id=1, source_target_pairs={{0,4},{4,0},{1,5},{5,1},{2,6},{6,2},{3,7},{7,3},{8,12},{12,8},{9,1... | collective-permute-start | bytes 3145736 | tf_op jit(solution)/shard_map/ppermute | solution.py:33
  667.6 50.0 %collective-permute-start.39 = (bf16[256,2048]{1,0:T(8,128)(2,1)}, bf16[256,2048]{1,0:T(8,128)(2,1)}, u32[]{:S(2)}, u32[]{:S(2)}) collective-permute-start(bf16[256,2048]{1,0:T(8,128)(2,1)} %add_convert_fusion.2), channel_id=1, source_target_pairs={{0,1},{1,0},{2,3},{3,2},{4,5},{5,4},{6,7},{7,6},{8,9},{9,8},{10,11... | collective-permute-start | bytes 3145736 | tf_op jit(solution)/shard_map/ppermute | solution.py:33
  717.6 197.4 %reduce-scatter.8.cloned.1.call-start = ((), (), s32[]{:S(2)}) async-start(), calls=%async_computation.8 | async-start | bytes 10485760 | tf_op jit(solution)/shard_map/reduce_scatter | solution.py:73
  719.3 2.7 collective-permute-start.37
  719.4 33.0 %collective-permute-start.36 = (bf16[256,2048]{1,0:T(8,128)(2,1)S(1)}, bf16[256,2048]{1,0:T(8,128)(2,1)}, u32[]{:S(2)}, u32[]{:S(2)}) collective-permute-start(bf16[256,2048]{1,0:T(8,128)(2,1)S(1)} %subtract_convert_fusion.1), channel_id=1, source_target_pairs={{0,1},{1,0},{2,3},{3,2},{4,5},{5,4},{6,7},{7,6},{8,9},{9,8},{10,11... | collective-permute-start | bytes 3145736 | tf_op jit(solution)/shard_map/ppermute | solution.py:33
  726.7 40.8 %collective-permute-start.42 = (bf16[256,2048]{1,0:T(8,128)(2,1)}, bf16[256,2048]{1,0:T(8,128)(2,1)}, u32[]{:S(2)}, u32[]{:S(2)}) collective-permute-start(bf16[256,2048]{1,0:T(8,128)(2,1)} %subtract_convert_fusion), channel_id=1, source_target_pairs={{0,1},{1,0},{2,3},{3,2},{4,5},{5,4},{6,7},{7,6},{8,9},{9,8},{10,11... | collective-permute-start | bytes 3145736 | tf_op jit(solution)/shard_map/ppermute | solution.py:33
  752.4 15.2 %copy-start.20 = (s32[2048,1]{1,0:T(8,128)S(1)}, s32[2048,1]{1,0:T(8,128)}, u32[]{:S(2)}) copy-start(s32[2048,1]{1,0:T(8,128)} %copy.51.places) | copy-start | bytes 24580
  771.4 6.5 collective-permute-start.35
  771.6 7.9 collective-permute-start.41
  776.1 14.1 %collective-permute-start.43 = (bf16[256,2048]{1,0:T(8,128)(2,1)}, bf16[256,2048]{1,0:T(8,128)(2,1)S(1)}, u32[]{:S(2)}, u32[]{:S(2)}) collective-permute-start(bf16[256,2048]{1,0:T(8,128)(2,1)} %collective-permute-done.42), channel_id=1, source_target_pairs={{0,4},{4,0},{1,5},{5,1},{2,6},{6,2},{3,7},{7,3},{8,12},{12,8},{9,1... | collective-permute-start | bytes 3145736 | tf_op jit(solution)/shard_map/ppermute | solution.py:33
  776.1 14.2 %collective-permute-start.40 = (bf16[256,2048]{1,0:T(8,128)(2,1)}, bf16[256,2048]{1,0:T(8,128)(2,1)S(1)}, u32[]{:S(2)}, u32[]{:S(2)}) collective-permute-start(bf16[256,2048]{1,0:T(8,128)(2,1)} %collective-permute-done.36), channel_id=1, source_target_pairs={{0,4},{4,0},{1,5},{5,1},{2,6},{6,2},{3,7},{7,3},{8,12},{12,8},{9,1... | collective-permute-start | bytes 3145736 | tf_op jit(solution)/shard_map/ppermute | solution.py:33
  804.2 87.3 %collective-permute-start.44 = (bf16[256,2048]{1,0:T(8,128)(2,1)S(1)}, bf16[256,2048]{1,0:T(8,128)(2,1)}, u32[]{:S(2)}, u32[]{:S(2)}) collective-permute-start(bf16[256,2048]{1,0:T(8,128)(2,1)S(1)} %get-tuple-element.267), channel_id=1, source_target_pairs={{2,4},{4,2},{3,5},{5,3},{10,12},{12,10},{11,13},{13,11},{18,20},{2... | collective-permute-start | bytes 3145736 | tf_op jit(solution)/shard_map/ppermute | solution.py:37
  805.9 11.2 copy-start.28
  805.9 85.6 %collective-permute-start.45 = (bf16[256,2048]{1,0:T(8,128)(2,1)}, bf16[256,2048]{1,0:T(8,128)(2,1)}, u32[]{:S(2)}, u32[]{:S(2)}) collective-permute-start(bf16[256,2048]{1,0:T(8,128)(2,1)} %get-tuple-element.354), channel_id=1, source_target_pairs={{2,0},{6,2},{4,6},{0,4},{3,1},{7,3},{5,7},{1,5},{10,8},{14,10},{12... | collective-permute-start | bytes 3145736 | tf_op jit(solution)/shard_map/ppermute | solution.py:80
  812.6 78.9 %collective-permute-start.46 = (bf16[256,2048]{1,0:T(8,128)(2,1)}, bf16[256,2048]{1,0:T(8,128)(2,1)}, u32[]{:S(2)}, u32[]{:S(2)}) collective-permute-start(bf16[256,2048]{1,0:T(8,128)(2,1)} %get-tuple-element.261), channel_id=1, source_target_pairs={{2,4},{4,2},{3,5},{5,3},{10,12},{12,10},{11,13},{13,11},{18,20},{2... | collective-permute-start | bytes 3145736 | tf_op jit(solution)/shard_map/ppermute | solution.py:37
  814.3 85.6 %collective-permute-start.47 = (bf16[256,2048]{1,0:T(8,128)(2,1)}, bf16[256,2048]{1,0:T(8,128)(2,1)}, u32[]{:S(2)}, u32[]{:S(2)}) collective-permute-start(bf16[256,2048]{1,0:T(8,128)(2,1)} %get-tuple-element.352), channel_id=1, source_target_pairs={{2,0},{6,2},{4,6},{0,4},{3,1},{7,3},{5,7},{1,5},{10,8},{14,10},{12... | collective-permute-start | bytes 3145736 | tf_op jit(solution)/shard_map/ppermute | solution.py:80
  913.0 93.2 %collective-permute-start.52 = (bf16[512,2048]{1,0:T(8,128)(2,1)}, bf16[512,2048]{1,0:T(8,128)(2,1)}, u32[]{:S(2)}, u32[]{:S(2)}) collective-permute-start(bf16[512,2048]{1,0:T(8,128)(2,1)} %pad_maximum_fusion.10), channel_id=1, source_target_pairs={{2,4},{4,2},{3,5},{5,3},{10,12},{12,10},{11,13},{13,11},{18,20},{2... | collective-permute-start | bytes 6291464 | tf_op jit(solution)/shard_map/ppermute | solution.py:37
  917.8 87.4 %collective-permute-start.50 = (bf16[256,2048]{1,0:T(8,128)(2,1)S(1)}, bf16[256,2048]{1,0:T(8,128)(2,1)}, u32[]{:S(2)}, u32[]{:S(2)}) collective-permute-start(bf16[256,2048]{1,0:T(8,128)(2,1)S(1)} %get-tuple-element.264), channel_id=1, source_target_pairs={{2,4},{4,2},{3,5},{5,3},{10,12},{12,10},{11,13},{13,11},{18,20},{2... | collective-permute-start | bytes 3145736 | tf_op jit(solution)/shard_map/ppermute | solution.py:37
  919.5 86.8 %collective-permute-start.51 = (bf16[256,2048]{1,0:T(8,128)(2,1)}, bf16[256,2048]{1,0:T(8,128)(2,1)}, u32[]{:S(2)}, u32[]{:S(2)}) collective-permute-start(bf16[256,2048]{1,0:T(8,128)(2,1)} %get-tuple-element.350), channel_id=1, source_target_pairs={{2,0},{6,2},{4,6},{0,4},{3,1},{7,3},{5,7},{1,5},{10,8},{14,10},{12... | collective-permute-start | bytes 3145736 | tf_op jit(solution)/shard_map/ppermute | solution.py:80
  922.1 4.8 collective-permute-start.48
  926.9 4.0 collective-permute-start.49
  (50 other events, 160.4 us)
Sparse Core Ops, SparseCore 0:
  145.9 93.6 all-gather.3
  241.5 87.6 all-gather.5
  331.0 87.6 all-gather.7
  608.3 90.7 reduce-scatter.3
  717.7 91.6 reduce-scatter.5
  812.4 86.4 reduce-scatter.7

commit v4 on v3

--- a/solution.py
+++ b/solution.py
@@ -316,13 +316,17 @@
                 near_copy(shard, place, base).wait_send()
 
 
-def leave_kernel(cuts, paired, *refs):
+def leave_kernel(cuts, paired, stacks, *refs):
     count = len(cuts)
     ringed = [index for index in range(count) if not paired[index]]
-    partial, resid, gains, totals = refs[0], refs[1], refs[2], refs[3 : 3 + count]
-    outs = refs[3 + count : 3 + count + 2 + sum(len(cut) for cut in cuts)]
+    partial, resid, gains, given = refs[0], refs[1], refs[2], refs[3 : 3 + len(stacks)]
+    totals = []
+    for ref, stack in zip(given, stacks):
+        totals += [ref] if stack == 1 else [ref.at[k] for k in range(stack)]
+    taken = 3 + len(stacks)
+    outs = refs[taken : taken + 2 + sum(len(cut) for cut in cuts)]
     rows_out, gains_out, shard_outs = outs[0], outs[1], outs[2:]
-    scratch = refs[3 + count + len(outs) :]
+    scratch = refs[taken + len(outs) :]
     peer_far, peer_near, far_sum, from_far, done_rows = scratch[:5]
     boxes, taken = [], 5
     for alone in paired:
@@ -614,11 +618,19 @@
             last_copies(index)[2].wait_send()
 
 
+def unstacked(totals):
+    flat = []
+    for total, parts, alone in totals:
+        for matrix in [total] if total.ndim == 2 else [total[k] for k in range(total.shape[0])]:
+            flat.append((matrix, parts, alone))
+    return flat
+
+
 def leave(partial, resid, gains, totals):
     if not small_grid():
         summed = finish_scatter_rows(start_scatter([partial.astype(jnp.bfloat16)]), None)
         shards = []
-        for total, parts, alone in totals:
+        for total, parts, alone in unstacked(totals):
             shard, first = finish_split(*start_split(total if alone else scatter_pair(total))), 0
             for width in parts:
                 shards.append(shard[:, first : first + width])
@@ -631,7 +643,9 @@
         jax.ShapeDtypeStruct((rows, columns), jnp.bfloat16),
         jax.ShapeDtypeStruct(gains.shape, jnp.float32),
     ]
-    for total, parts, alone in totals:
+    stacks = tuple(1 if total.ndim == 2 else total.shape[0] for total, _, _ in totals)
+    arrays = [total.astype(jnp.bfloat16) for total, _, _ in totals]
+    for total, parts, alone in unstacked(totals):
         height, width = total.shape[0] // (2 if alone else 8), total.shape[1]
         cuts.append(tuple(sum(parts[: index + 1]) for index in range(len(parts))))
         outs += [jax.ShapeDtypeStruct((height, part_width), jnp.float32) for part_width in parts]
@@ -639,11 +653,11 @@
         if not alone:
             shapes += [(height, width)] * 4 + [(2 * height, width)] * 3
         scratch += [pltpu.VMEM(shape, jnp.bfloat16) for shape in shapes]
-    paired = tuple(alone for _, _, alone in totals)
-    slots = 4 * CHUNKS + 10 * len(totals) + 5
+    paired = tuple(alone for _, _, alone in unstacked(totals))
+    slots = 4 * CHUNKS + 10 * len(paired) + 5
     vmem = pl.BlockSpec(memory_space=pltpu.VMEM)
     return pl.pallas_call(
-        functools.partial(leave_kernel, tuple(cuts), paired),
+        functools.partial(leave_kernel, tuple(cuts), paired, stacks),
         in_specs=[vmem] * (3 + len(totals)),
         out_specs=[pl.BlockSpec(memory_space=pl.ANY)] + [vmem] * (len(outs) - 1),
         out_shape=outs,
@@ -660,7 +674,7 @@
         ),
         cost_estimate=BESIDE,
         name="leave",
-    )(partial.astype(jnp.bfloat16), resid, gains, *[total.astype(jnp.bfloat16) for total, _, _ in totals])
+    )(partial.astype(jnp.bfloat16), resid, gains, *arrays)
 
 
 def enter(tokens, matrices):
@@ -848,51 +862,58 @@
     return (keys >= starts) & (keys <= queries)
 
 
+def head_columns(head):
+    return slice(head * HDIM, (head + 1) * HDIM)
+
+
 def forward_kernel(low_ref, q_ref, k_ref, v_ref, start_ref, attn_ref, full_ref, log_ref):
-    block = pl.program_id(1)
-    queries = q_ref[...]
+    block = pl.program_id(0)
+    heads = q_ref.shape[1] // HDIM
     starts = start_ref[...]
     scale = 1.0 / math.sqrt(HDIM)
 
     def step(index, carried):
-        peak, total, acc = carried
         rows = pl.ds(pl.multiple_of(index * BLOCK, BLOCK), BLOCK)
-        scores = contract_cols(k_ref[rows, :], queries) * scale
-        scores = jnp.where(
-            allowed_keys(starts, index * BLOCK, block * BLOCK), scores, masked_score
-        )
-        new_peak = jnp.maximum(peak, jnp.max(scores, axis=0, keepdims=True))
-        fade = jnp.exp(peak - new_peak)
-        weights = jnp.exp(scores - new_peak)
-        total = total * fade + jnp.sum(weights, axis=0, keepdims=True)
-        acc = acc * fade + contract_rows(v_ref[rows, :], weights.astype(jnp.bfloat16))
-        return (new_peak, total, acc)
+        allowed = allowed_keys(starts, index * BLOCK, block * BLOCK)
+        after_step = []
+        for head, (peak, total, acc) in enumerate(carried):
+            cols = head_columns(head)
+            scores = contract_cols(k_ref[rows, cols], q_ref[:, cols]) * scale
+            scores = jnp.where(allowed, scores, masked_score)
+            new_peak = jnp.maximum(peak, jnp.max(scores, axis=0, keepdims=True))
+            fade = jnp.exp(peak - new_peak)
+            weights = jnp.exp(scores - new_peak)
+            total = total * fade + jnp.sum(weights, axis=0, keepdims=True)
+            acc = acc * fade + contract_rows(v_ref[rows, cols], weights.astype(jnp.bfloat16))
+            after_step.append((new_peak, total, acc))
+        return tuple(after_step)
 
     start = (
         jnp.full((1, BLOCK), masked_score, jnp.float32),
         jnp.zeros((1, BLOCK), jnp.float32),
         jnp.zeros((HDIM, BLOCK), jnp.float32),
     )
-    carried = step(block, start)
-    peak, total, acc = lax.fori_loop(low_ref[block], block, step, carried)
-    out = jnp.transpose(acc / total)
-    full_ref[...] = out
-    attn_ref[...] = out.astype(jnp.bfloat16)
-    log_ref[...] = peak + jnp.log(total)
+    carried = step(block, (start,) * heads)
+    carried = lax.fori_loop(low_ref[block], block, step, carried)
+    for head, (peak, total, acc) in enumerate(carried):
+        out = jnp.transpose(acc / total)
+        full_ref[:, head_columns(head)] = out
+        attn_ref[:, head_columns(head)] = out.astype(jnp.bfloat16)
+        log_ref[head] = peak + jnp.log(total)
 
 
 def attention_forward(q_b, k_b, v_b, starts, low_block):
     rows, width = q_b.shape
     heads = width // HDIM
-    own = pl.BlockSpec((BLOCK, HDIM), lambda h, i, low: (i, h))
-    whole = pl.BlockSpec((rows, HDIM), lambda h, i, low: (0, h))
+    own = pl.BlockSpec((BLOCK, width), lambda i, low: (i, 0))
+    whole = pl.BlockSpec((rows, width), lambda i, low: (0, 0))
     return pl.pallas_call(
         forward_kernel,
         grid_spec=pltpu.PrefetchScalarGridSpec(
             num_scalar_prefetch=1,
-            grid=(heads, rows // BLOCK),
-            in_specs=[own, whole, whole, pl.BlockSpec((1, BLOCK), lambda h, i, low: (0, i))],
-            out_specs=[own, own, pl.BlockSpec((None, 1, BLOCK), lambda h, i, low: (h, 0, i))],
+            grid=(rows // BLOCK,),
+            in_specs=[own, whole, whole, pl.BlockSpec((1, BLOCK), lambda i, low: (0, i))],
+            out_specs=[own, own, pl.BlockSpec((heads, 1, BLOCK), lambda i, low: (0, 0, i))],
         ),
         out_shape=[
             jax.ShapeDtypeStruct((rows, width), jnp.bfloat16),
@@ -908,8 +929,9 @@
 def backward_kernel(
     high_ref, q_ref, k_ref, v_ref, grad_ref, full_ref, log_ref, start_ref, dq_ref, dk_ref, dv_ref, delta
 ):
-    block = pl.program_id(1)
-    blocks = pl.num_programs(1)
+    block = pl.program_id(0)
+    blocks = pl.num_programs(0)
+    heads = q_ref.shape[1] // HDIM
     scale = 1.0 / math.sqrt(HDIM)
 
     @pl.when(block == 0)
@@ -918,32 +940,40 @@
 
         def one(index, unused):
             rows = pl.ds(pl.multiple_of(index * BLOCK, BLOCK), BLOCK)
-            delta[:, rows] = row_sums(grad_ref[rows, :].astype(jnp.float32) * full_ref[rows, :])
+            for head in range(heads):
+                cols = head_columns(head)
+                delta[head, :, rows] = row_sums(
+                    grad_ref[rows, cols].astype(jnp.float32) * full_ref[rows, cols]
+                )
             return unused
 
         lax.fori_loop(0, blocks, one, 0)
 
     here = pl.ds(pl.multiple_of(block * BLOCK, BLOCK), BLOCK)
-    keys, values = k_ref[here, :], v_ref[here, :]
 
     def step(index, carried):
-        dk, dv = carried
         rows = pl.ds(pl.multiple_of(index * BLOCK, BLOCK), BLOCK)
-        queries, grads = q_ref[rows, :], grad_ref[rows, :]
-        scores = contract_cols(keys, queries) * scale
         allowed = allowed_keys(start_ref[:, rows], block * BLOCK, index * BLOCK)
-        probs = jnp.where(allowed, jnp.exp(scores - log_ref[:, rows]), 0.0)
-        dv = dv + dot(probs.astype(jnp.bfloat16), grads)
-        d_probs = contract_cols(values, grads)
-        d_scores = (probs * (d_probs - delta[:, rows])).astype(jnp.bfloat16)
-        dk = dk + dot(d_scores, queries)
-        dq_ref[rows, :] += contract_rows(d_scores, keys)
-        return (dk, dv)
+        after_step = []
+        for head, (dk, dv) in enumerate(carried):
+            cols = head_columns(head)
+            keys, values = k_ref[here, cols], v_ref[here, cols]
+            queries, grads = q_ref[rows, cols], grad_ref[rows, cols]
+            scores = contract_cols(keys, queries) * scale
+            probs = jnp.where(allowed, jnp.exp(scores - log_ref[head, :, rows]), 0.0)
+            dv = dv + dot(probs.astype(jnp.bfloat16), grads)
+            d_probs = contract_cols(values, grads)
+            d_scores = (probs * (d_probs - delta[head, :, rows])).astype(jnp.bfloat16)
+            dk = dk + dot(d_scores, queries)
+            dq_ref[rows, cols] += contract_rows(d_scores, keys)
+            after_step.append((dk, dv))
+        return tuple(after_step)
 
     zero = jnp.zeros((BLOCK, HDIM), jnp.float32)
-    dk, dv = lax.fori_loop(block, high_ref[block] + 1, step, (zero, zero))
-    dk_ref[...] = dk * scale
-    dv_ref[...] = dv
+    carried = lax.fori_loop(block, high_ref[block] + 1, step, ((zero, zero),) * heads)
+    for head, (dk, dv) in enumerate(carried):
+        dk_ref[:, head_columns(head)] = dk * scale
+        dv_ref[:, head_columns(head)] = dv
 
     @pl.when(block == blocks - 1)
     def _():
@@ -953,21 +983,21 @@
 def attention_backward(q_b, k_b, v_b, grads, full, logs, starts, high_block):
     rows, width = q_b.shape
     heads = width // HDIM
-    own = pl.BlockSpec((BLOCK, HDIM), lambda h, i, high: (i, h))
-    whole = pl.BlockSpec((rows, HDIM), lambda h, i, high: (0, h))
+    own = pl.BlockSpec((BLOCK, width), lambda i, high: (i, 0))
+    whole = pl.BlockSpec((rows, width), lambda i, high: (0, 0))
     out = jax.ShapeDtypeStruct((rows, width), jnp.float32)
     return pl.pallas_call(
         backward_kernel,
         grid_spec=pltpu.PrefetchScalarGridSpec(
             num_scalar_prefetch=1,
-            grid=(heads, rows // BLOCK),
+            grid=(rows // BLOCK,),
             in_specs=[whole] * 5
             + [
-                pl.BlockSpec((None, 1, rows), lambda h, i, high: (h, 0, 0)),
-                pl.BlockSpec((1, rows), lambda h, i, high: (0, 0)),
+                pl.BlockSpec((heads, 1, rows), lambda i, high: (0, 0, 0)),
+                pl.BlockSpec((1, rows), lambda i, high: (0, 0)),
             ],
             out_specs=[whole, own, own],
-            scratch_shapes=[pltpu.VMEM((1, rows), jnp.float32)],
+            scratch_shapes=[pltpu.VMEM((heads, 1, rows), jnp.float32)],
         ),
         out_shape=[out] * 3,
         compiler_params=pltpu.CompilerParams(vmem_limit_bytes=VMEM_BYTES),
@@ -1191,21 +1221,47 @@
     refs[-1][...] = total.astype(jnp.bfloat16)
 
 
-def weight_grad(lefts, rights, first=0, width=None):
-    height, width = lefts[0].shape[1], rights[0].shape[1] if width is None else width
+def weight_grad(lefts, rights):
+    heights = [left.shape[0] for left in lefts]
+    if len(rights) == 1 < len(lefts):
+        rights, places = rights * len(lefts), list(range(len(lefts)))
+    else:
+        places = [0] * len(lefts)
+    height, width = lefts[0].shape[1], rights[0].shape[1]
     tall, wide = min(height, 512), min(width, 1024)
-    blocks = width // wide
     return pl.pallas_call(
         functools.partial(weight_grad_kernel, len(lefts)),
         grid=(width // wide, height // tall),
-        in_specs=[pl.BlockSpec((left.shape[0], tall), lambda j, i: (0, i)) for left in lefts]
-        + [pl.BlockSpec((right.shape[0], wide), lambda j, i: (0, first * blocks + j)) for right in rights],
+        in_specs=[pl.BlockSpec((rows, tall), lambda j, i: (0, i)) for rows in heights]
+        + [
+            pl.BlockSpec((rows, wide), functools.partial(lambda place, j, i: (place, j), place))
+            for rows, place in zip(heights, places)
+        ],
         out_specs=pl.BlockSpec((tall, wide), lambda j, i: (i, j)),
         out_shape=jax.ShapeDtypeStruct((height, width), jnp.bfloat16),
         compiler_params=matmul_params(),
         cost_estimate=BESIDE,
         name="weight_grad",
     )(*lefts, *rights)
+
+
+def stacked_weight_grad(left, right, count):
+    rows, height = left.shape
+    width = right.shape[1] // count
+    tall = min(height, 512)
+    return pl.pallas_call(
+        functools.partial(weight_grad_kernel, 1),
+        grid=(count, height // tall),
+        in_specs=[
+            pl.BlockSpec((rows, tall), lambda j, i: (0, i)),
+            pl.BlockSpec((rows, width), lambda j, i: (0, j)),
+        ],
+        out_specs=pl.BlockSpec((None, tall, width), lambda j, i: (j, i, 0)),
+        out_shape=jax.ShapeDtypeStruct((count, height, width), jnp.bfloat16),
+        compiler_params=matmul_params(),
+        cost_estimate=BESIDE,
+        name="stacked_weight_grad",
+    )(left, right)
 
 
 def move_rows(places, wanted_first, count, rows_ref):
@@ -1290,26 +1346,43 @@
     )(place_row[None], value, weight)
 
 
-def pick_kernel(places, rows_ref, out):
-    out[...] = pick_rows(places[...], rows_ref)
-
-
-def pick(place_row, value):
-    rows, depth = value.shape
-    count = 512
+def pick_products_kernel(count, *refs):
+    places, pieces, weight = refs[0], refs[1 : 1 + count], refs[1 + count]
+    out, products = refs[2 + count], refs[3 + count]
+    step, first = BLOCK, 0
+    for piece in pieces:
+        height = piece.shape[0]
+
+        def one(index, unused, piece=piece, first=first):
+            here = pl.ds(pl.multiple_of(index * step, step), step)
+            there = pl.ds(pl.multiple_of(first + index * step, step), step)
+            products[there, :] = dot(piece[here, :], weight[...]).astype(jnp.bfloat16)
+            return unused
+
+        lax.fori_loop(0, height // step, one, 0)
+        first += height
+
+    def pick_block(index, unused):
+        here = pl.ds(pl.multiple_of(index * step, step), step)
+        out[here, :] = pick_rows(places[here, :], products)
+        return unused
+
+    lax.fori_loop(0, out.shape[0] // step, pick_block, 0)
+
+
+def pick_products(place_row, pieces, weight):
+    rows, width = place_row.shape[0], weight.shape[1]
+    vmem = pl.BlockSpec(memory_space=pltpu.VMEM)
     return pl.pallas_call(
-        pick_kernel,
-        grid=(rows // count,),
-        in_specs=[
-            pl.BlockSpec((count, 1), lambda i: (i, 0)),
-            pl.BlockSpec((rows, depth), lambda i: (0, 0)),
-        ],
-        out_specs=pl.BlockSpec((count, depth), lambda i: (i, 0)),
-        out_shape=jax.ShapeDtypeStruct((rows, depth), jnp.bfloat16),
+        functools.partial(pick_products_kernel, len(pieces)),
+        in_specs=[vmem] * (2 + len(pieces)),
+        out_specs=vmem,
+        out_shape=jax.ShapeDtypeStruct((rows, width), jnp.bfloat16),
+        scratch_shapes=[pltpu.VMEM((rows, width), jnp.bfloat16)],
         compiler_params=matmul_params(),
         cost_estimate=BESIDE,
-        name="pick",
-    )(place_row[:, None], value)
+        name="pick_products",
+    )(place_row[:, None], *pieces, weight)
 
 
 def rms_back(values, rstd, gain_vec, grad):
@@ -1398,6 +1471,10 @@
         def complete(side, index):
             nonlocal token
             sums[side, index] = finish(*begun[side, index], token)
+            if scattered and sides == 2 and not late:
+                *others, last = scattered[-1]
+                sums[side, index], last = lax.optimization_barrier((sums[side, index], last))
+                scattered[-1] = (*others, last)
             token = sums[side, index]
 
         def scatter(index):
@@ -1406,11 +1483,13 @@
         for side, index in order:
             if side == 0:
                 gathered[index] = start_gather(make_rows(index, token))
-                if sides == 2 and index > 0:
+                if sides == 2 and index > 0 and not late:
                     far_pieces[index - 1] = forward_rows(gathered[index - 1], token)
                 piece = gathered[index][0]
             else:
-                if index == 0:
+                if late:
+                    far_pieces[index] = forward_rows(gathered[index], token)
+                elif index == 0:
                     far_pieces[parts - 1] = forward_rows(gathered[parts - 1], token)
                     if between is not None:
                         near = [gathered[each][0] for each in range(parts)]
@@ -1483,7 +1562,7 @@
     keys = sorted(saved)
     ffn_gain_part = sum(gain_parts)
     attn_gain_part = 0.0
-    d_resids, gathered = [], []
+    d_resids, gathered, near_pieces = [], [], []
     operands = [
         ([back[key][0] for key in keys], [saved[key][3] for key in keys]),
         ([saved[key][0] for key in keys], [back[key][1] for key in keys]),
@@ -1508,13 +1587,17 @@
         d_resids.append(d_resid)
         attn_gain_part = attn_gain_part + jnp.sum(d_resid * attn_out * rstd_a, axis=0)
         d_attn_b = rms_back(attn_out, rstd_a, attn_gain, d_resid).astype(jnp.bfloat16)
-        gathered.append(start_gather(d_attn_b))
+        if sides == 2:
+            near_pieces.append([d_attn_b, swap(d_attn_b, "core")])
+            gathered.append((None, swap(d_attn_b, "tl")))
+        else:
+            gathered.append(start_gather(d_attn_b))
         token = next_weight_grad((d_attn_b, token))
     far_pieces = []
     for index in range(parts):
         if sides == 2:
             far, weight_grads[-1] = lax.optimization_barrier((gathered[index][1], weight_grads[-1]))
-            far_pieces.append(jnp.concatenate([far, swap(far, "core")], axis=0))
+            far_pieces.append([far, swap(far, "core")])
             token = far
         if len(weight_grads) < 3:
             token = next_weight_grad(token)
@@ -1523,36 +1606,32 @@
     down_grad, gate_grad, up_grad = weight_grads
     d_attn_pieces = []
     for index in range(parts):
-        d_attn_pieces.append(gathered[index][0])
         if sides == 2:
-            d_attn_pieces.append(far_pieces[index])
-    d_givens = [dot(piece, out_full).astype(jnp.bfloat16) for piece in d_attn_pieces]
+            d_attn_pieces += [*near_pieces[index], *far_pieces[index]]
+        else:
+            d_attn_pieces.append(gathered[index][0])
     d_resid = jnp.concatenate(d_resids, axis=0)
-    d_given_b = jnp.concatenate(d_givens, axis=0)
-    out_total = weight_grad(
-        d_attn_pieces,
-        [piece for index in range(parts) for piece in pieces_of(attn_given, index)],
-    )
-    d_given_b, out_total = lax.optimization_barrier((d_given_b, out_total))
-    down_split, gate_split = start_split(scatter_pair(down_grad)), start_split(scatter_pair(gate_grad))
-    up_sum = scatter_pair(up_grad)
-    d_packed = pick(perm_place, d_given_b)
+    out_total = weight_grad(d_attn_pieces, [attn_given])
+    d_packed = pick_products(perm_place, d_attn_pieces, out_full)
+    down_split = start_split(scatter_pair(down_grad))
+    gate_sum, up_sum = scatter_pair(gate_grad), scatter_pair(up_grad)
+    layer_turn = start_turn(layer_out)
+    d_packed, out_total = lax.optimization_barrier((d_packed, out_total))
     d_q_rot, d_k_rot, d_v = attention_backward(
         q_b, k_b, v_b, d_packed, attn_f, logs, starts[None], high_block
     )
-    d_q_rot, down_split, gate_split = lax.optimization_barrier((d_q_rot, down_split, gate_split))
+    d_q_rot, down_split, layer_turn = lax.optimization_barrier((d_q_rot, down_split, layer_turn))
+    gate_split = start_split(after(d_q_rot, gate_sum))
     d_q_norm, d_k_norm, dots, q_parts, k_parts = norm_grads(
         d_q_rot, d_k_rot, raw, squares, gain_q, gain_k, cosine, sine
     )
-    up_split = start_split(after(d_q_norm, up_sum))
-    layer_turn = start_turn(after(d_q_norm, layer_out))
     q_gain_part, k_gain_part = jnp.sum(q_parts, axis=0), jnp.sum(k_parts, axis=0)
     dots = sum_over(dots, RANK)
     d_qkv_b = raw_grads(d_q_norm, d_k_norm, d_v, raw, squares, dots, gain_q, gain_k)
-    qkv_totals = [weight_grad([packed], [d_qkv_b], index, local_width) for index in range(3)]
-    last_total, d_qkv_b = lax.optimization_barrier((qkv_totals[-1], d_qkv_b))
+    qkv_totals = stacked_weight_grad(packed, d_qkv_b, 3)
+    up_split = start_split(after(d_qkv_b, up_sum))
     _, input_parts = give_back(perm_place, d_qkv_b, qkv_full)
-    input_parts, up_split, layer_turn = lax.optimization_barrier((input_parts, up_split, layer_turn))
+    input_parts, gate_split, up_split = lax.optimization_barrier((input_parts, gate_split, up_split))
     layer_out = finish_turn(*layer_turn)
     down_shard = finish_split(*down_split).T
     gate_shard, up_shard = finish_split(*gate_split), finish_split(*up_split)
@@ -1572,7 +1651,7 @@
         gains,
         [
             (out_total, [local_width], False),
-            *[(total, [local_width], False) for total in qkv_totals],
+            (qkv_totals, [local_width], False),
         ],
     )
 

time: 1210 us -> 1140 us (0.942)
  Pallas kernels: 853 us -> 801 us
    pallas_call x7 -> x4, Pallas kernels: 108 us -> 81.9 us  [weight_grad(): pl.pallas_call(functools.partial(weight_grad_kernel, len(lefts)), grid=(w...]
    ppermute x3, waiting for transfers between devices: 9.39 us -> 32.9 us  [start_split(): lax.ppermute(second, ('core', 'th'), CYCLE_BACK)]
    pallas_call x1, Pallas kernels: 62.3 us -> 46.7 us  [attention_backward(): pl.pallas_call(backward_kernel, grid_spec=pltpu.PrefetchScalarGridSpec(nu...]
    ppermute x41, waiting for transfers between devices: 101 us -> 88.1 us  [swap(): return lax.ppermute(value, axis, SWAP)]
    pallas_call x2 -> x3, Pallas kernels: 179 us -> 173 us  [the longest x1 133 us: leave(): pl.pallas_call(functools.partial(leave_kernel, tuple(cuts), paired, stack...]
    unnamed x125 -> x109, local copies, waits for them, and re-layouts: 31.7 us -> 26.8 us
  transfers between devices with their start and end apart: 59 -> 59, of which waited for: 16 -> 21; matrix products, arithmetic and copies ran while one was open for 11% -> 10% of each run, Pallas kernels for 43% -> 45%
where the time goes in v4:
time: 1140 us; the launch traced here: 1130 us
  Pallas kernels  801 us (70%)
  waiting for transfers between devices  121 us (11%)
  other arithmetic  94.9 us (8%)
  starting transfers between devices  50.9 us (4%)
  local copies, waits for them, and re-layouts  48.5 us (4%)
  between operations  17.1 us (2%)
    pallas_call x1, Pallas kernels, enter(): pl.pallas_call(functools.partial(entry_kernel, tuple(plan)), in_specs=[an...  137 us
    pallas_call x1, Pallas kernels, leave(): pl.pallas_call(functools.partial(leave_kernel, tuple(cuts), paired, stack...  133 us
    pallas_call x8, Pallas kernels, sum_products(): pl.pallas_call(functools.partial(products_kernel, len(lefts)), grid=(widt...  91.5 us
    ppermute x41, waiting for transfers between devices, swap(): return lax.ppermute(value, axis, SWAP)  88.1 us
    pallas_call x4, Pallas kernels, weight_grad(): pl.pallas_call(functools.partial(weight_grad_kernel, len(lefts)), grid=(w...  81.9 us
    pallas_call x4, Pallas kernels, hidden_units(): pl.pallas_call(hidden_kernel, grid=(width // block,), in_specs=[pl.BlockS...  58.2 us
    pallas_call x4, Pallas kernels, hidden_grads(): pl.pallas_call(hidden_grads_kernel, grid=(width // block,), in_specs=[pl....  47.9 us
    pallas_call x1, Pallas kernels, attention_backward(): pl.pallas_call(backward_kernel, grid_spec=pltpu.PrefetchScalarGridSpec(nu...  46.7 us
  transfers between devices with their start and end apart: 59, of which 21 were waited for; matrix products, arithmetic and copies ran while one was open for 10% of the time, Pallas kernels for 45%

profile of v4, /device:TPU:0, one launch (start us, length us, event | category | flops | bytes accessed | tf_op | source)
XLA Modules:
  0.0 1133.8 jit_solution(7677901038326228923)
XLA Ops:
  9.0 136.7 %enter.1 = (bf16[2048,2048]{1,0:T(8,128)(2,1)}, bf16[2048,1536]{1,0:T(8,128)(2,1)}, bf16[2048,512]{1,0:T(8,128)(2,1)}, bf16[512,2048]{1,0:T(8,128)(2,1)}) custom-call(bf16[512,2048]{1,0:T(8,128)(2,1)} %refs_0_.1, bf16[256,512]{1,0:T(8,128)(2,1)} %refs_1_.1, bf16[256,512]{1,0:T(8,128)(2,1)} %refs_2_.1, bf16[256,512]{1,0:T(8,128)(2,1)} %refs_3_.1, ...), custom_call_target="tpu_custom_call" | custom-call | flops 1 | bytes 1 | tf_op jit(solution)/shard_map/enter/pallas_call | solution.py:700
  146.5 5.4 collective-permute-start
  154.9 44.9 %pack.1 = (bf16[2048,2048]{1,0:T(8,128)(2,1)}, f32[2048,1536]{1,0:T(8,128)}, f32[2,2048]{1,0:T(2,128)}) custom-call(s32[2048,1]{1,0:T(8,128)} %copy.51.places, bf16[2048,2048]{1,0:T(8,128)(2,1)} %get-tuple-element.145.tokens_ref, bf16[2048,1536]{1,0:T(8,128)(2,1)} %get-tuple-element.146.weight), custom_call_target="tpu_custom_call" | custom-call | flops 1 | bytes 1 | tf_op jit(solution)/shard_map/pack/pallas_call | solution.py:1293
  212.7 4.1 collective-permute-start.4
  221.3 3.7 fusion.31
  227.7 11.9 %prepare.1 = (bf16[2048,512]{1,0:T(8,128)(2,1)}, bf16[2048,512]{1,0:T(8,128)(2,1)}, bf16[2048,512]{1,0:T(8,128)(2,1)}) custom-call(f32[2048,1536]{1,0:T(8,128)} %get-tuple-element.148.raw, f32[2,2048]{1,0:T(2,128)} %add.315.squares, f32[1,512]{1,0:T(1,128)} %bitcast.25, f32[1,512]{1,0:T(1,128)} %bitcast.28, f32[2048,128]{1,0:T(8,128)} %pad_maximum_fusion.8.cosine, ...), custom_call_target="tpu_custom_call" | custom-call | flops 1 | bytes 1 | tf_op jit(solution)/shard_map/prepare/pallas_call | solution.py:840
  241.1 34.2 %attention_forward.1 = (bf16[2048,512]{1,0:T(8,128)(2,1)S(1)}, f32[2048,512]{1,0:T(8,128)}, f32[4,1,2048]{2,1,0:T(1,128)S(1)}) custom-call(s32[8]{0:T(128)S(1)} %and_select_fusion.8.low_ref, bf16[2048,512]{1,0:T(8,128)(2,1)S(1)} %copy-done, bf16[2048,512]{1,0:T(8,128)(2,1)} %get-tuple-element.152.k_ref, bf16[2048,512]{1,0:T(8,128)(2,1)} %get-tuple-element.153.v_ref, ...), custom_call_target="tpu_custom_call" | custom-call | flops 1 | bytes 1 | tf_op jit(solution)/shard_map/attention_forward/pallas_call | solution.py:910
  276.7 13.0 %give_back.2 = (bf16[2048,512]{1,0:T(8,128)(2,1)}, bf16[2048,2048]{1,0:T(8,128)(2,1)}) custom-call(s32[1,2048]{1,0:T(1,128)} %get-tuple-element.363.places, bf16[2048,512]{1,0:T(8,128)(2,1)} %copy-done.3, bf16[2048,512]{1,0:T(8,128)(2,1)} %get-tuple-element.156.weight.refs_9_), custom_call_target="tpu_custom_call" | custom-call | flops 1 | bytes 1 | tf_op jit(solution)/shard_map/give_back/pallas_call | solution.py:1327
  292.0 3.7 fusion.37
  300.8 3.1 add_convert_fusion.6
  305.8 23.7 %collective-permute-done.9 = bf16[256,2048]{1,0:T(8,128)(2,1)S(1)} collective-permute-done((bf16[256,2048]{1,0:T(8,128)(2,1)S(1)}, bf16[256,2048]{1,0:T(8,128)(2,1)S(1)}, u32[]{:S(2)}, u32[]{:S(2)}) %collective-permute-start.9) | collective-permute-done | bytes 1048608 | tf_op jit(solution)/shard_map/ppermute | solution.py:33
  335.8 2.9 pad_maximum_fusion.3.x_ref.refs_0_
  338.7 15.1 %hidden_units.4 = (f32[512,2048]{1,0:T(8,128)}, f32[512,2048]{1,0:T(8,128)}, bf16[512,2048]{1,0:T(8,128)(2,1)}) custom-call(bf16[512,2048]{1,0:T(8,128)(2,1)} %pad_maximum_fusion.3.x_ref.refs_0_, bf16[2048,2048]{1,0:T(8,128)(2,1)} %all-gather.4.cloned.1.call-done.gate_w.refs_2_, bf16[2048,2048]{1,0:T(8,128)(2,1)} %all-gather.6.cloned.1.call-done.up_w.refs_3_), custom_call_target="tpu_custom_call" | custom-call | flops 1 | bytes 1 | tf_op jit(solution)/shard_map/hidden_units/pallas_call | solution.py:1141
  353.8 5.1 collective-permute-done.12
  368.0 14.4 %hidden_units.5 = (f32[512,2048]{1,0:T(8,128)}, f32[512,2048]{1,0:T(8,128)}, bf16[512,2048]{1,0:T(8,128)(2,1)}) custom-call(bf16[512,2048]{1,0:T(8,128)(2,1)} %pad_maximum_fusion.4.x_ref.refs_2_, bf16[2048,2048]{1,0:T(8,128)(2,1)} %all-gather.4.cloned.1.call-done.gate_w.refs_2_, bf16[2048,2048]{1,0:T(8,128)(2,1)} %all-gather.6.cloned.1.call-done.up_w.refs_3_), custom_call_target="tpu_custom_call" | custom-call | flops 1 | bytes 1 | tf_op jit(solution)/shard_map/hidden_units/pallas_call | solution.py:1141
  382.4 7.1 collective-permute-done.16
  394.0 14.4 %hidden_units.6 = (f32[512,2048]{1,0:T(8,128)}, f32[512,2048]{1,0:T(8,128)}, bf16[512,2048]{1,0:T(8,128)(2,1)}) custom-call(bf16[512,2048]{1,0:T(8,128)(2,1)} %copy-done.9, bf16[2048,2048]{1,0:T(8,128)(2,1)} %all-gather.4.cloned.1.call-done.gate_w.refs_2_, bf16[2048,2048]{1,0:T(8,128)(2,1)} %all-gather.6.cloned.1.call-done.up_w.refs_3_), custom_call_target="tpu_custom_call" | custom-call | flops 1 | bytes 1 | tf_op jit(solution)/shard_map/hidden_units/pallas_call | solution.py:1141
  408.4 6.7 collective-permute-done.15
  419.2 14.3 %hidden_units.7 = (f32[512,2048]{1,0:T(8,128)}, f32[512,2048]{1,0:T(8,128)}, bf16[512,2048]{1,0:T(8,128)(2,1)}) custom-call(bf16[512,2048]{1,0:T(8,128)(2,1)} %copy-done.10, bf16[2048,2048]{1,0:T(8,128)(2,1)} %all-gather.4.cloned.1.call-done.gate_w.refs_2_, bf16[2048,2048]{1,0:T(8,128)(2,1)} %all-gather.6.cloned.1.call-done.up_w.refs_3_), custom_call_target="tpu_custom_call" | custom-call | flops 1 | bytes 1 | tf_op jit(solution)/shard_map/hidden_units/pallas_call | solution.py:1141
  433.5 8.8 sum_products.8
  444.0 2.5 collective-permute-done.21
  449.6 8.8 sum_products.9
  460.8 8.9 sum_products.10
  469.6 9.0 sum_products.11
  480.6 8.6 collective-permute-done.22
  493.3 3.4 fusion.8
  501.4 2.9 pad_maximum_fusion.5.grad_ref.refs_0_
  504.3 11.6 %hidden_grads.4 = (bf16[512,2048]{1,0:T(8,128)(2,1)}, bf16[512,2048]{1,0:T(8,128)(2,1)}) custom-call(bf16[512,2048]{1,0:T(8,128)(2,1)} %pad_maximum_fusion.5.grad_ref.refs_0_, bf16[2048,2048]{1,0:T(8,128)(2,1)} %all-gather.8.cloned.1.call-done.refs_1_.weight, f32[512,2048]{1,0:T(8,128)} %get-tuple-element.182.gate_ref, f32[512,2048]{1,0:T(8,128)} %get-tuple-element.183.up_ref), custom_call_target="tpu_custom_call" | custom-call | flops 1 | bytes 1 | tf_op jit(solution)/shard_map/hidden_grads/pallas_call | solution.py:1174
  515.9 14.1 %sum_products.12 = bf16[512,2048]{1,0:T(8,128)(2,1)} custom-call(bf16[512,2048]{1,0:T(8,128)(2,1)} %get-tuple-element.219.refs_0_.refs_4_, bf16[512,2048]{1,0:T(8,128)(2,1)} %get-tuple-element.228.refs_1_.refs_4_, bf16[2048,2048]{1,0:T(8,128)(2,1)} %all-gather.4.cloned.1.call-done.gate_w.refs_2_, bf16[2048,2048]{1,0:T(8,128)(2,1)} %all-gather.6.cloned.1.call-done.up_w.refs_3_), custom_call_target="tpu_custom_call" | custom-call | flops 1 | bytes 1 | tf_op jit(solution)/shard_map/sum_products/pallas_call | solution.py:1203
  530.0 2.6 multiply_reduce_fusion.4
  532.6 6.9 add_convert_fusion.1
  539.5 2.5 fusion.5
  542.8 4.0 collective-permute-done.31
  548.4 11.6 %hidden_grads.5 = (bf16[512,2048]{1,0:T(8,128)(2,1)}, bf16[512,2048]{1,0:T(8,128)(2,1)}) custom-call(bf16[512,2048]{1,0:T(8,128)(2,1)} %pad_maximum_fusion.6.grad_ref.refs_2_, bf16[2048,2048]{1,0:T(8,128)(2,1)} %all-gather.8.cloned.1.call-done.refs_1_.weight, f32[512,2048]{1,0:T(8,128)} %get-tuple-element.189.gate_ref, f32[512,2048]{1,0:T(8,128)} %get-tuple-element.190.up_ref), custom_call_target="tpu_custom_call" | custom-call | flops 1 | bytes 1 | tf_op jit(solution)/shard_map/hidden_grads/pallas_call | solution.py:1174
  560.0 13.9 %sum_products.13 = bf16[512,2048]{1,0:T(8,128)(2,1)} custom-call(bf16[512,2048]{1,0:T(8,128)(2,1)} %get-tuple-element.221.refs_0_.refs_6_, bf16[512,2048]{1,0:T(8,128)(2,1)} %get-tuple-element.230.refs_1_.refs_6_, bf16[2048,2048]{1,0:T(8,128)(2,1)} %all-gather.4.cloned.1.call-done.gate_w.refs_2_, bf16[2048,2048]{1,0:T(8,128)(2,1)} %all-gather.6.cloned.1.call-done.up_w.refs_3_), custom_call_target="tpu_custom_call" | custom-call | flops 1 | bytes 1 | tf_op jit(solution)/shard_map/sum_products/pallas_call | solution.py:1203
  579.8 23.8 %weight_grad.4 = bf16[2048,2048]{1,0:T(8,128)(2,1)} custom-call(bf16[512,2048]{1,0:T(8,128)(2,1)} %pad_maximum_fusion.5.grad_ref.refs_0_, bf16[512,2048]{1,0:T(8,128)(2,1)} %copy-done.18, bf16[512,2048]{1,0:T(8,128)(2,1)} %pad_maximum_fusion.6.grad_ref.refs_2_, bf16[512,2048]{1,0:T(8,128)(2,1)} %copy-done.17, ...), custom_call_target="tpu_custom_call" | custom-call | flops 1 | bytes 1 | tf_op jit(solution)/shard_map/weight_grad/pallas_call | solution.py:1232
  603.7 12.6 %hidden_grads.6 = (bf16[512,2048]{1,0:T(8,128)(2,1)}, bf16[512,2048]{1,0:T(8,128)(2,1)}) custom-call(bf16[512,2048]{1,0:T(8,128)(2,1)} %copy-done.18, bf16[2048,2048]{1,0:T(8,128)(2,1)} %all-gather.8.cloned.1.call-done.refs_1_.weight, f32[512,2048]{1,0:T(8,128)} %get-tuple-element.201.gate_ref, f32[512,2048]{1,0:T(8,128)} %get-tuple-element.202.up_ref), custom_call_target="tpu_custom_call" | custom-call | flops 1 | bytes 1 | tf_op jit(solution)/shard_map/hidden_grads/pallas_call | solution.py:1174
  616.3 14.1 %sum_products.14 = bf16[512,2048]{1,0:T(8,128)(2,1)} custom-call(bf16[512,2048]{1,0:T(8,128)(2,1)} %get-tuple-element.220.refs_0_.refs_5_, bf16[512,2048]{1,0:T(8,128)(2,1)} %get-tuple-element.229.refs_1_.refs_5_, bf16[2048,2048]{1,0:T(8,128)(2,1)} %all-gather.4.cloned.1.call-done.gate_w.refs_2_, bf16[2048,2048]{1,0:T(8,128)(2,1)} %all-gather.6.cloned.1.call-done.up_w.refs_3_), custom_call_target="tpu_custom_call" | custom-call | flops 1 | bytes 1 | tf_op jit(solution)/shard_map/sum_products/pallas_call | solution.py:1203
  632.1 2.5 collective-permute-done.33
  635.7 12.0 %hidden_grads.7 = (bf16[512,2048]{1,0:T(8,128)(2,1)}, bf16[512,2048]{1,0:T(8,128)(2,1)}) custom-call(bf16[512,2048]{1,0:T(8,128)(2,1)} %copy-done.17, bf16[2048,2048]{1,0:T(8,128)(2,1)} %all-gather.8.cloned.1.call-done.refs_1_.weight, f32[512,2048]{1,0:T(8,128)} %get-tuple-element.207.gate_ref, f32[512,2048]{1,0:T(8,128)} %get-tuple-element.208.up_ref), custom_call_target="tpu_custom_call" | custom-call | flops 1 | bytes 1 | tf_op jit(solution)/shard_map/hidden_grads/pallas_call | solution.py:1174
  647.7 14.0 %sum_products.15 = bf16[512,2048]{1,0:T(8,128)(2,1)} custom-call(bf16[512,2048]{1,0:T(8,128)(2,1)} %get-tuple-element.222.refs_0_.refs_7_, bf16[512,2048]{1,0:T(8,128)(2,1)} %get-tuple-element.231.refs_1_.refs_7_, bf16[2048,2048]{1,0:T(8,128)(2,1)} %all-gather.4.cloned.1.call-done.gate_w.refs_2_, bf16[2048,2048]{1,0:T(8,128)(2,1)} %all-gather.6.cloned.1.call-done.up_w.refs_3_), custom_call_target="tpu_custom_call" | custom-call | flops 1 | bytes 1 | tf_op jit(solution)/shard_map/sum_products/pallas_call | solution.py:1203
  672.0 24.5 %weight_grad.5 = bf16[2048,2048]{1,0:T(8,128)(2,1)} custom-call(bf16[512,2048]{1,0:T(8,128)(2,1)} %pad_maximum_fusion.3.x_ref.refs_0_, bf16[512,2048]{1,0:T(8,128)(2,1)} %copy-done.9, bf16[512,2048]{1,0:T(8,128)(2,1)} %pad_maximum_fusion.4.x_ref.refs_2_, bf16[512,2048]{1,0:T(8,128)(2,1)} %copy-done.10, bf16[512,2048]{1,0:T(8,128)(2,1)} %get-tuple-element.219.refs_0_.refs_4_, ...), custom_call_target="tpu_custom_call" | custom-call | flops 1 | bytes 1 | tf_op jit(solution)/shard_map/weight_grad/pallas_call | solution.py:1232
  701.0 3.0 multiply_reduce_fusion
  706.4 24.4 %weight_grad.6 = bf16[2048,2048]{1,0:T(8,128)(2,1)} custom-call(bf16[512,2048]{1,0:T(8,128)(2,1)} %pad_maximum_fusion.3.x_ref.refs_0_, bf16[512,2048]{1,0:T(8,128)(2,1)} %copy-done.9, bf16[512,2048]{1,0:T(8,128)(2,1)} %pad_maximum_fusion.4.x_ref.refs_2_, bf16[512,2048]{1,0:T(8,128)(2,1)} %copy-done.10, bf16[512,2048]{1,0:T(8,128)(2,1)} %get-tuple-element.228.refs_1_.refs_4_, ...), custom_call_target="tpu_custom_call" | custom-call | flops 1 | bytes 1 | tf_op jit(solution)/shard_map/weight_grad/pallas_call | solution.py:1232
  730.8 15.6 %collective-permute-done.42.refs_7_.refs_6_ = bf16[256,2048]{1,0:T(8,128)(2,1)} collective-permute-done((bf16[256,2048]{1,0:T(8,128)(2,1)}, bf16[256,2048]{1,0:T(8,128)(2,1)}, u32[]{:S(2)}, u32[]{:S(2)}) %collective-permute-start.42) | collective-permute-done | bytes 1048608 | tf_op jit(solution)/shard_map/ppermute | solution.py:33
  751.2 2.7 broadcast_select_fusion.8
  754.6 3.9 collective-permute-start.45
  758.7 3.9 fusion.16.refs_0_
  762.6 16.9 %pick_products.1.grad_ref = bf16[2048,512]{1,0:T(8,128)(2,1)} custom-call(s32[2048,1]{1,0:T(8,128)} %fusion.16.refs_0_, bf16[256,2048]{1,0:T(8,128)(2,1)} %copy-done.20, bf16[256,2048]{1,0:T(8,128)(2,1)} %collective-permute-done.35.refs_2_.refs_1_, bf16[256,2048]{1,0:T(8,128)(2,1)} %collective-permute-done.36.refs_3_.refs_2_, ...), custom_call_target="tpu_custom_call" | custom-call | flops 1 | bytes 1 | tf_op jit(solution)/shard_map/pick_products/pallas_call | solution.py:1376
  779.5 9.1 weight_grad.7.refs_3_
  788.7 46.7 %attention_backward.1 = (f32[2048,512]{1,0:T(8,128)}, f32[2048,512]{1,0:T(8,128)}, f32[2048,512]{1,0:T(8,128)}) custom-call(s32[8]{0:T(128)S(1)} %and_select_fusion.9.high_ref, bf16[2048,512]{1,0:T(8,128)(2,1)S(1)} %copy-done.1, bf16[2048,512]{1,0:T(8,128)(2,1)S(1)} %copy-done.2, bf16[2048,512]{1,0:T(8,128)(2,1)} %get-tuple-element.153.v_ref, ...), custom_call_target="tpu_custom_call" | custom-call | flops 1 | bytes 1 | tf_op jit(solution)/shard_map/attention_backward/pallas_call | solution.py:989
  835.4 9.5 collective-permute-done.45
  844.9 14.3 %norm_grads.1 = (f32[2048,512]{1,0:T(8,128)}, f32[2048,512]{1,0:T(8,128)}, f32[2,2048]{1,0:T(2,128)}, f32[8,512]{1,0:T(8,128)}, f32[8,512]{1,0:T(8,128)}) custom-call(f32[2048,512]{1,0:T(8,128)} %get-tuple-element.242.dq_ref, f32[2048,512]{1,0:T(8,128)} %get-tuple-element.243.dk_ref, f32[2048,1536]{1,0:T(8,128)} %get-tuple-element.148.raw, ...), custom_call_target="tpu_custom_call" | custom-call | flops 1 | bytes 1 | tf_op jit(solution)/shard_map/norm_grads/pallas_call | solution.py:1046
  861.5 4.3 pad_maximum_fusion.refs_1_
  866.4 14.6 %raw_grads.1.rows_ref.refs_1_ = bf16[2048,1536]{1,0:T(8,128)(2,1)} custom-call(f32[2048,512]{1,0:T(8,128)} %get-tuple-element.244.dq_ref, f32[2048,512]{1,0:T(8,128)} %get-tuple-element.245.dk_ref, f32[2048,512]{1,0:T(8,128)} %get-tuple-element.246.dv_ref, f32[2048,1536]{1,0:T(8,128)} %get-tuple-element.148.raw, f32[2,2048]{1,0:T(2,128)} %add.315.squares, ...), custom_call_target="tpu_custom_call" | custom-call | flops 1 | bytes 1 | tf_op jit(solution)/shard_map/raw_grads/pallas_call | solution.py:1092
  881.0 3.0 broadcast_select_fusion.6
  886.6 3.1 broadcast_select_fusion.4
  891.3 2.6 collective-permute-start.52
  898.6 3.1 broadcast_select_fusion
  901.7 32.7 %give_back.3 = (bf16[2048,1536]{1,0:T(8,128)(2,1)}, bf16[2048,2048]{1,0:T(8,128)(2,1)}) custom-call(s32[1,2048]{1,0:T(1,128)} %get-tuple-element.363.places, bf16[2048,1536]{1,0:T(8,128)(2,1)} %raw_grads.1.rows_ref.refs_1_, bf16[2048,1536]{1,0:T(8,128)(2,1)} %get-tuple-element.146.weight), custom_call_target="tpu_custom_call" | custom-call | flops 1 | bytes 1 | tf_op jit(solution)/shard_map/give_back/pallas_call | solution.py:1327
  934.4 22.6 %stacked_weight_grad.1.refs_4_ = bf16[3,2048,512]{2,1,0:T(8,128)(2,1)} custom-call(bf16[2048,2048]{1,0:T(8,128)(2,1)} %get-tuple-element.257.refs_0_, bf16[2048,1536]{1,0:T(8,128)(2,1)} %raw_grads.1.rows_ref.refs_1_), custom_call_target="tpu_custom_call" | custom-call | flops 1 | bytes 1 | tf_op jit(solution)/shard_map/stacked_weight_grad/pallas_call | solution.py:1252
  957.8 22.5 %collective-permute-done.52 = bf16[256,2048]{1,0:T(8,128)(2,1)} collective-permute-done((bf16[256,2048]{1,0:T(8,128)(2,1)}, bf16[256,2048]{1,0:T(8,128)(2,1)}, u32[]{:S(2)}, u32[]{:S(2)}) %collective-permute-start.52) | collective-permute-done | bytes 1048608 | tf_op jit(solution)/shard_map/ppermute | solution.py:80
  980.3 133.3 %leave.1 = (bf16[512,2048]{1,0:T(8,128)(2,1)}, f32[8,2048]{1,0:T(8,128)}, f32[256,512]{1,0:T(8,128)}, f32[256,512]{1,0:T(8,128)}, f32[256,512]{1,0:T(8,128)}, /*index=5*/f32[256,512]{1,0:T(8,128)}) custom-call(bf16[2048,2048]{1,0:T(8,128)(2,1)} %get-tuple-element.253.refs_0_, f32[512,2048]{1,0:T(8,128)} %pad_maximum_fusion.refs_1_, ...), custom_call_target="tpu_custom_call" | custom-call | flops 1 | bytes 1 | tf_op jit(solution)/shard_map/leave/pallas_call | solution.py:659
  1117.3 5.5 convert_add_fusion.2
  (289 shorter events, 131.4 us)
Async XLA Ops:
  7.2 331.5 %all-gather.4.cloned.1.call-start = ((), (), s32[]{:S(2)}) async-start(), calls=%async_computation.3 | async-start | bytes 10485760 | tf_op jit(solution)/shard_map/all_gather | solution.py:69
  145.8 192.9 %all-gather.6.cloned.1.call-start = ((), (), s32[]{:S(2)}) async-start(), calls=%async_computation.4 | async-start | bytes 10485760 | tf_op jit(solution)/shard_map/all_gather | solution.py:69
  146.5 6.3 collective-permute-start
  151.9 48.0 %collective-permute-start.2 = (bf16[256,2048]{1,0:T(8,128)(2,1)S(1)}, bf16[256,2048]{1,0:T(8,128)(2,1)S(1)}, u32[]{:S(2)}, u32[]{:S(2)}) collective-permute-start(bf16[256,2048]{1,0:T(8,128)(2,1)S(1)} %copy-done.34), channel_id=1, source_target_pairs={{0,2},{2,6},{6,4},{4,0},{1,3},{3,7},{7,5},{5,1},{8,10},{10,14},{14... | collective-permute-start | bytes 3145736 | tf_op jit(solution)/shard_map/ppermute | solution.py:64
  152.0 47.8 %collective-permute-start.1 = (bf16[256,2048]{1,0:T(8,128)(2,1)S(1)}, bf16[256,2048]{1,0:T(8,128)(2,1)S(1)}, u32[]{:S(2)}, u32[]{:S(2)}) collective-permute-start(bf16[256,2048]{1,0:T(8,128)(2,1)S(1)} %copy-done.34), channel_id=1, source_target_pairs={{2,4},{4,2},{3,5},{5,3},{10,12},{12,10},{11,13},{13,11},{18,20},{2... | collective-permute-start | bytes 3145736 | tf_op jit(solution)/shard_map/ppermute | solution.py:37
  201.6 231.9 %all-gather.8.cloned.1.call-start = ((), (), s32[]{:S(2)}) async-start(), calls=%async_computation.5 | async-start | bytes 10485760 | tf_op jit(solution)/shard_map/all_gather | solution.py:69
  206.1 6.5 collective-permute-start.3
  212.7 5.8 collective-permute-start.4
  219.1 70.5 %collective-permute-start.6 = (bf16[256,2048]{1,0:T(8,128)(2,1)S(1)}, bf16[256,2048]{1,0:T(8,128)(2,1)S(1)}, u32[]{:S(2)}, u32[]{:S(2)}) collective-permute-start(bf16[256,2048]{1,0:T(8,128)(2,1)S(1)} %bitcast.20), channel_id=1, source_target_pairs={{0,2},{2,6},{6,4},{4,0},{1,3},{3,7},{7,5},{5,1},{8,10},{10,14},{14... | collective-permute-start | bytes 3145736 | tf_op jit(solution)/shard_map/ppermute | solution.py:64
  219.6 70.0 %collective-permute-start.5 = (bf16[256,2048]{1,0:T(8,128)(2,1)S(1)}, bf16[256,2048]{1,0:T(8,128)(2,1)S(1)}, u32[]{:S(2)}, u32[]{:S(2)}) collective-permute-start(bf16[256,2048]{1,0:T(8,128)(2,1)S(1)} %bitcast.21), channel_id=1, source_target_pairs={{2,4},{4,2},{3,5},{5,3},{10,12},{12,10},{11,13},{13,11},{18,20},{2... | collective-permute-start | bytes 3145736 | tf_op jit(solution)/shard_map/ppermute | solution.py:37
  291.4 459.8 %reduce-scatter.4.cloned.1.call-start = ((), (), s32[]{:S(2)}) async-start(), calls=%async_computation.6 | async-start | bytes 10485760 | tf_op jit(solution)/shard_map/reduce_scatter | solution.py:73
  295.7 3.6 collective-permute-start.11
  297.0 3.8 collective-permute-start.8
  297.0 8.8 collective-permute-start.7
  303.9 27.5 %copy-start.39 = (f32[2048]{0:T(1024)S(1)}, f32[2048]{0:T(1024)}, u32[]{:S(2)}) copy-start(f32[2048]{0:T(1024)} %param.28) | copy-start | bytes 24580
  303.9 25.6 %collective-permute-start.9 = (bf16[256,2048]{1,0:T(8,128)(2,1)S(1)}, bf16[256,2048]{1,0:T(8,128)(2,1)S(1)}, u32[]{:S(2)}, u32[]{:S(2)}) collective-permute-start(bf16[256,2048]{1,0:T(8,128)(2,1)S(1)} %get-tuple-element.346), channel_id=1, source_target_pairs={{0,1},{1,0},{2,3},{3,2},{4,5},{5,4},{6,7},{7,6},{8,9},{9,8},{10,11... | collective-permute-start | bytes 3145736 | tf_op jit(solution)/shard_map/ppermute | solution.py:33
  332.9 2.9 collective-permute-start.13
  333.0 25.9 %collective-permute-start.12 = (bf16[256,2048]{1,0:T(8,128)(2,1)}, bf16[256,2048]{1,0:T(8,128)(2,1)}, u32[]{:S(2)}, u32[]{:S(2)}) collective-permute-start(bf16[256,2048]{1,0:T(8,128)(2,1)} %get-tuple-element.345), channel_id=1, source_target_pairs={{0,1},{1,0},{2,3},{3,2},{4,5},{5,4},{6,7},{7,6},{8,9},{9,8},{10,11... | collective-permute-start | bytes 3145736 | tf_op jit(solution)/shard_map/ppermute | solution.py:33
  334.8 24.1 %collective-permute-start.10 = (bf16[256,2048]{1,0:T(8,128)(2,1)}, bf16[256,2048]{1,0:T(8,128)(2,1)}, u32[]{:S(2)}, u32[]{:S(2)}) collective-permute-start(bf16[256,2048]{1,0:T(8,128)(2,1)} %get-tuple-element.341), channel_id=1, source_target_pairs={{0,4},{4,0},{1,5},{5,1},{2,6},{6,2},{3,7},{7,3},{8,12},{12,8},{9,1... | collective-permute-start | bytes 3145736 | tf_op jit(solution)/shard_map/ppermute | solution.py:33
  363.7 2.7 collective-permute-start.14
  363.8 25.7 %collective-permute-start.16 = (bf16[256,2048]{1,0:T(8,128)(2,1)S(1)}, bf16[256,2048]{1,0:T(8,128)(2,1)}, u32[]{:S(2)}, u32[]{:S(2)}) collective-permute-start(bf16[256,2048]{1,0:T(8,128)(2,1)S(1)} %fusion.12), channel_id=1, source_target_pairs={{0,1},{1,0},{2,3},{3,2},{4,5},{5,4},{6,7},{7,6},{8,9},{9,8},{10,11... | collective-permute-start | bytes 3145736 | tf_op jit(solution)/shard_map/ppermute | solution.py:33
  389.5 3.1 collective-permute-start.17
  389.5 25.6 %collective-permute-start.15 = (bf16[256,2048]{1,0:T(8,128)(2,1)S(1)}, bf16[256,2048]{1,0:T(8,128)(2,1)S(1)}, u32[]{:S(2)}, u32[]{:S(2)}) collective-permute-start(bf16[256,2048]{1,0:T(8,128)(2,1)S(1)} %fusion.13), channel_id=1, source_target_pairs={{0,1},{1,0},{2,3},{3,2},{4,5},{5,4},{6,7},{7,6},{8,9},{9,8},{10,11... | collective-permute-start | bytes 3145736 | tf_op jit(solution)/shard_map/ppermute | solution.py:33
  415.1 2.7 collective-permute-start.18
  415.1 63.6 %collective-permute-start.19 = (bf16[512,2048]{1,0:T(8,128)(2,1)}, bf16[512,2048]{1,0:T(8,128)(2,1)}, u32[]{:S(2)}, u32[]{:S(2)}) collective-permute-start(bf16[512,2048]{1,0:T(8,128)(2,1)} %param.16), channel_id=1, source_target_pairs={{2,4},{4,2},{3,5},{5,3},{10,12},{12,10},{11,13},{13,11},{18,20},{2... | collective-permute-start | bytes 6291464 | tf_op jit(solution)/shard_map/ppermute | solution.py:37
  443.8 2.7 collective-permute-start.21
  447.9 41.3 %collective-permute-start.22 = (bf16[256,2048]{1,0:T(8,128)(2,1)}, bf16[256,2048]{1,0:T(8,128)(2,1)S(1)}, u32[]{:S(2)}, u32[]{:S(2)}) collective-permute-start(bf16[256,2048]{1,0:T(8,128)(2,1)} %add_convert_fusion.5), channel_id=1, source_target_pairs={{0,1},{1,0},{2,3},{3,2},{4,5},{5,4},{6,7},{7,6},{8,9},{9,8},{10,11... | collective-permute-start | bytes 3145736 | tf_op jit(solution)/shard_map/ppermute | solution.py:33
  460.8 28.4 %collective-permute-start.20 = (bf16[256,2048]{1,0:T(8,128)(2,1)}, bf16[256,2048]{1,0:T(8,128)(2,1)}, u32[]{:S(2)}, u32[]{:S(2)}) collective-permute-start(bf16[256,2048]{1,0:T(8,128)(2,1)} %slice.205), channel_id=1, source_target_pairs={{0,4},{4,0},{1,5},{5,1},{2,6},{6,2},{3,7},{7,3},{8,12},{12,8},{9,1... | collective-permute-start | bytes 3145736 | tf_op jit(solution)/shard_map/ppermute | solution.py:33
  478.7 18.0 %collective-permute-start.26 = (bf16[256,2048]{1,0:T(8,128)(2,1)S(1)}, bf16[256,2048]{1,0:T(8,128)(2,1)S(1)}, u32[]{:S(2)}, u32[]{:S(2)}) collective-permute-start(bf16[256,2048]{1,0:T(8,128)(2,1)S(1)} %slice.213), channel_id=1, source_target_pairs={{0,4},{4,0},{1,5},{5,1},{2,6},{6,2},{3,7},{7,3},{8,12},{12,8},{9,1... | collective-permute-start | bytes 3145736 | tf_op jit(solution)/shard_map/ppermute | solution.py:33
  480.5 59.0 %copy-start.7 = (bf16[512,2048]{1,0:T(8,128)(2,1)}, bf16[512,2048]{1,0:T(8,128)(2,1)S(1)}, u32[]{:S(2)}) copy-start(bf16[512,2048]{1,0:T(8,128)(2,1)S(1)} %broadcast_select_fusion.1) | copy-start | bytes 6291460
  496.6 4.7 collective-permute-start.23
  498.1 31.9 %collective-permute-start.27 = (bf16[256,2048]{1,0:T(8,128)(2,1)}, bf16[256,2048]{1,0:T(8,128)(2,1)}, u32[]{:S(2)}, u32[]{:S(2)}) collective-permute-start(bf16[256,2048]{1,0:T(8,128)(2,1)} %add_convert_fusion.4), channel_id=1, source_target_pairs={{0,1},{1,0},{2,3},{3,2},{4,5},{5,4},{6,7},{7,6},{8,9},{9,8},{10,11... | collective-permute-start | bytes 3145736 | tf_op jit(solution)/shard_map/ppermute | solution.py:33
  499.7 30.3 %collective-permute-start.25 = (bf16[256,2048]{1,0:T(8,128)(2,1)}, bf16[256,2048]{1,0:T(8,128)(2,1)}, u32[]{:S(2)}, u32[]{:S(2)}) collective-permute-start(bf16[256,2048]{1,0:T(8,128)(2,1)} %slice.211), channel_id=1, source_target_pairs={{0,4},{4,0},{1,5},{5,1},{2,6},{6,2},{3,7},{7,3},{8,12},{12,8},{9,1... | collective-permute-start | bytes 3145736 | tf_op jit(solution)/shard_map/ppermute | solution.py:33
  499.7 47.1 %collective-permute-start.31 = (bf16[256,2048]{1,0:T(8,128)(2,1)}, bf16[256,2048]{1,0:T(8,128)(2,1)}, u32[]{:S(2)}, u32[]{:S(2)}) collective-permute-start(bf16[256,2048]{1,0:T(8,128)(2,1)} %fusion.8), channel_id=1, source_target_pairs={{0,1},{1,0},{2,3},{3,2},{4,5},{5,4},{6,7},{7,6},{8,9},{9,8},{10,11... | collective-permute-start | bytes 3145736 | tf_op jit(solution)/shard_map/ppermute | solution.py:33
  542.0 4.8 collective-permute-start.29
  542.1 31.8 %collective-permute-start.28 = (bf16[256,2048]{1,0:T(8,128)(2,1)S(1)}, bf16[256,2048]{1,0:T(8,128)(2,1)S(1)}, u32[]{:S(2)}, u32[]{:S(2)}) collective-permute-start(bf16[256,2048]{1,0:T(8,128)(2,1)S(1)} %fusion.5), channel_id=1, source_target_pairs={{0,1},{1,0},{2,3},{3,2},{4,5},{5,4},{6,7},{7,6},{8,9},{9,8},{10,11... | collective-permute-start | bytes 3145736 | tf_op jit(solution)/shard_map/ppermute | solution.py:33
  546.8 29.0 %collective-permute-start.32 = (bf16[256,2048]{1,0:T(8,128)(2,1)}, bf16[256,2048]{1,0:T(8,128)(2,1)}, u32[]{:S(2)}, u32[]{:S(2)}) collective-permute-start(bf16[256,2048]{1,0:T(8,128)(2,1)} %collective-permute-done.31), channel_id=1, source_target_pairs={{0,4},{4,0},{1,5},{5,1},{2,6},{6,2},{3,7},{7,3},{8,12},{12,8},{9,1... | collective-permute-start | bytes 3145736 | tf_op jit(solution)/shard_map/ppermute | solution.py:33
  573.9 3.3 collective-permute-start.30
  603.6 277.4 %reduce-scatter.6.cloned.1.call-start = ((), (), s32[]{:S(2)}) async-start(), calls=%async_computation.7 | async-start | bytes 10485760 | tf_op jit(solution)/shard_map/reduce_scatter | solution.py:73
  631.9 2.7 collective-permute-start.33
  635.0 26.7 %collective-permute-start.34 = (bf16[256,2048]{1,0:T(8,128)(2,1)S(1)}, bf16[256,2048]{1,0:T(8,128)(2,1)S(1)}, u32[]{:S(2)}, u32[]{:S(2)}) collective-permute-start(bf16[256,2048]{1,0:T(8,128)(2,1)S(1)} %add_convert_fusion.3), channel_id=1, source_target_pairs={{0,1},{1,0},{2,3},{3,2},{4,5},{5,4},{6,7},{7,6},{8,9},{9,8},{10,11... | collective-permute-start | bytes 3145736 | tf_op jit(solution)/shard_map/ppermute | solution.py:33
  663.2 2.7 collective-permute-start.38
  663.7 5.0 collective-permute-start.24
  667.3 29.3 %collective-permute-start.39 = (bf16[256,2048]{1,0:T(8,128)(2,1)}, bf16[256,2048]{1,0:T(8,128)(2,1)}, u32[]{:S(2)}, u32[]{:S(2)}) collective-permute-start(bf16[256,2048]{1,0:T(8,128)(2,1)} %add_convert_fusion.2), channel_id=1, source_target_pairs={{0,1},{1,0},{2,3},{3,2},{4,5},{5,4},{6,7},{7,6},{8,9},{9,8},{10,11... | collective-permute-start | bytes 3145736 | tf_op jit(solution)/shard_map/ppermute | solution.py:33
  672.0 74.5 %copy-start.20 = (bf16[256,2048]{1,0:T(8,128)(2,1)}, bf16[256,2048]{1,0:T(8,128)(2,1)S(1)}, u32[]{:S(2)}) copy-start(bf16[256,2048]{1,0:T(8,128)(2,1)S(1)} %subtract_convert_fusion.1.refs_1_.refs_0_) | copy-start | bytes 3145732
  696.6 190.0 %reduce-scatter.8.cloned.1.call-start = ((), (), s32[]{:S(2)}) async-start(), calls=%async_computation.8 | async-start | bytes 10485760 | tf_op jit(solution)/shard_map/reduce_scatter | solution.py:73
  698.2 2.7 collective-permute-start.37
  698.3 32.5 %collective-permute-start.36 = (bf16[256,2048]{1,0:T(8,128)(2,1)S(1)}, bf16[256,2048]{1,0:T(8,128)(2,1)}, u32[]{:S(2)}, u32[]{:S(2)}) collective-permute-start(bf16[256,2048]{1,0:T(8,128)(2,1)S(1)} %subtract_convert_fusion.1.refs_1_.refs_0_), channel_id=1, source_target_pairs={{0,1},{1,0},{2,3},{3,2},{4,5},{5,4},{6,7},{7,6},{8,9},{9,8},{10,11... | collective-permute-start | bytes 3145736 | tf_op jit(solution)/shard_map/ppermute | solution.py:33
  705.7 40.8 %collective-permute-start.42 = (bf16[256,2048]{1,0:T(8,128)(2,1)}, bf16[256,2048]{1,0:T(8,128)(2,1)}, u32[]{:S(2)}, u32[]{:S(2)}) collective-permute-start(bf16[256,2048]{1,0:T(8,128)(2,1)} %subtract_convert_fusion.refs_5_.refs_4_), channel_id=1, source_target_pairs={{0,1},{1,0},{2,3},{3,2},{4,5},{5,4},{6,7},{7,6},{8,9},{9,8},{10,11... | collective-permute-start | bytes 3145736 | tf_op jit(solution)/shard_map/ppermute | solution.py:33
  746.5 7.4 collective-permute-start.35
  746.6 8.0 collective-permute-start.40
  748.5 86.8 %collective-permute-start.46 = (bf16[512,2048]{1,0:T(8,128)(2,1)}, bf16[512,2048]{1,0:T(8,128)(2,1)}, u32[]{:S(2)}, u32[]{:S(2)}) collective-permute-start(bf16[512,2048]{1,0:T(8,128)(2,1)} %pad_maximum_fusion.7), channel_id=1, source_target_pairs={{2,4},{4,2},{3,5},{5,3},{10,12},{12,10},{11,13},{13,11},{18,20},{2... | collective-permute-start | bytes 6291464 | tf_op jit(solution)/shard_map/ppermute | solution.py:37
  750.6 12.0 %collective-permute-start.41 = (bf16[256,2048]{1,0:T(8,128)(2,1)}, bf16[256,2048]{1,0:T(8,128)(2,1)}, u32[]{:S(2)}, u32[]{:S(2)}) collective-permute-start(bf16[256,2048]{1,0:T(8,128)(2,1)} %subtract_convert_fusion.refs_5_.refs_4_), channel_id=1, source_target_pairs={{0,4},{4,0},{1,5},{5,1},{2,6},{6,2},{3,7},{7,3},{8,12},{12,8},{9,1... | collective-permute-start | bytes 3145736 | tf_op jit(solution)/shard_map/ppermute | solution.py:33
  750.7 11.9 %collective-permute-start.43 = (bf16[256,2048]{1,0:T(8,128)(2,1)}, bf16[256,2048]{1,0:T(8,128)(2,1)}, u32[]{:S(2)}, u32[]{:S(2)}) collective-permute-start(bf16[256,2048]{1,0:T(8,128)(2,1)} %collective-permute-done.42.refs_7_.refs_6_), channel_id=1, source_target_pairs={{0,4},{4,0},{1,5},{5,1},{2,6},{6,2},{3,7},{7,3},{8,12},{12,8},{9,1... | collective-permute-start | bytes 3145736 | tf_op jit(solution)/shard_map/ppermute | solution.py:33
  753.8 25.6 %copy-start.29 = (bf16[256,2048]{1,0:T(8,128)(2,1)}, bf16[256,2048]{1,0:T(8,128)(2,1)S(1)}, u32[]{:S(2)}) copy-start(bf16[256,2048]{1,0:T(8,128)(2,1)S(1)} %get-tuple-element.269) | copy-start | bytes 3145732
  753.8 81.5 %collective-permute-start.44 = (bf16[256,2048]{1,0:T(8,128)(2,1)S(1)}, bf16[256,2048]{1,0:T(8,128)(2,1)S(1)}, u32[]{:S(2)}, u32[]{:S(2)}) collective-permute-start(bf16[256,2048]{1,0:T(8,128)(2,1)S(1)} %get-tuple-element.269), channel_id=1, source_target_pairs={{2,4},{4,2},{3,5},{5,3},{10,12},{12,10},{11,13},{13,11},{18,20},{2... | collective-permute-start | bytes 3145736 | tf_op jit(solution)/shard_map/ppermute | solution.py:37
  754.6 90.3 %collective-permute-start.45 = (bf16[256,2048]{1,0:T(8,128)(2,1)}, bf16[256,2048]{1,0:T(8,128)(2,1)}, u32[]{:S(2)}, u32[]{:S(2)}) collective-permute-start(bf16[256,2048]{1,0:T(8,128)(2,1)} %get-tuple-element.357), channel_id=1, source_target_pairs={{2,0},{6,2},{4,6},{0,4},{3,1},{7,3},{5,7},{1,5},{10,8},{14,10},{12... | collective-permute-start | bytes 3145736 | tf_op jit(solution)/shard_map/ppermute | solution.py:80
  835.4 23.8 %copy-start.35 = (bf16[256,2048]{1,0:T(8,128)(2,1)}, bf16[256,2048]{1,0:T(8,128)(2,1)S(1)}, u32[]{:S(2)}) copy-start(bf16[256,2048]{1,0:T(8,128)(2,1)S(1)} %collective-permute-done.44) | copy-start | bytes 3145732
  859.2 1.5 collective-permute-start.47
  861.4 4.4 collective-permute-start.48
  884.0 72.9 %collective-permute-start.49 = (bf16[256,2048]{1,0:T(8,128)(2,1)}, bf16[256,2048]{1,0:T(8,128)(2,1)}, u32[]{:S(2)}, u32[]{:S(2)}) collective-permute-start(bf16[256,2048]{1,0:T(8,128)(2,1)} %get-tuple-element.263), channel_id=1, source_target_pairs={{2,4},{4,2},{3,5},{5,3},{10,12},{12,10},{11,13},{13,11},{18,20},{2... | collective-permute-start | bytes 3145736 | tf_op jit(solution)/shard_map/ppermute | solution.py:37
  885.7 72.1 %collective-permute-start.50 = (bf16[256,2048]{1,0:T(8,128)(2,1)}, bf16[256,2048]{1,0:T(8,128)(2,1)}, u32[]{:S(2)}, u32[]{:S(2)}) collective-permute-start(bf16[256,2048]{1,0:T(8,128)(2,1)} %get-tuple-element.355), channel_id=1, source_target_pairs={{2,0},{6,2},{4,6},{0,4},{3,1},{7,3},{5,7},{1,5},{10,8},{14,10},{12... | collective-permute-start | bytes 3145736 | tf_op jit(solution)/shard_map/ppermute | solution.py:80
  889.7 68.2 %collective-permute-start.51 = (bf16[256,2048]{1,0:T(8,128)(2,1)}, bf16[256,2048]{1,0:T(8,128)(2,1)}, u32[]{:S(2)}, u32[]{:S(2)}) collective-permute-start(bf16[256,2048]{1,0:T(8,128)(2,1)} %get-tuple-element.266), channel_id=1, source_target_pairs={{2,4},{4,2},{3,5},{5,3},{10,12},{12,10},{11,13},{13,11},{18,20},{2... | collective-permute-start | bytes 3145736 | tf_op jit(solution)/shard_map/ppermute | solution.py:37
  891.3 89.0 %collective-permute-start.52 = (bf16[256,2048]{1,0:T(8,128)(2,1)}, bf16[256,2048]{1,0:T(8,128)(2,1)}, u32[]{:S(2)}, u32[]{:S(2)}) collective-permute-start(bf16[256,2048]{1,0:T(8,128)(2,1)} %get-tuple-element.353), channel_id=1, source_target_pairs={{2,0},{6,2},{4,6},{0,4},{3,1},{7,3},{5,7},{1,5},{10,8},{14,10},{12... | collective-permute-start | bytes 3145736 | tf_op jit(solution)/shard_map/ppermute | solution.py:80
  (43 other events, 208.3 us)
Sparse Core Ops, SparseCore 0:
  145.9 93.6 all-gather.3
  241.5 87.6 all-gather.5
  331.0 87.6 all-gather.7
  603.7 85.9 reduce-scatter.3
  696.7 86.2 reduce-scatter.5
  785.9 86.3 reduce-scatter.7

commit v5 on v4

--- a/solution.py
+++ b/solution.py
@@ -803,10 +803,13 @@
 
 
 def row_sums(values):
-    ones = jnp.ones((8, values.shape[1]), jnp.float32)
+    ones = jnp.ones((8, HDIM), jnp.float32)
+    folded = sum(
+        values[:, first : first + HDIM] for first in range(0, values.shape[1], HDIM)
+    )
     return lax.dot_general(
         ones,
-        values,
+        folded,
         (((1,), (1,)), ((), ())),
         precision=lax.Precision.HIGHEST,
         preferred_element_type=jnp.float32,
@@ -973,7 +976,7 @@
     carried = lax.fori_loop(block, high_ref[block] + 1, step, ((zero, zero),) * heads)
     for head, (dk, dv) in enumerate(carried):
         dk_ref[:, head_columns(head)] = dk * scale
-        dv_ref[:, head_columns(head)] = dv
+        dv_ref[:, head_columns(head)] = dv.astype(jnp.bfloat16)
 
     @pl.when(block == blocks - 1)
     def _():
@@ -999,7 +1002,7 @@
             out_specs=[whole, own, own],
             scratch_shapes=[pltpu.VMEM((heads, 1, rows), jnp.float32)],
         ),
-        out_shape=[out] * 3,
+        out_shape=[out, out, jax.ShapeDtypeStruct((rows, width), jnp.bfloat16)],
         compiler_params=pltpu.CompilerParams(vmem_limit_bytes=VMEM_BYTES),
         cost_estimate=BESIDE,
         name="attention_backward",
@@ -1049,7 +1052,7 @@
         in_specs=[
             own,
             own,
-            pl.BlockSpec((BLOCK, 3 * width), lambda i: (i, 0)),
+            pl.BlockSpec((BLOCK, 2 * width), lambda i: (i, 0)),
             pair,
             whole,
             whole,
@@ -1080,7 +1083,7 @@
             base = index * width + head * HDIM
             value = rstd * gain[:, cols] * grad[:, cols] - raw[:, base : base + HDIM] * share
             out[:, base : base + HDIM] = value.astype(jnp.bfloat16)
-    out[:, 2 * width :] = dv_ref[...].astype(jnp.bfloat16)
+    out[:, 2 * width :] = dv_ref[...]
 
 
 def raw_grads(d_q_norm, d_k_norm, d_v, raw, squares, dots, gain_q, gain_k):
@@ -1092,7 +1095,16 @@
     return pl.pallas_call(
         raw_grads_kernel,
         grid=(rows // BLOCK,),
-        in_specs=[own, own, own, wide, pair, pair, whole, whole],
+        in_specs=[
+            own,
+            own,
+            own,
+            pl.BlockSpec((BLOCK, 2 * width), lambda i: (i, 0)),
+            pair,
+            pair,
+            whole,
+            whole,
+        ],
         out_specs=wide,
         out_shape=jax.ShapeDtypeStruct((rows, 3 * width), jnp.bfloat16),
         cost_estimate=BESIDE,
@@ -1631,9 +1643,9 @@
     qkv_totals = stacked_weight_grad(packed, d_qkv_b, 3)
     up_split = start_split(after(d_qkv_b, up_sum))
     _, input_parts = give_back(perm_place, d_qkv_b, qkv_full)
+    down_shard, layer_out = finish_split(*down_split).T, finish_turn(*layer_turn)
+    qkv_totals, down_shard, layer_out = lax.optimization_barrier((qkv_totals, down_shard, layer_out))
     input_parts, gate_split, up_split = lax.optimization_barrier((input_parts, gate_split, up_split))
-    layer_out = finish_turn(*layer_turn)
-    down_shard = finish_split(*down_split).T
     gate_shard, up_shard = finish_split(*gate_split), finish_split(*up_split)
 
     def placed(part_sum):

time: 1140 us -> 1140 us (level)
  Pallas kernels: 801 us -> 785 us
  transfers between devices with their start and end apart: 59 -> 59, of which waited for: 21 -> 22; matrix products, arithmetic and copies ran while one was open for 10% -> 10% of each run, Pallas kernels for 45% -> 43%
where the time goes in v5:
time: 1140 us; the launch traced here: 1130 us
  Pallas kernels  785 us (69%)
  waiting for transfers between devices  127 us (11%)
  other arithmetic  93.7 us (8%)
  starting transfers between devices  51.2 us (4%)
  local copies, waits for them, and re-layouts  50.7 us (4%)
  between operations  17.1 us (2%)
    pallas_call x1, Pallas kernels, leave(): pl.pallas_call(functools.partial(leave_kernel, tuple(cuts), paired, stack...  138 us
    pallas_call x1, Pallas kernels, enter(): pl.pallas_call(functools.partial(entry_kernel, tuple(plan)), in_specs=[an...  137 us
    pallas_call x8, Pallas kernels, sum_products(): pl.pallas_call(functools.partial(products_kernel, len(lefts)), grid=(widt...  91.8 us
    ppermute x41, waiting for transfers between devices, swap(): return lax.ppermute(value, axis, SWAP)  89.2 us
    pallas_call x4, Pallas kernels, weight_grad(): pl.pallas_call(functools.partial(weight_grad_kernel, len(lefts)), grid=(w...  82.3 us
    pallas_call x4, Pallas kernels, hidden_units(): pl.pallas_call(hidden_kernel, grid=(width // block,), in_specs=[pl.BlockS...  58.2 us
    pallas_call x4, Pallas kernels, hidden_grads(): pl.pallas_call(hidden_grads_kernel, grid=(width // block,), in_specs=[pl....  47.4 us
    pallas_call x2, Pallas kernels, give_back(): pl.pallas_call(functools.partial(given_kernel, count), grid=(rows // coun...  45.9 us
  transfers between devices with their start and end apart: 59, of which 22 were waited for; matrix products, arithmetic and copies ran while one was open for 10% of the time, Pallas kernels for 43%

profile of v5, /device:TPU:0, one launch (start us, length us, event | category | flops | bytes accessed | tf_op | source)
XLA Modules:
  0.0 1125.2 jit_solution(4111749555638953258)
XLA Ops:
  9.0 136.7 %enter.1 = (bf16[2048,2048]{1,0:T(8,128)(2,1)}, bf16[2048,1536]{1,0:T(8,128)(2,1)}, bf16[2048,512]{1,0:T(8,128)(2,1)}, bf16[512,2048]{1,0:T(8,128)(2,1)}) custom-call(bf16[512,2048]{1,0:T(8,128)(2,1)} %refs_0_.1, bf16[256,512]{1,0:T(8,128)(2,1)} %refs_1_.1, bf16[256,512]{1,0:T(8,128)(2,1)} %refs_2_.1, bf16[256,512]{1,0:T(8,128)(2,1)} %refs_3_.1, ...), custom_call_target="tpu_custom_call" | custom-call | flops 1 | bytes 1 | tf_op jit(solution)/shard_map/enter/pallas_call | solution.py:700
  146.5 5.4 collective-permute-start
  154.9 40.7 %pack.1 = (bf16[2048,2048]{1,0:T(8,128)(2,1)}, f32[2048,1536]{1,0:T(8,128)}, f32[2,2048]{1,0:T(2,128)}) custom-call(s32[2048,1]{1,0:T(8,128)} %copy.51.places, bf16[2048,2048]{1,0:T(8,128)(2,1)} %get-tuple-element.147.tokens_ref, bf16[2048,1536]{1,0:T(8,128)(2,1)} %get-tuple-element.148.weight), custom_call_target="tpu_custom_call" | custom-call | flops 1 | bytes 1 | tf_op jit(solution)/shard_map/pack/pallas_call | solution.py:1305
  202.0 5.1 collective-permute-start.3
  212.6 2.7 collective-permute-done.4
  217.9 3.7 fusion.31
  224.2 11.9 %prepare.1 = (bf16[2048,512]{1,0:T(8,128)(2,1)}, bf16[2048,512]{1,0:T(8,128)(2,1)}, bf16[2048,512]{1,0:T(8,128)(2,1)}) custom-call(f32[2048,1536]{1,0:T(8,128)} %get-tuple-element.152.raw, f32[2,2048]{1,0:T(2,128)} %add.315.squares, f32[1,512]{1,0:T(1,128)} %bitcast.25, f32[1,512]{1,0:T(1,128)} %bitcast.28, f32[2048,128]{1,0:T(8,128)} %pad_maximum_fusion.8.cosine, ...), custom_call_target="tpu_custom_call" | custom-call | flops 1 | bytes 1 | tf_op jit(solution)/shard_map/prepare/pallas_call | solution.py:843
  237.7 27.4 %attention_forward.1 = (bf16[2048,512]{1,0:T(8,128)(2,1)S(1)}, f32[2048,512]{1,0:T(8,128)}, f32[4,1,2048]{2,1,0:T(1,128)S(1)}) custom-call(s32[8]{0:T(128)S(1)} %and_select_fusion.8.low_ref, bf16[2048,512]{1,0:T(8,128)(2,1)S(1)} %copy-done, bf16[2048,512]{1,0:T(8,128)(2,1)} %get-tuple-element.156.k_ref, bf16[2048,512]{1,0:T(8,128)(2,1)} %get-tuple-element.157.v_ref, ...), custom_call_target="tpu_custom_call" | custom-call | flops 1 | bytes 1 | tf_op jit(solution)/shard_map/attention_forward/pallas_call | solution.py:913
  266.3 13.0 %give_back.2 = (bf16[2048,512]{1,0:T(8,128)(2,1)}, bf16[2048,2048]{1,0:T(8,128)(2,1)}) custom-call(s32[1,2048]{1,0:T(1,128)} %get-tuple-element.369.places, bf16[2048,512]{1,0:T(8,128)(2,1)} %copy-done.3, bf16[2048,512]{1,0:T(8,128)(2,1)} %get-tuple-element.160.weight.refs_9_), custom_call_target="tpu_custom_call" | custom-call | flops 1 | bytes 1 | tf_op jit(solution)/shard_map/give_back/pallas_call | solution.py:1339
  281.7 4.7 fusion.37
  291.1 3.1 add_convert_fusion.6
  296.1 23.7 %collective-permute-done.9 = bf16[256,2048]{1,0:T(8,128)(2,1)S(1)} collective-permute-done((bf16[256,2048]{1,0:T(8,128)(2,1)S(1)}, bf16[256,2048]{1,0:T(8,128)(2,1)S(1)}, u32[]{:S(2)}, u32[]{:S(2)}) %collective-permute-start.9) | collective-permute-done | bytes 1048608 | tf_op jit(solution)/shard_map/ppermute | solution.py:33
  326.1 2.9 pad_maximum_fusion.3.x_ref.refs_0_
  329.1 15.1 %hidden_units.4 = (f32[512,2048]{1,0:T(8,128)}, f32[512,2048]{1,0:T(8,128)}, bf16[512,2048]{1,0:T(8,128)(2,1)}) custom-call(bf16[512,2048]{1,0:T(8,128)(2,1)} %pad_maximum_fusion.3.x_ref.refs_0_, bf16[2048,2048]{1,0:T(8,128)(2,1)} %all-gather.4.cloned.1.call-done.gate_w.refs_2_, bf16[2048,2048]{1,0:T(8,128)(2,1)} %all-gather.6.cloned.1.call-done.up_w.refs_3_), custom_call_target="tpu_custom_call" | custom-call | flops 1 | bytes 1 | tf_op jit(solution)/shard_map/hidden_units/pallas_call | solution.py:1153
  344.3 4.9 collective-permute-done.12
  349.2 2.4 multiply_reduce_fusion.6
  358.3 14.4 %hidden_units.5 = (f32[512,2048]{1,0:T(8,128)}, f32[512,2048]{1,0:T(8,128)}, bf16[512,2048]{1,0:T(8,128)(2,1)}) custom-call(bf16[512,2048]{1,0:T(8,128)(2,1)} %pad_maximum_fusion.4.x_ref.refs_2_, bf16[2048,2048]{1,0:T(8,128)(2,1)} %all-gather.4.cloned.1.call-done.gate_w.refs_2_, bf16[2048,2048]{1,0:T(8,128)(2,1)} %all-gather.6.cloned.1.call-done.up_w.refs_3_), custom_call_target="tpu_custom_call" | custom-call | flops 1 | bytes 1 | tf_op jit(solution)/shard_map/hidden_units/pallas_call | solution.py:1153
  372.7 7.1 collective-permute-done.16
  384.3 14.4 %hidden_units.6 = (f32[512,2048]{1,0:T(8,128)}, f32[512,2048]{1,0:T(8,128)}, bf16[512,2048]{1,0:T(8,128)(2,1)}) custom-call(bf16[512,2048]{1,0:T(8,128)(2,1)} %copy-done.9, bf16[2048,2048]{1,0:T(8,128)(2,1)} %all-gather.4.cloned.1.call-done.gate_w.refs_2_, bf16[2048,2048]{1,0:T(8,128)(2,1)} %all-gather.6.cloned.1.call-done.up_w.refs_3_), custom_call_target="tpu_custom_call" | custom-call | flops 1 | bytes 1 | tf_op jit(solution)/shard_map/hidden_units/pallas_call | solution.py:1153
  398.6 6.7 collective-permute-done.15
  409.5 14.3 %hidden_units.7 = (f32[512,2048]{1,0:T(8,128)}, f32[512,2048]{1,0:T(8,128)}, bf16[512,2048]{1,0:T(8,128)(2,1)}) custom-call(bf16[512,2048]{1,0:T(8,128)(2,1)} %copy-done.10, bf16[2048,2048]{1,0:T(8,128)(2,1)} %all-gather.4.cloned.1.call-done.gate_w.refs_2_, bf16[2048,2048]{1,0:T(8,128)(2,1)} %all-gather.6.cloned.1.call-done.up_w.refs_3_), custom_call_target="tpu_custom_call" | custom-call | flops 1 | bytes 1 | tf_op jit(solution)/shard_map/hidden_units/pallas_call | solution.py:1153
  423.8 8.8 sum_products.8
  441.2 8.8 sum_products.9
  452.5 8.9 sum_products.10
  461.3 9.0 sum_products.11
  472.3 7.2 collective-permute-done.22
  483.6 3.4 fusion.8
  491.7 2.9 pad_maximum_fusion.5.grad_ref.refs_0_
  494.6 11.6 %hidden_grads.4 = (bf16[512,2048]{1,0:T(8,128)(2,1)}, bf16[512,2048]{1,0:T(8,128)(2,1)}) custom-call(bf16[512,2048]{1,0:T(8,128)(2,1)} %pad_maximum_fusion.5.grad_ref.refs_0_, bf16[2048,2048]{1,0:T(8,128)(2,1)} %all-gather.8.cloned.1.call-done.refs_1_.weight, f32[512,2048]{1,0:T(8,128)} %get-tuple-element.186.gate_ref, f32[512,2048]{1,0:T(8,128)} %get-tuple-element.187.up_ref), custom_call_target="tpu_custom_call" | custom-call | flops 1 | bytes 1 | tf_op jit(solution)/shard_map/hidden_grads/pallas_call | solution.py:1186
  506.2 14.1 %sum_products.12 = bf16[512,2048]{1,0:T(8,128)(2,1)} custom-call(bf16[512,2048]{1,0:T(8,128)(2,1)} %get-tuple-element.223.refs_0_.refs_4_, bf16[512,2048]{1,0:T(8,128)(2,1)} %get-tuple-element.232.refs_1_.refs_4_, bf16[2048,2048]{1,0:T(8,128)(2,1)} %all-gather.4.cloned.1.call-done.gate_w.refs_2_, bf16[2048,2048]{1,0:T(8,128)(2,1)} %all-gather.6.cloned.1.call-done.up_w.refs_3_), custom_call_target="tpu_custom_call" | custom-call | flops 1 | bytes 1 | tf_op jit(solution)/shard_map/sum_products/pallas_call | solution.py:1215
  520.3 2.6 multiply_reduce_fusion.4
  522.9 6.9 add_convert_fusion.1
  529.8 2.5 fusion.5
  533.1 4.0 collective-permute-done.31
  538.7 11.6 %hidden_grads.5 = (bf16[512,2048]{1,0:T(8,128)(2,1)}, bf16[512,2048]{1,0:T(8,128)(2,1)}) custom-call(bf16[512,2048]{1,0:T(8,128)(2,1)} %pad_maximum_fusion.6.grad_ref.refs_2_, bf16[2048,2048]{1,0:T(8,128)(2,1)} %all-gather.8.cloned.1.call-done.refs_1_.weight, f32[512,2048]{1,0:T(8,128)} %get-tuple-element.193.gate_ref, f32[512,2048]{1,0:T(8,128)} %get-tuple-element.194.up_ref), custom_call_target="tpu_custom_call" | custom-call | flops 1 | bytes 1 | tf_op jit(solution)/shard_map/hidden_grads/pallas_call | solution.py:1186
  550.3 13.9 %sum_products.13 = bf16[512,2048]{1,0:T(8,128)(2,1)} custom-call(bf16[512,2048]{1,0:T(8,128)(2,1)} %get-tuple-element.225.refs_0_.refs_6_, bf16[512,2048]{1,0:T(8,128)(2,1)} %get-tuple-element.234.refs_1_.refs_6_, bf16[2048,2048]{1,0:T(8,128)(2,1)} %all-gather.4.cloned.1.call-done.gate_w.refs_2_, bf16[2048,2048]{1,0:T(8,128)(2,1)} %all-gather.6.cloned.1.call-done.up_w.refs_3_), custom_call_target="tpu_custom_call" | custom-call | flops 1 | bytes 1 | tf_op jit(solution)/shard_map/sum_products/pallas_call | solution.py:1215
  570.1 23.8 %weight_grad.4 = bf16[2048,2048]{1,0:T(8,128)(2,1)} custom-call(bf16[512,2048]{1,0:T(8,128)(2,1)} %pad_maximum_fusion.5.grad_ref.refs_0_, bf16[512,2048]{1,0:T(8,128)(2,1)} %copy-done.19, bf16[512,2048]{1,0:T(8,128)(2,1)} %pad_maximum_fusion.6.grad_ref.refs_2_, bf16[512,2048]{1,0:T(8,128)(2,1)} %copy-done.18, ...), custom_call_target="tpu_custom_call" | custom-call | flops 1 | bytes 1 | tf_op jit(solution)/shard_map/weight_grad/pallas_call | solution.py:1244
  594.0 12.0 %hidden_grads.6 = (bf16[512,2048]{1,0:T(8,128)(2,1)}, bf16[512,2048]{1,0:T(8,128)(2,1)}) custom-call(bf16[512,2048]{1,0:T(8,128)(2,1)} %copy-done.19, bf16[2048,2048]{1,0:T(8,128)(2,1)} %all-gather.8.cloned.1.call-done.refs_1_.weight, f32[512,2048]{1,0:T(8,128)} %get-tuple-element.205.gate_ref, f32[512,2048]{1,0:T(8,128)} %get-tuple-element.206.up_ref), custom_call_target="tpu_custom_call" | custom-call | flops 1 | bytes 1 | tf_op jit(solution)/shard_map/hidden_grads/pallas_call | solution.py:1186
  606.0 14.1 %sum_products.14 = bf16[512,2048]{1,0:T(8,128)(2,1)} custom-call(bf16[512,2048]{1,0:T(8,128)(2,1)} %get-tuple-element.224.refs_0_.refs_5_, bf16[512,2048]{1,0:T(8,128)(2,1)} %get-tuple-element.233.refs_1_.refs_5_, bf16[2048,2048]{1,0:T(8,128)(2,1)} %all-gather.4.cloned.1.call-done.gate_w.refs_2_, bf16[2048,2048]{1,0:T(8,128)(2,1)} %all-gather.6.cloned.1.call-done.up_w.refs_3_), custom_call_target="tpu_custom_call" | custom-call | flops 1 | bytes 1 | tf_op jit(solution)/shard_map/sum_products/pallas_call | solution.py:1215
  621.7 2.6 collective-permute-done.33
  625.0 12.1 %hidden_grads.7 = (bf16[512,2048]{1,0:T(8,128)(2,1)}, bf16[512,2048]{1,0:T(8,128)(2,1)}) custom-call(bf16[512,2048]{1,0:T(8,128)(2,1)} %copy-done.18, bf16[2048,2048]{1,0:T(8,128)(2,1)} %all-gather.8.cloned.1.call-done.refs_1_.weight, f32[512,2048]{1,0:T(8,128)} %get-tuple-element.211.gate_ref, f32[512,2048]{1,0:T(8,128)} %get-tuple-element.212.up_ref), custom_call_target="tpu_custom_call" | custom-call | flops 1 | bytes 1 | tf_op jit(solution)/shard_map/hidden_grads/pallas_call | solution.py:1186
  637.1 14.2 %sum_products.15 = bf16[512,2048]{1,0:T(8,128)(2,1)} custom-call(bf16[512,2048]{1,0:T(8,128)(2,1)} %get-tuple-element.226.refs_0_.refs_7_, bf16[512,2048]{1,0:T(8,128)(2,1)} %get-tuple-element.235.refs_1_.refs_7_, bf16[2048,2048]{1,0:T(8,128)(2,1)} %all-gather.4.cloned.1.call-done.gate_w.refs_2_, bf16[2048,2048]{1,0:T(8,128)(2,1)} %all-gather.6.cloned.1.call-done.up_w.refs_3_), custom_call_target="tpu_custom_call" | custom-call | flops 1 | bytes 1 | tf_op jit(solution)/shard_map/sum_products/pallas_call | solution.py:1215
  662.1 24.5 %weight_grad.5 = bf16[2048,2048]{1,0:T(8,128)(2,1)} custom-call(bf16[512,2048]{1,0:T(8,128)(2,1)} %pad_maximum_fusion.3.x_ref.refs_0_, bf16[512,2048]{1,0:T(8,128)(2,1)} %copy-done.9, bf16[512,2048]{1,0:T(8,128)(2,1)} %pad_maximum_fusion.4.x_ref.refs_2_, bf16[512,2048]{1,0:T(8,128)(2,1)} %copy-done.10, bf16[512,2048]{1,0:T(8,128)(2,1)} %get-tuple-element.223.refs_0_.refs_4_, ...), custom_call_target="tpu_custom_call" | custom-call | flops 1 | bytes 1 | tf_op jit(solution)/shard_map/weight_grad/pallas_call | solution.py:1244
  691.0 3.0 multiply_reduce_fusion
  696.2 24.8 %weight_grad.6 = bf16[2048,2048]{1,0:T(8,128)(2,1)} custom-call(bf16[512,2048]{1,0:T(8,128)(2,1)} %pad_maximum_fusion.3.x_ref.refs_0_, bf16[512,2048]{1,0:T(8,128)(2,1)} %copy-done.9, bf16[512,2048]{1,0:T(8,128)(2,1)} %pad_maximum_fusion.4.x_ref.refs_2_, bf16[512,2048]{1,0:T(8,128)(2,1)} %copy-done.10, bf16[512,2048]{1,0:T(8,128)(2,1)} %get-tuple-element.232.refs_1_.refs_4_, ...), custom_call_target="tpu_custom_call" | custom-call | flops 1 | bytes 1 | tf_op jit(solution)/shard_map/weight_grad/pallas_call | solution.py:1244
  721.1 15.5 %collective-permute-done.42.refs_7_.refs_6_ = bf16[256,2048]{1,0:T(8,128)(2,1)} collective-permute-done((bf16[256,2048]{1,0:T(8,128)(2,1)}, bf16[256,2048]{1,0:T(8,128)(2,1)}, u32[]{:S(2)}, u32[]{:S(2)}) %collective-permute-start.42) | collective-permute-done | bytes 1048608 | tf_op jit(solution)/shard_map/ppermute | solution.py:33
  745.3 2.9 collective-permute-start.45
  748.2 3.8 fusion.16.refs_0_
  752.0 2.4 pad_maximum_fusion.refs_1_
  754.5 16.6 %pick_products.1.grad_ref = bf16[2048,512]{1,0:T(8,128)(2,1)} custom-call(s32[2048,1]{1,0:T(8,128)} %fusion.16.refs_0_, bf16[256,2048]{1,0:T(8,128)(2,1)} %copy-done.21, bf16[256,2048]{1,0:T(8,128)(2,1)} %collective-permute-done.35.refs_2_.refs_1_, bf16[256,2048]{1,0:T(8,128)(2,1)} %collective-permute-done.36.refs_3_.refs_2_, ...), custom_call_target="tpu_custom_call" | custom-call | flops 1 | bytes 1 | tf_op jit(solution)/shard_map/pick_products/pallas_call | solution.py:1388
  771.1 9.2 weight_grad.7.refs_3_
  780.3 39.2 %attention_backward.1 = (f32[2048,512]{1,0:T(8,128)}, f32[2048,512]{1,0:T(8,128)}, bf16[2048,512]{1,0:T(8,128)(2,1)S(1)}) custom-call(s32[8]{0:T(128)S(1)} %and_select_fusion.9.high_ref, bf16[2048,512]{1,0:T(8,128)(2,1)S(1)} %copy-done.1, bf16[2048,512]{1,0:T(8,128)(2,1)} %get-tuple-element.156.k_ref, bf16[2048,512]{1,0:T(8,128)(2,1)} %get-tuple-element.157.v_ref, ...), custom_call_target="tpu_custom_call" | custom-call | flops 1 | bytes 1 | tf_op jit(solution)/shard_map/attention_backward/pallas_call | solution.py:992
  820.8 13.9 %collective-permute-done.45 = bf16[256,2048]{1,0:T(8,128)(2,1)S(1)} collective-permute-done((bf16[256,2048]{1,0:T(8,128)(2,1)S(1)}, bf16[256,2048]{1,0:T(8,128)(2,1)S(1)}, u32[]{:S(2)}, u32[]{:S(2)}) %collective-permute-start.45) | collective-permute-done | bytes 1048608 | tf_op jit(solution)/shard_map/ppermute | solution.py:80
  834.7 13.0 %norm_grads.1 = (f32[2048,512]{1,0:T(8,128)}, f32[2048,512]{1,0:T(8,128)}, f32[2,2048]{1,0:T(2,128)}, f32[8,512]{1,0:T(8,128)}, f32[8,512]{1,0:T(8,128)}) custom-call(f32[2048,512]{1,0:T(8,128)} %get-tuple-element.244.dq_ref, f32[2048,512]{1,0:T(8,128)} %get-tuple-element.245.dk_ref, f32[2048,1536]{1,0:T(8,128)} %get-tuple-element.152.raw, ...), custom_call_target="tpu_custom_call" | custom-call | flops 1 | bytes 1 | tf_op jit(solution)/shard_map/norm_grads/pallas_call | solution.py:1049
  850.9 3.0 collective-permute-done.48
  854.5 13.6 %raw_grads.1.refs_1_.rows_ref = bf16[2048,1536]{1,0:T(8,128)(2,1)} custom-call(f32[2048,512]{1,0:T(8,128)} %get-tuple-element.246.dq_ref, f32[2048,512]{1,0:T(8,128)} %get-tuple-element.247.dk_ref, bf16[2048,512]{1,0:T(8,128)(2,1)} %copy-done.2, f32[2048,1536]{1,0:T(8,128)} %get-tuple-element.152.raw, f32[2,2048]{1,0:T(2,128)} %add.315.squares, ...), custom_call_target="tpu_custom_call" | custom-call | flops 1 | bytes 1 | tf_op jit(solution)/shard_map/raw_grads/pallas_call | solution.py:1095
  868.1 3.0 broadcast_select_fusion.6
  874.0 3.1 broadcast_select_fusion.4
  882.6 3.1 broadcast_select_fusion
  885.8 32.9 %give_back.3 = (bf16[2048,1536]{1,0:T(8,128)(2,1)}, bf16[2048,2048]{1,0:T(8,128)(2,1)}) custom-call(s32[1,2048]{1,0:T(1,128)} %get-tuple-element.369.places, bf16[2048,1536]{1,0:T(8,128)(2,1)} %raw_grads.1.refs_1_.rows_ref, bf16[2048,1536]{1,0:T(8,128)(2,1)} %get-tuple-element.148.weight), custom_call_target="tpu_custom_call" | custom-call | flops 1 | bytes 1 | tf_op jit(solution)/shard_map/give_back/pallas_call | solution.py:1339
  918.7 22.6 %stacked_weight_grad.1.refs_4_ = bf16[3,2048,512]{2,1,0:T(8,128)(2,1)} custom-call(bf16[2048,2048]{1,0:T(8,128)(2,1)} %get-tuple-element.149.refs_0_, bf16[2048,1536]{1,0:T(8,128)(2,1)} %raw_grads.1.refs_1_.rows_ref), custom_call_target="tpu_custom_call" | custom-call | flops 1 | bytes 1 | tf_op jit(solution)/shard_map/stacked_weight_grad/pallas_call | solution.py:1264
  944.5 22.5 %collective-permute-done.52 = bf16[256,2048]{1,0:T(8,128)(2,1)} collective-permute-done((bf16[256,2048]{1,0:T(8,128)(2,1)}, bf16[256,2048]{1,0:T(8,128)(2,1)}, u32[]{:S(2)}, u32[]{:S(2)}) %collective-permute-start.52) | collective-permute-done | bytes 1048608 | tf_op jit(solution)/shard_map/ppermute | solution.py:80
  967.0 138.1 %leave.1 = (bf16[512,2048]{1,0:T(8,128)(2,1)}, f32[8,2048]{1,0:T(8,128)}, f32[256,512]{1,0:T(8,128)}, f32[256,512]{1,0:T(8,128)}, f32[256,512]{1,0:T(8,128)}, /*index=5*/f32[256,512]{1,0:T(8,128)}) custom-call(bf16[2048,2048]{1,0:T(8,128)(2,1)} %get-tuple-element.261.refs_0_, f32[512,2048]{1,0:T(8,128)} %pad_maximum_fusion.refs_1_, ...), custom_call_target="tpu_custom_call" | custom-call | flops 1 | bytes 1 | tf_op jit(solution)/shard_map/leave/pallas_call | solution.py:659
  1108.8 5.5 convert_add_fusion.2
  (289 shorter events, 136.5 us)
Async XLA Ops:
  7.2 321.8 %all-gather.4.cloned.1.call-start = ((), (), s32[]{:S(2)}) async-start(), calls=%async_computation.3 | async-start | bytes 10485760 | tf_op jit(solution)/shard_map/all_gather | solution.py:69
  145.8 183.3 %all-gather.6.cloned.1.call-start = ((), (), s32[]{:S(2)}) async-start(), calls=%async_computation.4 | async-start | bytes 10485760 | tf_op jit(solution)/shard_map/all_gather | solution.py:69
  146.5 6.3 collective-permute-start
  151.9 43.8 %collective-permute-start.2 = (bf16[256,2048]{1,0:T(8,128)(2,1)S(1)}, bf16[256,2048]{1,0:T(8,128)(2,1)S(1)}, u32[]{:S(2)}, u32[]{:S(2)}) collective-permute-start(bf16[256,2048]{1,0:T(8,128)(2,1)S(1)} %copy-done.35), channel_id=1, source_target_pairs={{0,2},{2,6},{6,4},{4,0},{1,3},{3,7},{7,5},{5,1},{8,10},{10,14},{14... | collective-permute-start | bytes 3145736 | tf_op jit(solution)/shard_map/ppermute | solution.py:64
  152.0 43.6 %collective-permute-start.1 = (bf16[256,2048]{1,0:T(8,128)(2,1)S(1)}, bf16[256,2048]{1,0:T(8,128)(2,1)S(1)}, u32[]{:S(2)}, u32[]{:S(2)}) collective-permute-start(bf16[256,2048]{1,0:T(8,128)(2,1)S(1)} %copy-done.35), channel_id=1, source_target_pairs={{2,4},{4,2},{3,5},{5,3},{10,12},{12,10},{11,13},{13,11},{18,20},{2... | collective-permute-start | bytes 3145736 | tf_op jit(solution)/shard_map/ppermute | solution.py:37
  197.4 226.3 %all-gather.8.cloned.1.call-start = ((), (), s32[]{:S(2)}) async-start(), calls=%async_computation.5 | async-start | bytes 10485760 | tf_op jit(solution)/shard_map/all_gather | solution.py:69
  202.0 9.6 collective-permute-start.3
  211.5 3.8 collective-permute-start.4
  215.9 63.4 %collective-permute-start.6 = (bf16[256,2048]{1,0:T(8,128)(2,1)S(1)}, bf16[256,2048]{1,0:T(8,128)(2,1)S(1)}, u32[]{:S(2)}, u32[]{:S(2)}) collective-permute-start(bf16[256,2048]{1,0:T(8,128)(2,1)S(1)} %bitcast.20), channel_id=1, source_target_pairs={{0,2},{2,6},{6,4},{4,0},{1,3},{3,7},{7,5},{5,1},{8,10},{10,14},{14... | collective-permute-start | bytes 3145736 | tf_op jit(solution)/shard_map/ppermute | solution.py:64
  216.2 63.1 %collective-permute-start.5 = (bf16[256,2048]{1,0:T(8,128)(2,1)S(1)}, bf16[256,2048]{1,0:T(8,128)(2,1)S(1)}, u32[]{:S(2)}, u32[]{:S(2)}) collective-permute-start(bf16[256,2048]{1,0:T(8,128)(2,1)S(1)} %bitcast.21), channel_id=1, source_target_pairs={{2,4},{4,2},{3,5},{5,3},{10,12},{12,10},{11,13},{13,11},{18,20},{2... | collective-permute-start | bytes 3145736 | tf_op jit(solution)/shard_map/ppermute | solution.py:37
  281.1 461.4 %reduce-scatter.4.cloned.1.call-start = ((), (), s32[]{:S(2)}) async-start(), calls=%async_computation.6 | async-start | bytes 10485760 | tf_op jit(solution)/shard_map/reduce_scatter | solution.py:73
  286.4 3.2 collective-permute-start.11
  287.3 3.8 collective-permute-start.8
  287.3 8.7 collective-permute-start.7
  294.2 27.4 %copy-start.41 = (f32[2048]{0:T(1024)S(1)}, f32[2048]{0:T(1024)}, u32[]{:S(2)}) copy-start(f32[2048]{0:T(1024)} %param.28) | copy-start | bytes 24580
  294.2 25.5 %collective-permute-start.9 = (bf16[256,2048]{1,0:T(8,128)(2,1)S(1)}, bf16[256,2048]{1,0:T(8,128)(2,1)S(1)}, u32[]{:S(2)}, u32[]{:S(2)}) collective-permute-start(bf16[256,2048]{1,0:T(8,128)(2,1)S(1)} %get-tuple-element.352), channel_id=1, source_target_pairs={{0,1},{1,0},{2,3},{3,2},{4,5},{5,4},{6,7},{7,6},{8,9},{9,8},{10,11... | collective-permute-start | bytes 3145736 | tf_op jit(solution)/shard_map/ppermute | solution.py:33
  323.2 2.9 collective-permute-start.13
  323.3 25.9 %collective-permute-start.12 = (bf16[256,2048]{1,0:T(8,128)(2,1)}, bf16[256,2048]{1,0:T(8,128)(2,1)}, u32[]{:S(2)}, u32[]{:S(2)}) collective-permute-start(bf16[256,2048]{1,0:T(8,128)(2,1)} %get-tuple-element.351), channel_id=1, source_target_pairs={{0,1},{1,0},{2,3},{3,2},{4,5},{5,4},{6,7},{7,6},{8,9},{9,8},{10,11... | collective-permute-start | bytes 3145736 | tf_op jit(solution)/shard_map/ppermute | solution.py:33
  325.1 24.1 %collective-permute-start.10 = (bf16[256,2048]{1,0:T(8,128)(2,1)}, bf16[256,2048]{1,0:T(8,128)(2,1)}, u32[]{:S(2)}, u32[]{:S(2)}) collective-permute-start(bf16[256,2048]{1,0:T(8,128)(2,1)} %get-tuple-element.347), channel_id=1, source_target_pairs={{0,4},{4,0},{1,5},{5,1},{2,6},{6,2},{3,7},{7,3},{8,12},{12,8},{9,1... | collective-permute-start | bytes 3145736 | tf_op jit(solution)/shard_map/ppermute | solution.py:33
  354.0 2.7 collective-permute-start.14
  354.1 25.7 %collective-permute-start.16 = (bf16[256,2048]{1,0:T(8,128)(2,1)S(1)}, bf16[256,2048]{1,0:T(8,128)(2,1)}, u32[]{:S(2)}, u32[]{:S(2)}) collective-permute-start(bf16[256,2048]{1,0:T(8,128)(2,1)S(1)} %fusion.12), channel_id=1, source_target_pairs={{0,1},{1,0},{2,3},{3,2},{4,5},{5,4},{6,7},{7,6},{8,9},{9,8},{10,11... | collective-permute-start | bytes 3145736 | tf_op jit(solution)/shard_map/ppermute | solution.py:33
  379.8 3.1 collective-permute-start.17
  379.8 25.6 %collective-permute-start.15 = (bf16[256,2048]{1,0:T(8,128)(2,1)S(1)}, bf16[256,2048]{1,0:T(8,128)(2,1)S(1)}, u32[]{:S(2)}, u32[]{:S(2)}) collective-permute-start(bf16[256,2048]{1,0:T(8,128)(2,1)S(1)} %fusion.13), channel_id=1, source_target_pairs={{0,1},{1,0},{2,3},{3,2},{4,5},{5,4},{6,7},{7,6},{8,9},{9,8},{10,11... | collective-permute-start | bytes 3145736 | tf_op jit(solution)/shard_map/ppermute | solution.py:33
  405.3 2.7 collective-permute-start.18
  405.4 65.0 %collective-permute-start.19 = (bf16[512,2048]{1,0:T(8,128)(2,1)}, bf16[512,2048]{1,0:T(8,128)(2,1)}, u32[]{:S(2)}, u32[]{:S(2)}) collective-permute-start(bf16[512,2048]{1,0:T(8,128)(2,1)} %param.16), channel_id=1, source_target_pairs={{2,4},{4,2},{3,5},{5,3},{10,12},{12,10},{11,13},{13,11},{18,20},{2... | collective-permute-start | bytes 6291464 | tf_op jit(solution)/shard_map/ppermute | solution.py:37
  434.1 4.6 collective-permute-start.21
  440.0 39.4 %collective-permute-start.22 = (bf16[256,2048]{1,0:T(8,128)(2,1)}, bf16[256,2048]{1,0:T(8,128)(2,1)S(1)}, u32[]{:S(2)}, u32[]{:S(2)}) collective-permute-start(bf16[256,2048]{1,0:T(8,128)(2,1)} %add_convert_fusion.5), channel_id=1, source_target_pairs={{0,1},{1,0},{2,3},{3,2},{4,5},{5,4},{6,7},{7,6},{8,9},{9,8},{10,11... | collective-permute-start | bytes 3145736 | tf_op jit(solution)/shard_map/ppermute | solution.py:33
  452.4 27.1 %collective-permute-start.20 = (bf16[256,2048]{1,0:T(8,128)(2,1)}, bf16[256,2048]{1,0:T(8,128)(2,1)}, u32[]{:S(2)}, u32[]{:S(2)}) collective-permute-start(bf16[256,2048]{1,0:T(8,128)(2,1)} %slice.205), channel_id=1, source_target_pairs={{0,4},{4,0},{1,5},{5,1},{2,6},{6,2},{3,7},{7,3},{8,12},{12,8},{9,1... | collective-permute-start | bytes 3145736 | tf_op jit(solution)/shard_map/ppermute | solution.py:33
  470.4 16.6 %collective-permute-start.26 = (bf16[256,2048]{1,0:T(8,128)(2,1)S(1)}, bf16[256,2048]{1,0:T(8,128)(2,1)S(1)}, u32[]{:S(2)}, u32[]{:S(2)}) collective-permute-start(bf16[256,2048]{1,0:T(8,128)(2,1)S(1)} %slice.213), channel_id=1, source_target_pairs={{0,4},{4,0},{1,5},{5,1},{2,6},{6,2},{3,7},{7,3},{8,12},{12,8},{9,1... | collective-permute-start | bytes 3145736 | tf_op jit(solution)/shard_map/ppermute | solution.py:33
  472.2 57.5 %copy-start.7 = (bf16[512,2048]{1,0:T(8,128)(2,1)}, bf16[512,2048]{1,0:T(8,128)(2,1)S(1)}, u32[]{:S(2)}) copy-start(bf16[512,2048]{1,0:T(8,128)(2,1)S(1)} %broadcast_select_fusion.1) | copy-start | bytes 6291460
  486.9 4.7 collective-permute-start.23
  488.4 31.9 %collective-permute-start.27 = (bf16[256,2048]{1,0:T(8,128)(2,1)}, bf16[256,2048]{1,0:T(8,128)(2,1)}, u32[]{:S(2)}, u32[]{:S(2)}) collective-permute-start(bf16[256,2048]{1,0:T(8,128)(2,1)} %add_convert_fusion.4), channel_id=1, source_target_pairs={{0,1},{1,0},{2,3},{3,2},{4,5},{5,4},{6,7},{7,6},{8,9},{9,8},{10,11... | collective-permute-start | bytes 3145736 | tf_op jit(solution)/shard_map/ppermute | solution.py:33
  490.0 30.3 %collective-permute-start.25 = (bf16[256,2048]{1,0:T(8,128)(2,1)}, bf16[256,2048]{1,0:T(8,128)(2,1)}, u32[]{:S(2)}, u32[]{:S(2)}) collective-permute-start(bf16[256,2048]{1,0:T(8,128)(2,1)} %slice.211), channel_id=1, source_target_pairs={{0,4},{4,0},{1,5},{5,1},{2,6},{6,2},{3,7},{7,3},{8,12},{12,8},{9,1... | collective-permute-start | bytes 3145736 | tf_op jit(solution)/shard_map/ppermute | solution.py:33
  490.0 47.1 %collective-permute-start.31 = (bf16[256,2048]{1,0:T(8,128)(2,1)}, bf16[256,2048]{1,0:T(8,128)(2,1)}, u32[]{:S(2)}, u32[]{:S(2)}) collective-permute-start(bf16[256,2048]{1,0:T(8,128)(2,1)} %fusion.8), channel_id=1, source_target_pairs={{0,1},{1,0},{2,3},{3,2},{4,5},{5,4},{6,7},{7,6},{8,9},{9,8},{10,11... | collective-permute-start | bytes 3145736 | tf_op jit(solution)/shard_map/ppermute | solution.py:33
  532.3 4.9 collective-permute-start.29
  532.4 31.8 %collective-permute-start.28 = (bf16[256,2048]{1,0:T(8,128)(2,1)S(1)}, bf16[256,2048]{1,0:T(8,128)(2,1)S(1)}, u32[]{:S(2)}, u32[]{:S(2)}) collective-permute-start(bf16[256,2048]{1,0:T(8,128)(2,1)S(1)} %fusion.5), channel_id=1, source_target_pairs={{0,1},{1,0},{2,3},{3,2},{4,5},{5,4},{6,7},{7,6},{8,9},{9,8},{10,11... | collective-permute-start | bytes 3145736 | tf_op jit(solution)/shard_map/ppermute | solution.py:33
  537.1 29.0 %collective-permute-start.32 = (bf16[256,2048]{1,0:T(8,128)(2,1)}, bf16[256,2048]{1,0:T(8,128)(2,1)}, u32[]{:S(2)}, u32[]{:S(2)}) collective-permute-start(bf16[256,2048]{1,0:T(8,128)(2,1)} %collective-permute-done.31), channel_id=1, source_target_pairs={{0,4},{4,0},{1,5},{5,1},{2,6},{6,2},{3,7},{7,3},{8,12},{12,8},{9,1... | collective-permute-start | bytes 3145736 | tf_op jit(solution)/shard_map/ppermute | solution.py:33
  564.2 3.3 collective-permute-start.30
  593.9 274.2 %reduce-scatter.6.cloned.1.call-start = ((), (), s32[]{:S(2)}) async-start(), calls=%async_computation.7 | async-start | bytes 10485760 | tf_op jit(solution)/shard_map/reduce_scatter | solution.py:73
  621.6 2.7 collective-permute-start.33
  624.7 26.6 %collective-permute-start.34 = (bf16[256,2048]{1,0:T(8,128)(2,1)S(1)}, bf16[256,2048]{1,0:T(8,128)(2,1)S(1)}, u32[]{:S(2)}, u32[]{:S(2)}) collective-permute-start(bf16[256,2048]{1,0:T(8,128)(2,1)S(1)} %add_convert_fusion.3), channel_id=1, source_target_pairs={{0,1},{1,0},{2,3},{3,2},{4,5},{5,4},{6,7},{7,6},{8,9},{9,8},{10,11... | collective-permute-start | bytes 3145736 | tf_op jit(solution)/shard_map/ppermute | solution.py:33
  652.8 2.7 collective-permute-start.38
  653.4 5.4 collective-permute-start.24
  656.9 29.7 %collective-permute-start.39 = (bf16[256,2048]{1,0:T(8,128)(2,1)}, bf16[256,2048]{1,0:T(8,128)(2,1)}, u32[]{:S(2)}, u32[]{:S(2)}) collective-permute-start(bf16[256,2048]{1,0:T(8,128)(2,1)} %add_convert_fusion.2), channel_id=1, source_target_pairs={{0,1},{1,0},{2,3},{3,2},{4,5},{5,4},{6,7},{7,6},{8,9},{9,8},{10,11... | collective-permute-start | bytes 3145736 | tf_op jit(solution)/shard_map/ppermute | solution.py:33
  662.1 74.5 %copy-start.21 = (bf16[256,2048]{1,0:T(8,128)(2,1)}, bf16[256,2048]{1,0:T(8,128)(2,1)S(1)}, u32[]{:S(2)}) copy-start(bf16[256,2048]{1,0:T(8,128)(2,1)S(1)} %subtract_convert_fusion.1.refs_1_.refs_0_) | copy-start | bytes 3145732
  686.7 187.3 %reduce-scatter.8.cloned.1.call-start = ((), (), s32[]{:S(2)}) async-start(), calls=%async_computation.8 | async-start | bytes 10485760 | tf_op jit(solution)/shard_map/reduce_scatter | solution.py:73
  688.3 2.7 collective-permute-start.37
  688.4 32.7 %collective-permute-start.36 = (bf16[256,2048]{1,0:T(8,128)(2,1)S(1)}, bf16[256,2048]{1,0:T(8,128)(2,1)}, u32[]{:S(2)}, u32[]{:S(2)}) collective-permute-start(bf16[256,2048]{1,0:T(8,128)(2,1)S(1)} %subtract_convert_fusion.1.refs_1_.refs_0_), channel_id=1, source_target_pairs={{0,1},{1,0},{2,3},{3,2},{4,5},{5,4},{6,7},{7,6},{8,9},{9,8},{10,11... | collective-permute-start | bytes 3145736 | tf_op jit(solution)/shard_map/ppermute | solution.py:33
  695.8 40.7 %collective-permute-start.42 = (bf16[256,2048]{1,0:T(8,128)(2,1)}, bf16[256,2048]{1,0:T(8,128)(2,1)}, u32[]{:S(2)}, u32[]{:S(2)}) collective-permute-start(bf16[256,2048]{1,0:T(8,128)(2,1)} %subtract_convert_fusion.refs_5_.refs_4_), channel_id=1, source_target_pairs={{0,1},{1,0},{2,3},{3,2},{4,5},{5,4},{6,7},{7,6},{8,9},{9,8},{10,11... | collective-permute-start | bytes 3145736 | tf_op jit(solution)/shard_map/ppermute | solution.py:33
  721.1 16.1 %copy-start.28 = (bf16[256,2048]{1,0:T(8,128)(2,1)S(1)}, bf16[256,2048]{1,0:T(8,128)(2,1)}, u32[]{:S(2)}) copy-start(bf16[256,2048]{1,0:T(8,128)(2,1)} %get-tuple-element.345) | copy-start | bytes 3145732
  721.1 16.1 %copy-start.29 = (bf16[256,2048]{1,0:T(8,128)(2,1)S(1)}, bf16[256,2048]{1,0:T(8,128)(2,1)}, u32[]{:S(2)}) copy-start(bf16[256,2048]{1,0:T(8,128)(2,1)} %get-tuple-element.346) | copy-start | bytes 3145732
  736.6 7.8 collective-permute-start.35
  736.7 8.6 collective-permute-start.40
  738.6 82.2 %collective-permute-start.46 = (bf16[512,2048]{1,0:T(8,128)(2,1)}, bf16[512,2048]{1,0:T(8,128)(2,1)}, u32[]{:S(2)}, u32[]{:S(2)}) collective-permute-start(bf16[512,2048]{1,0:T(8,128)(2,1)} %pad_maximum_fusion.7), channel_id=1, source_target_pairs={{2,4},{4,2},{3,5},{5,3},{10,12},{12,10},{11,13},{13,11},{18,20},{2... | collective-permute-start | bytes 6291464 | tf_op jit(solution)/shard_map/ppermute | solution.py:37
  740.8 13.7 %collective-permute-start.41 = (bf16[256,2048]{1,0:T(8,128)(2,1)}, bf16[256,2048]{1,0:T(8,128)(2,1)}, u32[]{:S(2)}, u32[]{:S(2)}) collective-permute-start(bf16[256,2048]{1,0:T(8,128)(2,1)} %subtract_convert_fusion.refs_5_.refs_4_), channel_id=1, source_target_pairs={{0,4},{4,0},{1,5},{5,1},{2,6},{6,2},{3,7},{7,3},{8,12},{12,8},{9,1... | collective-permute-start | bytes 3145736 | tf_op jit(solution)/shard_map/ppermute | solution.py:33
  742.4 12.1 %collective-permute-start.43 = (bf16[256,2048]{1,0:T(8,128)(2,1)}, bf16[256,2048]{1,0:T(8,128)(2,1)}, u32[]{:S(2)}, u32[]{:S(2)}) collective-permute-start(bf16[256,2048]{1,0:T(8,128)(2,1)} %collective-permute-done.42.refs_7_.refs_6_), channel_id=1, source_target_pairs={{0,4},{4,0},{1,5},{5,1},{2,6},{6,2},{3,7},{7,3},{8,12},{12,8},{9,1... | collective-permute-start | bytes 3145736 | tf_op jit(solution)/shard_map/ppermute | solution.py:33
  744.4 76.4 %collective-permute-start.44 = (bf16[256,2048]{1,0:T(8,128)(2,1)S(1)}, bf16[256,2048]{1,0:T(8,128)(2,1)S(1)}, u32[]{:S(2)}, u32[]{:S(2)}) collective-permute-start(bf16[256,2048]{1,0:T(8,128)(2,1)S(1)} %get-tuple-element.250), channel_id=1, source_target_pairs={{2,4},{4,2},{3,5},{5,3},{10,12},{12,10},{11,13},{13,11},{18,20},{2... | collective-permute-start | bytes 3145736 | tf_op jit(solution)/shard_map/ppermute | solution.py:37
  745.3 89.5 %collective-permute-start.45 = (bf16[256,2048]{1,0:T(8,128)(2,1)S(1)}, bf16[256,2048]{1,0:T(8,128)(2,1)S(1)}, u32[]{:S(2)}, u32[]{:S(2)}) collective-permute-start(bf16[256,2048]{1,0:T(8,128)(2,1)S(1)} %get-tuple-element.363), channel_id=1, source_target_pairs={{2,0},{6,2},{4,6},{0,4},{3,1},{7,3},{5,7},{1,5},{10,8},{14,10},{12... | collective-permute-start | bytes 3145736 | tf_op jit(solution)/shard_map/ppermute | solution.py:80
  847.8 1.6 collective-permute-start.47
  850.1 3.8 collective-permute-start.48
  871.1 72.0 %collective-permute-start.49 = (bf16[256,2048]{1,0:T(8,128)(2,1)}, bf16[256,2048]{1,0:T(8,128)(2,1)}, u32[]{:S(2)}, u32[]{:S(2)}) collective-permute-start(bf16[256,2048]{1,0:T(8,128)(2,1)} %get-tuple-element.271), channel_id=1, source_target_pairs={{2,4},{4,2},{3,5},{5,3},{10,12},{12,10},{11,13},{13,11},{18,20},{2... | collective-permute-start | bytes 3145736 | tf_op jit(solution)/shard_map/ppermute | solution.py:37
  872.8 71.7 %collective-permute-start.50 = (bf16[256,2048]{1,0:T(8,128)(2,1)}, bf16[256,2048]{1,0:T(8,128)(2,1)}, u32[]{:S(2)}, u32[]{:S(2)}) collective-permute-start(bf16[256,2048]{1,0:T(8,128)(2,1)} %get-tuple-element.361), channel_id=1, source_target_pairs={{2,0},{6,2},{4,6},{0,4},{3,1},{7,3},{5,7},{1,5},{10,8},{14,10},{12... | collective-permute-start | bytes 3145736 | tf_op jit(solution)/shard_map/ppermute | solution.py:80
  877.0 67.5 %collective-permute-start.51 = (bf16[256,2048]{1,0:T(8,128)(2,1)}, bf16[256,2048]{1,0:T(8,128)(2,1)}, u32[]{:S(2)}, u32[]{:S(2)}) collective-permute-start(bf16[256,2048]{1,0:T(8,128)(2,1)} %get-tuple-element.274), channel_id=1, source_target_pairs={{2,4},{4,2},{3,5},{5,3},{10,12},{12,10},{11,13},{13,11},{18,20},{2... | collective-permute-start | bytes 3145736 | tf_op jit(solution)/shard_map/ppermute | solution.py:37
  878.7 88.3 %collective-permute-start.52 = (bf16[256,2048]{1,0:T(8,128)(2,1)}, bf16[256,2048]{1,0:T(8,128)(2,1)}, u32[]{:S(2)}, u32[]{:S(2)}) collective-permute-start(bf16[256,2048]{1,0:T(8,128)(2,1)} %get-tuple-element.359), channel_id=1, source_target_pairs={{2,0},{6,2},{4,6},{0,4},{3,1},{7,3},{5,7},{1,5},{10,8},{14,10},{12... | collective-permute-start | bytes 3145736 | tf_op jit(solution)/shard_map/ppermute | solution.py:80
  (43 other events, 191.7 us)
Sparse Core Ops, SparseCore 0:
  145.9 93.6 all-gather.3
  241.4 87.6 all-gather.5
  331.0 87.5 all-gather.7
  594.1 90.0 reduce-scatter.3
  687.4 89.9 reduce-scatter.5
  780.3 86.3 reduce-scatter.7

commit v6 on v5

--- a/solution.py
+++ b/solution.py
@@ -1641,7 +1641,9 @@
     dots = sum_over(dots, RANK)
     d_qkv_b = raw_grads(d_q_norm, d_k_norm, d_v, raw, squares, dots, gain_q, gain_k)
     qkv_totals = stacked_weight_grad(packed, d_qkv_b, 3)
-    up_split = start_split(after(d_qkv_b, up_sum))
+    gate_last, _ = lax.optimization_barrier((gate_split[1:], d_qkv_b))
+    gate_split = (gate_split[0], *gate_last)
+    up_split = start_split(after((d_qkv_b, gate_last), up_sum))
     _, input_parts = give_back(perm_place, d_qkv_b, qkv_full)
     down_shard, layer_out = finish_split(*down_split).T, finish_turn(*layer_turn)
     qkv_totals, down_shard, layer_out = lax.optimization_barrier((qkv_totals, down_shard, layer_out))

time: 1140 us -> 1120 us (0.982); the launches traced: 1130 us -> 1120 us
  waiting for transfers between devices: 127 us -> 115 us
    ppermute x3, waiting for transfers between devices: 37.8 us -> 25.6 us  [start_split(): lax.ppermute(second, ('core', 'th'), CYCLE_BACK)]
  transfers between devices with their start and end apart: 59 -> 59, of which waited for: 22 -> 20; matrix products, arithmetic and copies ran while one was open for 10% -> 10% of each run, Pallas kernels for 43% -> 44%
where the time goes in v6:
time: 1120 us
  Pallas kernels  787 us (70%)
  waiting for transfers between devices  115 us (10%)
  other arithmetic  93.8 us (8%)
  starting transfers between devices  54.3 us (5%)
  local copies, waits for them, and re-layouts  50.1 us (4%)
  between operations  17.1 us (2%)
    pallas_call x1, Pallas kernels, leave(): pl.pallas_call(functools.partial(leave_kernel, tuple(cuts), paired, stack...  138 us
    pallas_call x1, Pallas kernels, enter(): pl.pallas_call(functools.partial(entry_kernel, tuple(plan)), in_specs=[an...  137 us
    pallas_call x8, Pallas kernels, sum_products(): pl.pallas_call(functools.partial(products_kernel, len(lefts)), grid=(widt...  92 us
    ppermute x41, waiting for transfers between devices, swap(): return lax.ppermute(value, axis, SWAP)  88.9 us
    pallas_call x4, Pallas kernels, weight_grad(): pl.pallas_call(functools.partial(weight_grad_kernel, len(lefts)), grid=(w...  81.4 us
    pallas_call x4, Pallas kernels, hidden_units(): pl.pallas_call(hidden_kernel, grid=(width // block,), in_specs=[pl.BlockS...  58.1 us
    pallas_call x4, Pallas kernels, hidden_grads(): pl.pallas_call(hidden_grads_kernel, grid=(width // block,), in_specs=[pl....  47.6 us
    pallas_call x2, Pallas kernels, give_back(): pl.pallas_call(functools.partial(given_kernel, count), grid=(rows // coun...  45.6 us
  transfers between devices with their start and end apart: 59, of which 20 were waited for; matrix products, arithmetic and copies ran while one was open for 10% of the time, Pallas kernels for 44%

profile of v6, /device:TPU:0, one launch (start us, length us, event | category | flops | bytes accessed | tf_op | source)
XLA Modules:
  0.0 1117.1 jit_solution(4691274464507498273)
XLA Ops:
  9.0 136.7 %enter.1 = (bf16[2048,2048]{1,0:T(8,128)(2,1)}, bf16[2048,1536]{1,0:T(8,128)(2,1)}, bf16[2048,512]{1,0:T(8,128)(2,1)}, bf16[512,2048]{1,0:T(8,128)(2,1)}) custom-call(bf16[512,2048]{1,0:T(8,128)(2,1)} %refs_0_.1, bf16[256,512]{1,0:T(8,128)(2,1)} %refs_1_.1, bf16[256,512]{1,0:T(8,128)(2,1)} %refs_2_.1, bf16[256,512]{1,0:T(8,128)(2,1)} %refs_3_.1, ...), custom_call_target="tpu_custom_call" | custom-call | flops 1 | bytes 1 | tf_op jit(solution)/shard_map/enter/pallas_call | solution.py:700
  146.5 5.4 collective-permute-start
  154.9 40.7 %pack.1 = (bf16[2048,2048]{1,0:T(8,128)(2,1)}, f32[2048,1536]{1,0:T(8,128)}, f32[2,2048]{1,0:T(2,128)}) custom-call(s32[2048,1]{1,0:T(8,128)} %copy.51.places, bf16[2048,2048]{1,0:T(8,128)(2,1)} %get-tuple-element.149.tokens_ref, bf16[2048,1536]{1,0:T(8,128)(2,1)} %get-tuple-element.150.weight), custom_call_target="tpu_custom_call" | custom-call | flops 1 | bytes 1 | tf_op jit(solution)/shard_map/pack/pallas_call | solution.py:1305
  202.0 5.1 collective-permute-start.3
  212.6 2.7 collective-permute-done.4
  217.7 3.7 fusion.31
  224.1 11.9 %prepare.1 = (bf16[2048,512]{1,0:T(8,128)(2,1)}, bf16[2048,512]{1,0:T(8,128)(2,1)}, bf16[2048,512]{1,0:T(8,128)(2,1)}) custom-call(f32[2048,1536]{1,0:T(8,128)} %get-tuple-element.154.raw, f32[2,2048]{1,0:T(2,128)} %add.315.squares, f32[1,512]{1,0:T(1,128)} %bitcast.25, f32[1,512]{1,0:T(1,128)} %bitcast.28, f32[2048,128]{1,0:T(8,128)} %pad_maximum_fusion.8.cosine, ...), custom_call_target="tpu_custom_call" | custom-call | flops 1 | bytes 1 | tf_op jit(solution)/shard_map/prepare/pallas_call | solution.py:843
  237.6 28.7 %attention_forward.1 = (bf16[2048,512]{1,0:T(8,128)(2,1)S(1)}, f32[2048,512]{1,0:T(8,128)}, f32[4,1,2048]{2,1,0:T(1,128)S(1)}) custom-call(s32[8]{0:T(128)S(1)} %and_select_fusion.8.low_ref, bf16[2048,512]{1,0:T(8,128)(2,1)S(1)} %copy-done, bf16[2048,512]{1,0:T(8,128)(2,1)} %get-tuple-element.158.k_ref, bf16[2048,512]{1,0:T(8,128)(2,1)} %get-tuple-element.159.v_ref, ...), custom_call_target="tpu_custom_call" | custom-call | flops 1 | bytes 1 | tf_op jit(solution)/shard_map/attention_forward/pallas_call | solution.py:913
  267.6 13.0 %give_back.2 = (bf16[2048,512]{1,0:T(8,128)(2,1)}, bf16[2048,2048]{1,0:T(8,128)(2,1)}) custom-call(s32[1,2048]{1,0:T(1,128)} %get-tuple-element.373.places, bf16[2048,512]{1,0:T(8,128)(2,1)} %copy-done.3, bf16[2048,512]{1,0:T(8,128)(2,1)} %get-tuple-element.162.weight.refs_9_), custom_call_target="tpu_custom_call" | custom-call | flops 1 | bytes 1 | tf_op jit(solution)/shard_map/give_back/pallas_call | solution.py:1339
  282.7 4.2 fusion.37
  291.6 3.1 add_convert_fusion.6
  296.6 23.7 %collective-permute-done.9 = bf16[256,2048]{1,0:T(8,128)(2,1)S(1)} collective-permute-done((bf16[256,2048]{1,0:T(8,128)(2,1)S(1)}, bf16[256,2048]{1,0:T(8,128)(2,1)S(1)}, u32[]{:S(2)}, u32[]{:S(2)}) %collective-permute-start.9) | collective-permute-done | bytes 1048608 | tf_op jit(solution)/shard_map/ppermute | solution.py:33
  326.6 2.9 pad_maximum_fusion.3.x_ref.refs_0_
  329.5 15.0 %hidden_units.4 = (f32[512,2048]{1,0:T(8,128)}, f32[512,2048]{1,0:T(8,128)}, bf16[512,2048]{1,0:T(8,128)(2,1)}) custom-call(bf16[512,2048]{1,0:T(8,128)(2,1)} %pad_maximum_fusion.3.x_ref.refs_0_, bf16[2048,2048]{1,0:T(8,128)(2,1)} %all-gather.4.cloned.1.call-done.gate_w.refs_2_, bf16[2048,2048]{1,0:T(8,128)(2,1)} %all-gather.6.cloned.1.call-done.up_w.refs_3_), custom_call_target="tpu_custom_call" | custom-call | flops 1 | bytes 1 | tf_op jit(solution)/shard_map/hidden_units/pallas_call | solution.py:1153
  344.6 5.2 collective-permute-done.12
  349.8 2.4 multiply_reduce_fusion.6
  358.8 14.4 %hidden_units.5 = (f32[512,2048]{1,0:T(8,128)}, f32[512,2048]{1,0:T(8,128)}, bf16[512,2048]{1,0:T(8,128)(2,1)}) custom-call(bf16[512,2048]{1,0:T(8,128)(2,1)} %pad_maximum_fusion.4.x_ref.refs_2_, bf16[2048,2048]{1,0:T(8,128)(2,1)} %all-gather.4.cloned.1.call-done.gate_w.refs_2_, bf16[2048,2048]{1,0:T(8,128)(2,1)} %all-gather.6.cloned.1.call-done.up_w.refs_3_), custom_call_target="tpu_custom_call" | custom-call | flops 1 | bytes 1 | tf_op jit(solution)/shard_map/hidden_units/pallas_call | solution.py:1153
  373.2 7.1 collective-permute-done.16
  384.8 14.4 %hidden_units.6 = (f32[512,2048]{1,0:T(8,128)}, f32[512,2048]{1,0:T(8,128)}, bf16[512,2048]{1,0:T(8,128)(2,1)}) custom-call(bf16[512,2048]{1,0:T(8,128)(2,1)} %copy-done.9, bf16[2048,2048]{1,0:T(8,128)(2,1)} %all-gather.4.cloned.1.call-done.gate_w.refs_2_, bf16[2048,2048]{1,0:T(8,128)(2,1)} %all-gather.6.cloned.1.call-done.up_w.refs_3_), custom_call_target="tpu_custom_call" | custom-call | flops 1 | bytes 1 | tf_op jit(solution)/shard_map/hidden_units/pallas_call | solution.py:1153
  399.2 6.7 collective-permute-done.15
  410.0 14.3 %hidden_units.7 = (f32[512,2048]{1,0:T(8,128)}, f32[512,2048]{1,0:T(8,128)}, bf16[512,2048]{1,0:T(8,128)(2,1)}) custom-call(bf16[512,2048]{1,0:T(8,128)(2,1)} %copy-done.10, bf16[2048,2048]{1,0:T(8,128)(2,1)} %all-gather.4.cloned.1.call-done.gate_w.refs_2_, bf16[2048,2048]{1,0:T(8,128)(2,1)} %all-gather.6.cloned.1.call-done.up_w.refs_3_), custom_call_target="tpu_custom_call" | custom-call | flops 1 | bytes 1 | tf_op jit(solution)/shard_map/hidden_units/pallas_call | solution.py:1153
  424.3 8.8 sum_products.8
  434.6 7.9 collective-permute-start.21
  447.2 8.8 sum_products.9
  458.4 8.9 sum_products.10
  467.3 9.0 sum_products.11
  478.2 6.7 collective-permute-done.22
  489.0 3.4 fusion.8
  497.1 2.9 pad_maximum_fusion.5.grad_ref.refs_0_
  500.0 11.6 %hidden_grads.4 = (bf16[512,2048]{1,0:T(8,128)(2,1)}, bf16[512,2048]{1,0:T(8,128)(2,1)}) custom-call(bf16[512,2048]{1,0:T(8,128)(2,1)} %pad_maximum_fusion.5.grad_ref.refs_0_, bf16[2048,2048]{1,0:T(8,128)(2,1)} %all-gather.8.cloned.1.call-done.refs_1_.weight, f32[512,2048]{1,0:T(8,128)} %get-tuple-element.188.gate_ref, f32[512,2048]{1,0:T(8,128)} %get-tuple-element.189.up_ref), custom_call_target="tpu_custom_call" | custom-call | flops 1 | bytes 1 | tf_op jit(solution)/shard_map/hidden_grads/pallas_call | solution.py:1186
  511.7 14.0 %sum_products.12 = bf16[512,2048]{1,0:T(8,128)(2,1)} custom-call(bf16[512,2048]{1,0:T(8,128)(2,1)} %get-tuple-element.225.refs_0_.refs_4_, bf16[512,2048]{1,0:T(8,128)(2,1)} %get-tuple-element.234.refs_1_.refs_4_, bf16[2048,2048]{1,0:T(8,128)(2,1)} %all-gather.4.cloned.1.call-done.gate_w.refs_2_, bf16[2048,2048]{1,0:T(8,128)(2,1)} %all-gather.6.cloned.1.call-done.up_w.refs_3_), custom_call_target="tpu_custom_call" | custom-call | flops 1 | bytes 1 | tf_op jit(solution)/shard_map/sum_products/pallas_call | solution.py:1215
  525.7 2.6 multiply_reduce_fusion.4
  528.3 6.9 add_convert_fusion.1
  535.2 2.5 fusion.5
  538.5 4.1 collective-permute-done.31
  544.2 11.6 %hidden_grads.5 = (bf16[512,2048]{1,0:T(8,128)(2,1)}, bf16[512,2048]{1,0:T(8,128)(2,1)}) custom-call(bf16[512,2048]{1,0:T(8,128)(2,1)} %pad_maximum_fusion.6.grad_ref.refs_2_, bf16[2048,2048]{1,0:T(8,128)(2,1)} %all-gather.8.cloned.1.call-done.refs_1_.weight, f32[512,2048]{1,0:T(8,128)} %get-tuple-element.195.gate_ref, f32[512,2048]{1,0:T(8,128)} %get-tuple-element.196.up_ref), custom_call_target="tpu_custom_call" | custom-call | flops 1 | bytes 1 | tf_op jit(solution)/shard_map/hidden_grads/pallas_call | solution.py:1186
  555.8 13.9 %sum_products.13 = bf16[512,2048]{1,0:T(8,128)(2,1)} custom-call(bf16[512,2048]{1,0:T(8,128)(2,1)} %get-tuple-element.227.refs_0_.refs_6_, bf16[512,2048]{1,0:T(8,128)(2,1)} %get-tuple-element.236.refs_1_.refs_6_, bf16[2048,2048]{1,0:T(8,128)(2,1)} %all-gather.4.cloned.1.call-done.gate_w.refs_2_, bf16[2048,2048]{1,0:T(8,128)(2,1)} %all-gather.6.cloned.1.call-done.up_w.refs_3_), custom_call_target="tpu_custom_call" | custom-call | flops 1 | bytes 1 | tf_op jit(solution)/shard_map/sum_products/pallas_call | solution.py:1215
  575.6 23.8 %weight_grad.4 = bf16[2048,2048]{1,0:T(8,128)(2,1)} custom-call(bf16[512,2048]{1,0:T(8,128)(2,1)} %pad_maximum_fusion.5.grad_ref.refs_0_, bf16[512,2048]{1,0:T(8,128)(2,1)} %copy-done.19, bf16[512,2048]{1,0:T(8,128)(2,1)} %pad_maximum_fusion.6.grad_ref.refs_2_, bf16[512,2048]{1,0:T(8,128)(2,1)} %copy-done.18, ...), custom_call_target="tpu_custom_call" | custom-call | flops 1 | bytes 1 | tf_op jit(solution)/shard_map/weight_grad/pallas_call | solution.py:1244
  599.4 12.3 %hidden_grads.6 = (bf16[512,2048]{1,0:T(8,128)(2,1)}, bf16[512,2048]{1,0:T(8,128)(2,1)}) custom-call(bf16[512,2048]{1,0:T(8,128)(2,1)} %copy-done.19, bf16[2048,2048]{1,0:T(8,128)(2,1)} %all-gather.8.cloned.1.call-done.refs_1_.weight, f32[512,2048]{1,0:T(8,128)} %get-tuple-element.207.gate_ref, f32[512,2048]{1,0:T(8,128)} %get-tuple-element.208.up_ref), custom_call_target="tpu_custom_call" | custom-call | flops 1 | bytes 1 | tf_op jit(solution)/shard_map/hidden_grads/pallas_call | solution.py:1186
  611.8 14.5 %sum_products.14 = bf16[512,2048]{1,0:T(8,128)(2,1)} custom-call(bf16[512,2048]{1,0:T(8,128)(2,1)} %get-tuple-element.226.refs_0_.refs_5_, bf16[512,2048]{1,0:T(8,128)(2,1)} %get-tuple-element.235.refs_1_.refs_5_, bf16[2048,2048]{1,0:T(8,128)(2,1)} %all-gather.4.cloned.1.call-done.gate_w.refs_2_, bf16[2048,2048]{1,0:T(8,128)(2,1)} %all-gather.6.cloned.1.call-done.up_w.refs_3_), custom_call_target="tpu_custom_call" | custom-call | flops 1 | bytes 1 | tf_op jit(solution)/shard_map/sum_products/pallas_call | solution.py:1215
  627.9 2.6 collective-permute-done.33
  631.0 12.0 %hidden_grads.7 = (bf16[512,2048]{1,0:T(8,128)(2,1)}, bf16[512,2048]{1,0:T(8,128)(2,1)}) custom-call(bf16[512,2048]{1,0:T(8,128)(2,1)} %copy-done.18, bf16[2048,2048]{1,0:T(8,128)(2,1)} %all-gather.8.cloned.1.call-done.refs_1_.weight, f32[512,2048]{1,0:T(8,128)} %get-tuple-element.213.gate_ref, f32[512,2048]{1,0:T(8,128)} %get-tuple-element.214.up_ref), custom_call_target="tpu_custom_call" | custom-call | flops 1 | bytes 1 | tf_op jit(solution)/shard_map/hidden_grads/pallas_call | solution.py:1186
  643.1 14.1 %sum_products.15 = bf16[512,2048]{1,0:T(8,128)(2,1)} custom-call(bf16[512,2048]{1,0:T(8,128)(2,1)} %get-tuple-element.228.refs_0_.refs_7_, bf16[512,2048]{1,0:T(8,128)(2,1)} %get-tuple-element.237.refs_1_.refs_7_, bf16[2048,2048]{1,0:T(8,128)(2,1)} %all-gather.4.cloned.1.call-done.gate_w.refs_2_, bf16[2048,2048]{1,0:T(8,128)(2,1)} %all-gather.6.cloned.1.call-done.up_w.refs_3_), custom_call_target="tpu_custom_call" | custom-call | flops 1 | bytes 1 | tf_op jit(solution)/shard_map/sum_products/pallas_call | solution.py:1215
  668.0 24.5 %weight_grad.5 = bf16[2048,2048]{1,0:T(8,128)(2,1)} custom-call(bf16[512,2048]{1,0:T(8,128)(2,1)} %pad_maximum_fusion.3.x_ref.refs_0_, bf16[512,2048]{1,0:T(8,128)(2,1)} %copy-done.9, bf16[512,2048]{1,0:T(8,128)(2,1)} %pad_maximum_fusion.4.x_ref.refs_2_, bf16[512,2048]{1,0:T(8,128)(2,1)} %copy-done.10, bf16[512,2048]{1,0:T(8,128)(2,1)} %get-tuple-element.225.refs_0_.refs_4_, ...), custom_call_target="tpu_custom_call" | custom-call | flops 1 | bytes 1 | tf_op jit(solution)/shard_map/weight_grad/pallas_call | solution.py:1244
  694.3 2.5 collective-permute-done.37
  696.8 3.0 multiply_reduce_fusion
  701.5 23.9 %weight_grad.6 = bf16[2048,2048]{1,0:T(8,128)(2,1)} custom-call(bf16[512,2048]{1,0:T(8,128)(2,1)} %pad_maximum_fusion.3.x_ref.refs_0_, bf16[512,2048]{1,0:T(8,128)(2,1)} %copy-done.9, bf16[512,2048]{1,0:T(8,128)(2,1)} %pad_maximum_fusion.4.x_ref.refs_2_, bf16[512,2048]{1,0:T(8,128)(2,1)} %copy-done.10, bf16[512,2048]{1,0:T(8,128)(2,1)} %get-tuple-element.234.refs_1_.refs_4_, ...), custom_call_target="tpu_custom_call" | custom-call | flops 1 | bytes 1 | tf_op jit(solution)/shard_map/weight_grad/pallas_call | solution.py:1244
  725.4 16.9 %collective-permute-done.42.refs_7_.refs_6_ = bf16[256,2048]{1,0:T(8,128)(2,1)} collective-permute-done((bf16[256,2048]{1,0:T(8,128)(2,1)}, bf16[256,2048]{1,0:T(8,128)(2,1)}, u32[]{:S(2)}, u32[]{:S(2)}) %collective-permute-start.42) | collective-permute-done | bytes 1048608 | tf_op jit(solution)/shard_map/ppermute | solution.py:33
  750.8 3.1 collective-permute-start.45
  754.2 3.9 fusion.16.refs_0_
  758.1 16.4 %pick_products.1.grad_ref = bf16[2048,512]{1,0:T(8,128)(2,1)} custom-call(s32[2048,1]{1,0:T(8,128)} %fusion.16.refs_0_, bf16[256,2048]{1,0:T(8,128)(2,1)} %copy-done.21, bf16[256,2048]{1,0:T(8,128)(2,1)} %collective-permute-done.35.refs_2_.refs_1_, bf16[256,2048]{1,0:T(8,128)(2,1)} %collective-permute-done.36.refs_3_.refs_2_, ...), custom_call_target="tpu_custom_call" | custom-call | flops 1 | bytes 1 | tf_op jit(solution)/shard_map/pick_products/pallas_call | solution.py:1388
  774.5 9.1 weight_grad.7.refs_3_
  783.6 40.7 %attention_backward.1 = (f32[2048,512]{1,0:T(8,128)}, f32[2048,512]{1,0:T(8,128)}, bf16[2048,512]{1,0:T(8,128)(2,1)S(1)}) custom-call(s32[8]{0:T(128)S(1)} %and_select_fusion.9.high_ref, bf16[2048,512]{1,0:T(8,128)(2,1)S(1)} %copy-done.1, bf16[2048,512]{1,0:T(8,128)(2,1)} %get-tuple-element.158.k_ref, bf16[2048,512]{1,0:T(8,128)(2,1)} %get-tuple-element.159.v_ref, ...), custom_call_target="tpu_custom_call" | custom-call | flops 1 | bytes 1 | tf_op jit(solution)/shard_map/attention_backward/pallas_call | solution.py:992
  825.7 14.9 %collective-permute-done.45 = bf16[256,2048]{1,0:T(8,128)(2,1)S(1)} collective-permute-done((bf16[256,2048]{1,0:T(8,128)(2,1)S(1)}, bf16[256,2048]{1,0:T(8,128)(2,1)S(1)}, u32[]{:S(2)}, u32[]{:S(2)}) %collective-permute-start.45) | collective-permute-done | bytes 1048608 | tf_op jit(solution)/shard_map/ppermute | solution.py:80
  840.7 3.5 broadcast_select_fusion.6
  848.4 13.1 %norm_grads.1 = (f32[2048,512]{1,0:T(8,128)}, f32[2048,512]{1,0:T(8,128)}, f32[2,2048]{1,0:T(2,128)}, f32[8,512]{1,0:T(8,128)}, f32[8,512]{1,0:T(8,128)}) custom-call(f32[2048,512]{1,0:T(8,128)} %get-tuple-element.246.dq_ref, f32[2048,512]{1,0:T(8,128)} %get-tuple-element.247.dk_ref, f32[2048,1536]{1,0:T(8,128)} %get-tuple-element.154.raw, ...), custom_call_target="tpu_custom_call" | custom-call | flops 1 | bytes 1 | tf_op jit(solution)/shard_map/norm_grads/pallas_call | solution.py:1049
  868.3 13.3 %raw_grads.1.refs_1_.rows_ref = bf16[2048,1536]{1,0:T(8,128)(2,1)} custom-call(f32[2048,512]{1,0:T(8,128)} %get-tuple-element.248.dq_ref, f32[2048,512]{1,0:T(8,128)} %get-tuple-element.249.dk_ref, bf16[2048,512]{1,0:T(8,128)(2,1)} %copy-done.2, f32[2048,1536]{1,0:T(8,128)} %get-tuple-element.154.raw, f32[2,2048]{1,0:T(2,128)} %add.315.squares, ...), custom_call_target="tpu_custom_call" | custom-call | flops 1 | bytes 1 | tf_op jit(solution)/shard_map/raw_grads/pallas_call | solution.py:1095
  881.6 10.7 collective-permute-done.50
  892.4 3.0 broadcast_select_fusion.4
  898.7 3.1 broadcast_select_fusion
  901.9 32.7 %give_back.3 = (bf16[2048,1536]{1,0:T(8,128)(2,1)}, bf16[2048,2048]{1,0:T(8,128)(2,1)}) custom-call(s32[1,2048]{1,0:T(1,128)} %get-tuple-element.373.places, bf16[2048,1536]{1,0:T(8,128)(2,1)} %raw_grads.1.refs_1_.rows_ref, bf16[2048,1536]{1,0:T(8,128)(2,1)} %get-tuple-element.150.weight), custom_call_target="tpu_custom_call" | custom-call | flops 1 | bytes 1 | tf_op jit(solution)/shard_map/give_back/pallas_call | solution.py:1339
  934.5 22.6 %stacked_weight_grad.1.refs_4_ = bf16[3,2048,512]{2,1,0:T(8,128)(2,1)} custom-call(bf16[2048,2048]{1,0:T(8,128)(2,1)} %get-tuple-element.151.refs_0_, bf16[2048,1536]{1,0:T(8,128)(2,1)} %raw_grads.1.refs_1_.rows_ref), custom_call_target="tpu_custom_call" | custom-call | flops 1 | bytes 1 | tf_op jit(solution)/shard_map/stacked_weight_grad/pallas_call | solution.py:1264
  958.9 138.2 %leave.1 = (bf16[512,2048]{1,0:T(8,128)(2,1)}, f32[8,2048]{1,0:T(8,128)}, f32[256,512]{1,0:T(8,128)}, f32[256,512]{1,0:T(8,128)}, f32[256,512]{1,0:T(8,128)}, /*index=5*/f32[256,512]{1,0:T(8,128)}) custom-call(bf16[2048,2048]{1,0:T(8,128)(2,1)} %get-tuple-element.265.refs_0_, f32[512,2048]{1,0:T(8,128)} %pad_maximum_fusion.refs_1_, ...), custom_call_target="tpu_custom_call" | custom-call | flops 1 | bytes 1 | tf_op jit(solution)/shard_map/leave/pallas_call | solution.py:659
  1100.7 5.5 convert_add_fusion.2
  (289 shorter events, 131.0 us)
Async XLA Ops:
  7.2 322.4 %all-gather.4.cloned.1.call-start = ((), (), s32[]{:S(2)}) async-start(), calls=%async_computation.3 | async-start | bytes 10485760 | tf_op jit(solution)/shard_map/all_gather | solution.py:69
  145.8 183.7 %all-gather.6.cloned.1.call-start = ((), (), s32[]{:S(2)}) async-start(), calls=%async_computation.4 | async-start | bytes 10485760 | tf_op jit(solution)/shard_map/all_gather | solution.py:69
  146.5 6.3 collective-permute-start
  151.9 43.8 %collective-permute-start.2 = (bf16[256,2048]{1,0:T(8,128)(2,1)S(1)}, bf16[256,2048]{1,0:T(8,128)(2,1)S(1)}, u32[]{:S(2)}, u32[]{:S(2)}) collective-permute-start(bf16[256,2048]{1,0:T(8,128)(2,1)S(1)} %copy-done.35), channel_id=1, source_target_pairs={{0,2},{2,6},{6,4},{4,0},{1,3},{3,7},{7,5},{5,1},{8,10},{10,14},{14... | collective-permute-start | bytes 3145736 | tf_op jit(solution)/shard_map/ppermute | solution.py:64
  152.0 43.6 %collective-permute-start.1 = (bf16[256,2048]{1,0:T(8,128)(2,1)S(1)}, bf16[256,2048]{1,0:T(8,128)(2,1)S(1)}, u32[]{:S(2)}, u32[]{:S(2)}) collective-permute-start(bf16[256,2048]{1,0:T(8,128)(2,1)S(1)} %copy-done.35), channel_id=1, source_target_pairs={{2,4},{4,2},{3,5},{5,3},{10,12},{12,10},{11,13},{13,11},{18,20},{2... | collective-permute-start | bytes 3145736 | tf_op jit(solution)/shard_map/ppermute | solution.py:37
  197.4 226.9 %all-gather.8.cloned.1.call-start = ((), (), s32[]{:S(2)}) async-start(), calls=%async_computation.5 | async-start | bytes 10485760 | tf_op jit(solution)/shard_map/all_gather | solution.py:69
  202.0 9.5 collective-permute-start.3
  211.5 3.8 collective-permute-start.4
  215.9 64.6 %collective-permute-start.6 = (bf16[256,2048]{1,0:T(8,128)(2,1)S(1)}, bf16[256,2048]{1,0:T(8,128)(2,1)S(1)}, u32[]{:S(2)}, u32[]{:S(2)}) collective-permute-start(bf16[256,2048]{1,0:T(8,128)(2,1)S(1)} %bitcast.20), channel_id=1, source_target_pairs={{0,2},{2,6},{6,4},{4,0},{1,3},{3,7},{7,5},{5,1},{8,10},{10,14},{14... | collective-permute-start | bytes 3145736 | tf_op jit(solution)/shard_map/ppermute | solution.py:64
  216.2 64.4 %collective-permute-start.5 = (bf16[256,2048]{1,0:T(8,128)(2,1)S(1)}, bf16[256,2048]{1,0:T(8,128)(2,1)S(1)}, u32[]{:S(2)}, u32[]{:S(2)}) collective-permute-start(bf16[256,2048]{1,0:T(8,128)(2,1)S(1)} %bitcast.21), channel_id=1, source_target_pairs={{2,4},{4,2},{3,5},{5,3},{10,12},{12,10},{11,13},{13,11},{18,20},{2... | collective-permute-start | bytes 3145736 | tf_op jit(solution)/shard_map/ppermute | solution.py:37
  282.4 465.9 %reduce-scatter.4.cloned.1.call-start = ((), (), s32[]{:S(2)}) async-start(), calls=%async_computation.6 | async-start | bytes 10485760 | tf_op jit(solution)/shard_map/reduce_scatter | solution.py:73
  286.9 3.2 collective-permute-start.11
  287.8 3.8 collective-permute-start.8
  287.9 8.8 collective-permute-start.7
  294.7 27.4 %copy-start.41 = (f32[2048]{0:T(1024)S(1)}, f32[2048]{0:T(1024)}, u32[]{:S(2)}) copy-start(f32[2048]{0:T(1024)} %param.28) | copy-start | bytes 24580
  294.7 25.5 %collective-permute-start.9 = (bf16[256,2048]{1,0:T(8,128)(2,1)S(1)}, bf16[256,2048]{1,0:T(8,128)(2,1)S(1)}, u32[]{:S(2)}, u32[]{:S(2)}) collective-permute-start(bf16[256,2048]{1,0:T(8,128)(2,1)S(1)} %get-tuple-element.356), channel_id=1, source_target_pairs={{0,1},{1,0},{2,3},{3,2},{4,5},{5,4},{6,7},{7,6},{8,9},{9,8},{10,11... | collective-permute-start | bytes 3145736 | tf_op jit(solution)/shard_map/ppermute | solution.py:33
  323.8 2.9 collective-permute-start.13
  323.9 25.9 %collective-permute-start.12 = (bf16[256,2048]{1,0:T(8,128)(2,1)}, bf16[256,2048]{1,0:T(8,128)(2,1)}, u32[]{:S(2)}, u32[]{:S(2)}) collective-permute-start(bf16[256,2048]{1,0:T(8,128)(2,1)} %get-tuple-element.355), channel_id=1, source_target_pairs={{0,1},{1,0},{2,3},{3,2},{4,5},{5,4},{6,7},{7,6},{8,9},{9,8},{10,11... | collective-permute-start | bytes 3145736 | tf_op jit(solution)/shard_map/ppermute | solution.py:33
  325.7 24.1 %collective-permute-start.10 = (bf16[256,2048]{1,0:T(8,128)(2,1)}, bf16[256,2048]{1,0:T(8,128)(2,1)}, u32[]{:S(2)}, u32[]{:S(2)}) collective-permute-start(bf16[256,2048]{1,0:T(8,128)(2,1)} %get-tuple-element.351), channel_id=1, source_target_pairs={{0,4},{4,0},{1,5},{5,1},{2,6},{6,2},{3,7},{7,3},{8,12},{12,8},{9,1... | collective-permute-start | bytes 3145736 | tf_op jit(solution)/shard_map/ppermute | solution.py:33
  354.6 2.7 collective-permute-start.14
  354.6 25.7 %collective-permute-start.16 = (bf16[256,2048]{1,0:T(8,128)(2,1)S(1)}, bf16[256,2048]{1,0:T(8,128)(2,1)}, u32[]{:S(2)}, u32[]{:S(2)}) collective-permute-start(bf16[256,2048]{1,0:T(8,128)(2,1)S(1)} %fusion.12), channel_id=1, source_target_pairs={{0,1},{1,0},{2,3},{3,2},{4,5},{5,4},{6,7},{7,6},{8,9},{9,8},{10,11... | collective-permute-start | bytes 3145736 | tf_op jit(solution)/shard_map/ppermute | solution.py:33
  380.3 3.1 collective-permute-start.17
  380.3 25.6 %collective-permute-start.15 = (bf16[256,2048]{1,0:T(8,128)(2,1)S(1)}, bf16[256,2048]{1,0:T(8,128)(2,1)S(1)}, u32[]{:S(2)}, u32[]{:S(2)}) collective-permute-start(bf16[256,2048]{1,0:T(8,128)(2,1)S(1)} %fusion.13), channel_id=1, source_target_pairs={{0,1},{1,0},{2,3},{3,2},{4,5},{5,4},{6,7},{7,6},{8,9},{9,8},{10,11... | collective-permute-start | bytes 3145736 | tf_op jit(solution)/shard_map/ppermute | solution.py:33
  405.9 2.7 collective-permute-start.18
  405.9 70.4 %collective-permute-start.19 = (bf16[512,2048]{1,0:T(8,128)(2,1)}, bf16[512,2048]{1,0:T(8,128)(2,1)}, u32[]{:S(2)}, u32[]{:S(2)}) collective-permute-start(bf16[512,2048]{1,0:T(8,128)(2,1)} %param.16), channel_id=1, source_target_pairs={{2,4},{4,2},{3,5},{5,3},{10,12},{12,10},{11,13},{13,11},{18,20},{2... | collective-permute-start | bytes 6291464 | tf_op jit(solution)/shard_map/ppermute | solution.py:37
  434.6 10.2 collective-permute-start.21
  446.2 38.7 %collective-permute-start.22 = (bf16[256,2048]{1,0:T(8,128)(2,1)}, bf16[256,2048]{1,0:T(8,128)(2,1)S(1)}, u32[]{:S(2)}, u32[]{:S(2)}) collective-permute-start(bf16[256,2048]{1,0:T(8,128)(2,1)} %add_convert_fusion.5), channel_id=1, source_target_pairs={{0,1},{1,0},{2,3},{3,2},{4,5},{5,4},{6,7},{7,6},{8,9},{9,8},{10,11... | collective-permute-start | bytes 3145736 | tf_op jit(solution)/shard_map/ppermute | solution.py:33
  458.3 26.6 %collective-permute-start.20 = (bf16[256,2048]{1,0:T(8,128)(2,1)}, bf16[256,2048]{1,0:T(8,128)(2,1)}, u32[]{:S(2)}, u32[]{:S(2)}) collective-permute-start(bf16[256,2048]{1,0:T(8,128)(2,1)} %slice.205), channel_id=1, source_target_pairs={{0,4},{4,0},{1,5},{5,1},{2,6},{6,2},{3,7},{7,3},{8,12},{12,8},{9,1... | collective-permute-start | bytes 3145736 | tf_op jit(solution)/shard_map/ppermute | solution.py:33
  476.3 16.1 %collective-permute-start.26 = (bf16[256,2048]{1,0:T(8,128)(2,1)S(1)}, bf16[256,2048]{1,0:T(8,128)(2,1)S(1)}, u32[]{:S(2)}, u32[]{:S(2)}) collective-permute-start(bf16[256,2048]{1,0:T(8,128)(2,1)S(1)} %slice.213), channel_id=1, source_target_pairs={{0,4},{4,0},{1,5},{5,1},{2,6},{6,2},{3,7},{7,3},{8,12},{12,8},{9,1... | collective-permute-start | bytes 3145736 | tf_op jit(solution)/shard_map/ppermute | solution.py:33
  478.2 57.0 %copy-start.7 = (bf16[512,2048]{1,0:T(8,128)(2,1)}, bf16[512,2048]{1,0:T(8,128)(2,1)S(1)}, u32[]{:S(2)}) copy-start(bf16[512,2048]{1,0:T(8,128)(2,1)S(1)} %broadcast_select_fusion.1) | copy-start | bytes 6291460
  492.4 4.7 collective-permute-start.23
  493.8 31.9 %collective-permute-start.27 = (bf16[256,2048]{1,0:T(8,128)(2,1)}, bf16[256,2048]{1,0:T(8,128)(2,1)}, u32[]{:S(2)}, u32[]{:S(2)}) collective-permute-start(bf16[256,2048]{1,0:T(8,128)(2,1)} %add_convert_fusion.4), channel_id=1, source_target_pairs={{0,1},{1,0},{2,3},{3,2},{4,5},{5,4},{6,7},{7,6},{8,9},{9,8},{10,11... | collective-permute-start | bytes 3145736 | tf_op jit(solution)/shard_map/ppermute | solution.py:33
  495.4 30.3 %collective-permute-start.25 = (bf16[256,2048]{1,0:T(8,128)(2,1)}, bf16[256,2048]{1,0:T(8,128)(2,1)}, u32[]{:S(2)}, u32[]{:S(2)}) collective-permute-start(bf16[256,2048]{1,0:T(8,128)(2,1)} %slice.211), channel_id=1, source_target_pairs={{0,4},{4,0},{1,5},{5,1},{2,6},{6,2},{3,7},{7,3},{8,12},{12,8},{9,1... | collective-permute-start | bytes 3145736 | tf_op jit(solution)/shard_map/ppermute | solution.py:33
  495.4 47.1 %collective-permute-start.31 = (bf16[256,2048]{1,0:T(8,128)(2,1)}, bf16[256,2048]{1,0:T(8,128)(2,1)}, u32[]{:S(2)}, u32[]{:S(2)}) collective-permute-start(bf16[256,2048]{1,0:T(8,128)(2,1)} %fusion.8), channel_id=1, source_target_pairs={{0,1},{1,0},{2,3},{3,2},{4,5},{5,4},{6,7},{7,6},{8,9},{9,8},{10,11... | collective-permute-start | bytes 3145736 | tf_op jit(solution)/shard_map/ppermute | solution.py:33
  537.7 4.9 collective-permute-start.29
  537.9 31.8 %collective-permute-start.28 = (bf16[256,2048]{1,0:T(8,128)(2,1)S(1)}, bf16[256,2048]{1,0:T(8,128)(2,1)S(1)}, u32[]{:S(2)}, u32[]{:S(2)}) collective-permute-start(bf16[256,2048]{1,0:T(8,128)(2,1)S(1)} %fusion.5), channel_id=1, source_target_pairs={{0,1},{1,0},{2,3},{3,2},{4,5},{5,4},{6,7},{7,6},{8,9},{9,8},{10,11... | collective-permute-start | bytes 3145736 | tf_op jit(solution)/shard_map/ppermute | solution.py:33
  542.6 29.0 %collective-permute-start.32 = (bf16[256,2048]{1,0:T(8,128)(2,1)}, bf16[256,2048]{1,0:T(8,128)(2,1)}, u32[]{:S(2)}, u32[]{:S(2)}) collective-permute-start(bf16[256,2048]{1,0:T(8,128)(2,1)} %collective-permute-done.31), channel_id=1, source_target_pairs={{0,4},{4,0},{1,5},{5,1},{2,6},{6,2},{3,7},{7,3},{8,12},{12,8},{9,1... | collective-permute-start | bytes 3145736 | tf_op jit(solution)/shard_map/ppermute | solution.py:33
  569.6 3.3 collective-permute-start.30
  599.4 241.3 %reduce-scatter.6.cloned.1.call-start = ((), (), s32[]{:S(2)}) async-start(), calls=%async_computation.7 | async-start | bytes 10485760 | tf_op jit(solution)/shard_map/reduce_scatter | solution.py:73
  627.8 2.7 collective-permute-start.33
  631.0 26.3 %collective-permute-start.34 = (bf16[256,2048]{1,0:T(8,128)(2,1)S(1)}, bf16[256,2048]{1,0:T(8,128)(2,1)S(1)}, u32[]{:S(2)}, u32[]{:S(2)}) collective-permute-start(bf16[256,2048]{1,0:T(8,128)(2,1)S(1)} %add_convert_fusion.3), channel_id=1, source_target_pairs={{0,1},{1,0},{2,3},{3,2},{4,5},{5,4},{6,7},{7,6},{8,9},{9,8},{10,11... | collective-permute-start | bytes 3145736 | tf_op jit(solution)/shard_map/ppermute | solution.py:33
  658.7 2.7 collective-permute-start.38
  659.2 5.5 collective-permute-start.24
  662.8 29.8 %collective-permute-start.39 = (bf16[256,2048]{1,0:T(8,128)(2,1)}, bf16[256,2048]{1,0:T(8,128)(2,1)}, u32[]{:S(2)}, u32[]{:S(2)}) collective-permute-start(bf16[256,2048]{1,0:T(8,128)(2,1)} %add_convert_fusion.2), channel_id=1, source_target_pairs={{0,1},{1,0},{2,3},{3,2},{4,5},{5,4},{6,7},{7,6},{8,9},{9,8},{10,11... | collective-permute-start | bytes 3145736 | tf_op jit(solution)/shard_map/ppermute | solution.py:33
  668.0 74.3 %copy-start.21 = (bf16[256,2048]{1,0:T(8,128)(2,1)}, bf16[256,2048]{1,0:T(8,128)(2,1)S(1)}, u32[]{:S(2)}) copy-start(bf16[256,2048]{1,0:T(8,128)(2,1)S(1)} %subtract_convert_fusion.1.refs_1_.refs_0_) | copy-start | bytes 3145732
  692.6 199.8 %reduce-scatter.8.cloned.1.call-start = ((), (), s32[]{:S(2)}) async-start(), calls=%async_computation.8 | async-start | bytes 10485760 | tf_op jit(solution)/shard_map/reduce_scatter | solution.py:73
  694.1 2.7 collective-permute-start.37
  694.1 31.3 %collective-permute-start.36 = (bf16[256,2048]{1,0:T(8,128)(2,1)S(1)}, bf16[256,2048]{1,0:T(8,128)(2,1)}, u32[]{:S(2)}, u32[]{:S(2)}) collective-permute-start(bf16[256,2048]{1,0:T(8,128)(2,1)S(1)} %subtract_convert_fusion.1.refs_1_.refs_0_), channel_id=1, source_target_pairs={{0,1},{1,0},{2,3},{3,2},{4,5},{5,4},{6,7},{7,6},{8,9},{9,8},{10,11... | collective-permute-start | bytes 3145736 | tf_op jit(solution)/shard_map/ppermute | solution.py:33
  701.5 40.8 %collective-permute-start.42 = (bf16[256,2048]{1,0:T(8,128)(2,1)}, bf16[256,2048]{1,0:T(8,128)(2,1)}, u32[]{:S(2)}, u32[]{:S(2)}) collective-permute-start(bf16[256,2048]{1,0:T(8,128)(2,1)} %subtract_convert_fusion.refs_5_.refs_4_), channel_id=1, source_target_pairs={{0,1},{1,0},{2,3},{3,2},{4,5},{5,4},{6,7},{7,6},{8,9},{9,8},{10,11... | collective-permute-start | bytes 3145736 | tf_op jit(solution)/shard_map/ppermute | solution.py:33
  725.4 17.5 %copy-start.29 = (bf16[256,2048]{1,0:T(8,128)(2,1)S(1)}, bf16[256,2048]{1,0:T(8,128)(2,1)}, u32[]{:S(2)}) copy-start(bf16[256,2048]{1,0:T(8,128)(2,1)} %get-tuple-element.350) | copy-start | bytes 3145732
  742.3 7.7 collective-permute-start.35
  742.4 8.4 collective-permute-start.40
  744.4 81.3 %collective-permute-start.46 = (bf16[512,2048]{1,0:T(8,128)(2,1)}, bf16[512,2048]{1,0:T(8,128)(2,1)}, u32[]{:S(2)}, u32[]{:S(2)}) collective-permute-start(bf16[512,2048]{1,0:T(8,128)(2,1)} %pad_maximum_fusion.7), channel_id=1, source_target_pairs={{2,4},{4,2},{3,5},{5,3},{10,12},{12,10},{11,13},{13,11},{18,20},{2... | collective-permute-start | bytes 6291464 | tf_op jit(solution)/shard_map/ppermute | solution.py:37
  746.5 11.6 %collective-permute-start.41 = (bf16[256,2048]{1,0:T(8,128)(2,1)}, bf16[256,2048]{1,0:T(8,128)(2,1)}, u32[]{:S(2)}, u32[]{:S(2)}) collective-permute-start(bf16[256,2048]{1,0:T(8,128)(2,1)} %subtract_convert_fusion.refs_5_.refs_4_), channel_id=1, source_target_pairs={{0,4},{4,0},{1,5},{5,1},{2,6},{6,2},{3,7},{7,3},{8,12},{12,8},{9,1... | collective-permute-start | bytes 3145736 | tf_op jit(solution)/shard_map/ppermute | solution.py:33
  748.3 9.8 collective-permute-start.43
  750.0 24.5 %copy-start.30 = (bf16[256,2048]{1,0:T(8,128)(2,1)}, bf16[256,2048]{1,0:T(8,128)(2,1)S(1)}, u32[]{:S(2)}) copy-start(bf16[256,2048]{1,0:T(8,128)(2,1)S(1)} %get-tuple-element.252) | copy-start | bytes 3145732
  750.1 75.6 %collective-permute-start.44 = (bf16[256,2048]{1,0:T(8,128)(2,1)S(1)}, bf16[256,2048]{1,0:T(8,128)(2,1)S(1)}, u32[]{:S(2)}, u32[]{:S(2)}) collective-permute-start(bf16[256,2048]{1,0:T(8,128)(2,1)S(1)} %get-tuple-element.252), channel_id=1, source_target_pairs={{2,4},{4,2},{3,5},{5,3},{10,12},{12,10},{11,13},{13,11},{18,20},{2... | collective-permute-start | bytes 3145736 | tf_op jit(solution)/shard_map/ppermute | solution.py:37
  750.8 89.8 %collective-permute-start.45 = (bf16[256,2048]{1,0:T(8,128)(2,1)S(1)}, bf16[256,2048]{1,0:T(8,128)(2,1)S(1)}, u32[]{:S(2)}, u32[]{:S(2)}) collective-permute-start(bf16[256,2048]{1,0:T(8,128)(2,1)S(1)} %get-tuple-element.367), channel_id=1, source_target_pairs={{2,0},{6,2},{4,6},{0,4},{3,1},{7,3},{5,7},{1,5},{10,8},{14,10},{12... | collective-permute-start | bytes 3145736 | tf_op jit(solution)/shard_map/ppermute | solution.py:80
  844.1 37.5 %collective-permute-start.49 = (bf16[256,2048]{1,0:T(8,128)(2,1)}, bf16[256,2048]{1,0:T(8,128)(2,1)}, u32[]{:S(2)}, u32[]{:S(2)}) collective-permute-start(bf16[256,2048]{1,0:T(8,128)(2,1)} %get-tuple-element.275), channel_id=1, source_target_pairs={{2,4},{4,2},{3,5},{5,3},{10,12},{12,10},{11,13},{13,11},{18,20},{2... | collective-permute-start | bytes 3145736 | tf_op jit(solution)/shard_map/ppermute | solution.py:37
  845.9 46.5 %collective-permute-start.50 = (bf16[256,2048]{1,0:T(8,128)(2,1)}, bf16[256,2048]{1,0:T(8,128)(2,1)}, u32[]{:S(2)}, u32[]{:S(2)}) collective-permute-start(bf16[256,2048]{1,0:T(8,128)(2,1)} %get-tuple-element.365), channel_id=1, source_target_pairs={{2,0},{6,2},{4,6},{0,4},{3,1},{7,3},{5,7},{1,5},{10,8},{14,10},{12... | collective-permute-start | bytes 3145736 | tf_op jit(solution)/shard_map/ppermute | solution.py:80
  861.6 1.6 collective-permute-start.47
  863.9 3.8 collective-permute-start.48
  895.4 63.5 %collective-permute-start.51 = (bf16[256,2048]{1,0:T(8,128)(2,1)}, bf16[256,2048]{1,0:T(8,128)(2,1)}, u32[]{:S(2)}, u32[]{:S(2)}) collective-permute-start(bf16[256,2048]{1,0:T(8,128)(2,1)} %get-tuple-element.278), channel_id=1, source_target_pairs={{2,4},{4,2},{3,5},{5,3},{10,12},{12,10},{11,13},{13,11},{18,20},{2... | collective-permute-start | bytes 3145736 | tf_op jit(solution)/shard_map/ppermute | solution.py:37
  897.0 61.9 %collective-permute-start.52 = (bf16[256,2048]{1,0:T(8,128)(2,1)}, bf16[256,2048]{1,0:T(8,128)(2,1)}, u32[]{:S(2)}, u32[]{:S(2)}) collective-permute-start(bf16[256,2048]{1,0:T(8,128)(2,1)} %get-tuple-element.363), channel_id=1, source_target_pairs={{2,0},{6,2},{4,6},{0,4},{3,1},{7,3},{5,7},{1,5},{10,8},{14,10},{12... | collective-permute-start | bytes 3145736 | tf_op jit(solution)/shard_map/ppermute | solution.py:80
  (43 other events, 204.5 us)
Sparse Core Ops, SparseCore 0:
  145.9 93.6 all-gather.3
  241.4 87.6 all-gather.5
  331.0 87.6 all-gather.7
  599.5 86.8 reduce-scatter.3
  692.7 86.8 reduce-scatter.5
  782.5 86.3 reduce-scatter.7
